TPU v7x, 32 devices: a whole 2x2x4 slice. The times are simulated.
32 devices in a mesh: dp: 8 (over z, x), tensor: 4 (over y, core).
Axes of the slice: x: 2, y: 2, z: 4, core: 2. Of those that a mesh axis runs over, the one named last changes fastest.
Arguments:
- tokens: bfloat16 [4096, 8192], P('dp', 'tensor'), may hold values from -6 to 6
- query_weight: bfloat16 [8192, 4096], P(None, 'tensor'), may hold values from -0.0625 to 0.0625
- keyvalue_weight: bfloat16 [8192, 2048], P(None, 'tensor'), may hold values from -0.0625 to 0.0625
- adapter_down_weight: bfloat16 [256, 8192, 64], P('dp', 'tensor'), may hold values from -0.0625 to 0.0625
- adapter_up_weight: bfloat16 [256, 64, 4096], P('dp', None, 'tensor'), may hold values from -0.75 to 0.75
- keyvalue_page_store: bfloat16 [384, 64, 2048], P('dp', None, 'tensor')
- span_token_length: int32 [8, 16], P('dp'), may hold values from 1 to 128, 512 in all within a row
- adapter_owner: int32 [128, 1], P('dp'), may hold values from 0 to 7; in each aligned block of 16 rows (0 to 15, 16 to 31, ...) at most 2 rows name the same one
- adapter_local_index: int32 [128], P('dp'), may hold values from 0 to 31
- page_owner: int32 [512, 1], P('dp'), may hold values from 0 to 7; in each aligned block of 64 rows (0 to 63, 64 to 127, ...) at most 16 rows name the same one
- page_local_index: int32 [512], P('dp'), may hold values from 0 to 47
Outputs:
- attn_out: bfloat16 [4096, 4096], P('dp', 'tensor')
- new_cache: bfloat16 [4096, 2048], P('dp', 'tensor')
Inputs may be any that keep to these rules, and one draw needn't show every extreme that they name: `adapter_owner`: in each aligned block of 16 rows (the requests of one index of dp) at most 2 rows name the same holder. `page_owner`: in each aligned block of 64 rows (the pages of one index of dp) at most 16 rows name the same holder. `span_token_length`: each row sums to 512.
All inputs are finite; a program needn't handle non-finite values.
Results may differ from a plain program's by a relative error of at most 0.012.
The roundings to bfloat16 on the way count: a program that leaves them out, or rounds other values in their place, can miss the bound.
Values may be sent and summed in bfloat16 or wider, within the bound.
No kernel may reach another device: no remote copies, remote signals or barrier semaphores. Data moves between devices by JAX's collectives and lax.ppermute only.
A program may use at most 192 MiB of HBM per device.

v0:
```python
import jax
import jax.numpy as jnp
from jax import lax
from jax.sharding import PartitionSpec as P

HEAD_WIDTH = 128
ADP_CAP = 2
PAGE = 64
HITS = 4
MOST = 128


ADAPTER_SCALE = 0.5
NEGATIVE = -1e30


def bucket_positions(holder, peers, capacity):
    onehot = (holder[:, None] == jnp.arange(peers, dtype=jnp.int32)[None, :]).astype(jnp.int32)
    earlier = jnp.cumsum(onehot, axis=0) - onehot
    return holder * capacity + jnp.sum(earlier * onehot, axis=1)


def fill_requests(position, wanted, slots_total):
    match = position[None, :] == jnp.arange(slots_total, dtype=jnp.int32)[:, None]
    return jnp.sum(jnp.where(match, wanted[None, :], 0), axis=1)


def causal_mask(rows):
    steps = jnp.arange(rows, dtype=jnp.int32)
    return steps[None, :] <= steps[:, None]


def attend_joint(rows_q, prefix, fresh):
    rows = rows_q.shape[0]
    keys = jnp.concatenate([prefix[:, :, 0], fresh[:, :, 0]], axis=0)
    values = jnp.concatenate([prefix[:, :, 1], fresh[:, :, 1]], axis=0)
    visible = jnp.concatenate([jnp.ones((rows, prefix.shape[0]), bool), causal_mask(rows)], axis=1)
    scores = jnp.einsum(
        "qkgd,pkd->kgqp", rows_q, keys, preferred_element_type=jnp.float32
    ) * rows_q.shape[-1] ** (-0.5)
    scores = jnp.where(visible, scores, NEGATIVE)
    top = jnp.max(scores, axis=-1, keepdims=True)
    expo = jnp.where(visible, jnp.exp(scores - top), 0.0)
    total = jnp.sum(expo, axis=-1)
    summed = jnp.einsum(
        "kgqp,pkd->qkgd", expo.astype(jnp.bfloat16), values, preferred_element_type=jnp.float32
    )
    return summed / jnp.transpose(total, (2, 0, 1))[..., None]


def on_device(
    tokens,
    query_weight,
    keyvalue_weight,
    adapter_down_weight,
    adapter_up_weight,
    keyvalue_page_store,
    span_token_length,
    adapter_owner,
    adapter_local_index,
    page_owner,
    page_local_index,
):
    peers = lax.axis_size("dp")
    tok_rows = tokens.shape[0]
    req_count = span_token_length.shape[1]
    q_cols = query_weight.shape[1]
    kv_cols = keyvalue_weight.shape[1]
    adapter_rank_width = adapter_down_weight.shape[2]
    page_cap = max(2, 2 * page_local_index.shape[0] // peers)
    adapter_pos = bucket_positions(adapter_owner[:, 0], peers, ADP_CAP)
    adapter_wanted = fill_requests(adapter_pos, adapter_local_index, peers * ADP_CAP)
    page_pos = bucket_positions(page_owner[:, 0], peers, page_cap)
    page_wanted = fill_requests(page_pos, page_local_index, peers * page_cap)
    page_asked, adapter_requested = (
        lax.all_to_all(page_wanted, "dp", split_axis=0, concat_axis=0, tiled=True),
        lax.all_to_all(adapter_wanted, "dp", split_axis=0, concat_axis=0, tiled=True),
    )
    page_sent, down_sent, up_sent = (
        lax.all_to_all(
            keyvalue_page_store[page_asked], "dp", split_axis=0, concat_axis=0, tiled=True
        ),
        lax.all_to_all(
            adapter_down_weight[adapter_requested], "dp", split_axis=0, concat_axis=0, tiled=True
        ),
        lax.all_to_all(
            adapter_up_weight[adapter_requested], "dp", split_axis=0, concat_axis=0, tiled=True
        ),
    )
    prefix_pages = page_sent[page_pos]
    down_tiles = down_sent[adapter_pos]
    up_tiles = up_sent[adapter_pos]
    lengths = span_token_length[0]
    ends = jnp.cumsum(lengths)
    starts = ends - lengths
    steps = jnp.arange(tok_rows, dtype=jnp.int32)[:, None]
    member = ((steps >= starts[None, :]) & (steps < ends[None, :])).astype(jnp.float32)
    down_whole = lax.all_gather(down_tiles, "tensor", axis=1, tiled=True)
    piece = lax.all_gather(tokens, "tensor", axis=1, tiled=True)
    query_share = jnp.dot(piece, query_weight, preferred_element_type=jnp.float32)
    cache_part = jnp.dot(piece, keyvalue_weight, preferred_element_type=jnp.float32)
    down_part = jnp.einsum("tn,rnk->trk", piece, down_whole, preferred_element_type=jnp.float32)
    shrink = jnp.sum(member[:, :, None] * down_part, axis=1)
    up_product = (
        (member[:, :, None] * shrink[:, None, :])
        .astype(jnp.bfloat16)
        .reshape(tok_rows, req_count * adapter_rank_width)
    )
    query_correction = jnp.dot(
        up_product,
        up_tiles.reshape(req_count * adapter_rank_width, q_cols),
        preferred_element_type=jnp.float32,
    )
    query_final = (query_share + ADAPTER_SCALE * query_correction).astype(jnp.bfloat16)
    new_cache = cache_part.astype(jnp.bfloat16)
    kv_heads = kv_cols // (2 * HEAD_WIDTH)
    group = q_cols // HEAD_WIDTH // kv_heads
    prefix = prefix_pages.reshape(req_count, HITS * PAGE, kv_heads, 2, HEAD_WIDTH)
    query_pad = jnp.concatenate([query_final, jnp.zeros((MOST, q_cols), jnp.bfloat16)], axis=0)
    cache_pad = jnp.concatenate([new_cache, jnp.zeros((MOST, kv_cols), jnp.bfloat16)], axis=0)
    output = jnp.zeros((tok_rows + MOST, q_cols), jnp.bfloat16)
    for index in range(req_count):
        start = starts[index]
        rows_q = lax.dynamic_slice_in_dim(query_pad, start, MOST, 0).reshape(
            MOST, kv_heads, group, HEAD_WIDTH
        )
        fresh = lax.dynamic_slice_in_dim(cache_pad, start, MOST, 0).reshape(
            MOST, kv_heads, 2, HEAD_WIDTH
        )
        result = attend_joint(rows_q, prefix[index], fresh)
        output = lax.dynamic_update_slice_in_dim(
            output, result.reshape(MOST, q_cols).astype(jnp.bfloat16), start, 0
        )
    return (output[:tok_rows], new_cache)


def solution(mesh):
    return jax.shard_map(
        on_device,
        mesh=mesh,
        in_specs=(
            P("dp", "tensor"),
            P(None, "tensor"),
            P(None, "tensor"),
            P("dp", "tensor", None),
            P("dp", None, "tensor"),
            P("dp", None, "tensor"),
            P("dp", None),
            P("dp", None),
            P("dp"),
            P("dp", None),
            P("dp"),
        ),
        out_specs=(P("dp", "tensor"), P("dp", "tensor")),
        check_vma=False,
    )
```

profile of v0, /device:TPU:0, one launch (start us, length us, event | category | flops | bytes accessed | tf_op | source)
XLA Modules:
  0.0 658.6 jit_solution(14359589984251517636)
XLA Ops:
  8.5 13.5 %all_to_all.39 = s32[8,2,1]{1,2,0:T(1,128)S(1)} all-to-all(s32[8,2,1]{1,2,0:T(1,128)S(1)} %bitcast.886), channel_id=1, replica_groups=mesh['dp'=8,'tensor'=4] {'dp'}, dimensions={0} | all-to-all | bytes 128 | tf_op jit(solution)/shard_map/all_to_all | solution.py:77
  23.3 6.6 gather_fusion.2
  29.9 4.5 all-to-all-start.3
  34.5 93.0 %all-to-all-done.3 = bf16[16,2048,64]{1,2,0:T(8,128)(2,1)} async-done(((bf16[16,2048,64]{1,2,0:T(8,128)(2,1)}), bf16[16,2048,64]{1,2,0:T(8,128)(2,1)}, u32[]{:S(2)}, u32[]{:S(2)}) %all-to-all-start.3) | async-done | bytes 4194336 | tf_op jit(solution)/shard_map/all_to_all | solution.py:83
  127.5 4.9 gather_fusion.3
  134.2 3.6 all-to-all-start
  137.8 4.9 gather_fusion.4
  144.2 4.5 all-to-all-start.4
  149.5 6.3 gather_fusion
  155.9 40.9 %all-to-all-done.4 = bf16[16,64,1024]{2,1,0:T(8,128)(2,1)} async-done(((bf16[16,64,1024]{2,1,0:T(8,128)(2,1)}), bf16[16,64,1024]{2,1,0:T(8,128)(2,1)}, u32[]{:S(2)}, u32[]{:S(2)}) %all-to-all-start.4) | async-done | bytes 2097184 | tf_op jit(solution)/shard_map/all_to_all | solution.py:86
  196.7 5.3 all-to-all-start.1
  235.9 10.5 %convolution_convert_fusion = bf16[512,512]{0,1:T(8,128)(2,1)S(1)} fusion(bf16[512,8192]{1,0:T(8,128)(2,1)} %all-gather.4.cloned.1.call-done, bf16[8192,512]{1,0:T(8,128)(2,1)} %param.13), kind=kOutput, calls=%fused_computation.78 | convolution fusion | flops 4295229440 | bytes 17301504 | tf_op jit(solution)/shard_map/dot_general | solution.py:101
  273.1 110.6 %all-to-all-done.1 = bf16[128,64,512]{2,1,0:T(8,128)(2,1)} async-done(((bf16[128,64,512]{2,1,0:T(8,128)(2,1)}), bf16[128,64,512]{2,1,0:T(8,128)(2,1)}, u32[]{:S(2)}, u32[]{:S(2)}) %all-to-all-start.1) | async-done | bytes 8388640 | tf_op jit(solution)/shard_map/all_to_all | solution.py:80
  383.7 6.2 gather_fusion.1
  390.0 3.9 fusion.291
  456.9 14.8 %fusion.20 = f32[512,64]{0,1:T(8,128)S(1)} fusion(bf16[16,8192,64]{1,2,0:T(8,128)(2,1)} %all-gather.6.cloned.1.call-done, bf16[512,8192]{1,0:T(8,128)(2,1)} %all-gather.4.cloned.1.call-done, f32[512,16]{0,1:T(8,128)S(1)} %copy-done.47), kind=kOutput, calls=%fused_computation.28 | convolution fusion | flops 8590950400 | bytes 25329664 | tf_op jit(solution)/shard_map/tn,rnk->trk/dot_general | solution.py:102
  473.1 15.0 %fusion.19 = bf16[512,1024]{1,0:T(8,128)(2,1)S(1)} fusion(f32[512,1024,1]{1,0,2:T(8,128)S(1)} %fusion.71, bf16[512,8192]{1,0:T(8,128)(2,1)} %all-gather.4.cloned.1.call-done, bf16[8192,1024]{1,0:T(8,128)(2,1)} %param.12), kind=kOutput, calls=%fused_computation.26 | convolution fusion | flops 8591507456 | bytes 28311552 | tf_op jit(solution)/shard_map/dot_general | solution.py:100
  493.0 2.5 bitcast_select_fusion.5
  498.7 2.5 pad_dynamic-slice_fusion
  537.9 2.4 fusion.66
  543.2 2.5 fusion.64
  548.5 2.5 fusion.62
  551.2 3.4 fusion.61
  555.8 3.2 fusion.60
  560.8 3.2 fusion.59
  565.8 3.2 fusion.58
  570.8 3.1 fusion.57
  575.8 3.2 fusion.56
  580.7 3.1 fusion.55
  585.7 3.2 fusion.67
  590.7 3.2 fusion.68
  595.7 3.2 fusion.69
  605.0 2.8 dynamic_update_slice.48
  607.8 2.8 dynamic_update_slice.49
  610.5 2.7 dynamic_update_slice.50
  613.3 2.7 dynamic_update_slice.51
  616.0 2.7 dynamic_update_slice.52
  618.7 2.7 dynamic_update_slice.53
  621.5 2.8 dynamic_update_slice.54
  624.2 2.8 dynamic_update_slice.55
  627.0 2.7 dynamic_update_slice.56
  629.7 2.7 dynamic_update_slice.57
  632.5 2.7 dynamic_update_slice.58
  635.2 2.7 dynamic_update_slice.59
  637.9 2.7 dynamic_update_slice.60
  640.7 2.9 dynamic_update_slice.61
  643.6 2.8 dynamic_update_slice.62
  646.3 2.8 dynamic_update_slice.63
  (385 shorter events, 175.7 us)
Async XLA Ops:
  7.2 142.4 %copy-start = (bf16[48,64,512]{2,1,0:T(8,128)(2,1)S(1)}, bf16[48,64,512]{2,1,0:T(8,128)(2,1)}, u32[]{:S(2)}) copy-start(bf16[48,64,512]{2,1,0:T(8,128)(2,1)} %param.16) | copy-start | bytes 9437188
  7.2 228.7 %all-gather.4.cloned.1.call-start = ((), (), s32[]{:S(2)}) async-start(), calls=%async_computation.5 | async-start | bytes 10485760 | tf_op jit(solution)/shard_map/all_gather | solution.py:99
  29.9 97.6 %all-to-all-start.3 = ((bf16[16,2048,64]{1,2,0:T(8,128)(2,1)}), bf16[16,2048,64]{1,2,0:T(8,128)(2,1)}, u32[]{:S(2)}, u32[]{:S(2)}) async-start(bf16[16,2048,64]{1,2,0:T(8,128)(2,1)} %gather_fusion.2), calls=%async_computation.3 | async-start | bytes 8388608 | tf_op jit(solution)/shard_map/all_to_all | solution.py:83
  34.4 422.5 %all-gather.6.cloned.1.call-start = ((), (), s32[]{:S(2)}) async-start(), calls=%async_computation.6 | async-start | bytes 20971520 | tf_op jit(solution)/shard_map/all_gather | solution.py:98
  134.2 10.0 %all-to-all-start = ((s32[8,16,1]{1,2,0:T(1,128)}), s32[8,16,1]{1,2,0:T(1,128)S(1)}, u32[]{:S(2)}, u32[]{:S(2)}) async-start(s32[8,16,1]{1,2,0:T(1,128)} %bitcast.1), calls=%async_computation | async-start | bytes 8192 | tf_op jit(solution)/shard_map/all_to_all | solution.py:76
  144.2 52.5 %all-to-all-start.4 = ((bf16[16,64,1024]{2,1,0:T(8,128)(2,1)}), bf16[16,64,1024]{2,1,0:T(8,128)(2,1)}, u32[]{:S(2)}, u32[]{:S(2)}) async-start(bf16[16,64,1024]{2,1,0:T(8,128)(2,1)} %gather_fusion.4), calls=%async_computation.4 | async-start | bytes 4194304 | tf_op jit(solution)/shard_map/all_to_all | solution.py:86
  155.9 46.1 %copy-start.76 = (s32[1,16]{1,0:T(1,128)S(1)}, s32[1,16]{1,0:T(1,128)}, u32[]{:S(2)}) copy-start(s32[1,16]{1,0:T(1,128)} %param.17) | copy-start | bytes 196
  196.7 187.0 %all-to-all-start.1 = ((bf16[128,64,512]{2,1,0:T(8,128)(2,1)}), bf16[128,64,512]{2,1,0:T(8,128)(2,1)}, u32[]{:S(2)}, u32[]{:S(2)}) async-start(bf16[128,64,512]{2,1,0:T(8,128)(2,1)} %gather_fusion), calls=%async_computation.1 | async-start | bytes 16777216 | tf_op jit(solution)/shard_map/all_to_all | solution.py:80
  253.5 8.0 %copy-start.30 = (bf16[128,512]{0,1:T(8,128)(2,1)S(1)}, bf16[128,512]{0,1:T(8,128)(2,1)}, u32[]{:S(2)}) copy-start(bf16[128,512]{0,1:T(8,128)(2,1)} %get-tuple-element.46) | copy-start | bytes 393220
  253.5 9.4 %copy-start.29 = (bf16[128,512]{0,1:T(8,128)(2,1)S(1)}, bf16[128,512]{0,1:T(8,128)(2,1)}, u32[]{:S(2)}) copy-start(bf16[128,512]{0,1:T(8,128)(2,1)} %get-tuple-element.45) | copy-start | bytes 393220
  253.5 10.8 %copy-start.28 = (bf16[128,512]{0,1:T(8,128)(2,1)S(1)}, bf16[128,512]{0,1:T(8,128)(2,1)}, u32[]{:S(2)}) copy-start(bf16[128,512]{0,1:T(8,128)(2,1)} %get-tuple-element.44) | copy-start | bytes 393220
  453.6 3.4 copy-start.47
  498.7 3.6 copy-start.42
  501.2 2.7 copy-start.43
  543.1 2.7 copy-start.51
  543.2 2.7 copy-start.73
  543.2 2.7 copy-start.86
  548.5 2.7 copy-start.53
  548.5 2.7 copy-start.72
  551.2 4.6 copy-start.54
  551.2 4.6 copy-start.83
  555.7 5.0 copy-start.55
  555.7 5.0 copy-start.69
  555.8 5.0 copy-start.82
  560.7 5.0 copy-start.56
  560.8 5.0 copy-start.81
  565.8 5.0 copy-start.57
  565.8 5.0 copy-start.67
  565.8 5.0 copy-start.80
  570.8 5.0 copy-start.58
  570.8 5.0 copy-start.79
  575.7 5.0 copy-start.59
  575.7 5.0 copy-start.66
  580.7 5.0 copy-start.60
  585.7 5.0 copy-start.61
  585.7 5.0 copy-start.65
  590.7 5.0 copy-start.62
  595.7 5.0 copy-start.63
  595.7 5.0 copy-start.64
  601.9 3.1 copy-start.13
  601.9 5.9 copy-start.12
  601.9 8.7 %copy-start.11 = (bf16[128,1024]{1,0:T(8,128)(2,1)S(1)}, bf16[128,1024]{1,0:T(8,128)(2,1)}, u32[]{:S(2)}) copy-start(bf16[128,1024]{1,0:T(8,128)(2,1)} %copy.351) | copy-start | bytes 786436
  603.8 9.5 %copy-start.9 = (bf16[128,1024]{1,0:T(8,128)(2,1)S(1)}, bf16[128,1024]{1,0:T(8,128)(2,1)}, u32[]{:S(2)}) copy-start(bf16[128,1024]{1,0:T(8,128)(2,1)} %copy.359) | copy-start | bytes 786436
  603.8 12.2 %copy-start.7 = (bf16[128,1024]{1,0:T(8,128)(2,1)S(1)}, bf16[128,1024]{1,0:T(8,128)(2,1)}, u32[]{:S(2)}) copy-start(bf16[128,1024]{1,0:T(8,128)(2,1)} %copy.367) | copy-start | bytes 786436
  605.0 13.7 %copy-start.6 = (bf16[128,1024]{1,0:T(8,128)(2,1)S(1)}, bf16[128,1024]{1,0:T(8,128)(2,1)}, u32[]{:S(2)}) copy-start(bf16[128,1024]{1,0:T(8,128)(2,1)} %copy.375) | copy-start | bytes 786436
  621.5 16.5 %copy-start.8 = (bf16[128,1024]{1,0:T(8,128)(2,1)S(1)}, bf16[128,1024]{1,0:T(8,128)(2,1)}, u32[]{:S(2)}) copy-start(bf16[128,1024]{1,0:T(8,128)(2,1)} %copy.431) | copy-start | bytes 786436
  624.2 16.4 %copy-start.10 = (bf16[128,1024]{1,0:T(8,128)(2,1)S(1)}, bf16[128,1024]{1,0:T(8,128)(2,1)}, u32[]{:S(2)}) copy-start(bf16[128,1024]{1,0:T(8,128)(2,1)} %copy.439) | copy-start | bytes 786436
  640.7 10.7 %copy-start.1 = (bf16[48,64,512]{2,1,0:T(8,128)(2,1)S(1)}, bf16[48,64,512]{2,1,0:T(8,128)(2,1)}, u32[]{:S(2)}) copy-start(bf16[48,64,512]{2,1,0:T(8,128)(2,1)} %param.16) | copy-start | bytes 9437188
  (45 other events, 69.1 us)
Sparse Core Ops, SparseCore 0:
  9.6 60.9 all-gather.3
  132.6 105.0 all-gather.5
where the time goes:
time: 665 us; the launch traced here: 659 us
  waiting for transfers between devices  247 us (37%)
  local copies, waits for them, and re-layouts  203 us (31%)
  matrix products  129 us (19%)
  between operations  45.5 us (7%)
  starting transfers between devices  18 us (3%)
  blocking collectives  13.5 us (2%)
    all_to_all x1, waiting for transfers between devices, on_device(): lax.all_to_all(keyvalue_page_store[page_asked], 'dp', split_axis=0, conca...  111 us
    all_to_all x1, waiting for transfers between devices, on_device(): lax.all_to_all(adapter_down_weight[adapter_requested], 'dp', split_axis=0...  93 us
    unnamed x223, local copies, waits for them, and re-layouts  47.4 us
    dot_general x16, matrix products, attend_joint(): jnp.einsum('kgqp,pkd->qkgd', expo.astype(jnp.bfloat16), values, preferred...  45.5 us
    dynamic_update_slice x16, local copies, waits for them, and re-layouts, on_device(): lax.dynamic_update_slice_in_dim(output, result.reshape(MOST, q_cols).asty...  44.1 us
    all_to_all x1, waiting for transfers between devices, on_device(): lax.all_to_all(adapter_up_weight[adapter_requested], 'dp', split_axis=0,...  40.9 us
    dot_general x16, matrix products, attend_joint(): jnp.einsum('qkgd,pkd->kgqp', rows_q, keys, preferred_element_type=jnp.flo...  25.1 us
    convert_element_type x16, local copies, waits for them, and re-layouts, on_device(): result.reshape(MOST, q_cols).astype(jnp.bfloat16)  19.9 us
  transfers between devices with their start and end apart: 6, of which 4 were waited for; matrix products, arithmetic and copies ran while one was open for 21% of the time, Pallas kernels for 0%

commit v1 on v0

v1 whole, which is shorter than its diff:
```python
import functools

import jax
import jax.numpy as jnp
from jax import lax
from jax.experimental import pallas as pl
from jax.experimental.pallas import tpu as pltpu
from jax.sharding import PartitionSpec as P

HEAD_WIDTH = 128
ADP_CAP = 2
PAGE = 64
HITS = 4
MOST = 128
BLOCK = 32

ADAPTER_SCALE = 0.5
NEGATIVE = -1e30


def bucket_positions(holder, peers, capacity):
    onehot = (holder[:, None] == jnp.arange(peers, dtype=jnp.int32)[None, :]).astype(jnp.int32)
    earlier = jnp.cumsum(onehot, axis=0) - onehot
    return holder * capacity + jnp.sum(earlier * onehot, axis=1)


def fill_requests(position, wanted, slots_total):
    match = position[None, :] == jnp.arange(slots_total, dtype=jnp.int32)[:, None]
    return jnp.sum(jnp.where(match, wanted[None, :], 0), axis=1)


def attention_steps(starts, ends, total):
    first = starts // BLOCK
    count = (ends - 1) // BLOCK - first + 1
    upto = jnp.cumsum(count)
    step = jnp.minimum(jnp.arange(total, dtype=jnp.int32), upto[-1] - 1)
    request = jnp.sum((upto[None, :] <= step[:, None]).astype(jnp.int32), axis=1)
    pick = request[:, None] == jnp.arange(starts.shape[0], dtype=jnp.int32)[None, :]

    def at(values):
        return jnp.sum(jnp.where(pick, values[None, :], 0), axis=1)

    block = at(first) + step - at(upto - count)
    return jnp.stack([request, block, at(starts), at(ends)])


def attention_kernel(steps_ref, query_ref, cache_ref, pages_ref, out_ref):
    rows_total, q_cols = query_ref.shape
    kv_heads = cache_ref.shape[1] // (2 * HEAD_WIDTH)
    group = q_cols // HEAD_WIDTH // kv_heads
    window = min(rows_total, MOST + BLOCK)
    scale = HEAD_WIDTH ** -0.5
    out_ref[...] = jnp.zeros_like(out_ref)

    def step(index, carry):
        request = steps_ref[0, index]
        row = pl.multiple_of(steps_ref[1, index] * BLOCK, BLOCK)
        start = steps_ref[2, index]
        end = steps_ref[3, index]
        base = pl.multiple_of(jnp.minimum(start // BLOCK * BLOCK, rows_total - window), BLOCK)
        q_at = row + lax.broadcasted_iota(jnp.int32, (group * BLOCK, window), 0) % BLOCK
        k_at = base + lax.broadcasted_iota(jnp.int32, (group * BLOCK, window), 1)
        visible = (k_at >= start) & (k_at <= q_at)
        own_at = row + lax.broadcasted_iota(jnp.int32, (BLOCK, HEAD_WIDTH), 0)
        own = (own_at >= start) & (own_at < end)
        for head in range(kv_heads):
            at = head * 2 * HEAD_WIDTH
            wide = head * group * HEAD_WIDTH
            rows_q = jnp.concatenate(
                [
                    query_ref[pl.ds(row, BLOCK), wide + g * HEAD_WIDTH : wide + (g + 1) * HEAD_WIDTH]
                    for g in range(group)
                ],
                axis=0,
            )
            old_k = pages_ref[pl.ds(request * HITS, HITS), :, at : at + HEAD_WIDTH].reshape(HITS * PAGE, HEAD_WIDTH)
            old_v = pages_ref[
                pl.ds(request * HITS, HITS), :, at + HEAD_WIDTH : at + 2 * HEAD_WIDTH
            ].reshape(HITS * PAGE, HEAD_WIDTH)
            new_k = cache_ref[pl.ds(base, window), at : at + HEAD_WIDTH]
            new_v = cache_ref[pl.ds(base, window), at + HEAD_WIDTH : at + 2 * HEAD_WIDTH]
            dims = (((1,), (1,)), ((), ()))
            old_s = lax.dot_general(rows_q, old_k, dims, preferred_element_type=jnp.float32) * scale
            new_s = lax.dot_general(rows_q, new_k, dims, preferred_element_type=jnp.float32) * scale
            new_s = jnp.where(visible, new_s, NEGATIVE)
            top = jnp.maximum(
                jnp.max(old_s, axis=1, keepdims=True), jnp.max(new_s, axis=1, keepdims=True)
            )
            old_e = jnp.exp(old_s - top)
            new_e = jnp.where(visible, jnp.exp(new_s - top), 0.0)
            total = jnp.sum(old_e, axis=1, keepdims=True) + jnp.sum(new_e, axis=1, keepdims=True)
            summed = jnp.dot(old_e.astype(jnp.bfloat16), old_v, preferred_element_type=jnp.float32)
            summed += jnp.dot(new_e.astype(jnp.bfloat16), new_v, preferred_element_type=jnp.float32)
            result = summed / total
            for g in range(group):
                cols = slice(wide + g * HEAD_WIDTH, wide + (g + 1) * HEAD_WIDTH)
                before = out_ref[pl.ds(row, BLOCK), cols]
                mine = result[g * BLOCK : (g + 1) * BLOCK].astype(jnp.bfloat16)
                out_ref[pl.ds(row, BLOCK), cols] = jnp.where(own, mine, before)
        return carry

    lax.fori_loop(0, steps_ref.shape[1], step, 0)


def attend(query, cache, pages, starts, ends):
    rows, q_cols = query.shape
    steps_total = rows // BLOCK + starts.shape[0] - 1
    steps = attention_steps(starts, ends, steps_total)
    vmem = pl.BlockSpec(memory_space=pltpu.VMEM)
    return pl.pallas_call(
        attention_kernel,
        out_shape=jax.ShapeDtypeStruct((rows, q_cols), jnp.bfloat16),
        in_specs=[pl.BlockSpec(memory_space=pltpu.SMEM), vmem, vmem, vmem],
        out_specs=vmem,
        compiler_params=pltpu.CompilerParams(vmem_limit_bytes=40 * 1024 * 1024),
        cost_estimate=pl.CostEstimate(
            flops=4 * steps_total * BLOCK * q_cols * (HITS * PAGE + MOST + BLOCK),
            bytes_accessed=2 * (query.size * 2 + cache.size + pages.size),
            transcendentals=0,
        ),
        name="attend",
    )(steps, query, cache, pages)


def on_device(
    tokens,
    query_weight,
    keyvalue_weight,
    adapter_down_weight,
    adapter_up_weight,
    keyvalue_page_store,
    span_token_length,
    adapter_owner,
    adapter_local_index,
    page_owner,
    page_local_index,
):
    peers = lax.axis_size("dp")
    tok_rows = tokens.shape[0]
    q_cols = query_weight.shape[1]
    rank = adapter_down_weight.shape[2]
    adapter_slots = peers * ADP_CAP
    page_cap = max(2, 2 * page_local_index.shape[0] // peers)
    adapter_pos = bucket_positions(adapter_owner[:, 0], peers, ADP_CAP)
    adapter_wanted = fill_requests(adapter_pos, adapter_local_index, adapter_slots)
    page_pos = bucket_positions(page_owner[:, 0], peers, page_cap)
    page_wanted = fill_requests(page_pos, page_local_index, peers * page_cap)
    wanted = jnp.concatenate(
        [adapter_wanted.reshape(peers, ADP_CAP), page_wanted.reshape(peers, page_cap)], axis=1
    )
    asked = lax.all_to_all(wanted, "dp", split_axis=0, concat_axis=0, tiled=True)
    adapter_asked = asked[:, :ADP_CAP].reshape(-1)
    page_asked = asked[:, ADP_CAP:].reshape(-1)
    down_sent = lax.all_to_all(
        adapter_down_weight[adapter_asked], "dp", split_axis=0, concat_axis=0, tiled=True
    )
    up_sent = lax.all_to_all(
        adapter_up_weight[adapter_asked], "dp", split_axis=0, concat_axis=0, tiled=True
    )
    page_sent = lax.all_to_all(
        keyvalue_page_store[page_asked], "dp", split_axis=0, concat_axis=0, tiled=True
    )
    prefix_pages = page_sent[page_pos]

    lengths = span_token_length[0]
    ends = jnp.cumsum(lengths)
    starts = ends - lengths
    steps = jnp.arange(tok_rows, dtype=jnp.int32)[:, None]
    member = (steps >= starts[None, :]) & (steps < ends[None, :])
    slot = jnp.sum(jnp.where(member, adapter_pos[None, :], 0), axis=1)
    in_slot = slot[:, None] == jnp.arange(adapter_slots, dtype=jnp.int32)[None, :]

    down_part = jnp.einsum("tn,snk->tsk", tokens, down_sent, preferred_element_type=jnp.float32)
    shrink_part = jnp.sum(jnp.where(in_slot[:, :, None], down_part, 0.0), axis=1)
    shrink = lax.psum(shrink_part, "tensor").astype(jnp.bfloat16)

    piece = lax.all_gather(tokens, "tensor", axis=1, tiled=True)
    query_base = jnp.dot(piece, query_weight, preferred_element_type=jnp.float32)
    new_cache = jnp.dot(piece, keyvalue_weight, preferred_element_type=jnp.float32).astype(jnp.bfloat16)

    spread = jnp.where(in_slot[:, :, None], shrink[:, None, :], 0).reshape(tok_rows, adapter_slots * rank)
    correction = jnp.dot(
        spread, up_sent.reshape(adapter_slots * rank, q_cols), preferred_element_type=jnp.float32
    )
    query = (query_base + ADAPTER_SCALE * correction).astype(jnp.bfloat16)
    out = attend(query, new_cache, prefix_pages, starts, ends)
    return (out, new_cache)


def solution(mesh):
    return jax.shard_map(
        on_device,
        mesh=mesh,
        in_specs=(
            P("dp", "tensor"),
            P(None, "tensor"),
            P(None, "tensor"),
            P("dp", "tensor", None),
            P("dp", None, "tensor"),
            P("dp", None, "tensor"),
            P("dp", None),
            P("dp", None),
            P("dp"),
            P("dp", None),
            P("dp"),
        ),
        out_specs=(P("dp", "tensor"), P("dp", "tensor")),
        check_vma=False,
    )
```

time: 665 us -> 410 us (0.62)
  local copies, waits for them, and re-layouts: 203 us -> 28.4 us
  matrix products: 129 us -> 32.1 us
  between operations: 45.5 us -> 14.8 us
  Pallas kernels: 0 us -> 24.1 us
  waiting for transfers between devices: 247 us -> 262 us
  blocking collectives: 13.5 us -> 26.1 us
    dot_general x34 -> x2, matrix products: 86.7 us -> 7.42 us  [the longest x1 4.56 us: on_device(): jnp.einsum('tn,snk->tsk', tokens, down_sent, preferred_element_type=jnp.f...]
    dynamic_update_slice x16 -> x0, local copies, waits for them, and re-layouts: 44.1 us -> none  [on_device(): lax.dynamic_update_slice_in_dim(output, result.reshape(MOST, q_cols).asty...]
    unnamed x223 -> x18, local copies, waits for them, and re-layouts: 47.4 us -> 4.48 us
    squeeze x32 -> x0, local copies, waits for them, and re-layouts: 26 us -> none  [the longest x16 13.4 us: on_device(): result = attend_joint(rows_q, prefix[index], fresh)]
    all_to_all x1, waiting for transfers between devices: 111 us -> 135 us  [on_device(): lax.all_to_all(keyvalue_page_store[page_asked], 'dp', split_axis=0, conca...]
    pallas_call x0 -> x1, Pallas kernels: none -> 24.1 us  [attend(): pl.pallas_call(attention_kernel, out_shape=jax.ShapeDtypeStruct((rows, q_...]
    slice x19 -> x2, local copies, waits for them, and re-layouts: 22.3 us -> 0.59 us  [the longest x1 0.52 us: attention_steps(): step = jnp.minimum(jnp.arange(total, dtype=jnp.int32), upto[-1] - 1)]
    convert_element_type x16 -> x0, local copies, waits for them, and re-layouts: 19.9 us -> none  [on_device(): result.reshape(MOST, q_cols).astype(jnp.bfloat16)]
  transfers between devices with their start and end apart: 6 -> 4, of which waited for: 4 -> 3; matrix products, arithmetic and copies ran while one was open for 21% -> 11% of each run, Pallas kernels for 0% -> 0%
where the time goes in v1:
time: 410 us; the launch traced here: 409 us
  waiting for transfers between devices  262 us (64%)
  matrix products  32.1 us (8%)
  local copies, waits for them, and re-layouts  28.4 us (7%)
  blocking collectives  26.1 us (6%)
  Pallas kernels  24.1 us (6%)
  between operations  14.8 us (4%)
  starting transfers between devices  14 us (3%)
  other arithmetic  7.13 us (2%)
    all_to_all x1, waiting for transfers between devices, on_device(): lax.all_to_all(keyvalue_page_store[page_asked], 'dp', split_axis=0, conca...  135 us
    all_to_all x1, waiting for transfers between devices, on_device(): lax.all_to_all(adapter_down_weight[adapter_asked], 'dp', split_axis=0, co...  85.3 us
    all_to_all x1, waiting for transfers between devices, on_device(): lax.all_to_all(adapter_up_weight[adapter_asked], 'dp', split_axis=0, conc...  41 us
    pallas_call x1, Pallas kernels, attend(): pl.pallas_call(attention_kernel, out_shape=jax.ShapeDtypeStruct((rows, q_...  24.1 us
    all_to_all x1, blocking collectives, on_device(): lax.all_to_all(wanted, 'dp', split_axis=0, concat_axis=0, tiled=True)  13.5 us
    dot_general x1, matrix products, on_device(): jnp.dot(piece, query_weight, preferred_element_type=jnp.float32)  13.5 us
    psum x1, blocking collectives, on_device(): shrink = lax.psum(shrink_part, 'tensor').astype(jnp.bfloat16)  12.6 us
    dot_general x1, matrix products, on_device(): jnp.dot(piece, keyvalue_weight, preferred_element_type=jnp.float32)  11.2 us
  transfers between devices with their start and end apart: 4, of which 3 were waited for; matrix products, arithmetic and copies ran while one was open for 11% of the time, Pallas kernels for 0%

profile of v1, /device:TPU:0, one launch (start us, length us, event | category | flops | bytes accessed | tf_op | source)
XLA Modules:
  0.0 408.9 jit_solution(17266017273211437516)
XLA Ops:
  7.2 0.0 copy-start
  7.2 0.9 fusion.12
  8.1 0.1 reduce_window_sum.32
  8.2 0.8 select_reduce_fusion.1
  9.0 0.7 multiply_add_fusion
  9.7 0.7 select_reduce_fusion
  10.4 0.1 reshape.339
  10.5 0.7 fusion.19
  11.3 0.8 select_reduce_fusion.4
  12.1 0.7 multiply_add_fusion.1
  12.8 0.8 select_reduce_fusion.3
  13.5 0.1 reshape.338
  13.6 0.1 pad_add_fusion
  13.7 13.5 %all_to_all.27 = s32[8,1,18]{2,1,0:T(1,128)S(1)} all-to-all(s32[8,1,18]{2,1,0:T(1,128)S(1)} %bitcast.70), channel_id=1, replica_groups=mesh['dp'=8,'tensor'=4] {'dp'}, dimensions={0} | all-to-all | bytes 1152 | tf_op jit(solution)/shard_map/all_to_all | solution.py:151
  27.2 0.1 reshape.376
  27.3 0.1 fusion.18
  27.4 4.2 %gather_fusion.1 = bf16[16,64,1024]{2,1,0:T(8,128)(2,1)} fusion(bf16[32,64,1024]{2,1,0:T(8,128)(2,1)} %param.15, s32[1024]{0:T(1024)S(1)} %pad_clamp_fusion.2), kind=kCustom, calls=%fused_computation.1 | custom fusion | bytes 4194368 | tf_op jit(solution)/shard_map/gather | solution.py:158
  31.6 4.4 %all-to-all-start.2 = ((bf16[16,64,1024]{2,1,0:T(8,128)(2,1)}), bf16[16,64,1024]{2,1,0:T(8,128)(2,1)}, u32[]{:S(2)}, u32[]{:S(2)}) async-start(bf16[16,64,1024]{2,1,0:T(8,128)(2,1)} %gather_fusion.1), calls=%async_computation.2 | async-start | bytes 4194304 | tf_op jit(solution)/shard_map/all_to_all | solution.py:157
  36.0 6.1 %gather_fusion = bf16[16,2048,64]{1,2,0:T(8,128)(2,1)} fusion(bf16[32,2048,64]{1,2,0:T(8,128)(2,1)} %param.14, s32[1024]{0:T(1024)S(1)} %pad_clamp_fusion.2), kind=kCustom, calls=%fused_computation | custom fusion | bytes 8388672 | tf_op jit(solution)/shard_map/gather | solution.py:155
  42.1 41.0 %all-to-all-done.2 = bf16[16,64,1024]{2,1,0:T(8,128)(2,1)} async-done(((bf16[16,64,1024]{2,1,0:T(8,128)(2,1)}), bf16[16,64,1024]{2,1,0:T(8,128)(2,1)}, u32[]{:S(2)}, u32[]{:S(2)}) %all-to-all-start.2) | async-done | bytes 2097184 | tf_op jit(solution)/shard_map/all_to_all | solution.py:157
  83.0 4.6 %all-to-all-start.1 = ((bf16[16,2048,64]{1,2,0:T(8,128)(2,1)}), bf16[16,2048,64]{1,2,0:T(8,128)(2,1)}, u32[]{:S(2)}, u32[]{:S(2)}) async-start(bf16[16,2048,64]{1,2,0:T(8,128)(2,1)} %gather_fusion), calls=%async_computation.1 | async-start | bytes 8388608 | tf_op jit(solution)/shard_map/all_to_all | solution.py:154
  87.7 0.0 all-gather.2.cloned.1.call-start
  87.7 0.7 all-gather.2.cloned.1.call-update
  88.4 0.1 slice.12
  88.5 0.1 reshape.341
  88.6 6.3 %gather_fusion.2 = bf16[128,64,512]{2,1,0:T(8,128)(2,1)} fusion(bf16[48,64,512]{2,1,0:T(8,128)(2,1)S(1)} %copy-done, s32[1024]{0:T(1024)S(1)} %pad_clamp_fusion.1), kind=kCustom, calls=%fused_computation.2 | custom fusion | bytes 16777728 | tf_op jit(solution)/shard_map/gather | solution.py:161
  94.9 85.3 %all-to-all-done.1 = bf16[16,2048,64]{1,2,0:T(8,128)(2,1)} async-done(((bf16[16,2048,64]{1,2,0:T(8,128)(2,1)}), bf16[16,2048,64]{1,2,0:T(8,128)(2,1)}, u32[]{:S(2)}, u32[]{:S(2)}) %all-to-all-start.1) | async-done | bytes 4194336 | tf_op jit(solution)/shard_map/all_to_all | solution.py:154
  180.1 5.0 %all-to-all-start.3 = ((bf16[128,64,512]{2,1,0:T(8,128)(2,1)}), bf16[128,64,512]{2,1,0:T(8,128)(2,1)}, u32[]{:S(2)}, u32[]{:S(2)}) async-start(bf16[128,64,512]{2,1,0:T(8,128)(2,1)} %gather_fusion.2), calls=%async_computation.3 | async-start | bytes 16777216 | tf_op jit(solution)/shard_map/all_to_all | solution.py:160
  185.1 0.0 copy-done.7
  185.1 0.1 copy.29
  185.2 0.1 fusion.27
  185.4 0.1 reduce
  185.5 0.5 slice.21
  186.7 0.1 convert_reduce_fusion
  186.8 0.1 select_reduce_fusion.8
  187.0 0.1 select_reduce_fusion.2
  187.1 4.6 %fusion.2 = f32[512,64]{0,1:T(8,128)S(1)} fusion(bf16[16,2048,64]{1,2,0:T(8,128)(2,1)} %all-to-all-done.1, bf16[512,2048]{1,0:T(8,128)(2,1)S(1)} %copy-done.5, pred[512,16]{0,1:T(8,128)(4,1)S(1)} %iota_compare_fusion.2), kind=kOutput, calls=%fused_computation.8 | convolution fusion | flops 2148499456 | bytes 6430720 | tf_op jit(solution)/shard_map/tn,snk->tsk/dot_general | solution.py:173
  191.7 12.6 %all-reduce.1 = bf16[512,64]{0,1:T(8,128)(2,1)S(1)} all-reduce(f32[512,64]{0,1:T(8,128)S(1)} %fusion.2), channel_id=1, replica_groups=mesh['dp'=8,'tensor'=4] {'tensor'}, use_global_device_ids=true, to_apply=%region_15.16 | all-reduce | flops 32768 | bytes 196608 | tf_op jit(solution)/shard_map/psum | solution.py:175
  204.2 2.9 fusion.7
  207.1 0.0 all-gather.2.cloned.1.call-done
  207.1 11.2 %convolution_convert_fusion.cache_ref = bf16[512,512]{1,0:T(8,128)(2,1)} fusion(bf16[512,8192]{1,0:T(8,128)(2,1)} %all-gather.2.cloned.1.call-done, bf16[8192,512]{1,0:T(8,128)(2,1)} %param.13), kind=kOutput, calls=%fused_computation.11 | convolution fusion | flops 4295229440 | bytes 17301504 | tf_op jit(solution)/shard_map/dot_general | solution.py:179
  218.3 13.5 %fusion.1.query_ref = bf16[512,1024]{1,0:T(8,128)(2,1)} fusion(f32[512,1024,1]{1,0,2:T(8,128)S(1)} %fusion.7, bf16[512,8192]{1,0:T(8,128)(2,1)S(1)} %copy-done.8, bf16[8192,1024]{1,0:T(8,128)(2,1)} %param.12), kind=kOutput, calls=%fused_computation.6 | convolution fusion | flops 8591507456 | bytes 28311552 | tf_op jit(solution)/shard_map/dot_general | solution.py:178
  231.8 135.3 %all-to-all-done.3 = bf16[128,64,512]{2,1,0:T(8,128)(2,1)} async-done(((bf16[128,64,512]{2,1,0:T(8,128)(2,1)}), bf16[128,64,512]{2,1,0:T(8,128)(2,1)}, u32[]{:S(2)}, u32[]{:S(2)}) %all-to-all-start.3) | async-done | bytes 8388640 | tf_op jit(solution)/shard_map/all_to_all | solution.py:160
  367.1 6.3 %gather_fusion.3 = bf16[64,64,512]{2,1,0:T(8,128)(2,1)} fusion(bf16[128,64,512]{2,1,0:T(8,128)(2,1)} %all-to-all-done.3, s32[1024]{0:T(1024)S(1)} %pad_clamp_fusion), kind=kCustom, calls=%fused_computation.3 | custom fusion | bytes 8388864 | tf_op jit(solution)/shard_map/gather | solution.py:163
  373.4 2.2 copy-done.2
  375.6 1.2 copy-done.3
  376.9 1.0 copy-done.4
  377.9 24.1 %attend.1 = bf16[512,1024]{1,0:T(8,128)(2,1)} custom-call(s32[4,31]{1,0:T(4,128)S(1)} %pad_add_fusion.1.steps_ref, bf16[512,1024]{1,0:T(8,128)(2,1)S(1)} %copy-done.3, bf16[512,512]{1,0:T(8,128)(2,1)S(1)} %copy-done.4, bf16[64,64,512]{2,1,0:T(8,128)(2,1)S(1)} %copy-done.2), custom_call_target="tpu_custom_call" | custom-call | flops 1690304512 | bytes 6815744 | tf_op jit(solution)/shard_map/attend/pallas_call | solution.py:110
  (26 shorter events, 0.2 us)
Async XLA Ops:
  7.2 81.4 %copy-start = (bf16[48,64,512]{2,1,0:T(8,128)(2,1)S(1)}, bf16[48,64,512]{2,1,0:T(8,128)(2,1)}, u32[]{:S(2)}) copy-start(bf16[48,64,512]{2,1,0:T(8,128)(2,1)} %param.16) | copy-start | bytes 9437188
  31.6 51.4 %all-to-all-start.2 = ((bf16[16,64,1024]{2,1,0:T(8,128)(2,1)}), bf16[16,64,1024]{2,1,0:T(8,128)(2,1)}, u32[]{:S(2)}, u32[]{:S(2)}) async-start(bf16[16,64,1024]{2,1,0:T(8,128)(2,1)} %gather_fusion.1), calls=%async_computation.2 | async-start | bytes 4194304 | tf_op jit(solution)/shard_map/all_to_all | solution.py:157
  83.0 97.1 %all-to-all-start.1 = ((bf16[16,2048,64]{1,2,0:T(8,128)(2,1)}), bf16[16,2048,64]{1,2,0:T(8,128)(2,1)}, u32[]{:S(2)}, u32[]{:S(2)}) async-start(bf16[16,2048,64]{1,2,0:T(8,128)(2,1)} %gather_fusion), calls=%async_computation.1 | async-start | bytes 8388608 | tf_op jit(solution)/shard_map/all_to_all | solution.py:154
  87.7 119.5 %all-gather.2.cloned.1.call-start = ((), (), s32[]{:S(2)}) async-start(), calls=%async_computation.4 | async-start | bytes 10485760 | tf_op jit(solution)/shard_map/all_gather | solution.py:177
  94.9 90.2 %copy-start.7 = (s32[1,16]{1,0:T(1,128)S(1)}, s32[1,16]{1,0:T(1,128)}, u32[]{:S(2)}) copy-start(s32[1,16]{1,0:T(1,128)} %param.17) | copy-start | bytes 196
  94.9 92.1 %copy-start.6 = (s32[64,1]{0,1:T(1,128)S(1)}, s32[64,1]{0,1:T(1,128)}, u32[]{:S(2)}) copy-start(s32[64,1]{0,1:T(1,128)} %param.20) | copy-start | bytes 772
  94.9 92.2 %copy-start.5 = (bf16[512,2048]{1,0:T(8,128)(2,1)S(1)}, bf16[512,2048]{1,0:T(8,128)(2,1)}, u32[]{:S(2)}) copy-start(bf16[512,2048]{1,0:T(8,128)(2,1)} %param.11) | copy-start | bytes 6291460
  180.1 187.0 %all-to-all-start.3 = ((bf16[128,64,512]{2,1,0:T(8,128)(2,1)}), bf16[128,64,512]{2,1,0:T(8,128)(2,1)}, u32[]{:S(2)}, u32[]{:S(2)}) async-start(bf16[128,64,512]{2,1,0:T(8,128)(2,1)} %gather_fusion.2), calls=%async_computation.3 | async-start | bytes 16777216 | tf_op jit(solution)/shard_map/all_to_all | solution.py:160
  207.1 11.2 %copy-start.8 = (bf16[512,8192]{1,0:T(8,128)(2,1)S(1)}, bf16[512,8192]{1,0:T(8,128)(2,1)}, u32[]{:S(2)}) copy-start(bf16[512,8192]{1,0:T(8,128)(2,1)} %all-gather.2.cloned.1.call-done) | copy-start | bytes 25165828
  367.1 34.9 %copy-start.1 = (bf16[48,64,512]{2,1,0:T(8,128)(2,1)S(1)}, bf16[48,64,512]{2,1,0:T(8,128)(2,1)}, u32[]{:S(2)}) copy-start(bf16[48,64,512]{2,1,0:T(8,128)(2,1)} %param.16) | copy-start | bytes 9437188
  373.4 2.2 copy-start.2
  375.6 1.2 copy-start.3
  376.9 1.0 copy-start.4
Sparse Core Ops, SparseCore 0:
  90.1 59.6 all-gather.1

commit v2 on v1

v2 whole, which is shorter than its diff:
```python
import math

import jax
import jax.numpy as jnp
from jax import lax
from jax.experimental import pallas as pl
from jax.experimental.pallas import tpu as pltpu
from jax.sharding import PartitionSpec as P

HEAD_WIDTH = 128
ADP_CAP = 2
PAGE = 64
HITS = 4
MOST = 128
BLOCK = 32

ADAPTER_SCALE = 0.5
NEGATIVE = -1e30


def bucket_positions(holder, peers, capacity):
    onehot = (holder[:, None] == jnp.arange(peers, dtype=jnp.int32)[None, :]).astype(jnp.int32)
    earlier = jnp.cumsum(onehot, axis=0) - onehot
    return holder * capacity + jnp.sum(earlier * onehot, axis=1)


def fill_requests(position, wanted, slots_total):
    match = position[None, :] == jnp.arange(slots_total, dtype=jnp.int32)[:, None]
    return jnp.sum(jnp.where(match, wanted[None, :], 0), axis=1)


def attention_steps(starts, ends, total):
    first = starts // BLOCK
    count = (ends - 1) // BLOCK - first + 1
    upto = jnp.cumsum(count)
    step = jnp.minimum(jnp.arange(total, dtype=jnp.int32), upto[-1] - 1)
    request = jnp.sum((upto[None, :] <= step[:, None]).astype(jnp.int32), axis=1)
    pick = request[:, None] == jnp.arange(starts.shape[0], dtype=jnp.int32)[None, :]

    def at(values):
        return jnp.sum(jnp.where(pick, values[None, :], 0), axis=1)

    block = at(first) + step - at(upto - count)
    return jnp.stack([request, block, at(starts), at(ends)])


def attention_kernel(steps_ref, base_ref, spread_ref, up_ref, cache_ref, pages_ref, out_ref, query_ref):
    rows_total, q_cols = base_ref.shape
    kv_heads = cache_ref.shape[1] // (2 * HEAD_WIDTH)
    group = q_cols // HEAD_WIDTH // kv_heads
    window = min(rows_total, MOST + BLOCK)
    sharp = HEAD_WIDTH ** -0.5 * math.log2(math.e)

    def project(index, carry):
        cols = pl.ds(pl.multiple_of(index * 256, 256), 256)
        correction = jnp.dot(spread_ref[...], up_ref[:, cols], preferred_element_type=jnp.float32)
        query_ref[:, cols] = (base_ref[:, cols] + ADAPTER_SCALE * correction).astype(jnp.bfloat16)
        return carry

    lax.fori_loop(0, q_cols // 256, project, 0)

    def step(index, carry):
        request = steps_ref[0, index]
        row = pl.multiple_of(steps_ref[1, index] * BLOCK, BLOCK)
        start = steps_ref[2, index]
        end = steps_ref[3, index]
        base = pl.multiple_of(jnp.minimum(start // BLOCK * BLOCK, rows_total - window), BLOCK)
        q_at = row + lax.broadcasted_iota(jnp.int32, (group * BLOCK, window), 0) % BLOCK
        k_at = base + lax.broadcasted_iota(jnp.int32, (group * BLOCK, window), 1)
        visible = (k_at >= start) & (k_at <= q_at)
        own_at = row + lax.broadcasted_iota(jnp.int32, (BLOCK, HEAD_WIDTH), 0)
        own = (own_at >= start) & (own_at < end)
        dims = (((1,), (1,)), ((), ()))
        scores = []
        for head in range(kv_heads):
            at = head * 2 * HEAD_WIDTH
            wide = head * group * HEAD_WIDTH
            rows_q = jnp.concatenate(
                [
                    query_ref[pl.ds(row, BLOCK), wide + g * HEAD_WIDTH : wide + (g + 1) * HEAD_WIDTH]
                    for g in range(group)
                ],
                axis=0,
            )
            old_k = pages_ref[pl.ds(request * HITS, HITS), :, at : at + HEAD_WIDTH].reshape(HITS * PAGE, HEAD_WIDTH)
            new_k = cache_ref[pl.ds(base, window), at : at + HEAD_WIDTH]
            old_s = lax.dot_general(rows_q, old_k, dims, preferred_element_type=jnp.float32)
            new_s = lax.dot_general(rows_q, new_k, dims, preferred_element_type=jnp.float32)
            scores.append((old_s, jnp.where(visible, new_s, NEGATIVE)))
        weights = []
        for old_s, new_s in scores:
            top = jnp.maximum(
                jnp.max(old_s, axis=1, keepdims=True), jnp.max(new_s, axis=1, keepdims=True)
            )
            old_e = jnp.exp2((old_s - top) * sharp)
            new_e = jnp.exp2((new_s - top) * sharp)
            total = jnp.sum(old_e, axis=1, keepdims=True) + jnp.sum(new_e, axis=1, keepdims=True)
            weights.append((old_e.astype(jnp.bfloat16), new_e.astype(jnp.bfloat16), total))
        for head in range(kv_heads):
            at = head * 2 * HEAD_WIDTH + HEAD_WIDTH
            wide = head * group * HEAD_WIDTH
            old_e, new_e, total = weights[head]
            old_v = pages_ref[pl.ds(request * HITS, HITS), :, at : at + HEAD_WIDTH].reshape(HITS * PAGE, HEAD_WIDTH)
            new_v = cache_ref[pl.ds(base, window), at : at + HEAD_WIDTH]
            summed = jnp.dot(old_e, old_v, preferred_element_type=jnp.float32)
            summed += jnp.dot(new_e, new_v, preferred_element_type=jnp.float32)
            result = (summed / total).astype(jnp.bfloat16)
            for g in range(group):
                cols = slice(wide + g * HEAD_WIDTH, wide + (g + 1) * HEAD_WIDTH)
                before = out_ref[pl.ds(row, BLOCK), cols]
                out_ref[pl.ds(row, BLOCK), cols] = jnp.where(own, result[g * BLOCK : (g + 1) * BLOCK], before)
        return carry

    lax.fori_loop(0, steps_ref.shape[1], step, 0)


def attend(query_base, spread, up, cache, pages, starts, ends):
    rows, q_cols = query_base.shape
    steps_total = rows // BLOCK + starts.shape[0] - 1
    steps = attention_steps(starts, ends, steps_total)
    vmem = pl.BlockSpec(memory_space=pltpu.VMEM)
    return pl.pallas_call(
        attention_kernel,
        out_shape=jax.ShapeDtypeStruct((rows, q_cols), jnp.bfloat16),
        in_specs=[pl.BlockSpec(memory_space=pltpu.SMEM)] + [vmem] * 5,
        out_specs=vmem,
        scratch_shapes=[pltpu.VMEM((rows, q_cols), jnp.bfloat16)],
        compiler_params=pltpu.CompilerParams(vmem_limit_bytes=40 * 1024 * 1024),
        cost_estimate=pl.CostEstimate(
            flops=4 * steps_total * BLOCK * q_cols * (HITS * PAGE + MOST + BLOCK) + 2 * spread.size * q_cols,
            bytes_accessed=4 * query_base.size + 2 * (2 * spread.size + up.size + cache.size + pages.size),
            transcendentals=0,
        ),
        name="attend",
    )(steps, query_base, spread, up, cache, pages)


def on_device(
    tokens,
    query_weight,
    keyvalue_weight,
    adapter_down_weight,
    adapter_up_weight,
    keyvalue_page_store,
    span_token_length,
    adapter_owner,
    adapter_local_index,
    page_owner,
    page_local_index,
):
    peers = lax.axis_size("dp")
    half = peers // 2
    me = lax.axis_index("dp")
    tok_rows = tokens.shape[0]
    q_cols = query_weight.shape[1]
    rank = adapter_down_weight.shape[2]
    adapter_slots = peers * ADP_CAP

    def swap(array, distance):
        return lax.ppermute(array, "dp", [(peer, peer ^ distance) for peer in range(peers)])

    mirrored_store = swap(keyvalue_page_store, half)

    page_cap = max(2, 2 * page_local_index.shape[0] // peers)
    adapter_pos = bucket_positions(adapter_owner[:, 0], peers, ADP_CAP)
    adapter_wanted = fill_requests(adapter_pos, adapter_local_index, adapter_slots).reshape(peers, ADP_CAP)
    page_pos = bucket_positions(page_owner[:, 0] ^ me, peers, page_cap)
    page_wanted = fill_requests(page_pos, page_local_index, peers * page_cap).reshape(peers, page_cap)
    by_peer = page_wanted[jnp.arange(peers, dtype=jnp.int32) ^ me]
    by_mirror = page_wanted[jnp.arange(peers, dtype=jnp.int32) ^ me ^ half]
    wanted = jnp.concatenate([adapter_wanted, by_peer, by_mirror], axis=1)
    asked = lax.all_to_all(wanted, "dp", split_axis=0, concat_axis=0, tiled=True)
    adapter_asked = asked[:, :ADP_CAP].reshape(-1)
    page_asked = asked[jnp.arange(half, dtype=jnp.int32) ^ me][:, ADP_CAP:]

    near = [keyvalue_page_store[page_asked[i, :page_cap]] for i in range(half)]
    near = [near[0]] + [swap(near[i], i) for i in range(1, half)]
    far = [mirrored_store[page_asked[i, page_cap:]] for i in range(half)]
    down_rows, *far = lax.optimization_barrier((adapter_down_weight[adapter_asked], *far))
    far = [far[0]] + [swap(far[i], i) for i in range(1, half)]
    prefix_pages = jnp.concatenate(near + far, axis=0)[page_pos]

    down_sent = lax.all_to_all(down_rows, "dp", split_axis=0, concat_axis=0, tiled=True)
    up_rows, down_sent = lax.optimization_barrier((adapter_up_weight[adapter_asked], down_sent))
    up_sent = lax.all_to_all(up_rows, "dp", split_axis=0, concat_axis=0, tiled=True)

    lengths = span_token_length[0]
    ends = jnp.cumsum(lengths)
    starts = ends - lengths
    steps = jnp.arange(tok_rows, dtype=jnp.int32)[:, None]
    member = (steps >= starts[None, :]) & (steps < ends[None, :])
    slot = jnp.sum(jnp.where(member, adapter_pos[None, :], 0), axis=1)
    in_slot = slot[:, None] == jnp.arange(adapter_slots, dtype=jnp.int32)[None, :]

    down_part = jnp.einsum("tn,snk->tsk", tokens, down_sent, preferred_element_type=jnp.float32)
    shrink_part = jnp.sum(jnp.where(in_slot[:, :, None], down_part, 0.0), axis=1)
    shrink = lax.psum(shrink_part, "tensor").astype(jnp.bfloat16)
    spread = jnp.where(in_slot[:, :, None], shrink[:, None, :], 0).reshape(tok_rows, adapter_slots * rank)

    piece = lax.all_gather(tokens, "tensor", axis=1, tiled=True)
    query_base = jnp.dot(piece, query_weight, preferred_element_type=jnp.float32)
    new_cache = jnp.dot(piece, keyvalue_weight, preferred_element_type=jnp.float32).astype(jnp.bfloat16)

    up = up_sent.reshape(adapter_slots * rank, q_cols)
    out = attend(query_base, spread, up, new_cache, prefix_pages, starts, ends)
    return (out, new_cache)


def solution(mesh):
    return jax.shard_map(
        on_device,
        mesh=mesh,
        in_specs=(
            P("dp", "tensor"),
            P(None, "tensor"),
            P(None, "tensor"),
            P("dp", "tensor", None),
            P("dp", None, "tensor"),
            P("dp", None, "tensor"),
            P("dp", None),
            P("dp", None),
            P("dp"),
            P("dp", None),
            P("dp"),
        ),
        out_specs=(P("dp", "tensor"), P("dp", "tensor")),
        check_vma=False,
    )
```

time: 410 us -> 446 us (1.088)
  local copies, waits for them, and re-layouts: 28.4 us -> 63 us
  blocking collectives: 26.1 us -> 11.7 us
  starting transfers between devices: 14 us -> 25.6 us
  waiting for transfers between devices: 262 us -> 273 us
  Pallas kernels: 24.1 us -> 18.8 us
    ppermute x0 -> x7, waiting for transfers between devices: none -> 124 us  [swap(): lax.ppermute(array, 'dp', [(peer, peer ^ distance) for peer in range(peer...]
    all_to_all x3, waiting for transfers between devices: 262 us -> 149 us  [the longest x1 125 us: on_device(): lax.all_to_all(wanted, 'dp', split_axis=0, concat_axis=0, tiled=True)]
    gather x2 -> x12, local copies, waits for them, and re-layouts: 12.6 us -> 28.3 us  [the longest x4 14.1 us: on_device(): far = [mirrored_store[page_asked[i, page_cap:]] for i in range(half)]]
    unnamed x18 -> x25, local copies, waits for them, and re-layouts: 4.48 us -> 19.8 us
    all_to_all x1 -> x0, blocking collectives: 13.5 us -> none  [on_device(): lax.all_to_all(wanted, 'dp', split_axis=0, concat_axis=0, tiled=True)]
    ppermute x0 -> x7, starting transfers between devices: none -> 12.3 us  [swap(): lax.ppermute(array, 'dp', [(peer, peer ^ distance) for peer in range(peer...]
    pallas_call x1, Pallas kernels: 24.1 us -> 18.8 us  [attend(): pl.pallas_call(attention_kernel, out_shape=jax.ShapeDtypeStruct((rows, q_...]
  transfers between devices with their start and end apart: 4 -> 11, of which waited for: 3 -> 7; matrix products, arithmetic and copies ran while one was open for 11% -> 21% of each run, Pallas kernels for 0% -> 0%
where the time goes in v2:
time: 446 us; the launch traced here: 445 us
  waiting for transfers between devices  273 us (61%)
  local copies, waits for them, and re-layouts  63 us (14%)
  matrix products  29.3 us (7%)
  starting transfers between devices  25.6 us (6%)
  Pallas kernels  18.8 us (4%)
  between operations  14.9 us (3%)
  blocking collectives  11.7 us (3%)
  other arithmetic  8 us (2%)
    all_to_all x1, waiting for transfers between devices, on_device(): lax.all_to_all(wanted, 'dp', split_axis=0, concat_axis=0, tiled=True)  125 us
    ppermute x7, waiting for transfers between devices, swap(): lax.ppermute(array, 'dp', [(peer, peer ^ distance) for peer in range(peer...  124 us
    all_to_all x1, waiting for transfers between devices, on_device(): lax.all_to_all(up_rows, 'dp', split_axis=0, concat_axis=0, tiled=True)  23 us
    unnamed x25, local copies, waits for them, and re-layouts  19.8 us
    pallas_call x1, Pallas kernels, attend(): pl.pallas_call(attention_kernel, out_shape=jax.ShapeDtypeStruct((rows, q_...  18.8 us
    gather x4, local copies, waits for them, and re-layouts, on_device(): far = [mirrored_store[page_asked[i, page_cap:]] for i in range(half)]  14.1 us
    dot_general x1, matrix products, on_device(): jnp.dot(piece, query_weight, preferred_element_type=jnp.float32)  13.6 us
    ppermute x7, starting transfers between devices, swap(): lax.ppermute(array, 'dp', [(peer, peer ^ distance) for peer in range(peer...  12.3 us
  transfers between devices with their start and end apart: 11, of which 7 were waited for; matrix products, arithmetic and copies ran while one was open for 21% of the time, Pallas kernels for 0%

profile of v2, /device:TPU:0, one launch (start us, length us, event | category | flops | bytes accessed | tf_op | source)
XLA Modules:
  0.0 444.7 jit_solution(2142326937218155502)
XLA Ops:
  7.2 0.7 all-gather.2.cloned.1.call-update
  7.9 4.1 collective-permute-start
  13.7 0.8 select_reduce_fusion
  15.7 0.7 fusion.20
  16.4 0.8 select_reduce_fusion.4
  17.9 0.8 select_reduce_fusion.3
  19.5 3.8 all-to-all-start
  23.3 125.5 %all-to-all-done = s32[8,1,34]{2,1,0:T(1,128)S(1)} async-done(((s32[8,1,34]{2,1,0:T(1,128)}), s32[8,1,34]{2,1,0:T(1,128)S(1)}, u32[]{:S(2)}, u32[]{:S(2)}) %all-to-all-start) | async-done | bytes 1120 | tf_op jit(solution)/shard_map/all_to_all | solution.py:172
  149.9 6.1 %gather_fusion.3 = bf16[16,2048,64]{1,2,0:T(8,128)(2,1)} fusion(bf16[32,2048,64]{1,2,0:T(8,128)(2,1)} %param.14, s32[1024]{0:T(1024)S(1)} %pad_clamp_fusion.10), kind=kCustom, calls=%fused_computation.3 | custom fusion | bytes 8388672 | tf_op jit(solution)/shard_map/gather | solution.py:179
  156.6 3.6 gather_fusion.5
  160.2 3.5 gather_fusion.6
  163.7 3.5 gather_fusion.7
  167.1 3.6 gather_fusion.8
  170.7 4.9 %all-to-all-start.1 = ((bf16[16,2048,64]{1,2,0:T(8,128)(2,1)}), bf16[16,2048,64]{1,2,0:T(8,128)(2,1)}, u32[]{:S(2)}, u32[]{:S(2)}) async-start(bf16[16,2048,64]{1,2,0:T(8,128)(2,1)} %gather_fusion.3), calls=%async_computation.1 | async-start | bytes 8388608 | tf_op jit(solution)/shard_map/all_to_all | solution.py:183
  177.6 1.6 gather_fusion.10
  179.2 2.0 collective-permute-start.1
  181.5 1.6 gather_fusion.11
  183.1 1.5 collective-permute-start.2
  184.8 1.6 gather_fusion.12
  186.4 2.0 collective-permute-start.4
  188.5 1.5 collective-permute-start.5
  190.1 56.8 %collective-permute-done.1 = bf16[16,64,512]{2,1,0:T(8,128)(2,1)} collective-permute-done((bf16[16,64,512]{2,1,0:T(8,128)(2,1)}, bf16[16,64,512]{2,1,0:T(8,128)(2,1)}, u32[]{:S(2)}, u32[]{:S(2)}) %collective-permute-start.1) | collective-permute-done | bytes 1048608 | tf_op jit(solution)/shard_map/ppermute | solution.py:160
  246.9 1.2 collective-permute-start.6
  248.2 1.6 gather_fusion.9
  249.7 4.3 gather_fusion.2
  254.0 2.4 constant_dynamic-update-slice_fusion.7
  256.4 2.3 constant_dynamic-update-slice_fusion.6
  258.7 10.7 %collective-permute-done.2 = bf16[16,64,512]{2,1,0:T(8,128)(2,1)} collective-permute-done((bf16[16,64,512]{2,1,0:T(8,128)(2,1)}, bf16[16,64,512]{2,1,0:T(8,128)(2,1)}, u32[]{:S(2)}, u32[]{:S(2)}) %collective-permute-start.2) | collective-permute-done | bytes 1048608 | tf_op jit(solution)/shard_map/ppermute | solution.py:160
  269.4 2.3 constant_dynamic-update-slice_fusion.5
  271.7 20.9 %collective-permute-done.3 = bf16[16,64,512]{2,1,0:T(8,128)(2,1)} collective-permute-done((bf16[16,64,512]{2,1,0:T(8,128)(2,1)}, bf16[16,64,512]{2,1,0:T(8,128)(2,1)}, u32[]{:S(2)}, u32[]{:S(2)}) %collective-permute-start.3) | collective-permute-done | bytes 1048608 | tf_op jit(solution)/shard_map/ppermute | solution.py:160
  292.6 2.3 constant_dynamic-update-slice_fusion.4
  294.9 1.1 constant_dynamic-update-slice_fusion.3
  296.0 2.3 constant_dynamic-update-slice_fusion.2
  298.3 16.0 %collective-permute-done.5 = bf16[16,64,512]{2,1,0:T(8,128)(2,1)} collective-permute-done((bf16[16,64,512]{2,1,0:T(8,128)(2,1)}, bf16[16,64,512]{2,1,0:T(8,128)(2,1)}, u32[]{:S(2)}, u32[]{:S(2)}) %collective-permute-start.5) | collective-permute-done | bytes 1048608 | tf_op jit(solution)/shard_map/ppermute | solution.py:160
  314.3 2.3 constant_dynamic-update-slice_fusion.1
  316.6 19.9 %collective-permute-done.6 = bf16[16,64,512]{2,1,0:T(8,128)(2,1)} collective-permute-done((bf16[16,64,512]{2,1,0:T(8,128)(2,1)}, bf16[16,64,512]{2,1,0:T(8,128)(2,1)}, u32[]{:S(2)}, u32[]{:S(2)}) %collective-permute-start.6) | collective-permute-done | bytes 1048608 | tf_op jit(solution)/shard_map/ppermute | solution.py:160
  336.5 2.3 constant_dynamic-update-slice_fusion
  338.8 6.2 %gather_fusion.13 = bf16[64,64,512]{2,1,0:T(8,128)(2,1)} fusion(bf16[128,64,512]{2,1,0:T(8,128)(2,1)} %constant_dynamic-update-slice_fusion, s32[1024]{0:T(1024)S(1)} %pad_clamp_fusion), kind=kCustom, calls=%fused_computation.13 | custom fusion | bytes 8388864 | tf_op jit(solution)/shard_map/gather | solution.py:181
  345.0 4.6 %fusion = f32[512,64]{0,1:T(8,128)S(1)} fusion(bf16[16,2048,64]{1,2,0:T(8,128)(2,1)} %all-to-all-done.1, bf16[512,2048]{1,0:T(8,128)(2,1)S(1)} %copy-done.5, pred[512,16]{0,1:T(8,128)(4,1)S(1)} %iota_compare_fusion.2), kind=kOutput, calls=%fused_computation.15 | convolution fusion | flops 2148499456 | bytes 6430720 | tf_op jit(solution)/shard_map/tn,snk->tsk/dot_general | solution.py:195
  349.5 11.7 %all-reduce.1 = bf16[512,64]{0,1:T(8,128)(2,1)S(1)} all-reduce(f32[512,64]{0,1:T(8,128)S(1)} %fusion), channel_id=1, replica_groups=mesh['dp'=8,'tensor'=4] {'tensor'}, use_global_device_ids=true, to_apply=%region_15.16 | all-reduce | flops 32768 | bytes 196608 | tf_op jit(solution)/shard_map/psum | solution.py:197
  361.9 4.6 %all-to-all-start.2 = ((bf16[16,64,1024]{2,1,0:T(8,128)(2,1)}), bf16[16,64,1024]{2,1,0:T(8,128)(2,1)S(1)}, u32[]{:S(2)}, u32[]{:S(2)}) async-start(bf16[16,64,1024]{2,1,0:T(8,128)(2,1)} %gather_fusion.2), calls=%async_computation.2 | async-start | bytes 4194304 | tf_op jit(solution)/shard_map/all_to_all | solution.py:185
  366.5 11.2 %convolution_convert_fusion.cache_ref = bf16[512,512]{1,0:T(8,128)(2,1)} fusion(bf16[512,8192]{1,0:T(8,128)(2,1)} %all-gather.2.cloned.1.call-done, bf16[8192,512]{1,0:T(8,128)(2,1)} %param.13), kind=kOutput, calls=%fused_computation.18 | convolution fusion | flops 4295229440 | bytes 17301504 | tf_op jit(solution)/shard_map/dot_general | solution.py:202
  377.7 13.6 %fusion.31.base_ref = f32[512,1024]{1,0:T(8,128)} fusion(bf16[512,8192]{1,0:T(8,128)(2,1)S(1)} %copy-done.8, bf16[8192,1024]{1,0:T(8,128)(2,1)} %param.12), kind=kOutput, calls=%fused_computation.137 | convolution fusion | flops 8589934592 | bytes 27262976 | tf_op jit(solution)/shard_map/dot_general | solution.py:201
  391.2 23.0 %all-to-all-done.2 = bf16[16,64,1024]{2,1,0:T(8,128)(2,1)S(1)} async-done(((bf16[16,64,1024]{2,1,0:T(8,128)(2,1)}), bf16[16,64,1024]{2,1,0:T(8,128)(2,1)S(1)}, u32[]{:S(2)}, u32[]{:S(2)}) %all-to-all-start.2) | async-done | bytes 2097184 | tf_op jit(solution)/shard_map/all_to_all | solution.py:185
  414.2 2.2 copy-done
  416.4 1.6 copy-done.1
  418.0 1.0 copy-done.2
  419.1 18.8 %attend.1 = bf16[512,1024]{1,0:T(8,128)(2,1)} custom-call(s32[4,31]{1,0:T(4,128)S(1)} %pad_add_fusion.1.steps_ref, f32[512,1024]{1,0:T(8,128)S(1)} %copy-done.1, bf16[512,1024]{1,0:T(8,128)(2,1)S(1)} %copy.134.spread_ref, bf16[1024,1024]{1,0:T(8,128)(2,1)S(1)} %bitcast.85, bf16[512,512]{1,0:T(8,128)(2,1)S(1)} %copy-done.2, bf16[64,64,512]{2,1,0:T(8,128)(2,1)S(1)} %copy-done), custom_call_target="tpu_custom_call" | custom-call | flops 2764046336 | bytes 11010048 | tf_op jit(solution)/shard_map/attend/pallas_call | solution.py:122
  (85 shorter events, 8.8 us)
Async XLA Ops:
  7.2 359.3 %all-gather.2.cloned.1.call-start = ((), (), s32[]{:S(2)}) async-start(), calls=%async_computation.3 | async-start | bytes 10485760 | tf_op jit(solution)/shard_map/all_gather | solution.py:200
  7.9 148.7 %collective-permute-start = (bf16[48,64,512]{2,1,0:T(8,128)(2,1)}, bf16[48,64,512]{2,1,0:T(8,128)(2,1)}, u32[]{:S(2)}, u32[]{:S(2)}) collective-permute-start(bf16[48,64,512]{2,1,0:T(8,128)(2,1)} %param.16), channel_id=1, source_target_pairs={{0,16},{4,20},{8,24},{12,28},{16,0},{20,4},{24,8},{28,12},{1,17},{... | collective-permute-start | bytes 9437192 | tf_op jit(solution)/shard_map/ppermute | solution.py:160
  19.5 129.3 %all-to-all-start = ((s32[8,1,34]{2,1,0:T(1,128)}), s32[8,1,34]{2,1,0:T(1,128)S(1)}, u32[]{:S(2)}, u32[]{:S(2)}) async-start(s32[8,1,34]{2,1,0:T(1,128)} %bitcast.16), calls=%async_computation | async-start | bytes 8192 | tf_op jit(solution)/shard_map/all_to_all | solution.py:172
  156.5 19.1 %copy-start.6 = (s32[1,16]{1,0:T(1,128)S(1)}, s32[1,16]{1,0:T(1,128)}, u32[]{:S(2)}) copy-start(s32[1,16]{1,0:T(1,128)} %param.17) | copy-start | bytes 196
  156.5 20.8 %copy-start.7 = (s32[64,1]{0,1:T(1,128)S(1)}, s32[64,1]{0,1:T(1,128)}, u32[]{:S(2)}) copy-start(s32[64,1]{0,1:T(1,128)} %param.20) | copy-start | bytes 772
  156.6 21.1 %copy-start.3 = (bf16[48,64,512]{2,1,0:T(8,128)(2,1)S(1)}, bf16[48,64,512]{2,1,0:T(8,128)(2,1)}, u32[]{:S(2)}) copy-start(bf16[48,64,512]{2,1,0:T(8,128)(2,1)} %param.16) | copy-start | bytes 9437188
  170.7 174.3 %all-to-all-start.1 = ((bf16[16,2048,64]{1,2,0:T(8,128)(2,1)}), bf16[16,2048,64]{1,2,0:T(8,128)(2,1)}, u32[]{:S(2)}, u32[]{:S(2)}) async-start(bf16[16,2048,64]{1,2,0:T(8,128)(2,1)} %gather_fusion.3), calls=%async_computation.1 | async-start | bytes 8388608 | tf_op jit(solution)/shard_map/all_to_all | solution.py:183
  179.2 67.7 %collective-permute-start.1 = (bf16[16,64,512]{2,1,0:T(8,128)(2,1)}, bf16[16,64,512]{2,1,0:T(8,128)(2,1)}, u32[]{:S(2)}, u32[]{:S(2)}) collective-permute-start(bf16[16,64,512]{2,1,0:T(8,128)(2,1)} %gather_fusion.10), channel_id=1, source_target_pairs={{0,4},{4,0},{8,12},{12,8},{16,20},{20,16},{24,28},{28,24},{1,5},{5... | collective-permute-start | bytes 3145736 | tf_op jit(solution)/shard_map/ppermute | solution.py:160
  183.1 86.3 %collective-permute-start.2 = (bf16[16,64,512]{2,1,0:T(8,128)(2,1)}, bf16[16,64,512]{2,1,0:T(8,128)(2,1)}, u32[]{:S(2)}, u32[]{:S(2)}) collective-permute-start(bf16[16,64,512]{2,1,0:T(8,128)(2,1)} %gather_fusion.11), channel_id=1, source_target_pairs={{0,8},{4,12},{8,0},{12,4},{16,24},{20,28},{24,16},{28,20},{1,9},{5... | collective-permute-start | bytes 3145736 | tf_op jit(solution)/shard_map/ppermute | solution.py:160
  186.4 106.2 %collective-permute-start.3 = (bf16[16,64,512]{2,1,0:T(8,128)(2,1)}, bf16[16,64,512]{2,1,0:T(8,128)(2,1)}, u32[]{:S(2)}, u32[]{:S(2)}) collective-permute-start(bf16[16,64,512]{2,1,0:T(8,128)(2,1)} %gather_fusion.12), channel_id=1, source_target_pairs={{0,12},{4,8},{8,4},{12,0},{16,28},{20,24},{24,20},{28,16},{1,13},{... | collective-permute-start | bytes 3145736 | tf_op jit(solution)/shard_map/ppermute | solution.py:160
  186.4 109.6 %collective-permute-start.4 = (bf16[16,64,512]{2,1,0:T(8,128)(2,1)}, bf16[16,64,512]{2,1,0:T(8,128)(2,1)}, u32[]{:S(2)}, u32[]{:S(2)}) collective-permute-start(bf16[16,64,512]{2,1,0:T(8,128)(2,1)} %gather_fusion.6), channel_id=1, source_target_pairs={{0,4},{4,0},{8,12},{12,8},{16,20},{20,16},{24,28},{28,24},{1,5},{5... | collective-permute-start | bytes 3145736 | tf_op jit(solution)/shard_map/ppermute | solution.py:160
  188.5 125.8 %collective-permute-start.5 = (bf16[16,64,512]{2,1,0:T(8,128)(2,1)}, bf16[16,64,512]{2,1,0:T(8,128)(2,1)}, u32[]{:S(2)}, u32[]{:S(2)}) collective-permute-start(bf16[16,64,512]{2,1,0:T(8,128)(2,1)} %gather_fusion.7), channel_id=1, source_target_pairs={{0,8},{4,12},{8,0},{12,4},{16,24},{20,28},{24,16},{28,20},{1,9},{5... | collective-permute-start | bytes 3145736 | tf_op jit(solution)/shard_map/ppermute | solution.py:160
  246.9 89.6 %collective-permute-start.6 = (bf16[16,64,512]{2,1,0:T(8,128)(2,1)}, bf16[16,64,512]{2,1,0:T(8,128)(2,1)}, u32[]{:S(2)}, u32[]{:S(2)}) collective-permute-start(bf16[16,64,512]{2,1,0:T(8,128)(2,1)} %gather_fusion.8), channel_id=1, source_target_pairs={{0,12},{4,8},{8,4},{12,0},{16,28},{20,24},{24,20},{28,16},{1,13},{... | collective-permute-start | bytes 3145736 | tf_op jit(solution)/shard_map/ppermute | solution.py:160
  249.7 45.1 %copy-start.4 = (bf16[16,64,512]{2,1,0:T(8,128)(2,1)S(1)}, bf16[16,64,512]{2,1,0:T(8,128)(2,1)}, u32[]{:S(2)}) copy-start(bf16[16,64,512]{2,1,0:T(8,128)(2,1)} %gather_fusion.5) | copy-start | bytes 3145732
  294.9 50.1 %copy-start.5 = (bf16[512,2048]{1,0:T(8,128)(2,1)S(1)}, bf16[512,2048]{1,0:T(8,128)(2,1)}, u32[]{:S(2)}) copy-start(bf16[512,2048]{1,0:T(8,128)(2,1)} %param.11) | copy-start | bytes 6291460
  361.9 52.4 %all-to-all-start.2 = ((bf16[16,64,1024]{2,1,0:T(8,128)(2,1)}), bf16[16,64,1024]{2,1,0:T(8,128)(2,1)S(1)}, u32[]{:S(2)}, u32[]{:S(2)}) async-start(bf16[16,64,1024]{2,1,0:T(8,128)(2,1)} %gather_fusion.2), calls=%async_computation.2 | async-start | bytes 4194304 | tf_op jit(solution)/shard_map/all_to_all | solution.py:185
  366.5 11.2 %copy-start.8 = (bf16[512,8192]{1,0:T(8,128)(2,1)S(1)}, bf16[512,8192]{1,0:T(8,128)(2,1)}, u32[]{:S(2)}) copy-start(bf16[512,8192]{1,0:T(8,128)(2,1)} %all-gather.2.cloned.1.call-done) | copy-start | bytes 25165828
  414.2 2.2 copy-start
  416.4 1.6 copy-start.1
  418.0 1.0 copy-start.2
Sparse Core Ops, SparseCore 0:
  9.6 61.0 all-gather.1

commit v3 on v2

v3 whole, which is shorter than its diff:
```python
import math

import jax
import jax.numpy as jnp
from jax import lax
from jax.experimental import pallas as pl
from jax.experimental.pallas import tpu as pltpu
from jax.sharding import PartitionSpec as P

HEAD_WIDTH = 128
ADP_CAP = 2
PAGE = 64
HITS = 4
MOST = 128
BLOCK = 32
TOGETHER = 4

ADAPTER_SCALE = 0.5
NEGATIVE = -1e30


def earlier_alike(owner):
    count = owner.shape[-1]
    ahead = jnp.arange(count, dtype=jnp.int32)[None, :] < jnp.arange(count, dtype=jnp.int32)[:, None]
    alike = owner[..., None, :] == owner[..., :, None]
    return jnp.sum((alike & ahead).astype(jnp.int32), axis=-1)


def asked_of(holder, owner, order, local, capacity):
    place = jnp.arange(capacity, dtype=jnp.int32)[None, :, None]
    match = (owner[:, None, :] == holder) & (order[:, None, :] == place)
    return jnp.sum(jnp.where(match, local[:, None, :], 0), axis=2)


def attention_steps(starts, ends, total):
    first = starts // BLOCK
    count = (ends - 1) // BLOCK - first + 1
    upto = jnp.cumsum(count)
    step = jnp.minimum(jnp.arange(total, dtype=jnp.int32), upto[-1] - 1)
    request = jnp.sum((upto[None, :] <= step[:, None]).astype(jnp.int32), axis=1)
    pick = request[:, None] == jnp.arange(starts.shape[0], dtype=jnp.int32)[None, :]

    def at(values):
        return jnp.sum(jnp.where(pick, values[None, :], 0), axis=1)

    block = at(first) + step - at(upto - count)
    return jnp.stack([request, block, at(starts), at(ends)])


def attention_kernel(
    steps_ref, spread_ref, up_ref, base_hbm, cache_hbm, pages_hbm, out_ref, query_ref, base_ref, cache_ref, pages_ref, sems
):
    copies = [
        pltpu.make_async_copy(base_hbm, base_ref, sems.at[0]),
        pltpu.make_async_copy(cache_hbm, cache_ref, sems.at[1]),
        pltpu.make_async_copy(pages_hbm, pages_ref, sems.at[2]),
    ]
    for copy in copies:
        copy.start()
    rows_total, q_cols = base_ref.shape
    kv_heads = cache_ref.shape[1] // (2 * HEAD_WIDTH)
    group = q_cols // HEAD_WIDTH // kv_heads
    window = min(rows_total, MOST + BLOCK)
    sharp = HEAD_WIDTH ** -0.5 * math.log2(math.e)
    copies[0].wait()

    def project(index, carry):
        cols = pl.ds(pl.multiple_of(index * 256, 256), 256)
        correction = jnp.dot(spread_ref[...], up_ref[:, cols], preferred_element_type=jnp.float32)
        query_ref[:, cols] = (base_ref[:, cols] + ADAPTER_SCALE * correction).astype(jnp.bfloat16)
        return carry

    lax.fori_loop(0, q_cols // 256, project, 0)

    copies[1].wait()
    copies[2].wait()
    dims = (((1,), (1,)), ((), ()))

    def several(turn, carry):
        places = []
        for lane in range(TOGETHER):
            index = turn * TOGETHER + lane
            row = pl.multiple_of(steps_ref[1, index] * BLOCK, BLOCK)
            start = steps_ref[2, index]
            base = pl.multiple_of(jnp.minimum(start // BLOCK * BLOCK, rows_total - window), BLOCK)
            old = pl.ds(steps_ref[0, index] * HITS, HITS)
            places.append((row, pl.ds(base, window), old, base, start, steps_ref[3, index]))
        chains = [(place, head) for place in places for head in range(kv_heads)]
        scores = []
        for (row, new, old, base, start, _), head in chains:
            at = head * 2 * HEAD_WIDTH
            wide = head * group * HEAD_WIDTH
            q_at = row + lax.broadcasted_iota(jnp.int32, (group * BLOCK, window), 0) % BLOCK
            k_at = base + lax.broadcasted_iota(jnp.int32, (group * BLOCK, window), 1)
            visible = (k_at >= start) & (k_at <= q_at)
            rows_q = jnp.concatenate(
                [
                    query_ref[pl.ds(row, BLOCK), wide + g * HEAD_WIDTH : wide + (g + 1) * HEAD_WIDTH]
                    for g in range(group)
                ],
                axis=0,
            )
            old_k = pages_ref[old, :, at : at + HEAD_WIDTH].reshape(HITS * PAGE, HEAD_WIDTH)
            new_k = cache_ref[new, at : at + HEAD_WIDTH]
            old_s = lax.dot_general(rows_q, old_k, dims, preferred_element_type=jnp.float32)
            new_s = lax.dot_general(rows_q, new_k, dims, preferred_element_type=jnp.float32)
            scores.append((old_s, jnp.where(visible, new_s, NEGATIVE)))
        weights = []
        for old_s, new_s in scores:
            top = jnp.maximum(
                jnp.max(old_s, axis=1, keepdims=True), jnp.max(new_s, axis=1, keepdims=True)
            )
            old_e = jnp.exp2((old_s - top) * sharp)
            new_e = jnp.exp2((new_s - top) * sharp)
            total = jnp.sum(old_e, axis=1, keepdims=True) + jnp.sum(new_e, axis=1, keepdims=True)
            weights.append((old_e.astype(jnp.bfloat16), new_e.astype(jnp.bfloat16), total))
        results = []
        for ((_, new, old, _, _, _), head), (old_e, new_e, total) in zip(chains, weights):
            at = head * 2 * HEAD_WIDTH + HEAD_WIDTH
            old_v = pages_ref[old, :, at : at + HEAD_WIDTH].reshape(HITS * PAGE, HEAD_WIDTH)
            new_v = cache_ref[new, at : at + HEAD_WIDTH]
            summed = jnp.dot(old_e, old_v, preferred_element_type=jnp.float32)
            summed += jnp.dot(new_e, new_v, preferred_element_type=jnp.float32)
            results.append((summed / total).astype(jnp.bfloat16))
        for ((row, _, _, _, start, end), head), result in zip(chains, results):
            own_at = row + lax.broadcasted_iota(jnp.int32, (BLOCK, HEAD_WIDTH), 0)
            own = (own_at >= start) & (own_at < end)
            for g in range(group):
                col = (head * group + g) * HEAD_WIDTH
                cols = slice(col, col + HEAD_WIDTH)
                before = out_ref[pl.ds(row, BLOCK), cols]
                out_ref[pl.ds(row, BLOCK), cols] = jnp.where(own, result[g * BLOCK : (g + 1) * BLOCK], before)
        return carry

    lax.fori_loop(0, steps_ref.shape[1] // TOGETHER, several, 0)


def attend(query_base, spread, up, cache, pages, starts, ends):
    rows, q_cols = query_base.shape
    steps_total = -(-(rows // BLOCK + starts.shape[0] - 1) // TOGETHER) * TOGETHER
    steps = attention_steps(starts, ends, steps_total)
    vmem = pl.BlockSpec(memory_space=pltpu.VMEM)
    return pl.pallas_call(
        attention_kernel,
        out_shape=jax.ShapeDtypeStruct((rows, q_cols), jnp.bfloat16),
        in_specs=[pl.BlockSpec(memory_space=pltpu.SMEM)] + [vmem] * 2 + [pl.BlockSpec(memory_space=pl.ANY)] * 3,
        out_specs=vmem,
        scratch_shapes=[
            pltpu.VMEM((rows, q_cols), jnp.bfloat16),
            pltpu.VMEM(query_base.shape, query_base.dtype),
            pltpu.VMEM(cache.shape, cache.dtype),
            pltpu.VMEM(pages.shape, pages.dtype),
            pltpu.SemaphoreType.DMA((3,)),
        ],
        compiler_params=pltpu.CompilerParams(vmem_limit_bytes=48 * 1024 * 1024),
        cost_estimate=pl.CostEstimate(
            flops=4 * steps_total * BLOCK * q_cols * (HITS * PAGE + MOST + BLOCK) + 2 * spread.size * q_cols,
            bytes_accessed=4 * query_base.size + 2 * (2 * spread.size + up.size + cache.size + pages.size),
            transcendentals=0,
        ),
        name="attend",
    )(steps, spread, up, query_base, cache, pages)


def on_device(
    tokens,
    query_weight,
    keyvalue_weight,
    adapter_down_weight,
    adapter_up_weight,
    keyvalue_page_store,
    span_token_length,
    adapter_owner,
    adapter_local_index,
    page_owner,
    page_local_index,
):
    peers = lax.axis_size("dp")
    half = peers // 2
    me = lax.axis_index("dp")
    tok_rows = tokens.shape[0]
    q_cols = query_weight.shape[1]
    rank = adapter_down_weight.shape[2]
    adapter_slots = peers * ADP_CAP

    def swap(array, distance):
        return lax.ppermute(array, "dp", [(peer, peer ^ distance) for peer in range(peers)])

    page_count = page_local_index.shape[0]
    request_count = adapter_local_index.shape[0]
    raw = jnp.concatenate([page_owner[:, 0], page_local_index, adapter_owner[:, 0], adapter_local_index])
    everyone = lax.all_to_all(
        jnp.broadcast_to(raw[None], (peers, raw.shape[0])), "dp", split_axis=0, concat_axis=0, tiled=True
    )
    store, down_store, everyone = lax.optimization_barrier((keyvalue_page_store, adapter_down_weight, everyone))
    mirrored_store = swap(store, half)

    page_cap = max(2, 2 * page_count // peers)
    group = everyone[jnp.arange(half, dtype=jnp.int32) ^ me]
    group_owner = group[:, :page_count]
    group_local = group[:, page_count : 2 * page_count]
    group_order = earlier_alike(group_owner)
    near_asked = asked_of(me, group_owner, group_order, group_local, page_cap)
    far_asked = asked_of(me ^ half, group_owner, group_order, group_local, page_cap)
    all_owner = everyone[:, 2 * page_count : 2 * page_count + request_count]
    all_local = everyone[:, 2 * page_count + request_count :]
    adapter_asked = asked_of(me, all_owner, earlier_alike(all_owner), all_local, ADP_CAP).reshape(-1)
    adapter_pos = adapter_owner[:, 0] * ADP_CAP + earlier_alike(adapter_owner[:, 0])
    page_pos = (page_owner[:, 0] ^ me) * page_cap + earlier_alike(page_owner[:, 0])

    near = [store[near_asked[i]] for i in range(half)]
    near = [near[0]] + [swap(near[i], i) for i in range(1, half)]
    down_rows = down_store[adapter_asked]
    up_rows = adapter_up_weight[adapter_asked]

    piece = lax.all_gather(tokens, "tensor", axis=1, tiled=True)
    query_base = jnp.dot(piece, query_weight, preferred_element_type=jnp.float32)
    new_cache = jnp.dot(piece, keyvalue_weight, preferred_element_type=jnp.float32).astype(jnp.bfloat16)

    down_rows, mirrored_store, query_base, new_cache, *near = lax.optimization_barrier(
        (down_rows, mirrored_store, query_base, new_cache, *near)
    )
    down_sent = lax.all_to_all(down_rows, "dp", split_axis=0, concat_axis=0, tiled=True)
    far = [mirrored_store[far_asked[i]] for i in range(half)]
    far = [far[0]] + [swap(far[i], i) for i in range(1, half)]
    up_rows, down_sent = lax.optimization_barrier((up_rows, down_sent))
    up_sent = lax.all_to_all(up_rows, "dp", split_axis=0, concat_axis=0, tiled=True)

    lengths = span_token_length[0]
    ends = jnp.cumsum(lengths)
    starts = ends - lengths
    steps = jnp.arange(tok_rows, dtype=jnp.int32)[:, None]
    member = (steps >= starts[None, :]) & (steps < ends[None, :])
    slot = jnp.sum(jnp.where(member, adapter_pos[None, :], 0), axis=1)
    in_slot = slot[:, None] == jnp.arange(adapter_slots, dtype=jnp.int32)[None, :]

    down_part = jnp.einsum("tn,snk->tsk", tokens, down_sent, preferred_element_type=jnp.float32)
    shrink_part = jnp.sum(jnp.where(in_slot[:, :, None], down_part, 0.0), axis=1)
    shrink = lax.psum(shrink_part, "tensor").astype(jnp.bfloat16)
    shrink, *far = lax.optimization_barrier((shrink, *far))
    spread = jnp.where(in_slot[:, :, None], shrink[:, None, :], 0).reshape(tok_rows, adapter_slots * rank)
    prefix_pages = jnp.concatenate(near + far, axis=0)[page_pos]
    up = up_sent.reshape(adapter_slots * rank, q_cols)
    out = attend(query_base, spread, up, new_cache, prefix_pages, starts, ends)
    return (out, new_cache)


def solution(mesh):
    return jax.shard_map(
        on_device,
        mesh=mesh,
        in_specs=(
            P("dp", "tensor"),
            P(None, "tensor"),
            P(None, "tensor"),
            P("dp", "tensor", None),
            P("dp", None, "tensor"),
            P("dp", None, "tensor"),
            P("dp", None),
            P("dp", None),
            P("dp"),
            P("dp", None),
            P("dp"),
        ),
        out_specs=(P("dp", "tensor"), P("dp", "tensor")),
        check_vma=False,
    )
```

time: 446 us -> 387 us (0.87)
  waiting for transfers between devices: 273 us -> 219 us
  Pallas kernels: 18.8 us -> 12.5 us
  local copies, waits for them, and re-layouts: 63 us -> 68.9 us
    all_to_all x1, waiting for transfers between devices: 125 us -> 6.46 us  [on_device(): lax.all_to_all(jnp.broadcast_to(raw[None], (peers, raw.shape[0])), 'dp',...]
    all_to_all x1, waiting for transfers between devices: 0.01 us -> 87.4 us  [on_device(): lax.all_to_all(down_rows, 'dp', split_axis=0, concat_axis=0, tiled=True)]
    all_to_all x1, waiting for transfers between devices: 23 us -> 0.01 us  [on_device(): lax.all_to_all(up_rows, 'dp', split_axis=0, concat_axis=0, tiled=True)]
    ppermute x7, waiting for transfers between devices: 124 us -> 104 us  [swap(): lax.ppermute(array, 'dp', [(peer, peer ^ distance) for peer in range(peer...]
    all_gather x1, waiting for transfers between devices: 0.01 us -> 20.3 us  [on_device(): piece = lax.all_gather(tokens, 'tensor', axis=1, tiled=True)]
    gather x13 -> x11, local copies, waits for them, and re-layouts: 32.6 us -> 39.1 us  [the longest x4 14.1 us: on_device(): near = [store[near_asked[i]] for i in range(half)]]
    pallas_call x1, Pallas kernels: 18.8 us -> 12.5 us  [attend(): pl.pallas_call(attention_kernel, out_shape=jax.ShapeDtypeStruct((rows, q_...]
    ppermute x7, starting transfers between devices: 12.3 us -> 7.53 us  [swap(): lax.ppermute(array, 'dp', [(peer, peer ^ distance) for peer in range(peer...]
  transfers between devices with their start and end apart: 11 -> 11, of which waited for: 7 -> 9; matrix products, arithmetic and copies ran while one was open for 21% -> 26% of each run, Pallas kernels for 0% -> 0%
where the time goes in v3:
time: 387 us; the launch traced here: 386 us
  waiting for transfers between devices  219 us (57%)
  local copies, waits for them, and re-layouts  68.9 us (18%)
  matrix products  30.5 us (8%)
  starting transfers between devices  23 us (6%)
  between operations  14.9 us (4%)
  blocking collectives  12.6 us (3%)
  Pallas kernels  12.5 us (3%)
  other arithmetic  4.81 us (1%)
    ppermute x7, waiting for transfers between devices, swap(): lax.ppermute(array, 'dp', [(peer, peer ^ distance) for peer in range(peer...  104 us
    all_to_all x1, waiting for transfers between devices, on_device(): lax.all_to_all(down_rows, 'dp', split_axis=0, concat_axis=0, tiled=True)  87.4 us
    all_gather x1, waiting for transfers between devices, on_device(): piece = lax.all_gather(tokens, 'tensor', axis=1, tiled=True)  20.3 us
    dot_general x1, matrix products, on_device(): jnp.dot(piece, query_weight, preferred_element_type=jnp.float32)  18.2 us
    unnamed x26, local copies, waits for them, and re-layouts  17.6 us
    gather x4, local copies, waits for them, and re-layouts, on_device(): near = [store[near_asked[i]] for i in range(half)]  14.1 us
    gather x4, local copies, waits for them, and re-layouts, on_device(): far = [mirrored_store[far_asked[i]] for i in range(half)]  14 us
    psum x1, blocking collectives, on_device(): shrink = lax.psum(shrink_part, 'tensor').astype(jnp.bfloat16)  12.6 us
  transfers between devices with their start and end apart: 11, of which 9 were waited for; matrix products, arithmetic and copies ran while one was open for 26% of the time, Pallas kernels for 0%

profile of v3, /device:TPU:0, one launch (start us, length us, event | category | flops | bytes accessed | tf_op | source)
XLA Modules:
  0.0 385.8 jit_solution(18035902909511810821)
XLA Ops:
  7.2 0.7 all-gather.2.cloned.1.call-update
  7.9 0.8 pad_add_fusion.1
  8.7 0.6 broadcast_in_dim.181
  9.3 7.3 %all-to-all-start = ((s32[8,1,160]{2,1,0:T(1,128)}), s32[8,1,160]{2,1,0:T(1,128)S(1)}, u32[]{:S(2)}, u32[]{:S(2)}) async-start(s32[8,1,160]{2,1,0:T(1,128)} %broadcast_in_dim.181), calls=%async_computation | async-start | bytes 16384 | tf_op jit(solution)/shard_map/all_to_all | solution.py:192
  16.6 6.5 %all-to-all-done = s32[8,1,160]{2,1,0:T(1,128)S(1)} async-done(((s32[8,1,160]{2,1,0:T(1,128)}), s32[8,1,160]{2,1,0:T(1,128)S(1)}, u32[]{:S(2)}, u32[]{:S(2)}) %all-to-all-start) | async-done | bytes 5152 | tf_op jit(solution)/shard_map/all_to_all | solution.py:192
  25.7 3.5 gather_fusion.3
  29.6 3.6 gather_fusion.4
  33.2 0.6 collective-permute-start.1
  33.8 3.5 gather_fusion.5
  37.3 0.8 collective-permute-start.2
  38.4 3.6 gather_fusion.6
  42.0 2.1 collective-permute-start.3
  44.1 6.2 %gather_fusion.1 = bf16[16,2048,64]{1,2,0:T(8,128)(2,1)} fusion(bf16[32,2048,64]{1,2,0:T(8,128)(2,1)} %param.14, s32[1024]{0:T(1024)S(1)} %get-tuple-element.70), kind=kCustom, calls=%fused_computation.1 | custom fusion | bytes 8388672 | tf_op jit(solution)/shard_map/gather | solution.py:213
  50.3 20.3 %all-gather.2.cloned.1.call-done = bf16[512,8192]{1,0:T(8,128)(2,1)} async-done(((bf16[512,2048]{1,0:T(8,128)(2,1)}), bf16[512,8192]{1,0:T(8,128)(2,1)}) %all-gather.2.cloned.1.call-update) | async-done | bytes 8388624 | tf_op jit(solution)/shard_map/all_gather | solution.py:216
  70.6 18.2 %fusion.31.base_hbm = f32[512,1024]{1,0:T(8,128)} fusion(bf16[512,8192]{1,0:T(8,128)(2,1)} %all-gather.2.cloned.1.call-done, bf16[8192,1024]{1,0:T(8,128)(2,1)} %param.12), kind=kOutput, calls=%fused_computation.135 | convolution fusion | flops 8589934592 | bytes 27262976 | tf_op jit(solution)/shard_map/dot_general | solution.py:217
  88.8 7.7 %convolution_convert_fusion.cache_hbm = bf16[512,512]{1,0:T(8,128)(2,1)} fusion(bf16[512,8192]{1,0:T(8,128)(2,1)S(1)} %copy-done.8, bf16[8192,512]{1,0:T(8,128)(2,1)} %param.13), kind=kOutput, calls=%fused_computation.16 | convolution fusion | flops 4295229440 | bytes 17301504 | tf_op jit(solution)/shard_map/dot_general | solution.py:218
  96.5 20.3 %collective-permute-done.2 = bf16[16,64,512]{2,1,0:T(8,128)(2,1)} collective-permute-done((bf16[16,64,512]{2,1,0:T(8,128)(2,1)}, bf16[16,64,512]{2,1,0:T(8,128)(2,1)}, u32[]{:S(2)}, u32[]{:S(2)}) %collective-permute-start.2) | collective-permute-done | bytes 1048608 | tf_op jit(solution)/shard_map/ppermute | solution.py:187
  116.8 19.9 %collective-permute-done.3 = bf16[16,64,512]{2,1,0:T(8,128)(2,1)} collective-permute-done((bf16[16,64,512]{2,1,0:T(8,128)(2,1)}, bf16[16,64,512]{2,1,0:T(8,128)(2,1)}, u32[]{:S(2)}, u32[]{:S(2)}) %collective-permute-start.3) | collective-permute-done | bytes 1048608 | tf_op jit(solution)/shard_map/ppermute | solution.py:187
  136.7 25.1 %collective-permute-done = bf16[48,64,512]{2,1,0:T(8,128)(2,1)S(1)} collective-permute-done((bf16[48,64,512]{2,1,0:T(8,128)(2,1)}, bf16[48,64,512]{2,1,0:T(8,128)(2,1)S(1)}, u32[]{:S(2)}, u32[]{:S(2)}) %collective-permute-start) | collective-permute-done | bytes 3145760 | tf_op jit(solution)/shard_map/ppermute | solution.py:187
  161.8 4.6 %all-to-all-start.1 = ((bf16[16,2048,64]{1,2,0:T(8,128)(2,1)}), bf16[16,2048,64]{1,2,0:T(8,128)(2,1)}, u32[]{:S(2)}, u32[]{:S(2)}) async-start(bf16[16,2048,64]{1,2,0:T(8,128)(2,1)} %gather_fusion.1), calls=%async_computation.1 | async-start | bytes 8388608 | tf_op jit(solution)/shard_map/all_to_all | solution.py:223
  168.5 4.3 %gather_fusion = bf16[16,64,1024]{2,1,0:T(8,128)(2,1)} fusion(bf16[32,64,1024]{2,1,0:T(8,128)(2,1)} %param.15, s32[1024]{0:T(1024)S(1)} %get-tuple-element.70), kind=kCustom, calls=%fused_computation | custom fusion | bytes 4194368 | tf_op jit(solution)/shard_map/gather | solution.py:214
  172.7 87.4 %all-to-all-done.1 = bf16[16,2048,64]{1,2,0:T(8,128)(2,1)} async-done(((bf16[16,2048,64]{1,2,0:T(8,128)(2,1)}), bf16[16,2048,64]{1,2,0:T(8,128)(2,1)}, u32[]{:S(2)}, u32[]{:S(2)}) %all-to-all-start.1) | async-done | bytes 4194336 | tf_op jit(solution)/shard_map/all_to_all | solution.py:223
  260.1 3.6 all-to-all-start.2
  264.6 3.5 gather_fusion.7
  268.1 3.5 gather_fusion.8
  271.6 2.0 collective-permute-start.4
  273.6 3.6 gather_fusion.9
  277.2 1.5 collective-permute-start.5
  278.7 3.5 gather_fusion.10
  282.1 1.1 constant_dynamic-update-slice_fusion.7
  283.2 2.4 constant_dynamic-update-slice_fusion.6
  285.6 2.3 constant_dynamic-update-slice_fusion.5
  287.9 2.3 constant_dynamic-update-slice_fusion.4
  290.2 4.6 %fusion = f32[512,64]{0,1:T(8,128)S(1)} fusion(bf16[16,2048,64]{1,2,0:T(8,128)(2,1)} %all-to-all-done.1, bf16[512,2048]{1,0:T(8,128)(2,1)S(1)} %copy-done.4, pred[512,16]{0,1:T(8,128)(4,1)S(1)} %iota_compare_fusion.2), kind=kOutput, calls=%fused_computation.13 | convolution fusion | flops 2148499456 | bytes 6430720 | tf_op jit(solution)/shard_map/tn,snk->tsk/dot_general | solution.py:237
  294.7 12.6 %all-reduce.1 = bf16[512,64]{0,1:T(8,128)(2,1)S(1)} all-reduce(f32[512,64]{0,1:T(8,128)S(1)} %fusion), channel_id=1, replica_groups=mesh['dp'=8,'tensor'=4] {'tensor'}, use_global_device_ids=true, to_apply=%region_14.15 | all-reduce | flops 32768 | bytes 196608 | tf_op jit(solution)/shard_map/psum | solution.py:239
  307.3 4.4 %collective-permute-done.4 = bf16[16,64,512]{2,1,0:T(8,128)(2,1)} collective-permute-done((bf16[16,64,512]{2,1,0:T(8,128)(2,1)}, bf16[16,64,512]{2,1,0:T(8,128)(2,1)}, u32[]{:S(2)}, u32[]{:S(2)}) %collective-permute-start.4) | collective-permute-done | bytes 1048608 | tf_op jit(solution)/shard_map/ppermute | solution.py:187
  311.7 12.1 %collective-permute-done.5 = bf16[16,64,512]{2,1,0:T(8,128)(2,1)} collective-permute-done((bf16[16,64,512]{2,1,0:T(8,128)(2,1)}, bf16[16,64,512]{2,1,0:T(8,128)(2,1)}, u32[]{:S(2)}, u32[]{:S(2)}) %collective-permute-start.5) | collective-permute-done | bytes 1048608 | tf_op jit(solution)/shard_map/ppermute | solution.py:187
  323.8 22.2 %collective-permute-done.6 = bf16[16,64,512]{2,1,0:T(8,128)(2,1)} collective-permute-done((bf16[16,64,512]{2,1,0:T(8,128)(2,1)}, bf16[16,64,512]{2,1,0:T(8,128)(2,1)}, u32[]{:S(2)}, u32[]{:S(2)}) %collective-permute-start.6) | collective-permute-done | bytes 1048608 | tf_op jit(solution)/shard_map/ppermute | solution.py:187
  345.9 1.0 broadcast_select_fusion
  347.0 1.5 copy.133.spread_ref
  348.5 2.3 constant_dynamic-update-slice_fusion.3
  350.7 2.3 constant_dynamic-update-slice_fusion.2
  353.1 2.3 constant_dynamic-update-slice_fusion.1
  355.4 2.3 constant_dynamic-update-slice_fusion
  357.7 6.2 %gather_fusion.11 = bf16[64,64,512]{2,1,0:T(8,128)(2,1)} fusion(bf16[128,64,512]{2,1,0:T(8,128)(2,1)} %constant_dynamic-update-slice_fusion, s32[1024]{0:T(1024)S(1)} %pad_clamp_fusion), kind=kCustom, calls=%fused_computation.11 | custom fusion | bytes 8388864 | tf_op jit(solution)/shard_map/gather | solution.py:242
  363.9 1.6 copy-done
  365.5 1.0 copy-done.1
  366.5 12.5 %attend.1 = bf16[512,1024]{1,0:T(8,128)(2,1)} custom-call(s32[4,32]{1,0:T(4,128)S(1)} %pad_add_fusion.steps_ref, bf16[512,1024]{1,0:T(8,128)(2,1)S(1)} %copy.133.spread_ref, bf16[1024,1024]{1,0:T(8,128)(2,1)S(1)} %bitcast.76, f32[512,1024]{1,0:T(8,128)S(1)} %copy-done, bf16[512,512]{1,0:T(8,128)(2,1)S(1)} %copy-done.1, bf16[64,64,512]{2,1,0:T(8,128)(2,1)} %gather_fusion.11), custom_call_target="tpu_custom_call" | custom-call | flops 2818572288 | bytes 11010048 | tf_op jit(solution)/shard_map/attend/pallas_call | solution.py:143
  (80 shorter events, 5.8 us)
Async XLA Ops:
  7.2 63.4 %all-gather.2.cloned.1.call-start = ((), (), s32[]{:S(2)}) async-start(), calls=%async_computation.3 | async-start | bytes 10485760 | tf_op jit(solution)/shard_map/all_gather | solution.py:216
  9.3 13.8 %all-to-all-start = ((s32[8,1,160]{2,1,0:T(1,128)}), s32[8,1,160]{2,1,0:T(1,128)S(1)}, u32[]{:S(2)}, u32[]{:S(2)}) async-start(s32[8,1,160]{2,1,0:T(1,128)} %broadcast_in_dim.181), calls=%async_computation | async-start | bytes 16384 | tf_op jit(solution)/shard_map/all_to_all | solution.py:192
  24.9 136.9 %collective-permute-start = (bf16[48,64,512]{2,1,0:T(8,128)(2,1)}, bf16[48,64,512]{2,1,0:T(8,128)(2,1)S(1)}, u32[]{:S(2)}, u32[]{:S(2)}) collective-permute-start(bf16[48,64,512]{2,1,0:T(8,128)(2,1)} %param.16), channel_id=1, source_target_pairs={{0,16},{4,20},{8,24},{12,28},{16,0},{20,4},{24,8},{28,12},{1,17},{... | collective-permute-start | bytes 9437192 | tf_op jit(solution)/shard_map/ppermute | solution.py:187
  33.2 63.4 %collective-permute-start.1 = (bf16[16,64,512]{2,1,0:T(8,128)(2,1)}, bf16[16,64,512]{2,1,0:T(8,128)(2,1)}, u32[]{:S(2)}, u32[]{:S(2)}) collective-permute-start(bf16[16,64,512]{2,1,0:T(8,128)(2,1)} %gather_fusion.4), channel_id=1, source_target_pairs={{0,4},{4,0},{8,12},{12,8},{16,20},{20,16},{24,28},{28,24},{1,5},{5... | collective-permute-start | bytes 3145736 | tf_op jit(solution)/shard_map/ppermute | solution.py:187
  37.3 79.6 %collective-permute-start.2 = (bf16[16,64,512]{2,1,0:T(8,128)(2,1)}, bf16[16,64,512]{2,1,0:T(8,128)(2,1)}, u32[]{:S(2)}, u32[]{:S(2)}) collective-permute-start(bf16[16,64,512]{2,1,0:T(8,128)(2,1)} %gather_fusion.5), channel_id=1, source_target_pairs={{0,8},{4,12},{8,0},{12,4},{16,24},{20,28},{24,16},{28,20},{1,9},{5... | collective-permute-start | bytes 3145736 | tf_op jit(solution)/shard_map/ppermute | solution.py:187
  42.0 94.7 %collective-permute-start.3 = (bf16[16,64,512]{2,1,0:T(8,128)(2,1)}, bf16[16,64,512]{2,1,0:T(8,128)(2,1)}, u32[]{:S(2)}, u32[]{:S(2)}) collective-permute-start(bf16[16,64,512]{2,1,0:T(8,128)(2,1)} %gather_fusion.6), channel_id=1, source_target_pairs={{0,12},{4,8},{8,4},{12,0},{16,28},{20,24},{24,20},{28,16},{1,13},{... | collective-permute-start | bytes 3145736 | tf_op jit(solution)/shard_map/ppermute | solution.py:187
  70.6 18.2 %copy-start.8 = (bf16[512,8192]{1,0:T(8,128)(2,1)S(1)}, bf16[512,8192]{1,0:T(8,128)(2,1)}, u32[]{:S(2)}) copy-start(bf16[512,8192]{1,0:T(8,128)(2,1)} %all-gather.2.cloned.1.call-done) | copy-start | bytes 25165828
  96.5 69.9 %copy-start.5 = (s32[1,16]{1,0:T(1,128)S(1)}, s32[1,16]{1,0:T(1,128)}, u32[]{:S(2)}) copy-start(s32[1,16]{1,0:T(1,128)} %param.17) | copy-start | bytes 196
  96.5 71.7 %copy-start.6 = (s32[64,1]{0,1:T(1,128)S(1)}, s32[64,1]{0,1:T(1,128)}, u32[]{:S(2)}) copy-start(s32[64,1]{0,1:T(1,128)} %param.20) | copy-start | bytes 772
  96.5 167.2 %copy-start.7 = (s32[16,1]{0,1:T(1,128)S(1)}, s32[16,1]{0,1:T(1,128)}, u32[]{:S(2)}) copy-start(s32[16,1]{0,1:T(1,128)} %param.18) | copy-start | bytes 196
  161.8 6.4 %copy-start.2 = (bf16[48,64,512]{2,1,0:T(8,128)(2,1)}, bf16[48,64,512]{2,1,0:T(8,128)(2,1)S(1)}, u32[]{:S(2)}) copy-start(bf16[48,64,512]{2,1,0:T(8,128)(2,1)S(1)} %collective-permute-done) | copy-start | bytes 9437188
  161.8 98.2 %all-to-all-start.1 = ((bf16[16,2048,64]{1,2,0:T(8,128)(2,1)}), bf16[16,2048,64]{1,2,0:T(8,128)(2,1)}, u32[]{:S(2)}, u32[]{:S(2)}) async-start(bf16[16,2048,64]{1,2,0:T(8,128)(2,1)} %gather_fusion.1), calls=%async_computation.1 | async-start | bytes 8388608 | tf_op jit(solution)/shard_map/all_to_all | solution.py:223
  168.4 113.7 %copy-start.3 = (bf16[16,64,512]{2,1,0:T(8,128)(2,1)S(1)}, bf16[16,64,512]{2,1,0:T(8,128)(2,1)}, u32[]{:S(2)}) copy-start(bf16[16,64,512]{2,1,0:T(8,128)(2,1)} %gather_fusion.3) | copy-start | bytes 3145732
  260.1 103.8 %all-to-all-start.2 = ((bf16[16,64,1024]{2,1,0:T(8,128)(2,1)}), bf16[16,64,1024]{2,1,0:T(8,128)(2,1)S(1)}, u32[]{:S(2)}, u32[]{:S(2)}) async-start(bf16[16,64,1024]{2,1,0:T(8,128)(2,1)} %gather_fusion), calls=%async_computation.2 | async-start | bytes 4194304 | tf_op jit(solution)/shard_map/all_to_all | solution.py:227
  271.6 40.1 %collective-permute-start.4 = (bf16[16,64,512]{2,1,0:T(8,128)(2,1)}, bf16[16,64,512]{2,1,0:T(8,128)(2,1)}, u32[]{:S(2)}, u32[]{:S(2)}) collective-permute-start(bf16[16,64,512]{2,1,0:T(8,128)(2,1)} %gather_fusion.8), channel_id=1, source_target_pairs={{0,4},{4,0},{8,12},{12,8},{16,20},{20,16},{24,28},{28,24},{1,5},{5... | collective-permute-start | bytes 3145736 | tf_op jit(solution)/shard_map/ppermute | solution.py:187
  277.2 46.6 %collective-permute-start.5 = (bf16[16,64,512]{2,1,0:T(8,128)(2,1)}, bf16[16,64,512]{2,1,0:T(8,128)(2,1)}, u32[]{:S(2)}, u32[]{:S(2)}) collective-permute-start(bf16[16,64,512]{2,1,0:T(8,128)(2,1)} %gather_fusion.9), channel_id=1, source_target_pairs={{0,8},{4,12},{8,0},{12,4},{16,24},{20,28},{24,16},{28,20},{1,9},{5... | collective-permute-start | bytes 3145736 | tf_op jit(solution)/shard_map/ppermute | solution.py:187
  282.1 8.0 %copy-start.4 = (bf16[512,2048]{1,0:T(8,128)(2,1)S(1)}, bf16[512,2048]{1,0:T(8,128)(2,1)}, u32[]{:S(2)}) copy-start(bf16[512,2048]{1,0:T(8,128)(2,1)} %param.11) | copy-start | bytes 6291460
  282.1 63.8 %collective-permute-start.6 = (bf16[16,64,512]{2,1,0:T(8,128)(2,1)}, bf16[16,64,512]{2,1,0:T(8,128)(2,1)}, u32[]{:S(2)}, u32[]{:S(2)}) collective-permute-start(bf16[16,64,512]{2,1,0:T(8,128)(2,1)} %gather_fusion.10), channel_id=1, source_target_pairs={{0,12},{4,8},{8,4},{12,0},{16,28},{20,24},{24,20},{28,16},{1,13},{... | collective-permute-start | bytes 3145736 | tf_op jit(solution)/shard_map/ppermute | solution.py:187
  363.9 1.6 copy-start
  365.5 1.0 copy-start.1
Sparse Core Ops, SparseCore 0:
  9.6 60.9 all-gather.1

commit v4 on v3

--- a/solution.py
+++ b/solution.py
@@ -162,6 +162,66 @@
     )(steps, spread, up, query_base, cache, pages)
 
 
+def serve_kernel(asked_ref, store_ref, *refs):
+    outs, sems = refs[:-1], refs[-1]
+    for index, out in enumerate(outs):
+        for place in range(out.shape[0]):
+            page = asked_ref[index * out.shape[0] + place]
+            pltpu.make_async_copy(store_ref.at[page], out.at[place], sems.at[index]).start()
+    for index, out in enumerate(outs):
+        pltpu.make_async_copy(out, out, sems.at[index]).wait()
+
+
+def serve(asked, store):
+    blocks, capacity = asked.shape
+    anywhere = pl.BlockSpec(memory_space=pl.ANY)
+    shape = (capacity,) + store.shape[1:]
+    return pl.pallas_call(
+        serve_kernel,
+        out_shape=[jax.ShapeDtypeStruct(shape, store.dtype)] * blocks,
+        in_specs=[pl.BlockSpec(memory_space=pltpu.SMEM), anywhere],
+        out_specs=[anywhere] * blocks,
+        scratch_shapes=[pltpu.SemaphoreType.DMA((blocks,))],
+        cost_estimate=pl.CostEstimate(
+            flops=0, bytes_accessed=4 * blocks * math.prod(shape), transcendentals=0
+        ),
+        name="serve",
+    )(asked.reshape(-1), store)
+
+
+def assemble_kernel(source_ref, place_ref, *refs):
+    sources, out, sem = refs[:-2], refs[-2], refs[-1]
+
+    def one(index, carry):
+        source = source_ref[index]
+        place = place_ref[index]
+        for number, ref in enumerate(sources):
+
+            @pl.when(source == number)
+            def _():
+                pltpu.make_async_copy(ref.at[place], out.at[index], sem).start()
+
+        return carry
+
+    lax.fori_loop(0, out.shape[0], one, 0)
+    pltpu.make_async_copy(out, out, sem).wait()
+
+
+def assemble(source, place, sources):
+    anywhere = pl.BlockSpec(memory_space=pl.ANY)
+    scalars = pl.BlockSpec(memory_space=pltpu.SMEM)
+    shape = (source.shape[0],) + sources[0].shape[1:]
+    return pl.pallas_call(
+        assemble_kernel,
+        out_shape=jax.ShapeDtypeStruct(shape, sources[0].dtype),
+        in_specs=[scalars, scalars] + [anywhere] * len(sources),
+        out_specs=anywhere,
+        scratch_shapes=[pltpu.SemaphoreType.DMA],
+        cost_estimate=pl.CostEstimate(flops=0, bytes_accessed=4 * math.prod(shape), transcendentals=0),
+        name="assemble",
+    )(source, place, *sources)
+
+
 def on_device(
     tokens,
     query_weight,
@@ -206,10 +266,11 @@
     all_local = everyone[:, 2 * page_count + request_count :]
     adapter_asked = asked_of(me, all_owner, earlier_alike(all_owner), all_local, ADP_CAP).reshape(-1)
     adapter_pos = adapter_owner[:, 0] * ADP_CAP + earlier_alike(adapter_owner[:, 0])
-    page_pos = (page_owner[:, 0] ^ me) * page_cap + earlier_alike(page_owner[:, 0])
-
-    near = [store[near_asked[i]] for i in range(half)]
-    near = [near[0]] + [swap(near[i], i) for i in range(1, half)]
+    page_source = page_owner[:, 0] ^ me
+    page_place = jnp.where(page_source % half == 0, page_local_index, earlier_alike(page_owner[:, 0]))
+
+    near = serve(near_asked[1:], store)
+    near = [swap(pages, i + 1) for i, pages in enumerate(near)]
     down_rows = down_store[adapter_asked]
     up_rows = adapter_up_weight[adapter_asked]
 
@@ -221,9 +282,9 @@
         (down_rows, mirrored_store, query_base, new_cache, *near)
     )
     down_sent = lax.all_to_all(down_rows, "dp", split_axis=0, concat_axis=0, tiled=True)
-    far = [mirrored_store[far_asked[i]] for i in range(half)]
-    far = [far[0]] + [swap(far[i], i) for i in range(1, half)]
-    up_rows, down_sent = lax.optimization_barrier((up_rows, down_sent))
+    far = serve(far_asked[1:], mirrored_store)
+    far = [swap(pages, i + 1) for i, pages in enumerate(far)]
+    up_rows, down_sent, *far = lax.optimization_barrier((up_rows, down_sent, *far))
     up_sent = lax.all_to_all(up_rows, "dp", split_axis=0, concat_axis=0, tiled=True)
 
     lengths = span_token_length[0]
@@ -237,9 +298,8 @@
     down_part = jnp.einsum("tn,snk->tsk", tokens, down_sent, preferred_element_type=jnp.float32)
     shrink_part = jnp.sum(jnp.where(in_slot[:, :, None], down_part, 0.0), axis=1)
     shrink = lax.psum(shrink_part, "tensor").astype(jnp.bfloat16)
-    shrink, *far = lax.optimization_barrier((shrink, *far))
     spread = jnp.where(in_slot[:, :, None], shrink[:, None, :], 0).reshape(tok_rows, adapter_slots * rank)
-    prefix_pages = jnp.concatenate(near + far, axis=0)[page_pos]
+    prefix_pages = assemble(page_source, page_place, [store, *near, mirrored_store, *far])
     up = up_sent.reshape(adapter_slots * rank, q_cols)
     out = attend(query_base, spread, up, new_cache, prefix_pages, starts, ends)
     return (out, new_cache)

time: 387 us -> 539 us (1.39)
  Pallas kernels: 12.5 us -> 335 us
  waiting for transfers between devices: 219 us -> 97.5 us
  local copies, waits for them, and re-layouts: 68.9 us -> 19.5 us
    pallas_call x0 -> x3, Pallas kernels: none -> 323 us  [the longest x2 194 us: serve(): pl.pallas_call(serve_kernel, out_shape=[jax.ShapeDtypeStruct(shape, store...]
    all_to_all x1, waiting for transfers between devices: 87.4 us -> 0.01 us  [on_device(): lax.all_to_all(down_rows, 'dp', split_axis=0, concat_axis=0, tiled=True)]
    gather x9 -> x0, local copies, waits for them, and re-layouts: 34.3 us -> none  [the longest x4 14.1 us: on_device(): near = [store[near_asked[i]] for i in range(half)]]
    all_gather x1, waiting for transfers between devices: 20.3 us -> 0.01 us  [on_device(): piece = lax.all_gather(tokens, 'tensor', axis=1, tiled=True)]
    ppermute x7, waiting for transfers between devices: 104 us -> 90.3 us  [swap(): lax.ppermute(array, 'dp', [(peer, peer ^ distance) for peer in range(peer...]
    unnamed x26 -> x23, local copies, waits for them, and re-layouts: 17.6 us -> 4.34 us
  transfers between devices with their start and end apart: 11 -> 11, of which waited for: 9 -> 6; matrix products, arithmetic and copies ran while one was open for 26% -> 9% of each run, Pallas kernels for 0% -> 60%
where the time goes in v4:
time: 539 us; the launch traced here: 538 us
  Pallas kernels  335 us (62%)
  waiting for transfers between devices  97.5 us (18%)
  matrix products  28.9 us (5%)
  starting transfers between devices  25.2 us (5%)
  local copies, waits for them, and re-layouts  19.5 us (4%)
  between operations  14.9 us (3%)
  blocking collectives  12.2 us (2%)
    pallas_call x2, Pallas kernels, serve(): pl.pallas_call(serve_kernel, out_shape=[jax.ShapeDtypeStruct(shape, store...  194 us
    pallas_call x1, Pallas kernels, assemble(): pl.pallas_call(assemble_kernel, out_shape=jax.ShapeDtypeStruct(shape, sou...  129 us
    ppermute x7, waiting for transfers between devices, swap(): lax.ppermute(array, 'dp', [(peer, peer ^ distance) for peer in range(peer...  90.3 us
    dot_general x1, matrix products, on_device(): jnp.dot(piece, query_weight, preferred_element_type=jnp.float32)  15.9 us
    pallas_call x1, Pallas kernels, attend(): pl.pallas_call(attention_kernel, out_shape=jax.ShapeDtypeStruct((rows, q_...  12.5 us
    psum x1, blocking collectives, on_device(): shrink = lax.psum(shrink_part, 'tensor').astype(jnp.bfloat16)  12.2 us
  transfers between devices with their start and end apart: 11, of which 6 were waited for; matrix products, arithmetic and copies ran while one was open for 9% of the time, Pallas kernels for 60%

profile of v4, /device:TPU:0, one launch (start us, length us, event | category | flops | bytes accessed | tf_op | source)
XLA Modules:
  0.0 538.1 jit_solution(4821498072026877701)
XLA Ops:
  7.2 0.7 all-gather.2.cloned.1.call-update
  7.9 0.8 pad_add_fusion.1
  8.7 0.6 broadcast_in_dim.172
  9.3 7.3 %all-to-all-start = ((s32[8,1,160]{2,1,0:T(1,128)}), s32[8,1,160]{2,1,0:T(1,128)S(1)}, u32[]{:S(2)}, u32[]{:S(2)}) async-start(s32[8,1,160]{2,1,0:T(1,128)} %broadcast_in_dim.172), calls=%async_computation | async-start | bytes 16384 | tf_op jit(solution)/shard_map/all_to_all | solution.py:252
  16.6 6.5 %all-to-all-done = s32[8,1,160]{2,1,0:T(1,128)S(1)} async-done(((s32[8,1,160]{2,1,0:T(1,128)}), s32[8,1,160]{2,1,0:T(1,128)S(1)}, u32[]{:S(2)}, u32[]{:S(2)}) %all-to-all-start) | async-done | bytes 5152 | tf_op jit(solution)/shard_map/all_to_all | solution.py:252
  23.1 0.3 convert_reduce_fusion.1
  23.4 0.1 select_reduce_fusion.3
  23.7 0.6 collective-permute-start
  24.3 0.6 gather_fusion.2
  24.9 0.2 convert_reduce_fusion
  25.2 0.2 select_reduce_fusion
  25.4 0.6 reshape.363.asked_ref
  26.0 97.1 %serve.2 = (bf16[16,64,512]{2,1,0:T(8,128)(2,1)}, bf16[16,64,512]{2,1,0:T(8,128)(2,1)}, bf16[16,64,512]{2,1,0:T(8,128)(2,1)}) custom-call(s32[48]{0:T(128)} %reshape.363.asked_ref, bf16[48,64,512]{2,1,0:T(8,128)(2,1)} %refs_0_), custom_call_target="tpu_custom_call" | custom-call | bytes 6291456 | tf_op jit(solution)/shard_map/serve/pallas_call | solution.py:179
  123.1 0.6 collective-permute-start.1
  123.7 0.6 collective-permute-start.2
  124.3 2.3 collective-permute-start.3
  126.6 0.1 fusion.12
  126.8 6.2 %gather_fusion.1 = bf16[16,2048,64]{1,2,0:T(8,128)(2,1)} fusion(bf16[32,2048,64]{1,2,0:T(8,128)(2,1)} %param.14, s32[1024]{0:T(1024)S(1)} %pad_clamp_fusion.1), kind=kCustom, calls=%fused_computation.1 | custom fusion | bytes 8388672 | tf_op jit(solution)/shard_map/gather | solution.py:274
  132.9 15.9 %fusion.23.base_hbm = f32[512,1024]{1,0:T(8,128)} fusion(bf16[512,8192]{1,0:T(8,128)(2,1)} %all-gather.2.cloned.1.call-done, bf16[8192,1024]{1,0:T(8,128)(2,1)} %param.12), kind=kOutput, calls=%fused_computation.88 | convolution fusion | flops 8589934592 | bytes 27262976 | tf_op jit(solution)/shard_map/dot_general | solution.py:278
  148.9 7.7 %convolution_convert_fusion.cache_hbm = bf16[512,512]{1,0:T(8,128)(2,1)} fusion(bf16[512,8192]{1,0:T(8,128)(2,1)S(1)} %copy-done.10, bf16[8192,512]{1,0:T(8,128)(2,1)} %param.13), kind=kOutput, calls=%fused_computation.7 | convolution fusion | flops 4295229440 | bytes 17301504 | tf_op jit(solution)/shard_map/dot_general | solution.py:279
  156.6 26.7 %collective-permute-done.2.refs_2_ = bf16[16,64,512]{2,1,0:T(8,128)(2,1)} collective-permute-done((bf16[16,64,512]{2,1,0:T(8,128)(2,1)}, bf16[16,64,512]{2,1,0:T(8,128)(2,1)}, u32[]{:S(2)}, u32[]{:S(2)}) %collective-permute-start.2) | collective-permute-done | bytes 1048608 | tf_op jit(solution)/shard_map/ppermute | solution.py:247
  183.3 22.4 %collective-permute-done.3.refs_3_ = bf16[16,64,512]{2,1,0:T(8,128)(2,1)} collective-permute-done((bf16[16,64,512]{2,1,0:T(8,128)(2,1)}, bf16[16,64,512]{2,1,0:T(8,128)(2,1)}, u32[]{:S(2)}, u32[]{:S(2)}) %collective-permute-start.3) | collective-permute-done | bytes 1048608 | tf_op jit(solution)/shard_map/ppermute | solution.py:247
  205.7 1.7 copy-done.2
  207.4 4.5 all-to-all-start.1
  211.9 0.7 reshape.364.asked_ref
  212.6 97.1 %serve.3 = (bf16[16,64,512]{2,1,0:T(8,128)(2,1)}, bf16[16,64,512]{2,1,0:T(8,128)(2,1)}, bf16[16,64,512]{2,1,0:T(8,128)(2,1)}) custom-call(s32[48]{0:T(128)} %reshape.364.asked_ref, bf16[48,64,512]{2,1,0:T(8,128)(2,1)} %copy-done.2), custom_call_target="tpu_custom_call" | custom-call | bytes 6291456 | tf_op jit(solution)/shard_map/serve/pallas_call | solution.py:179
  309.7 2.0 collective-permute-start.4
  311.7 1.5 collective-permute-start.5
  313.1 0.2 collective-permute-start.6
  313.3 4.2 gather_fusion
  317.5 17.6 %collective-permute-done.4.refs_5_ = bf16[16,64,512]{2,1,0:T(8,128)(2,1)S(1)} collective-permute-done((bf16[16,64,512]{2,1,0:T(8,128)(2,1)}, bf16[16,64,512]{2,1,0:T(8,128)(2,1)S(1)}, u32[]{:S(2)}, u32[]{:S(2)}) %collective-permute-start.4) | collective-permute-done | bytes 1048608 | tf_op jit(solution)/shard_map/ppermute | solution.py:247
  335.1 2.8 collective-permute-done.5.refs_6_
  338.0 20.7 %collective-permute-done.6.refs_7_ = bf16[16,64,512]{2,1,0:T(8,128)(2,1)S(1)} collective-permute-done((bf16[16,64,512]{2,1,0:T(8,128)(2,1)}, bf16[16,64,512]{2,1,0:T(8,128)(2,1)S(1)}, u32[]{:S(2)}, u32[]{:S(2)}) %collective-permute-start.6) | collective-permute-done | bytes 1048608 | tf_op jit(solution)/shard_map/ppermute | solution.py:247
  358.7 5.6 %all-to-all-start.2 = ((bf16[16,64,1024]{2,1,0:T(8,128)(2,1)}), bf16[16,64,1024]{2,1,0:T(8,128)(2,1)S(1)}, u32[]{:S(2)}, u32[]{:S(2)}) async-start(bf16[16,64,1024]{2,1,0:T(8,128)(2,1)} %gather_fusion), calls=%async_computation.2 | async-start | bytes 4194304 | tf_op jit(solution)/shard_map/all_to_all | solution.py:288
  364.5 0.1 fusion.21
  364.6 0.1 reduce
  364.8 0.5 slice.35
  366.2 0.2 convert_reduce_fusion.3
  366.4 0.2 convert_reduce_fusion.2
  366.7 0.5 compare_select_fusion.4
  367.2 5.2 fusion
  372.5 12.2 %all-reduce.1 = bf16[512,64]{0,1:T(8,128)(2,1)S(1)} all-reduce(f32[512,64]{0,1:T(8,128)S(1)} %fusion), channel_id=1, replica_groups=mesh['dp'=8,'tensor'=4] {'tensor'}, use_global_device_ids=true, to_apply=%region_15.16 | all-reduce | flops 32768 | bytes 196608 | tf_op jit(solution)/shard_map/psum | solution.py:300
  384.7 1.0 broadcast_select_fusion
  385.7 1.5 copy.37.spread_ref
  387.2 128.8 %assemble.1.pages_hbm = bf16[64,64,512]{2,1,0:T(8,128)(2,1)} custom-call(s32[64]{0:T(128)} %get-tuple-element.51.source_ref, s32[64]{0:T(128)} %get-tuple-element.50.place_ref, bf16[48,64,512]{2,1,0:T(8,128)(2,1)} %refs_0_, bf16[16,64,512]{2,1,0:T(8,128)(2,1)} %collective-permute-done.1.refs_1_, bf16[16,64,512]{2,1,0:T(8,128)(2,1)} %collective-permute-done.2.refs_2_, ...), custom_call_target="tpu_custom_call" | custom-call | bytes 8388608 | tf_op jit(solution)/shard_map/assemble/pallas_call | solution.py:214
  516.1 1.6 copy-done
  517.7 1.0 copy-done.1
  518.7 12.5 %attend.1 = bf16[512,1024]{1,0:T(8,128)(2,1)} custom-call(s32[4,32]{1,0:T(4,128)S(1)} %pad_add_fusion.steps_ref, bf16[512,1024]{1,0:T(8,128)(2,1)S(1)} %copy.37.spread_ref, bf16[1024,1024]{1,0:T(8,128)(2,1)S(1)} %bitcast.56, f32[512,1024]{1,0:T(8,128)S(1)} %copy-done, bf16[512,512]{1,0:T(8,128)(2,1)S(1)} %copy-done.1, bf16[64,64,512]{2,1,0:T(8,128)(2,1)} %assemble.1.pages_hbm), custom_call_target="tpu_custom_call" | custom-call | flops 2818572288 | bytes 11010048 | tf_op jit(solution)/shard_map/attend/pallas_call | solution.py:143
  (51 shorter events, 0.9 us)
Async XLA Ops:
  7.2 125.8 %all-gather.2.cloned.1.call-start = ((), (), s32[]{:S(2)}) async-start(), calls=%async_computation.3 | async-start | bytes 10485760 | tf_op jit(solution)/shard_map/all_gather | solution.py:277
  9.3 13.8 %all-to-all-start = ((s32[8,1,160]{2,1,0:T(1,128)}), s32[8,1,160]{2,1,0:T(1,128)S(1)}, u32[]{:S(2)}, u32[]{:S(2)}) async-start(s32[8,1,160]{2,1,0:T(1,128)} %broadcast_in_dim.172), calls=%async_computation | async-start | bytes 16384 | tf_op jit(solution)/shard_map/all_to_all | solution.py:252
  23.7 182.0 %collective-permute-start = (bf16[48,64,512]{2,1,0:T(8,128)(2,1)}, bf16[48,64,512]{2,1,0:T(8,128)(2,1)S(1)}, u32[]{:S(2)}, u32[]{:S(2)}) collective-permute-start(bf16[48,64,512]{2,1,0:T(8,128)(2,1)} %refs_0_), channel_id=1, source_target_pairs={{0,16},{4,20},{8,24},{12,28},{16,0},{20,4},{24,8},{28,12},{1,17},{... | collective-permute-start | bytes 9437192 | tf_op jit(solution)/shard_map/ppermute | solution.py:247
  123.1 33.5 %collective-permute-start.1 = (bf16[16,64,512]{2,1,0:T(8,128)(2,1)}, bf16[16,64,512]{2,1,0:T(8,128)(2,1)}, u32[]{:S(2)}, u32[]{:S(2)}) collective-permute-start(bf16[16,64,512]{2,1,0:T(8,128)(2,1)} %get-tuple-element.26), channel_id=1, source_target_pairs={{0,4},{4,0},{8,12},{12,8},{16,20},{20,16},{24,28},{28,24},{1,5},{5... | collective-permute-start | bytes 3145736 | tf_op jit(solution)/shard_map/ppermute | solution.py:247
  123.7 59.6 %collective-permute-start.2 = (bf16[16,64,512]{2,1,0:T(8,128)(2,1)}, bf16[16,64,512]{2,1,0:T(8,128)(2,1)}, u32[]{:S(2)}, u32[]{:S(2)}) collective-permute-start(bf16[16,64,512]{2,1,0:T(8,128)(2,1)} %get-tuple-element.27), channel_id=1, source_target_pairs={{0,8},{4,12},{8,0},{12,4},{16,24},{20,28},{24,16},{28,20},{1,9},{5... | collective-permute-start | bytes 3145736 | tf_op jit(solution)/shard_map/ppermute | solution.py:247
  124.3 81.4 %collective-permute-start.3 = (bf16[16,64,512]{2,1,0:T(8,128)(2,1)}, bf16[16,64,512]{2,1,0:T(8,128)(2,1)}, u32[]{:S(2)}, u32[]{:S(2)}) collective-permute-start(bf16[16,64,512]{2,1,0:T(8,128)(2,1)} %get-tuple-element.28), channel_id=1, source_target_pairs={{0,12},{4,8},{8,4},{12,0},{16,28},{20,24},{24,20},{28,16},{1,13},{... | collective-permute-start | bytes 3145736 | tf_op jit(solution)/shard_map/ppermute | solution.py:247
  132.9 15.9 %copy-start.10 = (bf16[512,8192]{1,0:T(8,128)(2,1)S(1)}, bf16[512,8192]{1,0:T(8,128)(2,1)}, u32[]{:S(2)}) copy-start(bf16[512,8192]{1,0:T(8,128)(2,1)} %all-gather.2.cloned.1.call-done) | copy-start | bytes 25165828
  205.7 1.7 copy-start.2
  207.4 151.3 %all-to-all-start.1 = ((bf16[16,2048,64]{1,2,0:T(8,128)(2,1)}), bf16[16,2048,64]{1,2,0:T(8,128)(2,1)}, u32[]{:S(2)}, u32[]{:S(2)}) async-start(bf16[16,2048,64]{1,2,0:T(8,128)(2,1)} %gather_fusion.1), calls=%async_computation.1 | async-start | bytes 8388608 | tf_op jit(solution)/shard_map/all_to_all | solution.py:284
  309.7 25.4 %collective-permute-start.4 = (bf16[16,64,512]{2,1,0:T(8,128)(2,1)}, bf16[16,64,512]{2,1,0:T(8,128)(2,1)S(1)}, u32[]{:S(2)}, u32[]{:S(2)}) collective-permute-start(bf16[16,64,512]{2,1,0:T(8,128)(2,1)} %get-tuple-element.31), channel_id=1, source_target_pairs={{0,4},{4,0},{8,12},{12,8},{16,20},{20,16},{24,28},{28,24},{1,5},{5... | collective-permute-start | bytes 3145736 | tf_op jit(solution)/shard_map/ppermute | solution.py:247
  311.7 26.3 %collective-permute-start.5 = (bf16[16,64,512]{2,1,0:T(8,128)(2,1)}, bf16[16,64,512]{2,1,0:T(8,128)(2,1)S(1)}, u32[]{:S(2)}, u32[]{:S(2)}) collective-permute-start(bf16[16,64,512]{2,1,0:T(8,128)(2,1)} %get-tuple-element.32), channel_id=1, source_target_pairs={{0,8},{4,12},{8,0},{12,4},{16,24},{20,28},{24,16},{28,20},{1,9},{5... | collective-permute-start | bytes 3145736 | tf_op jit(solution)/shard_map/ppermute | solution.py:247
  313.1 51.2 %copy-start.6 = (s32[1,16]{1,0:T(1,128)S(1)}, s32[1,16]{1,0:T(1,128)}, u32[]{:S(2)}) copy-start(s32[1,16]{1,0:T(1,128)} %param.17) | copy-start | bytes 196
  313.1 53.1 %copy-start.9 = (s32[16,1]{0,1:T(1,128)S(1)}, s32[16,1]{0,1:T(1,128)}, u32[]{:S(2)}) copy-start(s32[16,1]{0,1:T(1,128)} %param.18) | copy-start | bytes 196
  313.1 53.3 %copy-start.8 = (s32[64,1]{0,1:T(1,128)S(1)}, s32[64,1]{0,1:T(1,128)}, u32[]{:S(2)}) copy-start(s32[64,1]{0,1:T(1,128)} %param.20) | copy-start | bytes 772
  313.1 53.5 %copy-start.7 = (s32[64]{0:T(128)S(1)}, s32[64]{0:T(128)}, u32[]{:S(2)}) copy-start(s32[64]{0:T(128)} %param.21) | copy-start | bytes 772
  313.1 45.6 %collective-permute-start.6 = (bf16[16,64,512]{2,1,0:T(8,128)(2,1)}, bf16[16,64,512]{2,1,0:T(8,128)(2,1)S(1)}, u32[]{:S(2)}, u32[]{:S(2)}) collective-permute-start(bf16[16,64,512]{2,1,0:T(8,128)(2,1)} %get-tuple-element.33), channel_id=1, source_target_pairs={{0,12},{4,8},{8,4},{12,0},{16,28},{20,24},{24,20},{28,16},{1,13},{... | collective-permute-start | bytes 3145736 | tf_op jit(solution)/shard_map/ppermute | solution.py:247
  335.1 23.6 %copy-start.3 = (bf16[16,64,512]{2,1,0:T(8,128)(2,1)}, bf16[16,64,512]{2,1,0:T(8,128)(2,1)S(1)}, u32[]{:S(2)}) copy-start(bf16[16,64,512]{2,1,0:T(8,128)(2,1)S(1)} %collective-permute-done.4.refs_5_) | copy-start | bytes 3145732
  338.0 20.8 %copy-start.4 = (bf16[16,64,512]{2,1,0:T(8,128)(2,1)}, bf16[16,64,512]{2,1,0:T(8,128)(2,1)S(1)}, u32[]{:S(2)}) copy-start(bf16[16,64,512]{2,1,0:T(8,128)(2,1)S(1)} %collective-permute-done.5.refs_6_) | copy-start | bytes 3145732
  358.7 7.5 %copy-start.5 = (bf16[16,64,512]{2,1,0:T(8,128)(2,1)}, bf16[16,64,512]{2,1,0:T(8,128)(2,1)S(1)}, u32[]{:S(2)}) copy-start(bf16[16,64,512]{2,1,0:T(8,128)(2,1)S(1)} %collective-permute-done.6.refs_7_) | copy-start | bytes 3145732
  358.7 157.4 %all-to-all-start.2 = ((bf16[16,64,1024]{2,1,0:T(8,128)(2,1)}), bf16[16,64,1024]{2,1,0:T(8,128)(2,1)S(1)}, u32[]{:S(2)}, u32[]{:S(2)}) async-start(bf16[16,64,1024]{2,1,0:T(8,128)(2,1)} %gather_fusion), calls=%async_computation.2 | async-start | bytes 4194304 | tf_op jit(solution)/shard_map/all_to_all | solution.py:288
  516.1 1.6 copy-start
  517.7 1.0 copy-start.1
Sparse Core Ops, SparseCore 0:
  9.6 61.0 all-gather.1

commit v5 on v4

--- a/solution.py
+++ b/solution.py
@@ -180,8 +180,9 @@
         serve_kernel,
         out_shape=[jax.ShapeDtypeStruct(shape, store.dtype)] * blocks,
         in_specs=[pl.BlockSpec(memory_space=pltpu.SMEM), anywhere],
-        out_specs=[anywhere] * blocks,
+        out_specs=[pl.BlockSpec(memory_space=pltpu.VMEM)] * blocks,
         scratch_shapes=[pltpu.SemaphoreType.DMA((blocks,))],
+        compiler_params=pltpu.CompilerParams(vmem_limit_bytes=16 * 1024 * 1024),
         cost_estimate=pl.CostEstimate(
             flops=0, bytes_accessed=4 * blocks * math.prod(shape), transcendentals=0
         ),
@@ -215,8 +216,9 @@
         assemble_kernel,
         out_shape=jax.ShapeDtypeStruct(shape, sources[0].dtype),
         in_specs=[scalars, scalars] + [anywhere] * len(sources),
-        out_specs=anywhere,
+        out_specs=pl.BlockSpec(memory_space=pltpu.VMEM),
         scratch_shapes=[pltpu.SemaphoreType.DMA],
+        compiler_params=pltpu.CompilerParams(vmem_limit_bytes=16 * 1024 * 1024),
         cost_estimate=pl.CostEstimate(flops=0, bytes_accessed=4 * math.prod(shape), transcendentals=0),
         name="assemble",
     )(source, place, *sources)

time: 539 us -> 359 us (0.67)
  Pallas kernels: 335 us -> 33.1 us
  waiting for transfers between devices: 97.5 us -> 209 us
  local copies, waits for them, and re-layouts: 19.5 us -> 28.5 us
    pallas_call x2, Pallas kernels: 194 us -> 12.9 us  [serve(): pl.pallas_call(serve_kernel, out_shape=[jax.ShapeDtypeStruct(shape, store...]
    pallas_call x1, Pallas kernels: 129 us -> 6.7 us  [assemble(): pl.pallas_call(assemble_kernel, out_shape=jax.ShapeDtypeStruct(shape, sou...]
    ppermute x7, waiting for transfers between devices: 90.3 us -> 166 us  [swap(): lax.ppermute(array, 'dp', [(peer, peer ^ distance) for peer in range(peer...]
    all_gather x1, waiting for transfers between devices: 0.01 us -> 26.8 us  [on_device(): piece = lax.all_gather(tokens, 'tensor', axis=1, tiled=True)]
    all_to_all x1, waiting for transfers between devices: 0.01 us -> 9.73 us  [on_device(): lax.all_to_all(up_rows, 'dp', split_axis=0, concat_axis=0, tiled=True)]
    unnamed x23 -> x39, local copies, waits for them, and re-layouts: 4.34 us -> 13.4 us
  transfers between devices with their start and end apart: 11 -> 11, of which waited for: 6 -> 9; matrix products, arithmetic and copies ran while one was open for 9% -> 14% of each run, Pallas kernels for 60% -> 5%
where the time goes in v5:
time: 359 us; the launch traced here: 358 us
  waiting for transfers between devices  209 us (58%)
  Pallas kernels  33.1 us (9%)
  matrix products  31.3 us (9%)
  local copies, waits for them, and re-layouts  28.5 us (8%)
  starting transfers between devices  23.9 us (7%)
  between operations  14.9 us (4%)
  blocking collectives  12.8 us (4%)
  other arithmetic  3.87 us (1%)
    ppermute x7, waiting for transfers between devices, swap(): lax.ppermute(array, 'dp', [(peer, peer ^ distance) for peer in range(peer...  166 us
    all_gather x1, waiting for transfers between devices, on_device(): piece = lax.all_gather(tokens, 'tensor', axis=1, tiled=True)  26.8 us
    dot_general x1, matrix products, on_device(): jnp.dot(piece, query_weight, preferred_element_type=jnp.float32)  18.3 us
    pallas_call x1, Pallas kernels, attend(): pl.pallas_call(attention_kernel, out_shape=jax.ShapeDtypeStruct((rows, q_...  13.5 us
    unnamed x39, local copies, waits for them, and re-layouts  13.4 us
    pallas_call x2, Pallas kernels, serve(): pl.pallas_call(serve_kernel, out_shape=[jax.ShapeDtypeStruct(shape, store...  12.9 us
    psum x1, blocking collectives, on_device(): shrink = lax.psum(shrink_part, 'tensor').astype(jnp.bfloat16)  12.8 us
    all_to_all x1, waiting for transfers between devices, on_device(): lax.all_to_all(up_rows, 'dp', split_axis=0, concat_axis=0, tiled=True)  9.73 us
  transfers between devices with their start and end apart: 11, of which 9 were waited for; matrix products, arithmetic and copies ran while one was open for 14% of the time, Pallas kernels for 5%

profile of v5, /device:TPU:0, one launch (start us, length us, event | category | flops | bytes accessed | tf_op | source)
XLA Modules:
  0.0 357.6 jit_solution(1588684451239369554)
XLA Ops:
  7.2 0.7 all-gather.2.cloned.1.call-update
  7.9 0.8 pad_add_fusion.1
  8.7 0.6 broadcast_in_dim.172
  9.3 7.3 %all-to-all-start = ((s32[8,1,160]{2,1,0:T(1,128)}), s32[8,1,160]{2,1,0:T(1,128)S(1)}, u32[]{:S(2)}, u32[]{:S(2)}) async-start(s32[8,1,160]{2,1,0:T(1,128)} %broadcast_in_dim.172), calls=%async_computation | async-start | bytes 16384 | tf_op jit(solution)/shard_map/all_to_all | solution.py:254
  16.6 6.5 %all-to-all-done = s32[8,1,160]{2,1,0:T(1,128)S(1)} async-done(((s32[8,1,160]{2,1,0:T(1,128)}), s32[8,1,160]{2,1,0:T(1,128)S(1)}, u32[]{:S(2)}, u32[]{:S(2)}) %all-to-all-start) | async-done | bytes 5152 | tf_op jit(solution)/shard_map/all_to_all | solution.py:254
  23.1 0.3 convert_reduce_fusion.1
  23.7 0.6 collective-permute-start
  24.3 0.6 gather_fusion.2
  24.9 0.2 convert_reduce_fusion
  25.2 0.2 select_reduce_fusion
  25.5 1.9 copy-done.1
  27.4 6.5 %serve.2 = (bf16[16,64,512]{2,1,0:T(8,128)(2,1)}, bf16[16,64,512]{2,1,0:T(8,128)(2,1)}, bf16[16,64,512]{2,1,0:T(8,128)(2,1)}) custom-call(s32[48]{0:T(128)S(1)} %reshape.363.asked_ref, bf16[48,64,512]{2,1,0:T(8,128)(2,1)S(1)} %copy-done.1), custom_call_target="tpu_custom_call" | custom-call | bytes 6291456 | tf_op jit(solution)/shard_map/serve/pallas_call | solution.py:179
  33.9 0.8 collective-permute-start.1
  34.7 0.7 collective-permute-start.2
  35.4 2.0 collective-permute-start.3
  37.5 6.3 %gather_fusion.1 = bf16[16,2048,64]{1,2,0:T(8,128)(2,1)} fusion(bf16[32,2048,64]{1,2,0:T(8,128)(2,1)} %param.14, s32[1024]{0:T(1024)S(1)} %pad_clamp_fusion.1), kind=kCustom, calls=%fused_computation.1 | custom fusion | bytes 8388672 | tf_op jit(solution)/shard_map/gather | solution.py:276
  43.8 26.8 %all-gather.2.cloned.1.call-done = bf16[512,8192]{1,0:T(8,128)(2,1)} async-done(((bf16[512,2048]{1,0:T(8,128)(2,1)}), bf16[512,8192]{1,0:T(8,128)(2,1)}) %all-gather.2.cloned.1.call-update) | async-done | bytes 8388624 | tf_op jit(solution)/shard_map/all_gather | solution.py:279
  70.6 18.3 %fusion.23.base_hbm = f32[512,1024]{1,0:T(8,128)} fusion(bf16[512,8192]{1,0:T(8,128)(2,1)} %all-gather.2.cloned.1.call-done, bf16[8192,1024]{1,0:T(8,128)(2,1)} %param.12), kind=kOutput, calls=%fused_computation.88 | convolution fusion | flops 8589934592 | bytes 27262976 | tf_op jit(solution)/shard_map/dot_general | solution.py:280
  88.9 7.7 %convolution_convert_fusion.cache_hbm = bf16[512,512]{1,0:T(8,128)(2,1)} fusion(bf16[512,8192]{1,0:T(8,128)(2,1)S(1)} %copy-done.18, bf16[8192,512]{1,0:T(8,128)(2,1)} %param.13), kind=kOutput, calls=%fused_computation.7 | convolution fusion | flops 4295229440 | bytes 17301504 | tf_op jit(solution)/shard_map/dot_general | solution.py:281
  96.7 19.0 %collective-permute-done.2.refs_2_ = bf16[16,64,512]{2,1,0:T(8,128)(2,1)} collective-permute-done((bf16[16,64,512]{2,1,0:T(8,128)(2,1)}, bf16[16,64,512]{2,1,0:T(8,128)(2,1)}, u32[]{:S(2)}, u32[]{:S(2)}) %collective-permute-start.2) | collective-permute-done | bytes 1048608 | tf_op jit(solution)/shard_map/ppermute | solution.py:249
  115.6 19.9 %collective-permute-done.3.refs_3_ = bf16[16,64,512]{2,1,0:T(8,128)(2,1)} collective-permute-done((bf16[16,64,512]{2,1,0:T(8,128)(2,1)}, bf16[16,64,512]{2,1,0:T(8,128)(2,1)}, u32[]{:S(2)}, u32[]{:S(2)}) %collective-permute-start.3) | collective-permute-done | bytes 1048608 | tf_op jit(solution)/shard_map/ppermute | solution.py:249
  135.5 25.1 %collective-permute-done.store_ref.refs_4_ = bf16[48,64,512]{2,1,0:T(8,128)(2,1)S(1)} collective-permute-done((bf16[48,64,512]{2,1,0:T(8,128)(2,1)}, bf16[48,64,512]{2,1,0:T(8,128)(2,1)S(1)}, u32[]{:S(2)}, u32[]{:S(2)}) %collective-permute-start) | collective-permute-done | bytes 3145760 | tf_op jit(solution)/shard_map/ppermute | solution.py:249
  160.6 4.6 %all-to-all-start.1 = ((bf16[16,2048,64]{1,2,0:T(8,128)(2,1)}), bf16[16,2048,64]{1,2,0:T(8,128)(2,1)}, u32[]{:S(2)}, u32[]{:S(2)}) async-start(bf16[16,2048,64]{1,2,0:T(8,128)(2,1)} %gather_fusion.1), calls=%async_computation.1 | async-start | bytes 8388608 | tf_op jit(solution)/shard_map/all_to_all | solution.py:286
  165.3 6.5 %serve.3 = (bf16[16,64,512]{2,1,0:T(8,128)(2,1)}, bf16[16,64,512]{2,1,0:T(8,128)(2,1)}, bf16[16,64,512]{2,1,0:T(8,128)(2,1)}) custom-call(s32[48]{0:T(128)S(1)} %reshape.364.asked_ref, bf16[48,64,512]{2,1,0:T(8,128)(2,1)S(1)} %collective-permute-done.store_ref.refs_4_), custom_call_target="tpu_custom_call" | custom-call | bytes 6291456 | tf_op jit(solution)/shard_map/serve/pallas_call | solution.py:179
  171.8 2.0 collective-permute-start.4
  173.7 1.5 collective-permute-start.5
  175.2 0.2 collective-permute-start.6
  175.4 4.2 %gather_fusion = bf16[16,64,1024]{2,1,0:T(8,128)(2,1)} fusion(bf16[32,64,1024]{2,1,0:T(8,128)(2,1)} %param.15, s32[1024]{0:T(1024)S(1)} %pad_clamp_fusion.1), kind=kCustom, calls=%fused_computation | custom fusion | bytes 4194368 | tf_op jit(solution)/shard_map/gather | solution.py:277
  179.6 55.7 %collective-permute-done.4.refs_5_ = bf16[16,64,512]{2,1,0:T(8,128)(2,1)S(1)} collective-permute-done((bf16[16,64,512]{2,1,0:T(8,128)(2,1)}, bf16[16,64,512]{2,1,0:T(8,128)(2,1)S(1)}, u32[]{:S(2)}, u32[]{:S(2)}) %collective-permute-start.4) | collective-permute-done | bytes 1048608 | tf_op jit(solution)/shard_map/ppermute | solution.py:249
  235.3 22.3 %collective-permute-done.5.refs_6_ = bf16[16,64,512]{2,1,0:T(8,128)(2,1)S(1)} collective-permute-done((bf16[16,64,512]{2,1,0:T(8,128)(2,1)}, bf16[16,64,512]{2,1,0:T(8,128)(2,1)S(1)}, u32[]{:S(2)}, u32[]{:S(2)}) %collective-permute-start.5) | collective-permute-done | bytes 1048608 | tf_op jit(solution)/shard_map/ppermute | solution.py:249
  257.6 23.6 %collective-permute-done.6.refs_7_ = bf16[16,64,512]{2,1,0:T(8,128)(2,1)S(1)} collective-permute-done((bf16[16,64,512]{2,1,0:T(8,128)(2,1)}, bf16[16,64,512]{2,1,0:T(8,128)(2,1)S(1)}, u32[]{:S(2)}, u32[]{:S(2)}) %collective-permute-start.6) | collective-permute-done | bytes 1048608 | tf_op jit(solution)/shard_map/ppermute | solution.py:249
  281.2 4.4 %all-to-all-start.2 = ((bf16[16,64,1024]{2,1,0:T(8,128)(2,1)}), bf16[16,64,1024]{2,1,0:T(8,128)(2,1)}, u32[]{:S(2)}, u32[]{:S(2)}) async-start(bf16[16,64,1024]{2,1,0:T(8,128)(2,1)} %gather_fusion), calls=%async_computation.2 | async-start | bytes 4194304 | tf_op jit(solution)/shard_map/all_to_all | solution.py:290
  286.0 0.5 slice.35
  287.9 5.2 %fusion = f32[512,64]{0,1:T(8,128)S(1)} fusion(bf16[16,2048,64]{1,2,0:T(8,128)(2,1)} %all-to-all-done.1, bf16[512,2048]{1,0:T(8,128)(2,1)} %param.11, pred[512,16]{0,1:T(8,128)(4,1)S(1)} %iota_compare_fusion.2), kind=kOutput, calls=%fused_computation.4 | convolution fusion | flops 2148499456 | bytes 6430720 | tf_op jit(solution)/shard_map/tn,snk->tsk/dot_general | solution.py:300
  293.2 12.8 %all-reduce.1 = bf16[512,64]{0,1:T(8,128)(2,1)S(1)} all-reduce(f32[512,64]{0,1:T(8,128)S(1)} %fusion), channel_id=1, replica_groups=mesh['dp'=8,'tensor'=4] {'tensor'}, use_global_device_ids=true, to_apply=%region_15.16 | all-reduce | flops 32768 | bytes 196608 | tf_op jit(solution)/shard_map/psum | solution.py:302
  306.0 1.0 broadcast_select_fusion
  307.1 2.3 copy.37.spread_ref
  309.3 1.9 copy-done.4
  311.2 1.2 copy-done.8
  312.5 1.2 copy-done.10
  313.7 1.2 copy-done.12
  314.9 6.7 %assemble.1.pages_hbm = bf16[64,64,512]{2,1,0:T(8,128)(2,1)S(1)} custom-call(s32[64]{0:T(128)S(1)} %get-tuple-element.51.source_ref, s32[64]{0:T(128)S(1)} %get-tuple-element.50.place_ref, bf16[48,64,512]{2,1,0:T(8,128)(2,1)S(1)} %copy-done.2, bf16[16,64,512]{2,1,0:T(8,128)(2,1)} %collective-permute-done.1.refs_1_, ...), custom_call_target="tpu_custom_call" | custom-call | bytes 8388608 | tf_op jit(solution)/shard_map/assemble/pallas_call | solution.py:215
  321.6 2.1 copy-done
  323.7 9.7 %all-to-all-done.2 = bf16[16,64,1024]{2,1,0:T(8,128)(2,1)} async-done(((bf16[16,64,1024]{2,1,0:T(8,128)(2,1)}), bf16[16,64,1024]{2,1,0:T(8,128)(2,1)}, u32[]{:S(2)}, u32[]{:S(2)}) %all-to-all-start.2) | async-done | bytes 2097184 | tf_op jit(solution)/shard_map/all_to_all | solution.py:290
  333.4 1.2 copy-done.5
  334.7 1.6 copy-done.6
  336.2 1.0 copy-done.13
  337.3 13.5 %attend.1 = bf16[512,1024]{1,0:T(8,128)(2,1)} custom-call(s32[4,32]{1,0:T(4,128)S(1)} %pad_add_fusion.steps_ref, bf16[512,1024]{1,0:T(8,128)(2,1)S(1)} %copy-done.5, bf16[1024,1024]{1,0:T(8,128)(2,1)} %bitcast.16.up_ref, f32[512,1024]{1,0:T(8,128)S(1)} %copy-done.6, bf16[512,512]{1,0:T(8,128)(2,1)S(1)} %copy-done.13, bf16[64,64,512]{2,1,0:T(8,128)(2,1)} %copy-done), custom_call_target="tpu_custom_call" | custom-call | flops 2818572288 | bytes 11010048 | tf_op jit(solution)/shard_map/attend/pallas_call | solution.py:143
  (67 shorter events, 2.0 us)
Async XLA Ops:
  7.2 63.5 %all-gather.2.cloned.1.call-start = ((), (), s32[]{:S(2)}) async-start(), calls=%async_computation.3 | async-start | bytes 10485760 | tf_op jit(solution)/shard_map/all_gather | solution.py:279
  9.3 13.8 %all-to-all-start = ((s32[8,1,160]{2,1,0:T(1,128)}), s32[8,1,160]{2,1,0:T(1,128)S(1)}, u32[]{:S(2)}, u32[]{:S(2)}) async-start(s32[8,1,160]{2,1,0:T(1,128)} %broadcast_in_dim.172), calls=%async_computation | async-start | bytes 16384 | tf_op jit(solution)/shard_map/all_to_all | solution.py:254
  23.7 136.9 %collective-permute-start = (bf16[48,64,512]{2,1,0:T(8,128)(2,1)}, bf16[48,64,512]{2,1,0:T(8,128)(2,1)S(1)}, u32[]{:S(2)}, u32[]{:S(2)}) collective-permute-start(bf16[48,64,512]{2,1,0:T(8,128)(2,1)} %refs_0_), channel_id=1, source_target_pairs={{0,16},{4,20},{8,24},{12,28},{16,0},{20,4},{24,8},{28,12},{1,17},{... | collective-permute-start | bytes 9437192 | tf_op jit(solution)/shard_map/ppermute | solution.py:249
  25.5 1.9 copy-start.1
  33.9 62.8 %collective-permute-start.1 = (bf16[16,64,512]{2,1,0:T(8,128)(2,1)}, bf16[16,64,512]{2,1,0:T(8,128)(2,1)}, u32[]{:S(2)}, u32[]{:S(2)}) collective-permute-start(bf16[16,64,512]{2,1,0:T(8,128)(2,1)} %get-tuple-element.26), channel_id=1, source_target_pairs={{0,4},{4,0},{8,12},{12,8},{16,20},{20,16},{24,28},{28,24},{1,5},{5... | collective-permute-start | bytes 3145736 | tf_op jit(solution)/shard_map/ppermute | solution.py:249
  34.7 81.0 %collective-permute-start.2 = (bf16[16,64,512]{2,1,0:T(8,128)(2,1)}, bf16[16,64,512]{2,1,0:T(8,128)(2,1)}, u32[]{:S(2)}, u32[]{:S(2)}) collective-permute-start(bf16[16,64,512]{2,1,0:T(8,128)(2,1)} %get-tuple-element.27), channel_id=1, source_target_pairs={{0,8},{4,12},{8,0},{12,4},{16,24},{20,28},{24,16},{28,20},{1,9},{5... | collective-permute-start | bytes 3145736 | tf_op jit(solution)/shard_map/ppermute | solution.py:249
  35.4 100.1 %collective-permute-start.3 = (bf16[16,64,512]{2,1,0:T(8,128)(2,1)}, bf16[16,64,512]{2,1,0:T(8,128)(2,1)}, u32[]{:S(2)}, u32[]{:S(2)}) collective-permute-start(bf16[16,64,512]{2,1,0:T(8,128)(2,1)} %get-tuple-element.28), channel_id=1, source_target_pairs={{0,12},{4,8},{8,4},{12,0},{16,28},{20,24},{24,20},{28,16},{1,13},{... | collective-permute-start | bytes 3145736 | tf_op jit(solution)/shard_map/ppermute | solution.py:249
  70.6 18.3 %copy-start.18 = (bf16[512,8192]{1,0:T(8,128)(2,1)S(1)}, bf16[512,8192]{1,0:T(8,128)(2,1)}, u32[]{:S(2)}) copy-start(bf16[512,8192]{1,0:T(8,128)(2,1)} %all-gather.2.cloned.1.call-done) | copy-start | bytes 25165828
  160.6 4.7 %copy-start.3 = (bf16[48,64,512]{2,1,0:T(8,128)(2,1)}, bf16[48,64,512]{2,1,0:T(8,128)(2,1)S(1)}, u32[]{:S(2)}) copy-start(bf16[48,64,512]{2,1,0:T(8,128)(2,1)S(1)} %collective-permute-done.store_ref.refs_4_) | copy-start | bytes 9437188
  160.6 120.6 %all-to-all-start.1 = ((bf16[16,2048,64]{1,2,0:T(8,128)(2,1)}), bf16[16,2048,64]{1,2,0:T(8,128)(2,1)}, u32[]{:S(2)}, u32[]{:S(2)}) async-start(bf16[16,2048,64]{1,2,0:T(8,128)(2,1)} %gather_fusion.1), calls=%async_computation.1 | async-start | bytes 8388608 | tf_op jit(solution)/shard_map/all_to_all | solution.py:286
  171.8 63.5 %collective-permute-start.4 = (bf16[16,64,512]{2,1,0:T(8,128)(2,1)}, bf16[16,64,512]{2,1,0:T(8,128)(2,1)S(1)}, u32[]{:S(2)}, u32[]{:S(2)}) collective-permute-start(bf16[16,64,512]{2,1,0:T(8,128)(2,1)} %get-tuple-element.31), channel_id=1, source_target_pairs={{0,4},{4,0},{8,12},{12,8},{16,20},{20,16},{24,28},{28,24},{1,5},{5... | collective-permute-start | bytes 3145736 | tf_op jit(solution)/shard_map/ppermute | solution.py:249
  173.7 83.9 %collective-permute-start.5 = (bf16[16,64,512]{2,1,0:T(8,128)(2,1)}, bf16[16,64,512]{2,1,0:T(8,128)(2,1)S(1)}, u32[]{:S(2)}, u32[]{:S(2)}) collective-permute-start(bf16[16,64,512]{2,1,0:T(8,128)(2,1)} %get-tuple-element.32), channel_id=1, source_target_pairs={{0,8},{4,12},{8,0},{12,4},{16,24},{20,28},{24,16},{28,20},{1,9},{5... | collective-permute-start | bytes 3145736 | tf_op jit(solution)/shard_map/ppermute | solution.py:249
  175.2 110.4 %copy-start.14 = (s32[1,16]{1,0:T(1,128)S(1)}, s32[1,16]{1,0:T(1,128)}, u32[]{:S(2)}) copy-start(s32[1,16]{1,0:T(1,128)} %param.17) | copy-start | bytes 196
  175.2 112.2 %copy-start.17 = (s32[16,1]{0,1:T(1,128)S(1)}, s32[16,1]{0,1:T(1,128)}, u32[]{:S(2)}) copy-start(s32[16,1]{0,1:T(1,128)} %param.18) | copy-start | bytes 196
  175.2 112.4 %copy-start.16 = (s32[64,1]{0,1:T(1,128)S(1)}, s32[64,1]{0,1:T(1,128)}, u32[]{:S(2)}) copy-start(s32[64,1]{0,1:T(1,128)} %param.20) | copy-start | bytes 772
  175.2 112.7 %copy-start.15 = (s32[64]{0:T(128)S(1)}, s32[64]{0:T(128)}, u32[]{:S(2)}) copy-start(s32[64]{0:T(128)} %param.21) | copy-start | bytes 772
  175.2 106.0 %collective-permute-start.6 = (bf16[16,64,512]{2,1,0:T(8,128)(2,1)}, bf16[16,64,512]{2,1,0:T(8,128)(2,1)S(1)}, u32[]{:S(2)}, u32[]{:S(2)}) collective-permute-start(bf16[16,64,512]{2,1,0:T(8,128)(2,1)} %get-tuple-element.33), channel_id=1, source_target_pairs={{0,12},{4,8},{8,4},{12,0},{16,28},{20,24},{24,20},{28,16},{1,13},{... | collective-permute-start | bytes 3145736 | tf_op jit(solution)/shard_map/ppermute | solution.py:249
  235.3 52.6 %copy-start.7 = (bf16[16,64,512]{2,1,0:T(8,128)(2,1)}, bf16[16,64,512]{2,1,0:T(8,128)(2,1)S(1)}, u32[]{:S(2)}) copy-start(bf16[16,64,512]{2,1,0:T(8,128)(2,1)S(1)} %collective-permute-done.4.refs_5_) | copy-start | bytes 3145732
  257.6 30.3 %copy-start.9 = (bf16[16,64,512]{2,1,0:T(8,128)(2,1)}, bf16[16,64,512]{2,1,0:T(8,128)(2,1)S(1)}, u32[]{:S(2)}) copy-start(bf16[16,64,512]{2,1,0:T(8,128)(2,1)S(1)} %collective-permute-done.5.refs_6_) | copy-start | bytes 3145732
  281.2 6.7 %copy-start.11 = (bf16[16,64,512]{2,1,0:T(8,128)(2,1)}, bf16[16,64,512]{2,1,0:T(8,128)(2,1)S(1)}, u32[]{:S(2)}) copy-start(bf16[16,64,512]{2,1,0:T(8,128)(2,1)S(1)} %collective-permute-done.6.refs_7_) | copy-start | bytes 3145732
  281.2 52.2 %all-to-all-start.2 = ((bf16[16,64,1024]{2,1,0:T(8,128)(2,1)}), bf16[16,64,1024]{2,1,0:T(8,128)(2,1)}, u32[]{:S(2)}, u32[]{:S(2)}) async-start(bf16[16,64,1024]{2,1,0:T(8,128)(2,1)} %gather_fusion), calls=%async_computation.2 | async-start | bytes 4194304 | tf_op jit(solution)/shard_map/all_to_all | solution.py:290
  293.2 16.2 %copy-start.2 = (bf16[48,64,512]{2,1,0:T(8,128)(2,1)S(1)}, bf16[48,64,512]{2,1,0:T(8,128)(2,1)}, u32[]{:S(2)}) copy-start(bf16[48,64,512]{2,1,0:T(8,128)(2,1)} %refs_0_) | copy-start | bytes 9437188
  309.3 1.9 copy-start.4
  311.2 1.2 copy-start.8
  312.5 1.2 copy-start.10
  313.7 1.2 copy-start.12
  321.6 2.1 copy-start
  333.4 1.2 copy-start.5
  334.6 1.6 copy-start.6
  336.2 1.0 copy-start.13
Sparse Core Ops, SparseCore 0:
  9.6 61.0 all-gather.1

commit v6 on v5

--- a/solution.py
+++ b/solution.py
@@ -14,6 +14,7 @@
 MOST = 128
 BLOCK = 32
 TOGETHER = 4
+HALVES = 2
 
 ADAPTER_SCALE = 0.5
 NEGATIVE = -1e30
@@ -47,14 +48,10 @@
     return jnp.stack([request, block, at(starts), at(ends)])
 
 
-def attention_kernel(
-    steps_ref, spread_ref, up_ref, base_hbm, cache_hbm, pages_hbm, out_ref, query_ref, base_ref, cache_ref, pages_ref, sems
-):
-    copies = [
-        pltpu.make_async_copy(base_hbm, base_ref, sems.at[0]),
-        pltpu.make_async_copy(cache_hbm, cache_ref, sems.at[1]),
-        pltpu.make_async_copy(pages_hbm, pages_ref, sems.at[2]),
-    ]
+def attention_kernel(steps_ref, spread_hbm, up_hbm, base_hbm, cache_hbm, pages_hbm, out_ref, query_ref, *rest):
+    spread_ref, up_ref, base_ref, cache_ref, pages_ref, sems = rest
+    pairs = [(spread_hbm, spread_ref), (up_hbm, up_ref), (base_hbm, base_ref), (cache_hbm, cache_ref), (pages_hbm, pages_ref)]
+    copies = [pltpu.make_async_copy(*pair, sems.at[index]) for index, pair in enumerate(pairs)]
     for copy in copies:
         copy.start()
     rows_total, q_cols = base_ref.shape
@@ -62,7 +59,8 @@
     group = q_cols // HEAD_WIDTH // kv_heads
     window = min(rows_total, MOST + BLOCK)
     sharp = HEAD_WIDTH ** -0.5 * math.log2(math.e)
-    copies[0].wait()
+    for copy in copies[:3]:
+        copy.wait()
 
     def project(index, carry):
         cols = pl.ds(pl.multiple_of(index * 256, 256), 256)
@@ -72,8 +70,8 @@
 
     lax.fori_loop(0, q_cols // 256, project, 0)
 
-    copies[1].wait()
-    copies[2].wait()
+    for copy in copies[3:]:
+        copy.wait()
     dims = (((1,), (1,)), ((), ()))
 
     def several(turn, carry):
@@ -139,18 +137,15 @@
     rows, q_cols = query_base.shape
     steps_total = -(-(rows // BLOCK + starts.shape[0] - 1) // TOGETHER) * TOGETHER
     steps = attention_steps(starts, ends, steps_total)
-    vmem = pl.BlockSpec(memory_space=pltpu.VMEM)
     return pl.pallas_call(
         attention_kernel,
         out_shape=jax.ShapeDtypeStruct((rows, q_cols), jnp.bfloat16),
-        in_specs=[pl.BlockSpec(memory_space=pltpu.SMEM)] + [vmem] * 2 + [pl.BlockSpec(memory_space=pl.ANY)] * 3,
-        out_specs=vmem,
+        in_specs=[pl.BlockSpec(memory_space=pltpu.SMEM)] + [pl.BlockSpec(memory_space=pltpu.HBM)] * 5,
+        out_specs=pl.BlockSpec(memory_space=pltpu.VMEM),
         scratch_shapes=[
             pltpu.VMEM((rows, q_cols), jnp.bfloat16),
-            pltpu.VMEM(query_base.shape, query_base.dtype),
-            pltpu.VMEM(cache.shape, cache.dtype),
-            pltpu.VMEM(pages.shape, pages.dtype),
-            pltpu.SemaphoreType.DMA((3,)),
+            *[pltpu.VMEM(each.shape, each.dtype) for each in (spread, up, query_base, cache, pages)],
+            pltpu.SemaphoreType.DMA((5,)),
         ],
         compiler_params=pltpu.CompilerParams(vmem_limit_bytes=48 * 1024 * 1024),
         cost_estimate=pl.CostEstimate(
@@ -174,12 +169,11 @@
 
 def serve(asked, store):
     blocks, capacity = asked.shape
-    anywhere = pl.BlockSpec(memory_space=pl.ANY)
     shape = (capacity,) + store.shape[1:]
     return pl.pallas_call(
         serve_kernel,
         out_shape=[jax.ShapeDtypeStruct(shape, store.dtype)] * blocks,
-        in_specs=[pl.BlockSpec(memory_space=pltpu.SMEM), anywhere],
+        in_specs=[pl.BlockSpec(memory_space=pltpu.SMEM), pl.BlockSpec(memory_space=pltpu.HBM)],
         out_specs=[pl.BlockSpec(memory_space=pltpu.VMEM)] * blocks,
         scratch_shapes=[pltpu.SemaphoreType.DMA((blocks,))],
         compiler_params=pltpu.CompilerParams(vmem_limit_bytes=16 * 1024 * 1024),
@@ -191,16 +185,25 @@
 
 
 def assemble_kernel(source_ref, place_ref, *refs):
-    sources, out, sem = refs[:-2], refs[-2], refs[-1]
+    out, sem = refs[-2:]
+    half = (len(refs) - 2) // (1 + HALVES)
+    near, far = refs[:half], refs[half:-2]
+    width = far[0].shape[2]
 
     def one(index, carry):
         source = source_ref[index]
         place = place_ref[index]
-        for number, ref in enumerate(sources):
+        for number in range(half):
 
             @pl.when(source == number)
             def _():
-                pltpu.make_async_copy(ref.at[place], out.at[index], sem).start()
+                pltpu.make_async_copy(near[number].at[place], out.at[index], sem).start()
+
+            @pl.when(source == half + number)
+            def _():
+                for part in range(HALVES):
+                    columns = out.at[index, :, part * width : (part + 1) * width]
+                    pltpu.make_async_copy(far[part * half + number].at[place], columns, sem).start()
 
         return carry
 
@@ -208,14 +211,14 @@
     pltpu.make_async_copy(out, out, sem).wait()
 
 
-def assemble(source, place, sources):
-    anywhere = pl.BlockSpec(memory_space=pl.ANY)
+def assemble(source, place, near, far):
     scalars = pl.BlockSpec(memory_space=pltpu.SMEM)
-    shape = (source.shape[0],) + sources[0].shape[1:]
+    sources = [*near, *far]
+    shape = (source.shape[0],) + near[0].shape[1:]
     return pl.pallas_call(
         assemble_kernel,
-        out_shape=jax.ShapeDtypeStruct(shape, sources[0].dtype),
-        in_specs=[scalars, scalars] + [anywhere] * len(sources),
+        out_shape=jax.ShapeDtypeStruct(shape, near[0].dtype),
+        in_specs=[scalars, scalars] + [pl.BlockSpec(memory_space=pltpu.HBM)] * len(sources),
         out_specs=pl.BlockSpec(memory_space=pltpu.VMEM),
         scratch_shapes=[pltpu.SemaphoreType.DMA],
         compiler_params=pltpu.CompilerParams(vmem_limit_bytes=16 * 1024 * 1024),
@@ -254,8 +257,11 @@
     everyone = lax.all_to_all(
         jnp.broadcast_to(raw[None], (peers, raw.shape[0])), "dp", split_axis=0, concat_axis=0, tiled=True
     )
-    store, down_store, everyone = lax.optimization_barrier((keyvalue_page_store, adapter_down_weight, everyone))
-    mirrored_store = swap(store, half)
+    width = keyvalue_page_store.shape[2] // HALVES
+    parts = [keyvalue_page_store[:, :, part * width : (part + 1) * width] for part in range(HALVES)]
+    store, down_store, everyone, *parts = lax.optimization_barrier(
+        (keyvalue_page_store, adapter_down_weight, everyone, *parts)
+    )
 
     page_cap = max(2, 2 * page_count // peers)
     group = everyone[jnp.arange(half, dtype=jnp.int32) ^ me]
@@ -280,14 +286,22 @@
     query_base = jnp.dot(piece, query_weight, preferred_element_type=jnp.float32)
     new_cache = jnp.dot(piece, keyvalue_weight, preferred_element_type=jnp.float32).astype(jnp.bfloat16)
 
-    down_rows, mirrored_store, query_base, new_cache, *near = lax.optimization_barrier(
-        (down_rows, mirrored_store, query_base, new_cache, *near)
+    mirrored = []
+    far = []
+    for part in range(HALVES):
+        mirrored.append(swap(parts[part], half))
+        if part + 1 < HALVES:
+            mirrored[part], parts[part + 1], down_rows = lax.optimization_barrier(
+                (mirrored[part], parts[part + 1], down_rows)
+            )
+        far.append(serve(far_asked[1:], mirrored[part]))
+    down_sent = lax.all_to_all(down_rows, "dp", split_axis=0, concat_axis=0, tiled=True)
+    far = [[swap(pages, i + 1) for i, pages in enumerate(block)] for block in far[:-1]] + far[-1:]
+    up_rows, down_sent, query_base, new_cache, far, near = lax.optimization_barrier(
+        (up_rows, down_sent, query_base, new_cache, far, near)
     )
-    down_sent = lax.all_to_all(down_rows, "dp", split_axis=0, concat_axis=0, tiled=True)
-    far = serve(far_asked[1:], mirrored_store)
-    far = [swap(pages, i + 1) for i, pages in enumerate(far)]
-    up_rows, down_sent, *far = lax.optimization_barrier((up_rows, down_sent, *far))
     up_sent = lax.all_to_all(up_rows, "dp", split_axis=0, concat_axis=0, tiled=True)
+    far[-1] = [swap(pages, i + 1) for i, pages in enumerate(far[-1])]
 
     lengths = span_token_length[0]
     ends = jnp.cumsum(lengths)
@@ -301,7 +315,8 @@
     shrink_part = jnp.sum(jnp.where(in_slot[:, :, None], down_part, 0.0), axis=1)
     shrink = lax.psum(shrink_part, "tensor").astype(jnp.bfloat16)
     spread = jnp.where(in_slot[:, :, None], shrink[:, None, :], 0).reshape(tok_rows, adapter_slots * rank)
-    prefix_pages = assemble(page_source, page_place, [store, *near, mirrored_store, *far])
+    far = [page for part in range(HALVES) for page in (mirrored[part], *far[part])]
+    prefix_pages = assemble(page_source, page_place, [store, *near], far)
     up = up_sent.reshape(adapter_slots * rank, q_cols)
     out = attend(query_base, spread, up, new_cache, prefix_pages, starts, ends)
     return (out, new_cache)

time: 359 us -> 392 us (1.092)
  waiting for transfers between devices: 209 us -> 237 us
  starting transfers between devices: 23.9 us -> 31.5 us
    ppermute x7 -> x11, waiting for transfers between devices: 166 us -> 233 us  [swap(): lax.ppermute(array, 'dp', [(peer, peer ^ distance) for peer in range(peer...]
    all_gather x1, waiting for transfers between devices: 26.8 us -> 0.01 us  [on_device(): piece = lax.all_gather(tokens, 'tensor', axis=1, tiled=True)]
    all_to_all x1, waiting for transfers between devices: 9.73 us -> 0.01 us  [on_device(): lax.all_to_all(up_rows, 'dp', split_axis=0, concat_axis=0, tiled=True)]
    ppermute x7 -> x11, starting transfers between devices: 7.72 us -> 14.9 us  [swap(): lax.ppermute(array, 'dp', [(peer, peer ^ distance) for peer in range(peer...]
    pallas_call x2 -> x3, Pallas kernels: 12.9 us -> 12.9 us  [serve(): pl.pallas_call(serve_kernel, out_shape=[jax.ShapeDtypeStruct(shape, store...]
    unnamed x39 -> x41, local copies, waits for them, and re-layouts: 13.4 us -> 13.4 us
  transfers between devices with their start and end apart: 11 -> 15, of which waited for: 9 -> 7; matrix products, arithmetic and copies ran while one was open for 14% -> 13% of each run, Pallas kernels for 5% -> 4%
where the time goes in v6:
time: 392 us; the launch traced here: 391 us
  waiting for transfers between devices  237 us (60%)
  local copies, waits for them, and re-layouts  32 us (8%)
  starting transfers between devices  31.5 us (8%)
  Pallas kernels  30.6 us (8%)
  matrix products  28.9 us (7%)
  between operations  15 us (4%)
  blocking collectives  12.4 us (3%)
    ppermute x11, waiting for transfers between devices, swap(): lax.ppermute(array, 'dp', [(peer, peer ^ distance) for peer in range(peer...  233 us
    dot_general x1, matrix products, on_device(): jnp.dot(piece, query_weight, preferred_element_type=jnp.float32)  15.9 us
    ppermute x11, starting transfers between devices, swap(): lax.ppermute(array, 'dp', [(peer, peer ^ distance) for peer in range(peer...  14.9 us
    pallas_call x1, Pallas kernels, attend(): pl.pallas_call(attention_kernel, out_shape=jax.ShapeDtypeStruct((rows, q_...  13.6 us
    unnamed x41, local copies, waits for them, and re-layouts  13.4 us
    pallas_call x3, Pallas kernels, serve(): pl.pallas_call(serve_kernel, out_shape=[jax.ShapeDtypeStruct(shape, store...  12.9 us
    psum x1, blocking collectives, on_device(): shrink = lax.psum(shrink_part, 'tensor').astype(jnp.bfloat16)  12.4 us
  transfers between devices with their start and end apart: 15, of which 7 were waited for; matrix products, arithmetic and copies ran while one was open for 13% of the time, Pallas kernels for 4%

profile of v6, /device:TPU:0, one launch (start us, length us, event | category | flops | bytes accessed | tf_op | source)
XLA Modules:
  0.0 391.1 jit_solution(9440275363606832832)
XLA Ops:
  7.2 0.7 all-gather.2.cloned.1.call-update
  7.9 0.8 pad_add_fusion.1
  8.7 0.6 broadcast_in_dim.172
  9.3 7.3 %all-to-all-start = ((s32[8,1,160]{2,1,0:T(1,128)}), s32[8,1,160]{2,1,0:T(1,128)S(1)}, u32[]{:S(2)}, u32[]{:S(2)}) async-start(s32[8,1,160]{2,1,0:T(1,128)} %broadcast_in_dim.172), calls=%async_computation | async-start | bytes 16384 | tf_op jit(solution)/shard_map/all_to_all | solution.py:257
  16.5 3.5 fusion.20
  20.1 3.0 all-to-all-done
  23.1 0.6 collective-permute-start
  24.4 6.3 %gather_fusion.1 = bf16[16,2048,64]{1,2,0:T(8,128)(2,1)} fusion(bf16[32,2048,64]{1,2,0:T(8,128)(2,1)} %param.14, s32[1024]{0:T(1024)S(1)} %pad_clamp_fusion.1), kind=kCustom, calls=%fused_computation.1 | custom fusion | bytes 8388672 | tf_op jit(solution)/shard_map/gather | solution.py:282
  30.7 61.6 %collective-permute-done.store_ref.refs_4_ = bf16[48,64,256]{2,1,0:T(8,128)(2,1)S(1)} collective-permute-done((bf16[48,64,256]{2,1,0:T(8,128)(2,1)S(1)}, bf16[48,64,256]{2,1,0:T(8,128)(2,1)S(1)}, u32[]{:S(2)}, u32[]{:S(2)}) %collective-permute-start) | collective-permute-done | bytes 1572896 | tf_op jit(solution)/shard_map/ppermute | solution.py:252
  92.3 1.2 copy-done.2
  93.5 4.6 %all-to-all-start.1 = ((bf16[16,2048,64]{1,2,0:T(8,128)(2,1)}), bf16[16,2048,64]{1,2,0:T(8,128)(2,1)}, u32[]{:S(2)}, u32[]{:S(2)}) async-start(bf16[16,2048,64]{1,2,0:T(8,128)(2,1)} %gather_fusion.1), calls=%async_computation.1 | async-start | bytes 8388608 | tf_op jit(solution)/shard_map/all_to_all | solution.py:298
  98.1 2.8 collective-permute-start.4
  101.0 0.6 gather_fusion.2
  102.2 4.2 %gather_fusion = bf16[16,64,1024]{2,1,0:T(8,128)(2,1)} fusion(bf16[32,64,1024]{2,1,0:T(8,128)(2,1)} %param.15, s32[1024]{0:T(1024)S(1)} %pad_clamp_fusion.1), kind=kCustom, calls=%fused_computation | custom fusion | bytes 4194368 | tf_op jit(solution)/shard_map/gather | solution.py:283
  106.5 6.4 %serve.5 = (bf16[16,64,512]{2,1,0:T(8,128)(2,1)}, bf16[16,64,512]{2,1,0:T(8,128)(2,1)}, bf16[16,64,512]{2,1,0:T(8,128)(2,1)}) custom-call(s32[48]{0:T(128)S(1)} %reshape.365.asked_ref, bf16[48,64,512]{2,1,0:T(8,128)(2,1)S(1)} %copy-done), custom_call_target="tpu_custom_call" | custom-call | bytes 6291456 | tf_op jit(solution)/shard_map/serve/pallas_call | solution.py:173
  112.9 1.5 collective-permute-start.5
  114.5 1.5 collective-permute-start.6
  116.5 3.8 serve.3
  120.3 0.8 copy-done.13
  121.1 1.5 collective-permute-start.1
  122.5 136.6 %collective-permute-done.4.store_ref.refs_8_ = bf16[48,64,256]{2,1,0:T(8,128)(2,1)} collective-permute-done((bf16[48,64,256]{2,1,0:T(8,128)(2,1)}, bf16[48,64,256]{2,1,0:T(8,128)(2,1)}, u32[]{:S(2)}, u32[]{:S(2)}) %collective-permute-start.4) | collective-permute-done | bytes 1572896 | tf_op jit(solution)/shard_map/ppermute | solution.py:252
  259.2 2.7 serve.4
  261.8 0.8 copy-done.10
  262.6 0.8 copy-done.11
  263.4 0.8 copy-done.12
  264.2 15.9 %fusion.24.base_hbm = f32[512,1024]{1,0:T(8,128)} fusion(bf16[512,8192]{1,0:T(8,128)(2,1)} %all-gather.2.cloned.1.call-done, bf16[8192,1024]{1,0:T(8,128)(2,1)} %param.12), kind=kOutput, calls=%fused_computation.89 | convolution fusion | flops 8589934592 | bytes 27262976 | tf_op jit(solution)/shard_map/dot_general | solution.py:286
  280.2 2.9 collective-permute-start.3
  283.1 7.7 %convolution_convert_fusion.cache_hbm = bf16[512,512]{1,0:T(8,128)(2,1)} fusion(bf16[512,8192]{1,0:T(8,128)(2,1)S(1)} %copy-done.19, bf16[8192,512]{1,0:T(8,128)(2,1)} %param.13), kind=kOutput, calls=%fused_computation.7 | convolution fusion | flops 4295229440 | bytes 17301504 | tf_op jit(solution)/shard_map/dot_general | solution.py:287
  290.8 3.3 collective-permute-done.3.refs_7_
  294.2 0.8 copy-done.8
  295.0 4.7 %all-to-all-start.2 = ((bf16[16,64,1024]{2,1,0:T(8,128)(2,1)}), bf16[16,64,1024]{2,1,0:T(8,128)(2,1)}, u32[]{:S(2)}, u32[]{:S(2)}) async-start(bf16[16,64,1024]{2,1,0:T(8,128)(2,1)} %gather_fusion), calls=%async_computation.2 | async-start | bytes 4194304 | tf_op jit(solution)/shard_map/all_to_all | solution.py:303
  302.0 2.1 collective-permute-start.8
  304.1 1.5 collective-permute-start.9
  305.7 5.2 %fusion = f32[512,64]{0,1:T(8,128)S(1)} fusion(bf16[16,2048,64]{1,2,0:T(8,128)(2,1)} %all-to-all-done.1, bf16[512,2048]{1,0:T(8,128)(2,1)} %param.11, pred[512,16]{0,1:T(8,128)(4,1)S(1)} %iota_compare_fusion.2), kind=kOutput, calls=%fused_computation.4 | convolution fusion | flops 2148499456 | bytes 6430720 | tf_op jit(solution)/shard_map/tn,snk->tsk/dot_general | solution.py:314
  310.9 12.4 %all-reduce.1 = bf16[512,64]{0,1:T(8,128)(2,1)S(1)} all-reduce(f32[512,64]{0,1:T(8,128)S(1)} %fusion), channel_id=1, replica_groups=mesh['dp'=8,'tensor'=4] {'tensor'}, use_global_device_ids=true, to_apply=%region_15.16 | all-reduce | flops 32768 | bytes 196608 | tf_op jit(solution)/shard_map/psum | solution.py:316
  323.3 1.0 broadcast_select_fusion
  324.3 2.3 copy.37.spread_hbm
  326.6 8.3 %collective-permute-done.8.refs_9_ = bf16[16,64,256]{2,1,0:T(8,128)(2,1)} collective-permute-done((bf16[16,64,256]{2,1,0:T(8,128)(2,1)}, bf16[16,64,256]{2,1,0:T(8,128)(2,1)}, u32[]{:S(2)}, u32[]{:S(2)}) %collective-permute-start.8) | collective-permute-done | bytes 524320 | tf_op jit(solution)/shard_map/ppermute | solution.py:252
  334.9 13.7 %collective-permute-done.9.refs_10_ = bf16[16,64,256]{2,1,0:T(8,128)(2,1)} collective-permute-done((bf16[16,64,256]{2,1,0:T(8,128)(2,1)}, bf16[16,64,256]{2,1,0:T(8,128)(2,1)}, u32[]{:S(2)}, u32[]{:S(2)}) %collective-permute-start.9) | collective-permute-done | bytes 524320 | tf_op jit(solution)/shard_map/ppermute | solution.py:252
  348.6 9.7 %collective-permute-done.10.refs_11_ = bf16[16,64,256]{2,1,0:T(8,128)(2,1)} collective-permute-done((bf16[16,64,256]{2,1,0:T(8,128)(2,1)}, bf16[16,64,256]{2,1,0:T(8,128)(2,1)}, u32[]{:S(2)}, u32[]{:S(2)}) %collective-permute-start.10) | collective-permute-done | bytes 524320 | tf_op jit(solution)/shard_map/ppermute | solution.py:252
  358.3 1.4 copy-done.4
  359.7 1.0 copy-done.9
  360.7 4.1 %assemble.1.pages_hbm = bf16[64,64,512]{2,1,0:T(8,128)(2,1)S(1)} custom-call(s32[64]{0:T(128)S(1)} %get-tuple-element.69.source_ref, s32[64]{0:T(128)S(1)} %get-tuple-element.68.place_ref, bf16[48,64,512]{2,1,0:T(8,128)(2,1)S(1)} %copy-done, bf16[16,64,512]{2,1,0:T(8,128)(2,1)} %collective-permute-done.5.refs_1_, ...), custom_call_target="tpu_custom_call" | custom-call | bytes 8388608 | tf_op jit(solution)/shard_map/assemble/pallas_call | solution.py:218
  364.8 1.9 copy-done.1
  366.7 1.2 copy-done.5
  368.0 1.6 copy-done.6
  369.6 1.0 copy-done.7
  370.6 13.6 %attend.1 = bf16[512,1024]{1,0:T(8,128)(2,1)} custom-call(s32[4,32]{1,0:T(4,128)S(1)} %pad_add_fusion.steps_ref, bf16[512,1024]{1,0:T(8,128)(2,1)S(1)} %copy-done.5, bf16[1024,1024]{1,0:T(8,128)(2,1)} %bitcast.16.up_hbm, f32[512,1024]{1,0:T(8,128)S(1)} %copy-done.6, bf16[512,512]{1,0:T(8,128)(2,1)S(1)} %copy-done.7, bf16[64,64,512]{2,1,0:T(8,128)(2,1)} %copy-done.1), custom_call_target="tpu_custom_call" | custom-call | flops 2818572288 | bytes 11010048 | tf_op jit(solution)/shard_map/attend/pallas_call | solution.py:140
  (79 shorter events, 3.9 us)
Async XLA Ops:
  7.2 257.1 %all-gather.2.cloned.1.call-start = ((), (), s32[]{:S(2)}) async-start(), calls=%async_computation.3 | async-start | bytes 10485760 | tf_op jit(solution)/shard_map/all_gather | solution.py:285
  9.3 13.8 %all-to-all-start = ((s32[8,1,160]{2,1,0:T(1,128)}), s32[8,1,160]{2,1,0:T(1,128)S(1)}, u32[]{:S(2)}, u32[]{:S(2)}) async-start(s32[8,1,160]{2,1,0:T(1,128)} %broadcast_in_dim.172), calls=%async_computation | async-start | bytes 16384 | tf_op jit(solution)/shard_map/all_to_all | solution.py:257
  23.1 69.3 %collective-permute-start = (bf16[48,64,256]{2,1,0:T(8,128)(2,1)S(1)}, bf16[48,64,256]{2,1,0:T(8,128)(2,1)S(1)}, u32[]{:S(2)}, u32[]{:S(2)}) collective-permute-start(bf16[48,64,256]{2,1,0:T(8,128)(2,1)S(1)} %get-tuple-element.33), channel_id=1, source_target_pairs={{0,16},{4,20},{8,24},{12,28},{16,0},{20,4},{24,8},{28,12},{1,17},{... | collective-permute-start | bytes 4718600 | tf_op jit(solution)/shard_map/ppermute | solution.py:252
  92.3 1.2 copy-start.2
  93.5 201.5 %all-to-all-start.1 = ((bf16[16,2048,64]{1,2,0:T(8,128)(2,1)}), bf16[16,2048,64]{1,2,0:T(8,128)(2,1)}, u32[]{:S(2)}, u32[]{:S(2)}) async-start(bf16[16,2048,64]{1,2,0:T(8,128)(2,1)} %gather_fusion.1), calls=%async_computation.1 | async-start | bytes 8388608 | tf_op jit(solution)/shard_map/all_to_all | solution.py:298
  98.1 8.4 %copy-start = (bf16[48,64,512]{2,1,0:T(8,128)(2,1)S(1)}, bf16[48,64,512]{2,1,0:T(8,128)(2,1)}, u32[]{:S(2)}) copy-start(bf16[48,64,512]{2,1,0:T(8,128)(2,1)} %refs_0_) | copy-start | bytes 9437188
  98.1 161.0 %collective-permute-start.4 = (bf16[48,64,256]{2,1,0:T(8,128)(2,1)}, bf16[48,64,256]{2,1,0:T(8,128)(2,1)}, u32[]{:S(2)}, u32[]{:S(2)}) collective-permute-start(bf16[48,64,256]{2,1,0:T(8,128)(2,1)} %get-tuple-element.41), channel_id=1, source_target_pairs={{0,16},{4,20},{8,24},{12,28},{16,0},{20,4},{24,8},{28,12},{1,17},{... | collective-permute-start | bytes 4718600 | tf_op jit(solution)/shard_map/ppermute | solution.py:252
  106.5 10.0 %copy-start.3 = (bf16[48,64,256]{2,1,0:T(8,128)(2,1)S(1)}, bf16[48,64,256]{2,1,0:T(8,128)(2,1)}, u32[]{:S(2)}) copy-start(bf16[48,64,256]{2,1,0:T(8,128)(2,1)} %copy-done.2) | copy-start | bytes 4718596
  112.9 167.3 %collective-permute-start.5 = (bf16[16,64,512]{2,1,0:T(8,128)(2,1)}, bf16[16,64,512]{2,1,0:T(8,128)(2,1)}, u32[]{:S(2)}, u32[]{:S(2)}) collective-permute-start(bf16[16,64,512]{2,1,0:T(8,128)(2,1)} %get-tuple-element.46), channel_id=1, source_target_pairs={{0,4},{4,0},{8,12},{12,8},{16,20},{20,16},{24,28},{28,24},{1,5},{5... | collective-permute-start | bytes 3145736 | tf_op jit(solution)/shard_map/ppermute | solution.py:252
  114.5 176.3 %collective-permute-start.6 = (bf16[16,64,512]{2,1,0:T(8,128)(2,1)}, bf16[16,64,512]{2,1,0:T(8,128)(2,1)}, u32[]{:S(2)}, u32[]{:S(2)}) collective-permute-start(bf16[16,64,512]{2,1,0:T(8,128)(2,1)} %get-tuple-element.47), channel_id=1, source_target_pairs={{0,8},{4,12},{8,0},{12,4},{16,24},{20,28},{24,16},{28,20},{1,9},{5... | collective-permute-start | bytes 3145736 | tf_op jit(solution)/shard_map/ppermute | solution.py:252
  115.9 174.9 %collective-permute-start.7 = (bf16[16,64,512]{2,1,0:T(8,128)(2,1)}, bf16[16,64,512]{2,1,0:T(8,128)(2,1)}, u32[]{:S(2)}, u32[]{:S(2)}) collective-permute-start(bf16[16,64,512]{2,1,0:T(8,128)(2,1)} %get-tuple-element.48), channel_id=1, source_target_pairs={{0,12},{4,8},{8,4},{12,0},{16,28},{20,24},{24,20},{28,16},{1,13},{... | collective-permute-start | bytes 3145736 | tf_op jit(solution)/shard_map/ppermute | solution.py:252
  120.3 0.8 copy-start.13
  121.1 169.8 %collective-permute-start.1 = (bf16[16,64,256]{2,1,0:T(8,128)(2,1)}, bf16[16,64,256]{2,1,0:T(8,128)(2,1)}, u32[]{:S(2)}, u32[]{:S(2)}) collective-permute-start(bf16[16,64,256]{2,1,0:T(8,128)(2,1)} %get-tuple-element.38), channel_id=1, source_target_pairs={{0,4},{4,0},{8,12},{12,8},{16,20},{20,16},{24,28},{28,24},{1,5},{5... | collective-permute-start | bytes 1572872 | tf_op jit(solution)/shard_map/ppermute | solution.py:252
  259.2 31.7 %collective-permute-start.2 = (bf16[16,64,256]{2,1,0:T(8,128)(2,1)}, bf16[16,64,256]{2,1,0:T(8,128)(2,1)}, u32[]{:S(2)}, u32[]{:S(2)}) collective-permute-start(bf16[16,64,256]{2,1,0:T(8,128)(2,1)} %get-tuple-element.39), channel_id=1, source_target_pairs={{0,8},{4,12},{8,0},{12,4},{16,24},{20,28},{24,16},{28,20},{1,9},{5... | collective-permute-start | bytes 1572872 | tf_op jit(solution)/shard_map/ppermute | solution.py:252
  261.8 0.8 copy-start.10
  262.6 0.8 copy-start.11
  263.4 0.8 copy-start.12
  264.2 15.9 %copy-start.14 = (bf16[16,64,256]{2,1,0:T(8,128)(2,1)S(1)}, bf16[16,64,256]{2,1,0:T(8,128)(2,1)}, u32[]{:S(2)}) copy-start(bf16[16,64,256]{2,1,0:T(8,128)(2,1)} %copy-done.13) | copy-start | bytes 1572868
  264.2 18.8 %copy-start.19 = (bf16[512,8192]{1,0:T(8,128)(2,1)S(1)}, bf16[512,8192]{1,0:T(8,128)(2,1)}, u32[]{:S(2)}) copy-start(bf16[512,8192]{1,0:T(8,128)(2,1)} %all-gather.2.cloned.1.call-done) | copy-start | bytes 25165828
  280.2 14.0 %collective-permute-start.3 = (bf16[16,64,256]{2,1,0:T(8,128)(2,1)S(1)}, bf16[16,64,256]{2,1,0:T(8,128)(2,1)S(1)}, u32[]{:S(2)}, u32[]{:S(2)}) collective-permute-start(bf16[16,64,256]{2,1,0:T(8,128)(2,1)S(1)} %copy-done.14), channel_id=1, source_target_pairs={{0,12},{4,8},{8,4},{12,0},{16,28},{20,24},{24,20},{28,16},{1,13},{... | collective-permute-start | bytes 1572872 | tf_op jit(solution)/shard_map/ppermute | solution.py:252
  290.8 8.9 %copy-start.15 = (s32[1,16]{1,0:T(1,128)S(1)}, s32[1,16]{1,0:T(1,128)}, u32[]{:S(2)}) copy-start(s32[1,16]{1,0:T(1,128)} %param.17) | copy-start | bytes 196
  290.8 10.7 %copy-start.18 = (s32[16,1]{0,1:T(1,128)S(1)}, s32[16,1]{0,1:T(1,128)}, u32[]{:S(2)}) copy-start(s32[16,1]{0,1:T(1,128)} %param.18) | copy-start | bytes 196
  290.8 10.9 %copy-start.17 = (s32[64,1]{0,1:T(1,128)S(1)}, s32[64,1]{0,1:T(1,128)}, u32[]{:S(2)}) copy-start(s32[64,1]{0,1:T(1,128)} %param.20) | copy-start | bytes 772
  290.8 11.2 %copy-start.16 = (s32[64]{0:T(128)S(1)}, s32[64]{0:T(128)}, u32[]{:S(2)}) copy-start(s32[64]{0:T(128)} %param.21) | copy-start | bytes 772
  294.2 0.8 copy-start.8
  295.0 71.7 %all-to-all-start.2 = ((bf16[16,64,1024]{2,1,0:T(8,128)(2,1)}), bf16[16,64,1024]{2,1,0:T(8,128)(2,1)}, u32[]{:S(2)}, u32[]{:S(2)}) async-start(bf16[16,64,1024]{2,1,0:T(8,128)(2,1)} %gather_fusion), calls=%async_computation.2 | async-start | bytes 4194304 | tf_op jit(solution)/shard_map/all_to_all | solution.py:303
  302.0 32.9 %collective-permute-start.8 = (bf16[16,64,256]{2,1,0:T(8,128)(2,1)}, bf16[16,64,256]{2,1,0:T(8,128)(2,1)}, u32[]{:S(2)}, u32[]{:S(2)}) collective-permute-start(bf16[16,64,256]{2,1,0:T(8,128)(2,1)} %copy-done.12), channel_id=1, source_target_pairs={{0,4},{4,0},{8,12},{12,8},{16,20},{20,16},{24,28},{28,24},{1,5},{5... | collective-permute-start | bytes 1572872 | tf_op jit(solution)/shard_map/ppermute | solution.py:252
  304.1 44.5 %collective-permute-start.9 = (bf16[16,64,256]{2,1,0:T(8,128)(2,1)}, bf16[16,64,256]{2,1,0:T(8,128)(2,1)}, u32[]{:S(2)}, u32[]{:S(2)}) collective-permute-start(bf16[16,64,256]{2,1,0:T(8,128)(2,1)} %copy-done.11), channel_id=1, source_target_pairs={{0,8},{4,12},{8,0},{12,4},{16,24},{20,28},{24,16},{28,20},{1,9},{5... | collective-permute-start | bytes 1572872 | tf_op jit(solution)/shard_map/ppermute | solution.py:252
  305.6 52.7 %collective-permute-start.10 = (bf16[16,64,256]{2,1,0:T(8,128)(2,1)}, bf16[16,64,256]{2,1,0:T(8,128)(2,1)}, u32[]{:S(2)}, u32[]{:S(2)}) collective-permute-start(bf16[16,64,256]{2,1,0:T(8,128)(2,1)} %copy-done.10), channel_id=1, source_target_pairs={{0,12},{4,8},{8,4},{12,0},{16,28},{20,24},{24,20},{28,16},{1,13},{... | collective-permute-start | bytes 1572872 | tf_op jit(solution)/shard_map/ppermute | solution.py:252
  358.3 1.4 copy-start.4
  359.7 1.0 copy-start.9
  364.8 1.9 copy-start.1
  366.7 1.2 copy-start.5
  368.0 1.6 copy-start.6
  369.6 1.0 copy-start.7
Sparse Core Ops, SparseCore 0:
  9.6 60.9 all-gather.1

commit v7 on v6

--- a/solution.py
+++ b/solution.py
@@ -14,7 +14,9 @@
 MOST = 128
 BLOCK = 32
 TOGETHER = 4
-HALVES = 2
+TILE = 256
+PARTS = ((0, 48), (48, 64))
+VMEM_GRANT = 60 * 1024 * 1024
 
 ADAPTER_SCALE = 0.5
 NEGATIVE = -1e30
@@ -49,28 +51,40 @@
 
 
 def attention_kernel(steps_ref, spread_hbm, up_hbm, base_hbm, cache_hbm, pages_hbm, out_ref, query_ref, *rest):
-    spread_ref, up_ref, base_ref, cache_ref, pages_ref, sems = rest
-    pairs = [(spread_hbm, spread_ref), (up_hbm, up_ref), (base_hbm, base_ref), (cache_hbm, cache_ref), (pages_hbm, pages_ref)]
+    spread_ref, up_ref, base_ref, cache_ref, pages_ref, sems, tile_sems = rest
+
+    def tile_copies(index):
+        cols = pl.ds(pl.multiple_of(index * TILE, TILE), TILE)
+        return (
+            pltpu.make_async_copy(up_hbm.at[:, cols], up_ref.at[:, cols], tile_sems.at[0, index]),
+            pltpu.make_async_copy(base_hbm.at[:, cols], base_ref.at[:, cols], tile_sems.at[1, index]),
+        )
+
+    pairs = [(spread_hbm, spread_ref), (cache_hbm, cache_ref), (pages_hbm, pages_ref)]
     copies = [pltpu.make_async_copy(*pair, sems.at[index]) for index, pair in enumerate(pairs)]
-    for copy in copies:
+    copies[0].start()
+    for index in range(base_ref.shape[1] // TILE):
+        for copy in tile_copies(index):
+            copy.start()
+    for copy in copies[1:]:
         copy.start()
     rows_total, q_cols = base_ref.shape
     kv_heads = cache_ref.shape[1] // (2 * HEAD_WIDTH)
     group = q_cols // HEAD_WIDTH // kv_heads
     window = min(rows_total, MOST + BLOCK)
     sharp = HEAD_WIDTH ** -0.5 * math.log2(math.e)
-    for copy in copies[:3]:
-        copy.wait()
+    copies[0].wait()
 
     def project(index, carry):
-        cols = pl.ds(pl.multiple_of(index * 256, 256), 256)
+        for copy in tile_copies(index):
+            copy.wait()
+        cols = pl.ds(pl.multiple_of(index * TILE, TILE), TILE)
         correction = jnp.dot(spread_ref[...], up_ref[:, cols], preferred_element_type=jnp.float32)
         query_ref[:, cols] = (base_ref[:, cols] + ADAPTER_SCALE * correction).astype(jnp.bfloat16)
         return carry
 
-    lax.fori_loop(0, q_cols // 256, project, 0)
-
-    for copy in copies[3:]:
+    lax.fori_loop(0, q_cols // TILE, project, 0)
+    for copy in copies[1:]:
         copy.wait()
     dims = (((1,), (1,)), ((), ()))
 
@@ -145,9 +159,10 @@
         scratch_shapes=[
             pltpu.VMEM((rows, q_cols), jnp.bfloat16),
             *[pltpu.VMEM(each.shape, each.dtype) for each in (spread, up, query_base, cache, pages)],
-            pltpu.SemaphoreType.DMA((5,)),
+            pltpu.SemaphoreType.DMA((3,)),
+            pltpu.SemaphoreType.DMA((2, q_cols // TILE)),
         ],
-        compiler_params=pltpu.CompilerParams(vmem_limit_bytes=48 * 1024 * 1024),
+        compiler_params=pltpu.CompilerParams(vmem_limit_bytes=VMEM_GRANT),
         cost_estimate=pl.CostEstimate(
             flops=4 * steps_total * BLOCK * q_cols * (HITS * PAGE + MOST + BLOCK) + 2 * spread.size * q_cols,
             bytes_accessed=4 * query_base.size + 2 * (2 * spread.size + up.size + cache.size + pages.size),
@@ -176,7 +191,7 @@
         in_specs=[pl.BlockSpec(memory_space=pltpu.SMEM), pl.BlockSpec(memory_space=pltpu.HBM)],
         out_specs=[pl.BlockSpec(memory_space=pltpu.VMEM)] * blocks,
         scratch_shapes=[pltpu.SemaphoreType.DMA((blocks,))],
-        compiler_params=pltpu.CompilerParams(vmem_limit_bytes=16 * 1024 * 1024),
+        compiler_params=pltpu.CompilerParams(vmem_limit_bytes=VMEM_GRANT),
         cost_estimate=pl.CostEstimate(
             flops=0, bytes_accessed=4 * blocks * math.prod(shape), transcendentals=0
         ),
@@ -186,9 +201,8 @@
 
 def assemble_kernel(source_ref, place_ref, *refs):
     out, sem = refs[-2:]
-    half = (len(refs) - 2) // (1 + HALVES)
+    half = (len(refs) - 2) // (1 + len(PARTS))
     near, far = refs[:half], refs[half:-2]
-    width = far[0].shape[2]
 
     def one(index, carry):
         source = source_ref[index]
@@ -201,9 +215,9 @@
 
             @pl.when(source == half + number)
             def _():
-                for part in range(HALVES):
-                    columns = out.at[index, :, part * width : (part + 1) * width]
-                    pltpu.make_async_copy(far[part * half + number].at[place], columns, sem).start()
+                for part, (first, end) in enumerate(PARTS):
+                    rows = out.at[index, first:end]
+                    pltpu.make_async_copy(far[part * half + number].at[place], rows, sem).start()
 
         return carry
 
@@ -221,7 +235,7 @@
         in_specs=[scalars, scalars] + [pl.BlockSpec(memory_space=pltpu.HBM)] * len(sources),
         out_specs=pl.BlockSpec(memory_space=pltpu.VMEM),
         scratch_shapes=[pltpu.SemaphoreType.DMA],
-        compiler_params=pltpu.CompilerParams(vmem_limit_bytes=16 * 1024 * 1024),
+        compiler_params=pltpu.CompilerParams(vmem_limit_bytes=VMEM_GRANT),
         cost_estimate=pl.CostEstimate(flops=0, bytes_accessed=4 * math.prod(shape), transcendentals=0),
         name="assemble",
     )(source, place, *sources)
@@ -257,8 +271,7 @@
     everyone = lax.all_to_all(
         jnp.broadcast_to(raw[None], (peers, raw.shape[0])), "dp", split_axis=0, concat_axis=0, tiled=True
     )
-    width = keyvalue_page_store.shape[2] // HALVES
-    parts = [keyvalue_page_store[:, :, part * width : (part + 1) * width] for part in range(HALVES)]
+    parts = [keyvalue_page_store[:, first:end] for first, end in PARTS]
     store, down_store, everyone, *parts = lax.optimization_barrier(
         (keyvalue_page_store, adapter_down_weight, everyone, *parts)
     )
@@ -286,22 +299,17 @@
     query_base = jnp.dot(piece, query_weight, preferred_element_type=jnp.float32)
     new_cache = jnp.dot(piece, keyvalue_weight, preferred_element_type=jnp.float32).astype(jnp.bfloat16)
 
-    mirrored = []
-    far = []
-    for part in range(HALVES):
-        mirrored.append(swap(parts[part], half))
-        if part + 1 < HALVES:
-            mirrored[part], parts[part + 1], down_rows = lax.optimization_barrier(
-                (mirrored[part], parts[part + 1], down_rows)
-            )
-        far.append(serve(far_asked[1:], mirrored[part]))
+    mirrored = [swap(parts[0], half)]
+    mirrored[0], parts[1], down_rows, near[:2], query_base, new_cache = lax.optimization_barrier(
+        (mirrored[0], parts[1], down_rows, near[:2], query_base, new_cache)
+    )
+    mirrored.append(swap(parts[1], half))
     down_sent = lax.all_to_all(down_rows, "dp", split_axis=0, concat_axis=0, tiled=True)
-    far = [[swap(pages, i + 1) for i, pages in enumerate(block)] for block in far[:-1]] + far[-1:]
-    up_rows, down_sent, query_base, new_cache, far, near = lax.optimization_barrier(
-        (up_rows, down_sent, query_base, new_cache, far, near)
-    )
+    far = [serve(far_asked[1:], pool) for pool in mirrored]
+    far[0] = [swap(pages, i + 1) for i, pages in enumerate(far[0])]
+    up_rows, down_sent, far, near = lax.optimization_barrier((up_rows, down_sent, far, near))
     up_sent = lax.all_to_all(up_rows, "dp", split_axis=0, concat_axis=0, tiled=True)
-    far[-1] = [swap(pages, i + 1) for i, pages in enumerate(far[-1])]
+    far[1] = [swap(pages, i + 1) for i, pages in enumerate(far[1])]
 
     lengths = span_token_length[0]
     ends = jnp.cumsum(lengths)
@@ -315,7 +323,7 @@
     shrink_part = jnp.sum(jnp.where(in_slot[:, :, None], down_part, 0.0), axis=1)
     shrink = lax.psum(shrink_part, "tensor").astype(jnp.bfloat16)
     spread = jnp.where(in_slot[:, :, None], shrink[:, None, :], 0).reshape(tok_rows, adapter_slots * rank)
-    far = [page for part in range(HALVES) for page in (mirrored[part], *far[part])]
+    far = [page for part in range(len(PARTS)) for page in (mirrored[part], *far[part])]
     prefix_pages = assemble(page_source, page_place, [store, *near], far)
     up = up_sent.reshape(adapter_slots * rank, q_cols)
     out = attend(query_base, spread, up, new_cache, prefix_pages, starts, ends)

time: 392 us -> 367 us (0.936)
  waiting for transfers between devices: 237 us -> 205 us
  local copies, waits for them, and re-layouts: 32 us -> 22.6 us
  starting transfers between devices: 31.5 us -> 40.8 us
    ppermute x11, waiting for transfers between devices: 233 us -> 172 us  [swap(): lax.ppermute(array, 'dp', [(peer, peer ^ distance) for peer in range(peer...]
    all_gather x1, waiting for transfers between devices: 0.01 us -> 29.6 us  [on_device(): piece = lax.all_gather(tokens, 'tensor', axis=1, tiled=True)]
    unnamed x41 -> x29, local copies, waits for them, and re-layouts: 13.4 us -> 3.67 us
    all_to_all x1, starting transfers between devices: 4.71 us -> 13.3 us  [on_device(): lax.all_to_all(up_rows, 'dp', split_axis=0, concat_axis=0, tiled=True)]
  transfers between devices with their start and end apart: 15 -> 15, of which waited for: 7 -> 8; matrix products, arithmetic and copies ran while one was open for 13% -> 15% of each run, Pallas kernels for 4% -> 5%
where the time goes in v7:
time: 367 us; the launch traced here: 365 us
  waiting for transfers between devices  205 us (56%)
  starting transfers between devices  40.8 us (11%)
  Pallas kernels  33.7 us (9%)
  matrix products  31.2 us (9%)
  local copies, waits for them, and re-layouts  22.6 us (6%)
  between operations  14.9 us (4%)
  blocking collectives  12.4 us (3%)
  other arithmetic  4.19 us (1%)
    ppermute x11, waiting for transfers between devices, swap(): lax.ppermute(array, 'dp', [(peer, peer ^ distance) for peer in range(peer...  172 us
    all_gather x1, waiting for transfers between devices, on_device(): piece = lax.all_gather(tokens, 'tensor', axis=1, tiled=True)  29.6 us
    dot_general x1, matrix products, on_device(): jnp.dot(piece, query_weight, preferred_element_type=jnp.float32)  18.2 us
    ppermute x11, starting transfers between devices, swap(): lax.ppermute(array, 'dp', [(peer, peer ^ distance) for peer in range(peer...  15.7 us
    pallas_call x3, Pallas kernels, serve(): pl.pallas_call(serve_kernel, out_shape=[jax.ShapeDtypeStruct(shape, store...  14.5 us
    pallas_call x1, Pallas kernels, attend(): pl.pallas_call(attention_kernel, out_shape=jax.ShapeDtypeStruct((rows, q_...  14.3 us
    all_to_all x1, starting transfers between devices, on_device(): lax.all_to_all(up_rows, 'dp', split_axis=0, concat_axis=0, tiled=True)  13.3 us
    psum x1, blocking collectives, on_device(): shrink = lax.psum(shrink_part, 'tensor').astype(jnp.bfloat16)  12.4 us
  transfers between devices with their start and end apart: 15, of which 8 were waited for; matrix products, arithmetic and copies ran while one was open for 15% of the time, Pallas kernels for 5%

profile of v7, /device:TPU:0, one launch (start us, length us, event | category | flops | bytes accessed | tf_op | source)
XLA Modules:
  0.0 364.7 jit_solution(16581573567748537624)
XLA Ops:
  7.2 0.7 all-gather.2.cloned.1.call-update
  7.9 1.0 pad_add_fusion.1
  8.9 0.6 broadcast_in_dim.172
  9.5 7.3 %all-to-all-start = ((s32[8,1,160]{2,1,0:T(1,128)}), s32[8,1,160]{2,1,0:T(1,128)S(1)}, u32[]{:S(2)}, u32[]{:S(2)}) async-start(s32[8,1,160]{2,1,0:T(1,128)} %broadcast_in_dim.172), calls=%async_computation | async-start | bytes 16384 | tf_op jit(solution)/shard_map/all_to_all | solution.py:271
  16.8 2.1 slice.31
  18.9 1.7 slice.30
  20.6 2.7 all-to-all-done
  23.3 0.6 gather_fusion.2
  23.9 0.2 convert_reduce_fusion
  24.4 0.6 reshape.364.asked_ref
  25.1 0.3 convert_reduce_fusion.1
  25.7 0.6 collective-permute-start
  26.2 5.7 %serve.3 = (bf16[16,64,512]{2,1,0:T(8,128)(2,1)}, bf16[16,64,512]{2,1,0:T(8,128)(2,1)}, bf16[16,64,512]{2,1,0:T(8,128)(2,1)}) custom-call(s32[48]{0:T(128)} %reshape.364.asked_ref, bf16[48,64,512]{2,1,0:T(8,128)(2,1)} %refs_0_), custom_call_target="tpu_custom_call" | custom-call | bytes 6291456 | tf_op jit(solution)/shard_map/serve/pallas_call | solution.py:188
  32.0 2.6 collective-permute-start.2
  34.7 6.3 %gather_fusion.1 = bf16[16,2048,64]{1,2,0:T(8,128)(2,1)} fusion(bf16[32,2048,64]{1,2,0:T(8,128)(2,1)} %param.14, s32[1024]{0:T(1024)S(1)} %pad_clamp_fusion.1), kind=kCustom, calls=%fused_computation.1 | custom fusion | bytes 8388672 | tf_op jit(solution)/shard_map/gather | solution.py:295
  41.0 29.6 %all-gather.2.cloned.1.call-done = bf16[512,8192]{1,0:T(8,128)(2,1)} async-done(((bf16[512,2048]{1,0:T(8,128)(2,1)}), bf16[512,8192]{1,0:T(8,128)(2,1)}) %all-gather.2.cloned.1.call-update) | async-done | bytes 8388624 | tf_op jit(solution)/shard_map/all_gather | solution.py:298
  70.6 18.2 %fusion.23.base_hbm = f32[512,1024]{1,0:T(8,128)} fusion(bf16[512,8192]{1,0:T(8,128)(2,1)} %all-gather.2.cloned.1.call-done, bf16[8192,1024]{1,0:T(8,128)(2,1)} %param.12), kind=kOutput, calls=%fused_computation.88 | convolution fusion | flops 8589934592 | bytes 27262976 | tf_op jit(solution)/shard_map/dot_general | solution.py:299
  88.8 7.7 %convolution_convert_fusion.cache_hbm = bf16[512,512]{1,0:T(8,128)(2,1)} fusion(bf16[512,8192]{1,0:T(8,128)(2,1)S(1)} %copy-done.13, bf16[8192,512]{1,0:T(8,128)(2,1)} %param.13), kind=kOutput, calls=%fused_computation.7 | convolution fusion | flops 4295229440 | bytes 17301504 | tf_op jit(solution)/shard_map/dot_general | solution.py:300
  96.5 2.1 collective-permute-done.2.refs_2_
  98.6 30.2 %collective-permute-done.store_ref.refs_4_ = bf16[48,48,512]{2,1,0:T(8,128)(2,1)S(1)} collective-permute-done((bf16[48,48,512]{2,1,0:T(8,128)(2,1)}, bf16[48,48,512]{2,1,0:T(8,128)(2,1)S(1)}, u32[]{:S(2)}, u32[]{:S(2)}) %collective-permute-start) | collective-permute-done | bytes 2359328 | tf_op jit(solution)/shard_map/ppermute | solution.py:266
  128.8 1.4 copy-done.1
  130.3 4.5 %all-to-all-start.1 = ((bf16[16,2048,64]{1,2,0:T(8,128)(2,1)}), bf16[16,2048,64]{1,2,0:T(8,128)(2,1)}, u32[]{:S(2)}, u32[]{:S(2)}) async-start(bf16[16,2048,64]{1,2,0:T(8,128)(2,1)} %gather_fusion.1), calls=%async_computation.1 | async-start | bytes 8388608 | tf_op jit(solution)/shard_map/all_to_all | solution.py:307
  134.8 2.8 collective-permute-start.7
  137.6 0.6 reshape.365.asked_ref
  138.2 2.4 collective-permute-start.6
  140.6 5.5 %serve.4 = (bf16[16,48,512]{2,1,0:T(8,128)(2,1)}, bf16[16,48,512]{2,1,0:T(8,128)(2,1)}, bf16[16,48,512]{2,1,0:T(8,128)(2,1)}) custom-call(s32[48]{0:T(128)} %reshape.365.asked_ref, bf16[48,48,512]{2,1,0:T(8,128)(2,1)} %copy-done.1), custom_call_target="tpu_custom_call" | custom-call | bytes 4718592 | tf_op jit(solution)/shard_map/serve/pallas_call | solution.py:188
  146.1 1.4 collective-permute-start.3
  147.4 0.3 collective-permute-start.4
  147.8 1.9 collective-permute-start.5
  149.7 4.2 %gather_fusion = bf16[16,64,1024]{2,1,0:T(8,128)(2,1)} fusion(bf16[32,64,1024]{2,1,0:T(8,128)(2,1)} %param.15, s32[1024]{0:T(1024)S(1)} %pad_clamp_fusion.1), kind=kCustom, calls=%fused_computation | custom fusion | bytes 4194368 | tf_op jit(solution)/shard_map/gather | solution.py:296
  153.9 108.2 %collective-permute-done.6.store_ref.refs_8_ = bf16[48,16,512]{2,1,0:T(8,128)(2,1)S(1)} collective-permute-done((bf16[48,16,512]{2,1,0:T(8,128)(2,1)}, bf16[48,16,512]{2,1,0:T(8,128)(2,1)S(1)}, u32[]{:S(2)}, u32[]{:S(2)}) %collective-permute-start.6) | collective-permute-done | bytes 786464 | tf_op jit(solution)/shard_map/ppermute | solution.py:266
  262.2 0.9 copy-done.3
  263.1 3.3 serve.5
  266.5 12.5 %collective-permute-done.5.refs_7_ = bf16[16,48,512]{2,1,0:T(8,128)(2,1)} collective-permute-done((bf16[16,48,512]{2,1,0:T(8,128)(2,1)}, bf16[16,48,512]{2,1,0:T(8,128)(2,1)}, u32[]{:S(2)}, u32[]{:S(2)}) %collective-permute-start.5) | collective-permute-done | bytes 786464 | tf_op jit(solution)/shard_map/ppermute | solution.py:266
  279.0 13.3 %all-to-all-start.2 = ((bf16[16,64,1024]{2,1,0:T(8,128)(2,1)}), bf16[16,64,1024]{2,1,0:T(8,128)(2,1)S(1)}, u32[]{:S(2)}, u32[]{:S(2)}) async-start(bf16[16,64,1024]{2,1,0:T(8,128)(2,1)} %gather_fusion), calls=%async_computation.2 | async-start | bytes 4194304 | tf_op jit(solution)/shard_map/all_to_all | solution.py:311
  292.6 0.6 slice.44
  294.1 0.6 pad_add_fusion.steps_ref
  295.1 0.5 compare_select_fusion.4
  295.7 5.2 %fusion = f32[512,64]{0,1:T(8,128)S(1)} fusion(bf16[16,2048,64]{1,2,0:T(8,128)(2,1)} %all-to-all-done.1, bf16[512,2048]{1,0:T(8,128)(2,1)} %param.11, pred[512,16]{0,1:T(8,128)(4,1)S(1)} %iota_compare_fusion.2), kind=kOutput, calls=%fused_computation.4 | convolution fusion | flops 2148499456 | bytes 6430720 | tf_op jit(solution)/shard_map/tn,snk->tsk/dot_general | solution.py:322
  300.9 2.1 collective-permute-start.8
  303.0 1.5 collective-permute-start.9
  304.6 12.4 %all-reduce.1 = bf16[512,64]{0,1:T(8,128)(2,1)S(1)} all-reduce(f32[512,64]{0,1:T(8,128)S(1)} %fusion), channel_id=1, replica_groups=mesh['dp'=8,'tensor'=4] {'tensor'}, use_global_device_ids=true, to_apply=%region_15.16 | all-reduce | flops 32768 | bytes 196608 | tf_op jit(solution)/shard_map/psum | solution.py:324
  317.0 1.4 copy.37.spread_hbm
  318.4 15.0 %collective-permute-done.9.refs_10_ = bf16[16,16,512]{2,1,0:T(8,128)(2,1)S(1)} collective-permute-done((bf16[16,16,512]{2,1,0:T(8,128)(2,1)}, bf16[16,16,512]{2,1,0:T(8,128)(2,1)S(1)}, u32[]{:S(2)}, u32[]{:S(2)}) %collective-permute-start.9) | collective-permute-done | bytes 262176 | tf_op jit(solution)/shard_map/ppermute | solution.py:266
  333.4 3.8 %collective-permute-done.10.refs_11_ = bf16[16,16,512]{2,1,0:T(8,128)(2,1)} collective-permute-done((bf16[16,16,512]{2,1,0:T(8,128)(2,1)}, bf16[16,16,512]{2,1,0:T(8,128)(2,1)}, u32[]{:S(2)}, u32[]{:S(2)}) %collective-permute-start.10) | collective-permute-done | bytes 262176 | tf_op jit(solution)/shard_map/ppermute | solution.py:266
  337.2 5.0 %assemble.1.pages_hbm = bf16[64,64,512]{2,1,0:T(8,128)(2,1)} custom-call(s32[64]{0:T(128)} %get-tuple-element.73.source_ref, s32[64]{0:T(128)} %get-tuple-element.72.place_ref, bf16[48,64,512]{2,1,0:T(8,128)(2,1)} %refs_0_, bf16[16,64,512]{2,1,0:T(8,128)(2,1)} %copy-done.4, bf16[16,64,512]{2,1,0:T(8,128)(2,1)} %collective-permute-done.2.refs_2_, ...), custom_call_target="tpu_custom_call" | custom-call | bytes 8388608 | tf_op jit(solution)/shard_map/assemble/pallas_call | solution.py:232
  342.2 1.3 copy-done.2
  343.5 14.3 %attend.1 = bf16[512,1024]{1,0:T(8,128)(2,1)} custom-call(s32[4,32]{1,0:T(4,128)} %pad_add_fusion.steps_ref, bf16[512,1024]{1,0:T(8,128)(2,1)} %copy.37.spread_hbm, bf16[1024,1024]{1,0:T(8,128)(2,1)} %bitcast.56, f32[512,1024]{1,0:T(8,128)} %fusion.23.base_hbm, bf16[512,512]{1,0:T(8,128)(2,1)} %convolution_convert_fusion.cache_hbm, ...), custom_call_target="tpu_custom_call" | custom-call | flops 2818572288 | bytes 11010048 | tf_op jit(solution)/shard_map/attend/pallas_call | solution.py:154
  (68 shorter events, 2.2 us)
Async XLA Ops:
  7.2 11.7 %copy-start = (bf16[48,64,512]{2,1,0:T(8,128)(2,1)S(1)}, bf16[48,64,512]{2,1,0:T(8,128)(2,1)}, u32[]{:S(2)}) copy-start(bf16[48,64,512]{2,1,0:T(8,128)(2,1)} %refs_0_) | copy-start | bytes 9437188
  7.2 63.4 %all-gather.2.cloned.1.call-start = ((), (), s32[]{:S(2)}) async-start(), calls=%async_computation.3 | async-start | bytes 10485760 | tf_op jit(solution)/shard_map/all_gather | solution.py:298
  9.5 13.8 %all-to-all-start = ((s32[8,1,160]{2,1,0:T(1,128)}), s32[8,1,160]{2,1,0:T(1,128)S(1)}, u32[]{:S(2)}, u32[]{:S(2)}) async-start(s32[8,1,160]{2,1,0:T(1,128)} %broadcast_in_dim.172), calls=%async_computation | async-start | bytes 16384 | tf_op jit(solution)/shard_map/all_to_all | solution.py:271
  25.7 103.2 %collective-permute-start = (bf16[48,48,512]{2,1,0:T(8,128)(2,1)}, bf16[48,48,512]{2,1,0:T(8,128)(2,1)S(1)}, u32[]{:S(2)}, u32[]{:S(2)}) collective-permute-start(bf16[48,48,512]{2,1,0:T(8,128)(2,1)} %slice.30), channel_id=1, source_target_pairs={{0,16},{4,20},{8,24},{12,28},{16,0},{20,4},{24,8},{28,12},{1,17},{... | collective-permute-start | bytes 7077896 | tf_op jit(solution)/shard_map/ppermute | solution.py:266
  31.9 64.6 %collective-permute-start.1 = (bf16[16,64,512]{2,1,0:T(8,128)(2,1)}, bf16[16,64,512]{2,1,0:T(8,128)(2,1)S(1)}, u32[]{:S(2)}, u32[]{:S(2)}) collective-permute-start(bf16[16,64,512]{2,1,0:T(8,128)(2,1)} %get-tuple-element.39), channel_id=1, source_target_pairs={{0,4},{4,0},{8,12},{12,8},{16,20},{20,16},{24,28},{28,24},{1,5},{5... | collective-permute-start | bytes 3145736 | tf_op jit(solution)/shard_map/ppermute | solution.py:266
  32.0 66.7 %collective-permute-start.2 = (bf16[16,64,512]{2,1,0:T(8,128)(2,1)}, bf16[16,64,512]{2,1,0:T(8,128)(2,1)}, u32[]{:S(2)}, u32[]{:S(2)}) collective-permute-start(bf16[16,64,512]{2,1,0:T(8,128)(2,1)} %get-tuple-element.40), channel_id=1, source_target_pairs={{0,8},{4,12},{8,0},{12,4},{16,24},{20,28},{24,16},{28,20},{1,9},{5... | collective-permute-start | bytes 3145736 | tf_op jit(solution)/shard_map/ppermute | solution.py:266
  70.6 18.2 %copy-start.13 = (bf16[512,8192]{1,0:T(8,128)(2,1)S(1)}, bf16[512,8192]{1,0:T(8,128)(2,1)}, u32[]{:S(2)}) copy-start(bf16[512,8192]{1,0:T(8,128)(2,1)} %all-gather.2.cloned.1.call-done) | copy-start | bytes 25165828
  96.5 32.3 %copy-start.4 = (bf16[16,64,512]{2,1,0:T(8,128)(2,1)}, bf16[16,64,512]{2,1,0:T(8,128)(2,1)S(1)}, u32[]{:S(2)}) copy-start(bf16[16,64,512]{2,1,0:T(8,128)(2,1)S(1)} %collective-permute-done.1.refs_1_) | copy-start | bytes 3145732
  128.8 1.4 copy-start.1
  130.3 148.7 %all-to-all-start.1 = ((bf16[16,2048,64]{1,2,0:T(8,128)(2,1)}), bf16[16,2048,64]{1,2,0:T(8,128)(2,1)}, u32[]{:S(2)}, u32[]{:S(2)}) async-start(bf16[16,2048,64]{1,2,0:T(8,128)(2,1)} %gather_fusion.1), calls=%async_computation.1 | async-start | bytes 8388608 | tf_op jit(solution)/shard_map/all_to_all | solution.py:307
  134.8 131.6 %collective-permute-start.7 = (bf16[16,64,512]{2,1,0:T(8,128)(2,1)}, bf16[16,64,512]{2,1,0:T(8,128)(2,1)S(1)}, u32[]{:S(2)}, u32[]{:S(2)}) collective-permute-start(bf16[16,64,512]{2,1,0:T(8,128)(2,1)} %get-tuple-element.52), channel_id=1, source_target_pairs={{0,12},{4,8},{8,4},{12,0},{16,28},{20,24},{24,20},{28,16},{1,13},{... | collective-permute-start | bytes 3145736 | tf_op jit(solution)/shard_map/ppermute | solution.py:266
  138.2 124.0 %collective-permute-start.6 = (bf16[48,16,512]{2,1,0:T(8,128)(2,1)}, bf16[48,16,512]{2,1,0:T(8,128)(2,1)S(1)}, u32[]{:S(2)}, u32[]{:S(2)}) collective-permute-start(bf16[48,16,512]{2,1,0:T(8,128)(2,1)} %slice.31), channel_id=1, source_target_pairs={{0,16},{4,20},{8,24},{12,28},{16,0},{20,4},{24,8},{28,12},{1,17},{... | collective-permute-start | bytes 2359304 | tf_op jit(solution)/shard_map/ppermute | solution.py:266
  146.1 120.3 %collective-permute-start.3 = (bf16[16,48,512]{2,1,0:T(8,128)(2,1)}, bf16[16,48,512]{2,1,0:T(8,128)(2,1)S(1)}, u32[]{:S(2)}, u32[]{:S(2)}) collective-permute-start(bf16[16,48,512]{2,1,0:T(8,128)(2,1)} %get-tuple-element.43), channel_id=1, source_target_pairs={{0,4},{4,0},{8,12},{12,8},{16,20},{20,16},{24,28},{28,24},{1,5},{5... | collective-permute-start | bytes 2359304 | tf_op jit(solution)/shard_map/ppermute | solution.py:266
  147.4 119.0 %collective-permute-start.4 = (bf16[16,48,512]{2,1,0:T(8,128)(2,1)}, bf16[16,48,512]{2,1,0:T(8,128)(2,1)S(1)}, u32[]{:S(2)}, u32[]{:S(2)}) collective-permute-start(bf16[16,48,512]{2,1,0:T(8,128)(2,1)} %get-tuple-element.44), channel_id=1, source_target_pairs={{0,8},{4,12},{8,0},{12,4},{16,24},{20,28},{24,16},{28,20},{1,9},{5... | collective-permute-start | bytes 2359304 | tf_op jit(solution)/shard_map/ppermute | solution.py:266
  147.8 144.5 %copy-start.9 = (s32[1,16]{1,0:T(1,128)S(1)}, s32[1,16]{1,0:T(1,128)}, u32[]{:S(2)}) copy-start(s32[1,16]{1,0:T(1,128)} %param.17) | copy-start | bytes 196
  147.8 146.9 %copy-start.12 = (s32[16,1]{0,1:T(1,128)S(1)}, s32[16,1]{0,1:T(1,128)}, u32[]{:S(2)}) copy-start(s32[16,1]{0,1:T(1,128)} %param.18) | copy-start | bytes 196
  147.8 147.1 %copy-start.11 = (s32[64,1]{0,1:T(1,128)S(1)}, s32[64,1]{0,1:T(1,128)}, u32[]{:S(2)}) copy-start(s32[64,1]{0,1:T(1,128)} %param.20) | copy-start | bytes 772
  147.8 147.4 %copy-start.10 = (s32[64]{0:T(128)S(1)}, s32[64]{0:T(128)}, u32[]{:S(2)}) copy-start(s32[64]{0:T(128)} %param.21) | copy-start | bytes 772
  147.8 131.2 %collective-permute-start.5 = (bf16[16,48,512]{2,1,0:T(8,128)(2,1)}, bf16[16,48,512]{2,1,0:T(8,128)(2,1)}, u32[]{:S(2)}, u32[]{:S(2)}) collective-permute-start(bf16[16,48,512]{2,1,0:T(8,128)(2,1)} %get-tuple-element.45), channel_id=1, source_target_pairs={{0,12},{4,8},{8,4},{12,0},{16,28},{20,24},{24,20},{28,16},{1,13},{... | collective-permute-start | bytes 2359304 | tf_op jit(solution)/shard_map/ppermute | solution.py:266
  262.2 0.9 copy-start.3
  266.4 12.6 %copy-start.5 = (bf16[16,64,512]{2,1,0:T(8,128)(2,1)}, bf16[16,64,512]{2,1,0:T(8,128)(2,1)S(1)}, u32[]{:S(2)}) copy-start(bf16[16,64,512]{2,1,0:T(8,128)(2,1)S(1)} %collective-permute-done.7.refs_3_) | copy-start | bytes 3145732
  266.4 12.6 %copy-start.6 = (bf16[16,48,512]{2,1,0:T(8,128)(2,1)}, bf16[16,48,512]{2,1,0:T(8,128)(2,1)S(1)}, u32[]{:S(2)}) copy-start(bf16[16,48,512]{2,1,0:T(8,128)(2,1)S(1)} %collective-permute-done.3.refs_5_) | copy-start | bytes 2359300
  266.5 34.5 %copy-start.7 = (bf16[16,48,512]{2,1,0:T(8,128)(2,1)}, bf16[16,48,512]{2,1,0:T(8,128)(2,1)S(1)}, u32[]{:S(2)}) copy-start(bf16[16,48,512]{2,1,0:T(8,128)(2,1)S(1)} %collective-permute-done.4.refs_6_) | copy-start | bytes 2359300
  279.0 63.2 %all-to-all-start.2 = ((bf16[16,64,1024]{2,1,0:T(8,128)(2,1)}), bf16[16,64,1024]{2,1,0:T(8,128)(2,1)S(1)}, u32[]{:S(2)}, u32[]{:S(2)}) async-start(bf16[16,64,1024]{2,1,0:T(8,128)(2,1)} %gather_fusion), calls=%async_computation.2 | async-start | bytes 4194304 | tf_op jit(solution)/shard_map/all_to_all | solution.py:311
  300.9 17.5 %collective-permute-start.8 = (bf16[16,16,512]{2,1,0:T(8,128)(2,1)}, bf16[16,16,512]{2,1,0:T(8,128)(2,1)}, u32[]{:S(2)}, u32[]{:S(2)}) collective-permute-start(bf16[16,16,512]{2,1,0:T(8,128)(2,1)} %get-tuple-element.63), channel_id=1, source_target_pairs={{0,4},{4,0},{8,12},{12,8},{16,20},{20,16},{24,28},{28,24},{1,5},{5... | collective-permute-start | bytes 786440 | tf_op jit(solution)/shard_map/ppermute | solution.py:266
  303.0 30.4 %collective-permute-start.9 = (bf16[16,16,512]{2,1,0:T(8,128)(2,1)}, bf16[16,16,512]{2,1,0:T(8,128)(2,1)S(1)}, u32[]{:S(2)}, u32[]{:S(2)}) collective-permute-start(bf16[16,16,512]{2,1,0:T(8,128)(2,1)} %get-tuple-element.64), channel_id=1, source_target_pairs={{0,8},{4,12},{8,0},{12,4},{16,24},{20,28},{24,16},{28,20},{1,9},{5... | collective-permute-start | bytes 786440 | tf_op jit(solution)/shard_map/ppermute | solution.py:266
  304.5 32.7 %collective-permute-start.10 = (bf16[16,16,512]{2,1,0:T(8,128)(2,1)}, bf16[16,16,512]{2,1,0:T(8,128)(2,1)}, u32[]{:S(2)}, u32[]{:S(2)}) collective-permute-start(bf16[16,16,512]{2,1,0:T(8,128)(2,1)} %get-tuple-element.65), channel_id=1, source_target_pairs={{0,12},{4,8},{8,4},{12,0},{16,28},{20,24},{24,20},{28,16},{1,13},{... | collective-permute-start | bytes 786440 | tf_op jit(solution)/shard_map/ppermute | solution.py:266
  333.4 3.8 %copy-start.8 = (bf16[16,16,512]{2,1,0:T(8,128)(2,1)}, bf16[16,16,512]{2,1,0:T(8,128)(2,1)S(1)}, u32[]{:S(2)}) copy-start(bf16[16,16,512]{2,1,0:T(8,128)(2,1)S(1)} %collective-permute-done.9.refs_10_) | copy-start | bytes 786436
  342.2 1.3 copy-start.2
Sparse Core Ops, SparseCore 0:
  9.6 60.9 all-gather.1

commit v8 on v7

--- a/solution.py
+++ b/solution.py
@@ -300,16 +300,16 @@
     new_cache = jnp.dot(piece, keyvalue_weight, preferred_element_type=jnp.float32).astype(jnp.bfloat16)
 
     mirrored = [swap(parts[0], half)]
-    mirrored[0], parts[1], down_rows, near[:2], query_base, new_cache = lax.optimization_barrier(
-        (mirrored[0], parts[1], down_rows, near[:2], query_base, new_cache)
+    mirrored[0], parts[1], near, query_base, new_cache = lax.optimization_barrier(
+        (mirrored[0], parts[1], near, query_base, new_cache)
     )
     mirrored.append(swap(parts[1], half))
+    far = [serve(far_asked[1:], pool) for pool in mirrored]
+    down_rows, far[0] = lax.optimization_barrier((down_rows, far[0]))
     down_sent = lax.all_to_all(down_rows, "dp", split_axis=0, concat_axis=0, tiled=True)
-    far = [serve(far_asked[1:], pool) for pool in mirrored]
-    far[0] = [swap(pages, i + 1) for i, pages in enumerate(far[0])]
-    up_rows, down_sent, far, near = lax.optimization_barrier((up_rows, down_sent, far, near))
+    far = [[swap(pages, i + 1) for i, pages in enumerate(block)] for block in far]
+    up_rows, down_sent, far = lax.optimization_barrier((up_rows, down_sent, far))
     up_sent = lax.all_to_all(up_rows, "dp", split_axis=0, concat_axis=0, tiled=True)
-    far[1] = [swap(pages, i + 1) for i, pages in enumerate(far[1])]
 
     lengths = span_token_length[0]
     ends = jnp.cumsum(lengths)

time: 367 us -> 369 us (level)
  waiting for transfers between devices: 205 us -> 214 us
  starting transfers between devices: 40.8 us -> 34.7 us
    all_to_all x1, waiting for transfers between devices: 0.01 us -> 20.5 us  [on_device(): lax.all_to_all(up_rows, 'dp', split_axis=0, concat_axis=0, tiled=True)]
    all_to_all x1, starting transfers between devices: 13.3 us -> 4.85 us  [on_device(): lax.all_to_all(up_rows, 'dp', split_axis=0, concat_axis=0, tiled=True)]
    ppermute x11, waiting for transfers between devices: 172 us -> 165 us  [swap(): lax.ppermute(array, 'dp', [(peer, peer ^ distance) for peer in range(peer...]
  transfers between devices with their start and end apart: 15 -> 15, of which waited for: 8 -> 10; matrix products, arithmetic and copies ran while one was open for 15% -> 15% of each run, Pallas kernels for 5% -> 3%
where the time goes in v8:
time: 369 us; the launch traced here: 368 us
  waiting for transfers between devices  214 us (58%)
  starting transfers between devices  34.7 us (9%)
  Pallas kernels  32.4 us (9%)
  matrix products  31.2 us (8%)
  local copies, waits for them, and re-layouts  24.3 us (7%)
  between operations  14.9 us (4%)
  blocking collectives  12.3 us (3%)
  other arithmetic  3.99 us (1%)
    ppermute x11, waiting for transfers between devices, swap(): lax.ppermute(array, 'dp', [(peer, peer ^ distance) for peer in range(peer...  165 us
    all_gather x1, waiting for transfers between devices, on_device(): piece = lax.all_gather(tokens, 'tensor', axis=1, tiled=True)  27.2 us
    all_to_all x1, waiting for transfers between devices, on_device(): lax.all_to_all(up_rows, 'dp', split_axis=0, concat_axis=0, tiled=True)  20.5 us
    dot_general x1, matrix products, on_device(): jnp.dot(piece, query_weight, preferred_element_type=jnp.float32)  18.2 us
    ppermute x11, starting transfers between devices, swap(): lax.ppermute(array, 'dp', [(peer, peer ^ distance) for peer in range(peer...  16.8 us
    pallas_call x1, Pallas kernels, attend(): pl.pallas_call(attention_kernel, out_shape=jax.ShapeDtypeStruct((rows, q_...  14.3 us
    pallas_call x3, Pallas kernels, serve(): pl.pallas_call(serve_kernel, out_shape=[jax.ShapeDtypeStruct(shape, store...  13.1 us
    psum x1, blocking collectives, on_device(): shrink = lax.psum(shrink_part, 'tensor').astype(jnp.bfloat16)  12.3 us
  transfers between devices with their start and end apart: 15, of which 10 were waited for; matrix products, arithmetic and copies ran while one was open for 15% of the time, Pallas kernels for 3%

profile of v8, /device:TPU:0, one launch (start us, length us, event | category | flops | bytes accessed | tf_op | source)
XLA Modules:
  0.0 368.1 jit_solution(15662790968746315345)
XLA Ops:
  7.2 0.7 all-gather.2.cloned.1.call-update
  7.9 0.8 pad_add_fusion.1
  8.7 0.6 broadcast_in_dim.172
  9.3 7.3 %all-to-all-start = ((s32[8,1,160]{2,1,0:T(1,128)}), s32[8,1,160]{2,1,0:T(1,128)S(1)}, u32[]{:S(2)}, u32[]{:S(2)}) async-start(s32[8,1,160]{2,1,0:T(1,128)} %broadcast_in_dim.172), calls=%async_computation | async-start | bytes 16384 | tf_op jit(solution)/shard_map/all_to_all | solution.py:271
  16.6 3.4 slice.30
  19.9 2.2 slice.31
  22.2 0.9 all-to-all-done
  23.1 0.6 gather_fusion.2
  24.2 0.6 reshape.365.asked_ref
  24.8 4.3 %serve.3 = (bf16[16,64,512]{2,1,0:T(8,128)(2,1)}, bf16[16,64,512]{2,1,0:T(8,128)(2,1)}, bf16[16,64,512]{2,1,0:T(8,128)(2,1)}) custom-call(s32[48]{0:T(128)} %reshape.365.asked_ref, bf16[48,64,512]{2,1,0:T(8,128)(2,1)} %refs_0_), custom_call_target="tpu_custom_call" | custom-call | bytes 6291456 | tf_op jit(solution)/shard_map/serve/pallas_call | solution.py:188
  29.0 3.1 collective-permute-start.1
  32.4 1.2 collective-permute-start.3
  33.7 2.1 collective-permute-start
  35.8 0.6 reshape.364.asked_ref
  37.2 6.2 %gather_fusion.1 = bf16[16,2048,64]{1,2,0:T(8,128)(2,1)} fusion(bf16[32,2048,64]{1,2,0:T(8,128)(2,1)} %param.14, s32[1024]{0:T(1024)S(1)} %pad_clamp_fusion.1), kind=kCustom, calls=%fused_computation.1 | custom fusion | bytes 8388672 | tf_op jit(solution)/shard_map/gather | solution.py:295
  43.4 27.2 %all-gather.2.cloned.1.call-done = bf16[512,8192]{1,0:T(8,128)(2,1)} async-done(((bf16[512,2048]{1,0:T(8,128)(2,1)}), bf16[512,8192]{1,0:T(8,128)(2,1)}) %all-gather.2.cloned.1.call-update) | async-done | bytes 8388624 | tf_op jit(solution)/shard_map/all_gather | solution.py:298
  70.6 18.2 %fusion.23.base_hbm = f32[512,1024]{1,0:T(8,128)} fusion(bf16[512,8192]{1,0:T(8,128)(2,1)} %all-gather.2.cloned.1.call-done, bf16[8192,1024]{1,0:T(8,128)(2,1)} %param.12), kind=kOutput, calls=%fused_computation.88 | convolution fusion | flops 8589934592 | bytes 27262976 | tf_op jit(solution)/shard_map/dot_general | solution.py:299
  88.8 7.7 %convolution_convert_fusion.cache_hbm = bf16[512,512]{1,0:T(8,128)(2,1)} fusion(bf16[512,8192]{1,0:T(8,128)(2,1)S(1)} %copy-done.12, bf16[8192,512]{1,0:T(8,128)(2,1)} %param.13), kind=kOutput, calls=%fused_computation.7 | convolution fusion | flops 4295229440 | bytes 17301504 | tf_op jit(solution)/shard_map/dot_general | solution.py:300
  96.5 6.2 %collective-permute-done.2.refs_2_ = bf16[16,64,512]{2,1,0:T(8,128)(2,1)} collective-permute-done((bf16[16,64,512]{2,1,0:T(8,128)(2,1)}, bf16[16,64,512]{2,1,0:T(8,128)(2,1)}, u32[]{:S(2)}, u32[]{:S(2)}) %collective-permute-start.2) | collective-permute-done | bytes 1048608 | tf_op jit(solution)/shard_map/ppermute | solution.py:266
  102.8 18.7 %collective-permute-done.3.refs_3_ = bf16[16,64,512]{2,1,0:T(8,128)(2,1)} collective-permute-done((bf16[16,64,512]{2,1,0:T(8,128)(2,1)}, bf16[16,64,512]{2,1,0:T(8,128)(2,1)}, u32[]{:S(2)}, u32[]{:S(2)}) %collective-permute-start.3) | collective-permute-done | bytes 1048608 | tf_op jit(solution)/shard_map/ppermute | solution.py:266
  121.5 15.5 %collective-permute-done.store_ref.refs_4_ = bf16[48,48,512]{2,1,0:T(8,128)(2,1)S(1)} collective-permute-done((bf16[48,48,512]{2,1,0:T(8,128)(2,1)}, bf16[48,48,512]{2,1,0:T(8,128)(2,1)S(1)}, u32[]{:S(2)}, u32[]{:S(2)}) %collective-permute-start) | collective-permute-done | bytes 2359328 | tf_op jit(solution)/shard_map/ppermute | solution.py:266
  137.0 1.4 copy-done
  138.4 5.6 %serve.4 = (bf16[16,48,512]{2,1,0:T(8,128)(2,1)}, bf16[16,48,512]{2,1,0:T(8,128)(2,1)}, bf16[16,48,512]{2,1,0:T(8,128)(2,1)}) custom-call(s32[48]{0:T(128)} %reshape.364.asked_ref, bf16[48,48,512]{2,1,0:T(8,128)(2,1)} %copy-done), custom_call_target="tpu_custom_call" | custom-call | bytes 4718592 | tf_op jit(solution)/shard_map/serve/pallas_call | solution.py:188
  144.0 5.8 %all-to-all-start.1 = ((bf16[16,2048,64]{1,2,0:T(8,128)(2,1)}), bf16[16,2048,64]{1,2,0:T(8,128)(2,1)}, u32[]{:S(2)}, u32[]{:S(2)}) async-start(bf16[16,2048,64]{1,2,0:T(8,128)(2,1)} %gather_fusion.1), calls=%async_computation.1 | async-start | bytes 8388608 | tf_op jit(solution)/shard_map/all_to_all | solution.py:309
  149.8 2.9 collective-permute-start.7
  152.7 1.5 collective-permute-start.4
  154.2 1.5 collective-permute-start.5
  155.7 0.6 collective-permute-start.6
  156.2 118.2 %collective-permute-done.7.store_ref.refs_8_ = bf16[48,16,512]{2,1,0:T(8,128)(2,1)S(1)} collective-permute-done((bf16[48,16,512]{2,1,0:T(8,128)(2,1)}, bf16[48,16,512]{2,1,0:T(8,128)(2,1)S(1)}, u32[]{:S(2)}, u32[]{:S(2)}) %collective-permute-start.7) | collective-permute-done | bytes 786464 | tf_op jit(solution)/shard_map/ppermute | solution.py:266
  274.5 0.9 copy-done.2
  275.4 3.3 serve.5
  278.8 1.6 collective-permute-start.8
  280.4 1.9 collective-permute-start.9
  282.3 4.2 %gather_fusion = bf16[16,64,1024]{2,1,0:T(8,128)(2,1)} fusion(bf16[32,64,1024]{2,1,0:T(8,128)(2,1)} %param.15, s32[1024]{0:T(1024)S(1)} %pad_clamp_fusion.1), kind=kCustom, calls=%fused_computation | custom fusion | bytes 4194368 | tf_op jit(solution)/shard_map/gather | solution.py:296
  286.6 2.0 collective-permute-done.10.refs_11_
  288.6 2.6 collective-permute-done.8.refs_9_
  291.2 1.8 collective-permute-done.9.refs_10_
  293.0 4.9 %all-to-all-start.2 = ((bf16[16,64,1024]{2,1,0:T(8,128)(2,1)}), bf16[16,64,1024]{2,1,0:T(8,128)(2,1)S(1)}, u32[]{:S(2)}, u32[]{:S(2)}) async-start(bf16[16,64,1024]{2,1,0:T(8,128)(2,1)} %gather_fusion), calls=%async_computation.2 | async-start | bytes 4194304 | tf_op jit(solution)/shard_map/all_to_all | solution.py:312
  298.3 0.5 slice.44
  299.7 0.6 pad_add_fusion.steps_ref
  300.7 0.5 compare_select_fusion.4
  301.3 5.2 %fusion = f32[512,64]{0,1:T(8,128)S(1)} fusion(bf16[16,2048,64]{1,2,0:T(8,128)(2,1)} %all-to-all-done.1, bf16[512,2048]{1,0:T(8,128)(2,1)} %param.11, pred[512,16]{0,1:T(8,128)(4,1)S(1)} %iota_compare_fusion.2), kind=kOutput, calls=%fused_computation.4 | convolution fusion | flops 2148499456 | bytes 6430720 | tf_op jit(solution)/shard_map/tn,snk->tsk/dot_general | solution.py:322
  306.6 12.3 %all-reduce.1 = bf16[512,64]{0,1:T(8,128)(2,1)S(1)} all-reduce(f32[512,64]{0,1:T(8,128)S(1)} %fusion), channel_id=1, replica_groups=mesh['dp'=8,'tensor'=4] {'tensor'}, use_global_device_ids=true, to_apply=%region_15.16 | all-reduce | flops 32768 | bytes 196608 | tf_op jit(solution)/shard_map/psum | solution.py:324
  318.9 1.3 copy.37.spread_hbm
  320.3 4.9 %assemble.1.pages_hbm = bf16[64,64,512]{2,1,0:T(8,128)(2,1)} custom-call(s32[64]{0:T(128)} %get-tuple-element.75.source_ref, s32[64]{0:T(128)} %get-tuple-element.74.place_ref, bf16[48,64,512]{2,1,0:T(8,128)(2,1)} %refs_0_, bf16[16,64,512]{2,1,0:T(8,128)(2,1)} %copy-done.3, bf16[16,64,512]{2,1,0:T(8,128)(2,1)} %collective-permute-done.2.refs_2_, ...), custom_call_target="tpu_custom_call" | custom-call | bytes 8388608 | tf_op jit(solution)/shard_map/assemble/pallas_call | solution.py:232
  325.2 20.5 %all-to-all-done.2 = bf16[16,64,1024]{2,1,0:T(8,128)(2,1)S(1)} async-done(((bf16[16,64,1024]{2,1,0:T(8,128)(2,1)}), bf16[16,64,1024]{2,1,0:T(8,128)(2,1)S(1)}, u32[]{:S(2)}, u32[]{:S(2)}) %all-to-all-start.2) | async-done | bytes 2097184 | tf_op jit(solution)/shard_map/all_to_all | solution.py:312
  345.6 1.3 copy-done.1
  347.0 14.3 %attend.1 = bf16[512,1024]{1,0:T(8,128)(2,1)} custom-call(s32[4,32]{1,0:T(4,128)} %pad_add_fusion.steps_ref, bf16[512,1024]{1,0:T(8,128)(2,1)} %copy.37.spread_hbm, bf16[1024,1024]{1,0:T(8,128)(2,1)} %bitcast.56, f32[512,1024]{1,0:T(8,128)} %fusion.23.base_hbm, bf16[512,512]{1,0:T(8,128)(2,1)} %convolution_convert_fusion.cache_hbm, ...), custom_call_target="tpu_custom_call" | custom-call | flops 2818572288 | bytes 11010048 | tf_op jit(solution)/shard_map/attend/pallas_call | solution.py:154
  (66 shorter events, 3.0 us)
Async XLA Ops:
  7.2 63.4 %all-gather.2.cloned.1.call-start = ((), (), s32[]{:S(2)}) async-start(), calls=%async_computation.3 | async-start | bytes 10485760 | tf_op jit(solution)/shard_map/all_gather | solution.py:298
  9.3 13.8 %all-to-all-start = ((s32[8,1,160]{2,1,0:T(1,128)}), s32[8,1,160]{2,1,0:T(1,128)S(1)}, u32[]{:S(2)}, u32[]{:S(2)}) async-start(s32[8,1,160]{2,1,0:T(1,128)} %broadcast_in_dim.172), calls=%async_computation | async-start | bytes 16384 | tf_op jit(solution)/shard_map/all_to_all | solution.py:271
  29.0 67.5 %collective-permute-start.1 = (bf16[16,64,512]{2,1,0:T(8,128)(2,1)}, bf16[16,64,512]{2,1,0:T(8,128)(2,1)S(1)}, u32[]{:S(2)}, u32[]{:S(2)}) collective-permute-start(bf16[16,64,512]{2,1,0:T(8,128)(2,1)} %get-tuple-element.40), channel_id=1, source_target_pairs={{0,4},{4,0},{8,12},{12,8},{16,20},{20,16},{24,28},{28,24},{1,5},{5... | collective-permute-start | bytes 3145736 | tf_op jit(solution)/shard_map/ppermute | solution.py:266
  32.1 70.7 %collective-permute-start.2 = (bf16[16,64,512]{2,1,0:T(8,128)(2,1)}, bf16[16,64,512]{2,1,0:T(8,128)(2,1)}, u32[]{:S(2)}, u32[]{:S(2)}) collective-permute-start(bf16[16,64,512]{2,1,0:T(8,128)(2,1)} %get-tuple-element.41), channel_id=1, source_target_pairs={{0,8},{4,12},{8,0},{12,4},{16,24},{20,28},{24,16},{28,20},{1,9},{5... | collective-permute-start | bytes 3145736 | tf_op jit(solution)/shard_map/ppermute | solution.py:266
  32.4 89.0 %collective-permute-start.3 = (bf16[16,64,512]{2,1,0:T(8,128)(2,1)}, bf16[16,64,512]{2,1,0:T(8,128)(2,1)}, u32[]{:S(2)}, u32[]{:S(2)}) collective-permute-start(bf16[16,64,512]{2,1,0:T(8,128)(2,1)} %get-tuple-element.42), channel_id=1, source_target_pairs={{0,12},{4,8},{8,4},{12,0},{16,28},{20,24},{24,20},{28,16},{1,13},{... | collective-permute-start | bytes 3145736 | tf_op jit(solution)/shard_map/ppermute | solution.py:266
  33.7 103.4 %collective-permute-start = (bf16[48,48,512]{2,1,0:T(8,128)(2,1)}, bf16[48,48,512]{2,1,0:T(8,128)(2,1)S(1)}, u32[]{:S(2)}, u32[]{:S(2)}) collective-permute-start(bf16[48,48,512]{2,1,0:T(8,128)(2,1)} %slice.30), channel_id=1, source_target_pairs={{0,16},{4,20},{8,24},{12,28},{16,0},{20,4},{24,8},{28,12},{1,17},{... | collective-permute-start | bytes 7077896 | tf_op jit(solution)/shard_map/ppermute | solution.py:266
  70.6 18.2 %copy-start.12 = (bf16[512,8192]{1,0:T(8,128)(2,1)S(1)}, bf16[512,8192]{1,0:T(8,128)(2,1)}, u32[]{:S(2)}) copy-start(bf16[512,8192]{1,0:T(8,128)(2,1)} %all-gather.2.cloned.1.call-done) | copy-start | bytes 25165828
  96.5 210.0 %copy-start.3 = (bf16[16,64,512]{2,1,0:T(8,128)(2,1)}, bf16[16,64,512]{2,1,0:T(8,128)(2,1)S(1)}, u32[]{:S(2)}) copy-start(bf16[16,64,512]{2,1,0:T(8,128)(2,1)S(1)} %collective-permute-done.1.refs_1_) | copy-start | bytes 3145732
  137.0 1.4 copy-start
  144.0 149.0 %all-to-all-start.1 = ((bf16[16,2048,64]{1,2,0:T(8,128)(2,1)}), bf16[16,2048,64]{1,2,0:T(8,128)(2,1)}, u32[]{:S(2)}, u32[]{:S(2)}) async-start(bf16[16,2048,64]{1,2,0:T(8,128)(2,1)} %gather_fusion.1), calls=%async_computation.1 | async-start | bytes 8388608 | tf_op jit(solution)/shard_map/all_to_all | solution.py:309
  149.8 124.6 %collective-permute-start.7 = (bf16[48,16,512]{2,1,0:T(8,128)(2,1)}, bf16[48,16,512]{2,1,0:T(8,128)(2,1)S(1)}, u32[]{:S(2)}, u32[]{:S(2)}) collective-permute-start(bf16[48,16,512]{2,1,0:T(8,128)(2,1)} %slice.31), channel_id=1, source_target_pairs={{0,16},{4,20},{8,24},{12,28},{16,0},{20,4},{24,8},{28,12},{1,17},{... | collective-permute-start | bytes 2359304 | tf_op jit(solution)/shard_map/ppermute | solution.py:266
  152.7 127.7 %collective-permute-start.4 = (bf16[16,48,512]{2,1,0:T(8,128)(2,1)}, bf16[16,48,512]{2,1,0:T(8,128)(2,1)S(1)}, u32[]{:S(2)}, u32[]{:S(2)}) collective-permute-start(bf16[16,48,512]{2,1,0:T(8,128)(2,1)} %get-tuple-element.48), channel_id=1, source_target_pairs={{0,4},{4,0},{8,12},{12,8},{16,20},{20,16},{24,28},{28,24},{1,5},{5... | collective-permute-start | bytes 2359304 | tf_op jit(solution)/shard_map/ppermute | solution.py:266
  154.2 132.4 %collective-permute-start.5 = (bf16[16,48,512]{2,1,0:T(8,128)(2,1)}, bf16[16,48,512]{2,1,0:T(8,128)(2,1)S(1)}, u32[]{:S(2)}, u32[]{:S(2)}) collective-permute-start(bf16[16,48,512]{2,1,0:T(8,128)(2,1)} %get-tuple-element.49), channel_id=1, source_target_pairs={{0,8},{4,12},{8,0},{12,4},{16,24},{20,28},{24,16},{28,20},{1,9},{5... | collective-permute-start | bytes 2359304 | tf_op jit(solution)/shard_map/ppermute | solution.py:266
  155.7 130.9 %collective-permute-start.6 = (bf16[16,48,512]{2,1,0:T(8,128)(2,1)}, bf16[16,48,512]{2,1,0:T(8,128)(2,1)}, u32[]{:S(2)}, u32[]{:S(2)}) collective-permute-start(bf16[16,48,512]{2,1,0:T(8,128)(2,1)} %get-tuple-element.50), channel_id=1, source_target_pairs={{0,12},{4,8},{8,4},{12,0},{16,28},{20,24},{24,20},{28,16},{1,13},{... | collective-permute-start | bytes 2359304 | tf_op jit(solution)/shard_map/ppermute | solution.py:266
  274.5 0.9 copy-start.2
  278.7 9.9 %collective-permute-start.10 = (bf16[16,16,512]{2,1,0:T(8,128)(2,1)}, bf16[16,16,512]{2,1,0:T(8,128)(2,1)S(1)}, u32[]{:S(2)}, u32[]{:S(2)}) collective-permute-start(bf16[16,16,512]{2,1,0:T(8,128)(2,1)} %get-tuple-element.54), channel_id=1, source_target_pairs={{0,12},{4,8},{8,4},{12,0},{16,28},{20,24},{24,20},{28,16},{1,13},{... | collective-permute-start | bytes 786440 | tf_op jit(solution)/shard_map/ppermute | solution.py:266
  278.8 12.4 %collective-permute-start.8 = (bf16[16,16,512]{2,1,0:T(8,128)(2,1)}, bf16[16,16,512]{2,1,0:T(8,128)(2,1)S(1)}, u32[]{:S(2)}, u32[]{:S(2)}) collective-permute-start(bf16[16,16,512]{2,1,0:T(8,128)(2,1)} %get-tuple-element.52), channel_id=1, source_target_pairs={{0,4},{4,0},{8,12},{12,8},{16,20},{20,16},{24,28},{28,24},{1,5},{5... | collective-permute-start | bytes 786440 | tf_op jit(solution)/shard_map/ppermute | solution.py:266
  280.4 12.6 %copy-start.4 = (bf16[16,48,512]{2,1,0:T(8,128)(2,1)}, bf16[16,48,512]{2,1,0:T(8,128)(2,1)S(1)}, u32[]{:S(2)}) copy-start(bf16[16,48,512]{2,1,0:T(8,128)(2,1)S(1)} %collective-permute-done.4.refs_5_) | copy-start | bytes 2359300
  280.4 17.5 %copy-start.8 = (s32[1,16]{1,0:T(1,128)S(1)}, s32[1,16]{1,0:T(1,128)}, u32[]{:S(2)}) copy-start(s32[1,16]{1,0:T(1,128)} %param.17) | copy-start | bytes 196
  280.4 19.9 %copy-start.10 = (s32[64,1]{0,1:T(1,128)S(1)}, s32[64,1]{0,1:T(1,128)}, u32[]{:S(2)}) copy-start(s32[64,1]{0,1:T(1,128)} %param.20) | copy-start | bytes 772
  280.4 20.0 %copy-start.11 = (s32[16,1]{0,1:T(1,128)S(1)}, s32[16,1]{0,1:T(1,128)}, u32[]{:S(2)}) copy-start(s32[16,1]{0,1:T(1,128)} %param.18) | copy-start | bytes 196
  280.4 20.3 %copy-start.9 = (s32[64]{0:T(128)S(1)}, s32[64]{0:T(128)}, u32[]{:S(2)}) copy-start(s32[64]{0:T(128)} %param.21) | copy-start | bytes 772
  280.4 12.6 %collective-permute-start.9 = (bf16[16,16,512]{2,1,0:T(8,128)(2,1)}, bf16[16,16,512]{2,1,0:T(8,128)(2,1)}, u32[]{:S(2)}, u32[]{:S(2)}) collective-permute-start(bf16[16,16,512]{2,1,0:T(8,128)(2,1)} %get-tuple-element.53), channel_id=1, source_target_pairs={{0,8},{4,12},{8,0},{12,4},{16,24},{20,28},{24,16},{28,20},{1,9},{5... | collective-permute-start | bytes 786440 | tf_op jit(solution)/shard_map/ppermute | solution.py:266
  286.6 6.4 %copy-start.5 = (bf16[16,48,512]{2,1,0:T(8,128)(2,1)}, bf16[16,48,512]{2,1,0:T(8,128)(2,1)S(1)}, u32[]{:S(2)}) copy-start(bf16[16,48,512]{2,1,0:T(8,128)(2,1)S(1)} %collective-permute-done.5.refs_6_) | copy-start | bytes 2359300
  288.6 4.4 %copy-start.6 = (bf16[16,16,512]{2,1,0:T(8,128)(2,1)}, bf16[16,16,512]{2,1,0:T(8,128)(2,1)S(1)}, u32[]{:S(2)}) copy-start(bf16[16,16,512]{2,1,0:T(8,128)(2,1)S(1)} %collective-permute-done.10.refs_11_) | copy-start | bytes 786436
  291.2 1.8 copy-start.7
  293.0 52.6 %all-to-all-start.2 = ((bf16[16,64,1024]{2,1,0:T(8,128)(2,1)}), bf16[16,64,1024]{2,1,0:T(8,128)(2,1)S(1)}, u32[]{:S(2)}, u32[]{:S(2)}) async-start(bf16[16,64,1024]{2,1,0:T(8,128)(2,1)} %gather_fusion), calls=%async_computation.2 | async-start | bytes 4194304 | tf_op jit(solution)/shard_map/all_to_all | solution.py:312
  345.6 1.3 copy-start.1
Sparse Core Ops, SparseCore 0:
  9.6 60.9 all-gather.1

commit v9 on v8

--- a/solution.py
+++ b/solution.py
@@ -15,7 +15,6 @@
 BLOCK = 32
 TOGETHER = 4
 TILE = 256
-PARTS = ((0, 48), (48, 64))
 VMEM_GRANT = 60 * 1024 * 1024
 
 ADAPTER_SCALE = 0.5
@@ -200,24 +199,16 @@
 
 
 def assemble_kernel(source_ref, place_ref, *refs):
-    out, sem = refs[-2:]
-    half = (len(refs) - 2) // (1 + len(PARTS))
-    near, far = refs[:half], refs[half:-2]
+    sources, out, sem = refs[:-2], refs[-2], refs[-1]
 
     def one(index, carry):
         source = source_ref[index]
         place = place_ref[index]
-        for number in range(half):
+        for number, ref in enumerate(sources):
 
             @pl.when(source == number)
             def _():
-                pltpu.make_async_copy(near[number].at[place], out.at[index], sem).start()
-
-            @pl.when(source == half + number)
-            def _():
-                for part, (first, end) in enumerate(PARTS):
-                    rows = out.at[index, first:end]
-                    pltpu.make_async_copy(far[part * half + number].at[place], rows, sem).start()
+                pltpu.make_async_copy(ref.at[place], out.at[index], sem).start()
 
         return carry
 
@@ -225,13 +216,12 @@
     pltpu.make_async_copy(out, out, sem).wait()
 
 
-def assemble(source, place, near, far):
+def assemble(source, place, sources):
     scalars = pl.BlockSpec(memory_space=pltpu.SMEM)
-    sources = [*near, *far]
-    shape = (source.shape[0],) + near[0].shape[1:]
+    shape = (source.shape[0],) + sources[0].shape[1:]
     return pl.pallas_call(
         assemble_kernel,
-        out_shape=jax.ShapeDtypeStruct(shape, near[0].dtype),
+        out_shape=jax.ShapeDtypeStruct(shape, sources[0].dtype),
         in_specs=[scalars, scalars] + [pl.BlockSpec(memory_space=pltpu.HBM)] * len(sources),
         out_specs=pl.BlockSpec(memory_space=pltpu.VMEM),
         scratch_shapes=[pltpu.SemaphoreType.DMA],
@@ -271,10 +261,8 @@
     everyone = lax.all_to_all(
         jnp.broadcast_to(raw[None], (peers, raw.shape[0])), "dp", split_axis=0, concat_axis=0, tiled=True
     )
-    parts = [keyvalue_page_store[:, first:end] for first, end in PARTS]
-    store, down_store, everyone, *parts = lax.optimization_barrier(
-        (keyvalue_page_store, adapter_down_weight, everyone, *parts)
-    )
+    store, down_store, everyone = lax.optimization_barrier((keyvalue_page_store, adapter_down_weight, everyone))
+    mirrored_store = swap(store, half)
 
     page_cap = max(2, 2 * page_count // peers)
     group = everyone[jnp.arange(half, dtype=jnp.int32) ^ me]
@@ -290,7 +278,7 @@
     page_source = page_owner[:, 0] ^ me
     page_place = jnp.where(page_source % half == 0, page_local_index, earlier_alike(page_owner[:, 0]))
 
-    near = serve(near_asked[1:], store)
+    near = list(serve(near_asked[1:], store))
     near = [swap(pages, i + 1) for i, pages in enumerate(near)]
     down_rows = down_store[adapter_asked]
     up_rows = adapter_up_weight[adapter_asked]
@@ -299,17 +287,15 @@
     query_base = jnp.dot(piece, query_weight, preferred_element_type=jnp.float32)
     new_cache = jnp.dot(piece, keyvalue_weight, preferred_element_type=jnp.float32).astype(jnp.bfloat16)
 
-    mirrored = [swap(parts[0], half)]
-    mirrored[0], parts[1], near, query_base, new_cache = lax.optimization_barrier(
-        (mirrored[0], parts[1], near, query_base, new_cache)
+    down_rows, mirrored_store, query_base, new_cache, near = lax.optimization_barrier(
+        (down_rows, mirrored_store, query_base, new_cache, near)
     )
-    mirrored.append(swap(parts[1], half))
-    far = [serve(far_asked[1:], pool) for pool in mirrored]
-    down_rows, far[0] = lax.optimization_barrier((down_rows, far[0]))
     down_sent = lax.all_to_all(down_rows, "dp", split_axis=0, concat_axis=0, tiled=True)
-    far = [[swap(pages, i + 1) for i, pages in enumerate(block)] for block in far]
+    far = list(serve(far_asked[1:], mirrored_store))
+    far = [swap(pages, i + 1) for i, pages in enumerate(far[:-1])] + far[-1:]
     up_rows, down_sent, far = lax.optimization_barrier((up_rows, down_sent, far))
     up_sent = lax.all_to_all(up_rows, "dp", split_axis=0, concat_axis=0, tiled=True)
+    far[-1] = swap(far[-1], half - 1)
 
     lengths = span_token_length[0]
     ends = jnp.cumsum(lengths)
@@ -323,8 +309,7 @@
     shrink_part = jnp.sum(jnp.where(in_slot[:, :, None], down_part, 0.0), axis=1)
     shrink = lax.psum(shrink_part, "tensor").astype(jnp.bfloat16)
     spread = jnp.where(in_slot[:, :, None], shrink[:, None, :], 0).reshape(tok_rows, adapter_slots * rank)
-    far = [page for part in range(len(PARTS)) for page in (mirrored[part], *far[part])]
-    prefix_pages = assemble(page_source, page_place, [store, *near], far)
+    prefix_pages = assemble(page_source, page_place, [store, *near, mirrored_store, *far])
     up = up_sent.reshape(adapter_slots * rank, q_cols)
     out = attend(query_base, spread, up, new_cache, prefix_pages, starts, ends)
     return (out, new_cache)

time: 369 us -> 355 us (0.962)
  starting transfers between devices: 34.7 us -> 26.7 us
  local copies, waits for them, and re-layouts: 24.3 us -> 18.2 us
    all_to_all x1, waiting for transfers between devices: 20.5 us -> 0.01 us  [on_device(): lax.all_to_all(up_rows, 'dp', split_axis=0, concat_axis=0, tiled=True)]
    ppermute x11 -> x7, waiting for transfers between devices: 165 us -> 176 us  [swap(): lax.ppermute(array, 'dp', [(peer, peer ^ distance) for peer in range(peer...]
    ppermute x11 -> x7, starting transfers between devices: 16.8 us -> 10.2 us  [swap(): lax.ppermute(array, 'dp', [(peer, peer ^ distance) for peer in range(peer...]
    all_to_all x1, waiting for transfers between devices: 0.9 us -> 6.46 us  [on_device(): lax.all_to_all(jnp.broadcast_to(raw[None], (peers, raw.shape[0])), 'dp',...]
    slice x4 -> x2, local copies, waits for them, and re-layouts: 5.57 us -> 0.01 us  [the longest x1 0.01 us: on_device(): near = list(serve(near_asked[1:], store))]
    pallas_call x3 -> x2, Pallas kernels: 13.1 us -> 12.6 us  [serve(): pl.pallas_call(serve_kernel, out_shape=[jax.ShapeDtypeStruct(shape, store...]
  transfers between devices with their start and end apart: 15 -> 11, of which waited for: 10 -> 9; matrix products, arithmetic and copies ran while one was open for 15% -> 14% of each run, Pallas kernels for 3% -> 5%
where the time goes in v9:
time: 355 us; the launch traced here: 353 us
  waiting for transfers between devices  214 us (60%)
  Pallas kernels  31.9 us (9%)
  matrix products  31.2 us (9%)
  starting transfers between devices  26.7 us (8%)
  local copies, waits for them, and re-layouts  18.2 us (5%)
  between operations  14.8 us (4%)
  blocking collectives  12.2 us (3%)
  other arithmetic  4.03 us (1%)
    ppermute x7, waiting for transfers between devices, swap(): lax.ppermute(array, 'dp', [(peer, peer ^ distance) for peer in range(peer...  176 us
    all_gather x1, waiting for transfers between devices, on_device(): piece = lax.all_gather(tokens, 'tensor', axis=1, tiled=True)  28.8 us
    dot_general x1, matrix products, on_device(): jnp.dot(piece, query_weight, preferred_element_type=jnp.float32)  18.2 us
    pallas_call x1, Pallas kernels, attend(): pl.pallas_call(attention_kernel, out_shape=jax.ShapeDtypeStruct((rows, q_...  14.3 us
    pallas_call x2, Pallas kernels, serve(): pl.pallas_call(serve_kernel, out_shape=[jax.ShapeDtypeStruct(shape, store...  12.6 us
    psum x1, blocking collectives, on_device(): shrink = lax.psum(shrink_part, 'tensor').astype(jnp.bfloat16)  12.2 us
    ppermute x7, starting transfers between devices, swap(): lax.ppermute(array, 'dp', [(peer, peer ^ distance) for peer in range(peer...  10.2 us
    dot_general x1, matrix products, on_device(): jnp.dot(piece, keyvalue_weight, preferred_element_type=jnp.float32)  7.7 us
  transfers between devices with their start and end apart: 11, of which 9 were waited for; matrix products, arithmetic and copies ran while one was open for 14% of the time, Pallas kernels for 5%

profile of v9, /device:TPU:0, one launch (start us, length us, event | category | flops | bytes accessed | tf_op | source)
XLA Modules:
  0.0 353.2 jit_solution(16020540079838686717)
XLA Ops:
  7.2 0.7 all-gather.2.cloned.1.call-update
  7.9 0.8 pad_add_fusion.1
  8.7 0.6 broadcast_in_dim.172
  9.3 7.3 %all-to-all-start = ((s32[8,1,160]{2,1,0:T(1,128)}), s32[8,1,160]{2,1,0:T(1,128)S(1)}, u32[]{:S(2)}, u32[]{:S(2)}) async-start(s32[8,1,160]{2,1,0:T(1,128)} %broadcast_in_dim.172), calls=%async_computation | async-start | bytes 16384 | tf_op jit(solution)/shard_map/all_to_all | solution.py:261
  16.6 6.5 %all-to-all-done = s32[8,1,160]{2,1,0:T(1,128)S(1)} async-done(((s32[8,1,160]{2,1,0:T(1,128)}), s32[8,1,160]{2,1,0:T(1,128)S(1)}, u32[]{:S(2)}, u32[]{:S(2)}) %all-to-all-start) | async-done | bytes 5152 | tf_op jit(solution)/shard_map/all_to_all | solution.py:261
  23.1 0.6 gather_fusion.2
  23.7 0.2 convert_reduce_fusion
  23.9 0.2 select_reduce_fusion
  24.2 0.6 reshape.363.asked_ref
  24.8 0.3 convert_reduce_fusion.1
  25.1 0.1 select_reduce_fusion.3
  25.4 0.6 collective-permute-start
  26.0 5.8 %serve.2 = (bf16[16,64,512]{2,1,0:T(8,128)(2,1)}, bf16[16,64,512]{2,1,0:T(8,128)(2,1)}, bf16[16,64,512]{2,1,0:T(8,128)(2,1)}) custom-call(s32[48]{0:T(128)} %reshape.363.asked_ref, bf16[48,64,512]{2,1,0:T(8,128)(2,1)} %refs_0_), custom_call_target="tpu_custom_call" | custom-call | bytes 6291456 | tf_op jit(solution)/shard_map/serve/pallas_call | solution.py:187
  31.8 0.3 collective-permute-start.1
  32.2 3.2 collective-permute-start.3
  35.5 6.3 %gather_fusion.1 = bf16[16,2048,64]{1,2,0:T(8,128)(2,1)} fusion(bf16[32,2048,64]{1,2,0:T(8,128)(2,1)} %param.14, s32[1024]{0:T(1024)S(1)} %pad_clamp_fusion.1), kind=kCustom, calls=%fused_computation.1 | custom fusion | bytes 8388672 | tf_op jit(solution)/shard_map/gather | solution.py:283
  41.8 28.8 %all-gather.2.cloned.1.call-done = bf16[512,8192]{1,0:T(8,128)(2,1)} async-done(((bf16[512,2048]{1,0:T(8,128)(2,1)}), bf16[512,8192]{1,0:T(8,128)(2,1)}) %all-gather.2.cloned.1.call-update) | async-done | bytes 8388624 | tf_op jit(solution)/shard_map/all_gather | solution.py:286
  70.6 18.2 %fusion.23.base_hbm = f32[512,1024]{1,0:T(8,128)} fusion(bf16[512,8192]{1,0:T(8,128)(2,1)} %all-gather.2.cloned.1.call-done, bf16[8192,1024]{1,0:T(8,128)(2,1)} %param.12), kind=kOutput, calls=%fused_computation.88 | convolution fusion | flops 8589934592 | bytes 27262976 | tf_op jit(solution)/shard_map/dot_general | solution.py:287
  88.8 7.7 %convolution_convert_fusion.cache_hbm = bf16[512,512]{1,0:T(8,128)(2,1)} fusion(bf16[512,8192]{1,0:T(8,128)(2,1)S(1)} %copy-done.8, bf16[8192,512]{1,0:T(8,128)(2,1)} %param.13), kind=kOutput, calls=%fused_computation.7 | convolution fusion | flops 4295229440 | bytes 17301504 | tf_op jit(solution)/shard_map/dot_general | solution.py:288
  96.5 20.8 %collective-permute-done.2.refs_2_ = bf16[16,64,512]{2,1,0:T(8,128)(2,1)} collective-permute-done((bf16[16,64,512]{2,1,0:T(8,128)(2,1)}, bf16[16,64,512]{2,1,0:T(8,128)(2,1)}, u32[]{:S(2)}, u32[]{:S(2)}) %collective-permute-start.2) | collective-permute-done | bytes 1048608 | tf_op jit(solution)/shard_map/ppermute | solution.py:256
  117.3 19.9 %collective-permute-done.3.refs_3_ = bf16[16,64,512]{2,1,0:T(8,128)(2,1)} collective-permute-done((bf16[16,64,512]{2,1,0:T(8,128)(2,1)}, bf16[16,64,512]{2,1,0:T(8,128)(2,1)}, u32[]{:S(2)}, u32[]{:S(2)}) %collective-permute-start.3) | collective-permute-done | bytes 1048608 | tf_op jit(solution)/shard_map/ppermute | solution.py:256
  137.2 25.1 %collective-permute-done.store_ref.refs_4_ = bf16[48,64,512]{2,1,0:T(8,128)(2,1)S(1)} collective-permute-done((bf16[48,64,512]{2,1,0:T(8,128)(2,1)}, bf16[48,64,512]{2,1,0:T(8,128)(2,1)S(1)}, u32[]{:S(2)}, u32[]{:S(2)}) %collective-permute-start) | collective-permute-done | bytes 3145760 | tf_op jit(solution)/shard_map/ppermute | solution.py:256
  162.3 1.7 copy-done
  164.0 4.5 %all-to-all-start.1 = ((bf16[16,2048,64]{1,2,0:T(8,128)(2,1)}), bf16[16,2048,64]{1,2,0:T(8,128)(2,1)}, u32[]{:S(2)}, u32[]{:S(2)}) async-start(bf16[16,2048,64]{1,2,0:T(8,128)(2,1)} %gather_fusion.1), calls=%async_computation.1 | async-start | bytes 8388608 | tf_op jit(solution)/shard_map/all_to_all | solution.py:293
  168.6 0.7 reshape.364.asked_ref
  169.2 6.8 %serve.3 = (bf16[16,64,512]{2,1,0:T(8,128)(2,1)}, bf16[16,64,512]{2,1,0:T(8,128)(2,1)}, bf16[16,64,512]{2,1,0:T(8,128)(2,1)}) custom-call(s32[48]{0:T(128)} %reshape.364.asked_ref, bf16[48,64,512]{2,1,0:T(8,128)(2,1)} %copy-done), custom_call_target="tpu_custom_call" | custom-call | bytes 6291456 | tf_op jit(solution)/shard_map/serve/pallas_call | solution.py:187
  176.0 0.7 collective-permute-start.4
  176.7 2.5 collective-permute-start.5
  179.2 4.2 %gather_fusion = bf16[16,64,1024]{2,1,0:T(8,128)(2,1)} fusion(bf16[32,64,1024]{2,1,0:T(8,128)(2,1)} %param.15, s32[1024]{0:T(1024)S(1)} %pad_clamp_fusion.1), kind=kCustom, calls=%fused_computation | custom fusion | bytes 4194368 | tf_op jit(solution)/shard_map/gather | solution.py:284
  183.4 55.3 %collective-permute-done.4.refs_5_ = bf16[16,64,512]{2,1,0:T(8,128)(2,1)S(1)} collective-permute-done((bf16[16,64,512]{2,1,0:T(8,128)(2,1)}, bf16[16,64,512]{2,1,0:T(8,128)(2,1)S(1)}, u32[]{:S(2)}, u32[]{:S(2)}) %collective-permute-start.4) | collective-permute-done | bytes 1048608 | tf_op jit(solution)/shard_map/ppermute | solution.py:256
  238.7 21.7 %collective-permute-done.5.refs_6_ = bf16[16,64,512]{2,1,0:T(8,128)(2,1)S(1)} collective-permute-done((bf16[16,64,512]{2,1,0:T(8,128)(2,1)}, bf16[16,64,512]{2,1,0:T(8,128)(2,1)S(1)}, u32[]{:S(2)}, u32[]{:S(2)}) %collective-permute-start.5) | collective-permute-done | bytes 1048608 | tf_op jit(solution)/shard_map/ppermute | solution.py:256
  260.4 1.8 all-to-all-done.1
  262.2 4.7 %all-to-all-start.2 = ((bf16[16,64,1024]{2,1,0:T(8,128)(2,1)}), bf16[16,64,1024]{2,1,0:T(8,128)(2,1)S(1)}, u32[]{:S(2)}, u32[]{:S(2)}) async-start(bf16[16,64,1024]{2,1,0:T(8,128)(2,1)} %gather_fusion), calls=%async_computation.2 | async-start | bytes 4194304 | tf_op jit(solution)/shard_map/all_to_all | solution.py:297
  267.0 0.1 fusion.21
  267.1 0.5 slice.35
  267.6 0.1 reduce
  268.4 0.2 convert_reduce_fusion.3
  268.5 0.2 convert_reduce_fusion.2
  269.1 0.6 compare_select_fusion.4
  269.6 3.0 collective-permute-start.6
  272.6 0.6 pad_add_fusion.steps_ref
  273.2 5.2 %fusion = f32[512,64]{0,1:T(8,128)S(1)} fusion(bf16[16,2048,64]{1,2,0:T(8,128)(2,1)} %all-to-all-done.1, bf16[512,2048]{1,0:T(8,128)(2,1)} %param.11, pred[512,16]{0,1:T(8,128)(4,1)S(1)} %iota_compare_fusion.2), kind=kOutput, calls=%fused_computation.4 | convolution fusion | flops 2148499456 | bytes 6430720 | tf_op jit(solution)/shard_map/tn,snk->tsk/dot_general | solution.py:308
  278.5 12.2 %all-reduce.1 = bf16[512,64]{0,1:T(8,128)(2,1)S(1)} all-reduce(f32[512,64]{0,1:T(8,128)S(1)} %fusion), channel_id=1, replica_groups=mesh['dp'=8,'tensor'=4] {'tensor'}, use_global_device_ids=true, to_apply=%region_15.16 | all-reduce | flops 32768 | bytes 196608 | tf_op jit(solution)/shard_map/psum | solution.py:310
  290.8 1.4 copy.37.spread_hbm
  292.2 33.6 %collective-permute-done.6.refs_7_ = bf16[16,64,512]{2,1,0:T(8,128)(2,1)} collective-permute-done((bf16[16,64,512]{2,1,0:T(8,128)(2,1)}, bf16[16,64,512]{2,1,0:T(8,128)(2,1)}, u32[]{:S(2)}, u32[]{:S(2)}) %collective-permute-start.6) | collective-permute-done | bytes 1048608 | tf_op jit(solution)/shard_map/ppermute | solution.py:256
  325.7 4.9 %assemble.1.pages_hbm = bf16[64,64,512]{2,1,0:T(8,128)(2,1)} custom-call(s32[64]{0:T(128)} %get-tuple-element.51.source_ref, s32[64]{0:T(128)} %get-tuple-element.50.place_ref, bf16[48,64,512]{2,1,0:T(8,128)(2,1)} %refs_0_, bf16[16,64,512]{2,1,0:T(8,128)(2,1)} %collective-permute-done.1.refs_1_, bf16[16,64,512]{2,1,0:T(8,128)(2,1)} %collective-permute-done.2.refs_2_, ...), custom_call_target="tpu_custom_call" | custom-call | bytes 8388608 | tf_op jit(solution)/shard_map/assemble/pallas_call | solution.py:222
  330.7 1.3 copy-done.1
  332.0 14.3 %attend.1 = bf16[512,1024]{1,0:T(8,128)(2,1)} custom-call(s32[4,32]{1,0:T(4,128)} %pad_add_fusion.steps_ref, bf16[512,1024]{1,0:T(8,128)(2,1)} %copy.37.spread_hbm, bf16[1024,1024]{1,0:T(8,128)(2,1)} %bitcast.56, f32[512,1024]{1,0:T(8,128)} %fusion.23.base_hbm, bf16[512,512]{1,0:T(8,128)(2,1)} %convolution_convert_fusion.cache_hbm, ...), custom_call_target="tpu_custom_call" | custom-call | flops 2818572288 | bytes 11010048 | tf_op jit(solution)/shard_map/attend/pallas_call | solution.py:153
  (47 shorter events, 1.1 us)
Async XLA Ops:
  7.2 63.4 %all-gather.2.cloned.1.call-start = ((), (), s32[]{:S(2)}) async-start(), calls=%async_computation.3 | async-start | bytes 10485760 | tf_op jit(solution)/shard_map/all_gather | solution.py:286
  9.3 13.8 %all-to-all-start = ((s32[8,1,160]{2,1,0:T(1,128)}), s32[8,1,160]{2,1,0:T(1,128)S(1)}, u32[]{:S(2)}, u32[]{:S(2)}) async-start(s32[8,1,160]{2,1,0:T(1,128)} %broadcast_in_dim.172), calls=%async_computation | async-start | bytes 16384 | tf_op jit(solution)/shard_map/all_to_all | solution.py:261
  25.4 136.9 %collective-permute-start = (bf16[48,64,512]{2,1,0:T(8,128)(2,1)}, bf16[48,64,512]{2,1,0:T(8,128)(2,1)S(1)}, u32[]{:S(2)}, u32[]{:S(2)}) collective-permute-start(bf16[48,64,512]{2,1,0:T(8,128)(2,1)} %refs_0_), channel_id=1, source_target_pairs={{0,16},{4,20},{8,24},{12,28},{16,0},{20,4},{24,8},{28,12},{1,17},{... | collective-permute-start | bytes 9437192 | tf_op jit(solution)/shard_map/ppermute | solution.py:256
  31.8 64.7 %collective-permute-start.1 = (bf16[16,64,512]{2,1,0:T(8,128)(2,1)}, bf16[16,64,512]{2,1,0:T(8,128)(2,1)}, u32[]{:S(2)}, u32[]{:S(2)}) collective-permute-start(bf16[16,64,512]{2,1,0:T(8,128)(2,1)} %get-tuple-element.26), channel_id=1, source_target_pairs={{0,4},{4,0},{8,12},{12,8},{16,20},{20,16},{24,28},{28,24},{1,5},{5... | collective-permute-start | bytes 3145736 | tf_op jit(solution)/shard_map/ppermute | solution.py:256
  32.2 85.2 %collective-permute-start.2 = (bf16[16,64,512]{2,1,0:T(8,128)(2,1)}, bf16[16,64,512]{2,1,0:T(8,128)(2,1)}, u32[]{:S(2)}, u32[]{:S(2)}) collective-permute-start(bf16[16,64,512]{2,1,0:T(8,128)(2,1)} %get-tuple-element.27), channel_id=1, source_target_pairs={{0,8},{4,12},{8,0},{12,4},{16,24},{20,28},{24,16},{28,20},{1,9},{5... | collective-permute-start | bytes 3145736 | tf_op jit(solution)/shard_map/ppermute | solution.py:256
  32.2 105.1 %collective-permute-start.3 = (bf16[16,64,512]{2,1,0:T(8,128)(2,1)}, bf16[16,64,512]{2,1,0:T(8,128)(2,1)}, u32[]{:S(2)}, u32[]{:S(2)}) collective-permute-start(bf16[16,64,512]{2,1,0:T(8,128)(2,1)} %get-tuple-element.28), channel_id=1, source_target_pairs={{0,12},{4,8},{8,4},{12,0},{16,28},{20,24},{24,20},{28,16},{1,13},{... | collective-permute-start | bytes 3145736 | tf_op jit(solution)/shard_map/ppermute | solution.py:256
  70.6 18.2 %copy-start.8 = (bf16[512,8192]{1,0:T(8,128)(2,1)S(1)}, bf16[512,8192]{1,0:T(8,128)(2,1)}, u32[]{:S(2)}) copy-start(bf16[512,8192]{1,0:T(8,128)(2,1)} %all-gather.2.cloned.1.call-done) | copy-start | bytes 25165828
  162.3 1.7 copy-start
  164.0 98.2 %all-to-all-start.1 = ((bf16[16,2048,64]{1,2,0:T(8,128)(2,1)}), bf16[16,2048,64]{1,2,0:T(8,128)(2,1)}, u32[]{:S(2)}, u32[]{:S(2)}) async-start(bf16[16,2048,64]{1,2,0:T(8,128)(2,1)} %gather_fusion.1), calls=%async_computation.1 | async-start | bytes 8388608 | tf_op jit(solution)/shard_map/all_to_all | solution.py:293
  176.0 62.6 %collective-permute-start.4 = (bf16[16,64,512]{2,1,0:T(8,128)(2,1)}, bf16[16,64,512]{2,1,0:T(8,128)(2,1)S(1)}, u32[]{:S(2)}, u32[]{:S(2)}) collective-permute-start(bf16[16,64,512]{2,1,0:T(8,128)(2,1)} %get-tuple-element.31), channel_id=1, source_target_pairs={{0,4},{4,0},{8,12},{12,8},{16,20},{20,16},{24,28},{28,24},{1,5},{5... | collective-permute-start | bytes 3145736 | tf_op jit(solution)/shard_map/ppermute | solution.py:256
  176.7 90.2 %copy-start.4 = (s32[1,16]{1,0:T(1,128)S(1)}, s32[1,16]{1,0:T(1,128)}, u32[]{:S(2)}) copy-start(s32[1,16]{1,0:T(1,128)} %param.17) | copy-start | bytes 196
  176.7 91.7 %copy-start.7 = (s32[16,1]{0,1:T(1,128)S(1)}, s32[16,1]{0,1:T(1,128)}, u32[]{:S(2)}) copy-start(s32[16,1]{0,1:T(1,128)} %param.18) | copy-start | bytes 196
  176.7 91.9 %copy-start.6 = (s32[64,1]{0,1:T(1,128)S(1)}, s32[64,1]{0,1:T(1,128)}, u32[]{:S(2)}) copy-start(s32[64,1]{0,1:T(1,128)} %param.20) | copy-start | bytes 772
  176.7 92.4 %copy-start.5 = (s32[64]{0:T(128)S(1)}, s32[64]{0:T(128)}, u32[]{:S(2)}) copy-start(s32[64]{0:T(128)} %param.21) | copy-start | bytes 772
  176.7 83.7 %collective-permute-start.5 = (bf16[16,64,512]{2,1,0:T(8,128)(2,1)}, bf16[16,64,512]{2,1,0:T(8,128)(2,1)S(1)}, u32[]{:S(2)}, u32[]{:S(2)}) collective-permute-start(bf16[16,64,512]{2,1,0:T(8,128)(2,1)} %get-tuple-element.32), channel_id=1, source_target_pairs={{0,8},{4,12},{8,0},{12,4},{16,24},{20,28},{24,16},{28,20},{1,9},{5... | collective-permute-start | bytes 3145736 | tf_op jit(solution)/shard_map/ppermute | solution.py:256
  238.7 23.5 %copy-start.2 = (bf16[16,64,512]{2,1,0:T(8,128)(2,1)}, bf16[16,64,512]{2,1,0:T(8,128)(2,1)S(1)}, u32[]{:S(2)}) copy-start(bf16[16,64,512]{2,1,0:T(8,128)(2,1)S(1)} %collective-permute-done.4.refs_5_) | copy-start | bytes 3145732
  260.4 1.8 copy-start.3
  262.2 68.5 %all-to-all-start.2 = ((bf16[16,64,1024]{2,1,0:T(8,128)(2,1)}), bf16[16,64,1024]{2,1,0:T(8,128)(2,1)S(1)}, u32[]{:S(2)}, u32[]{:S(2)}) async-start(bf16[16,64,1024]{2,1,0:T(8,128)(2,1)} %gather_fusion), calls=%async_computation.2 | async-start | bytes 4194304 | tf_op jit(solution)/shard_map/all_to_all | solution.py:297
  269.6 56.1 %collective-permute-start.6 = (bf16[16,64,512]{2,1,0:T(8,128)(2,1)}, bf16[16,64,512]{2,1,0:T(8,128)(2,1)}, u32[]{:S(2)}, u32[]{:S(2)}) collective-permute-start(bf16[16,64,512]{2,1,0:T(8,128)(2,1)} %get-tuple-element.43), channel_id=1, source_target_pairs={{0,12},{4,8},{8,4},{12,0},{16,28},{20,24},{24,20},{28,16},{1,13},{... | collective-permute-start | bytes 3145736 | tf_op jit(solution)/shard_map/ppermute | solution.py:256
  330.7 1.3 copy-start.1
Sparse Core Ops, SparseCore 0:
  9.6 60.9 all-gather.1

commit v10 on v9

--- a/solution.py
+++ b/solution.py
@@ -258,11 +258,9 @@
     page_count = page_local_index.shape[0]
     request_count = adapter_local_index.shape[0]
     raw = jnp.concatenate([page_owner[:, 0], page_local_index, adapter_owner[:, 0], adapter_local_index])
-    everyone = lax.all_to_all(
-        jnp.broadcast_to(raw[None], (peers, raw.shape[0])), "dp", split_axis=0, concat_axis=0, tiled=True
-    )
-    store, down_store, everyone = lax.optimization_barrier((keyvalue_page_store, adapter_down_weight, everyone))
-    mirrored_store = swap(store, half)
+    tile = jnp.pad(raw, (0, 8 * 128 - raw.shape[0])).reshape(8, 128)
+    everyone = lax.all_gather(tile, "dp", axis=0, tiled=True).reshape(peers, 8 * 128)
+    mirrored_store = swap(keyvalue_page_store, half)
 
     page_cap = max(2, 2 * page_count // peers)
     group = everyone[jnp.arange(half, dtype=jnp.int32) ^ me]
@@ -272,15 +270,15 @@
     near_asked = asked_of(me, group_owner, group_order, group_local, page_cap)
     far_asked = asked_of(me ^ half, group_owner, group_order, group_local, page_cap)
     all_owner = everyone[:, 2 * page_count : 2 * page_count + request_count]
-    all_local = everyone[:, 2 * page_count + request_count :]
+    all_local = everyone[:, 2 * page_count + request_count : raw.shape[0]]
     adapter_asked = asked_of(me, all_owner, earlier_alike(all_owner), all_local, ADP_CAP).reshape(-1)
     adapter_pos = adapter_owner[:, 0] * ADP_CAP + earlier_alike(adapter_owner[:, 0])
     page_source = page_owner[:, 0] ^ me
     page_place = jnp.where(page_source % half == 0, page_local_index, earlier_alike(page_owner[:, 0]))
 
-    near = list(serve(near_asked[1:], store))
+    near = list(serve(near_asked[1:], keyvalue_page_store))
     near = [swap(pages, i + 1) for i, pages in enumerate(near)]
-    down_rows = down_store[adapter_asked]
+    down_rows = adapter_down_weight[adapter_asked]
     up_rows = adapter_up_weight[adapter_asked]
 
     piece = lax.all_gather(tokens, "tensor", axis=1, tiled=True)
@@ -309,7 +307,7 @@
     shrink_part = jnp.sum(jnp.where(in_slot[:, :, None], down_part, 0.0), axis=1)
     shrink = lax.psum(shrink_part, "tensor").astype(jnp.bfloat16)
     spread = jnp.where(in_slot[:, :, None], shrink[:, None, :], 0).reshape(tok_rows, adapter_slots * rank)
-    prefix_pages = assemble(page_source, page_place, [store, *near, mirrored_store, *far])
+    prefix_pages = assemble(page_source, page_place, [keyvalue_page_store, *near, mirrored_store, *far])
     up = up_sent.reshape(adapter_slots * rank, q_cols)
     out = attend(query_base, spread, up, new_cache, prefix_pages, starts, ends)
     return (out, new_cache)

time: 355 us -> 407 us (1.15)
  blocking collectives: 12.2 us -> 169 us
  waiting for transfers between devices: 214 us -> 116 us
    all_gather x0 -> x1, blocking collectives: none -> 157 us  [on_device(): lax.all_gather(tile, 'dp', axis=0, tiled=True).reshape(peers, 8 * 128)]
    ppermute x7, waiting for transfers between devices: 176 us -> 112 us  [swap(): lax.ppermute(array, 'dp', [(peer, peer ^ distance) for peer in range(peer...]
    all_gather x1, waiting for transfers between devices: 28.8 us -> 0.01 us  [on_device(): piece = lax.all_gather(tokens, 'tensor', axis=1, tiled=True)]
    all_to_all x1 -> x0, starting transfers between devices: 7.25 us -> none  [on_device(): lax.all_to_all(jnp.broadcast_to(raw[None], (peers, raw.shape[0])), 'dp',...]
    all_to_all x1 -> x0, waiting for transfers between devices: 6.46 us -> none  [on_device(): lax.all_to_all(jnp.broadcast_to(raw[None], (peers, raw.shape[0])), 'dp',...]
  transfers between devices with their start and end apart: 11 -> 10, of which waited for: 9 -> 5; matrix products, arithmetic and copies ran while one was open for 14% -> 12% of each run, Pallas kernels for 5% -> 4%
where the time goes in v10:
time: 407 us; the launch traced here: 405 us
  blocking collectives  169 us (42%)
  waiting for transfers between devices  116 us (29%)
  Pallas kernels  31.6 us (8%)
  matrix products  28.8 us (7%)
  starting transfers between devices  22.7 us (6%)
  local copies, waits for them, and re-layouts  17.5 us (4%)
  between operations  14.9 us (4%)
    all_gather x1, blocking collectives, on_device(): lax.all_gather(tile, 'dp', axis=0, tiled=True).reshape(peers, 8 * 128)  157 us
    ppermute x7, waiting for transfers between devices, swap(): lax.ppermute(array, 'dp', [(peer, peer ^ distance) for peer in range(peer...  112 us
    dot_general x1, matrix products, on_device(): jnp.dot(piece, query_weight, preferred_element_type=jnp.float32)  15.9 us
    pallas_call x1, Pallas kernels, attend(): pl.pallas_call(attention_kernel, out_shape=jax.ShapeDtypeStruct((rows, q_...  14.3 us
    ppermute x7, starting transfers between devices, swap(): lax.ppermute(array, 'dp', [(peer, peer ^ distance) for peer in range(peer...  13.7 us
    pallas_call x2, Pallas kernels, serve(): pl.pallas_call(serve_kernel, out_shape=[jax.ShapeDtypeStruct(shape, store...  12.4 us
    psum x1, blocking collectives, on_device(): shrink = lax.psum(shrink_part, 'tensor').astype(jnp.bfloat16)  12.2 us
  transfers between devices with their start and end apart: 10, of which 5 were waited for; matrix products, arithmetic and copies ran while one was open for 12% of the time, Pallas kernels for 4%

profile of v10, /device:TPU:0, one launch (start us, length us, event | category | flops | bytes accessed | tf_op | source)
XLA Modules:
  0.0 404.6 jit_solution(6172323780401739565)
XLA Ops:
  7.2 0.7 all-gather.2.cloned.1.call-update
  7.9 4.1 %collective-permute-start = (bf16[48,64,512]{2,1,0:T(8,128)(2,1)}, bf16[48,64,512]{2,1,0:T(8,128)(2,1)S(1)}, u32[]{:S(2)}, u32[]{:S(2)}) collective-permute-start(bf16[48,64,512]{2,1,0:T(8,128)(2,1)} %refs_0_.1), channel_id=1, source_target_pairs={{0,16},{4,20},{8,24},{12,28},{16,0},{20,4},{24,8},{28,12},{1,17},{... | collective-permute-start | bytes 9437192 | tf_op jit(solution)/shard_map/ppermute | solution.py:256
  12.0 0.8 pad_add_fusion.1
  12.8 157.0 %all_gather.6 = s32[64,128]{1,0:T(8,128)S(1)} all-gather(s32[8,128]{1,0:T(8,128)S(1)} %pad_bitcast_fusion), channel_id=1, replica_groups=mesh['dp'=8,'tensor'=4] {'dp'}, dimensions={0}, use_global_device_ids=true | all-gather | bytes 36864 | tf_op jit(solution)/shard_map/all_gather | solution.py:262
  169.8 0.6 gather_fusion.2
  170.5 0.2 convert_reduce_fusion
  170.7 0.2 select_reduce_fusion
  171.0 0.6 reshape.365.asked_ref
  171.6 5.5 %serve.2 = (bf16[16,64,512]{2,1,0:T(8,128)(2,1)}, bf16[16,64,512]{2,1,0:T(8,128)(2,1)}, bf16[16,64,512]{2,1,0:T(8,128)(2,1)}) custom-call(s32[48]{0:T(128)} %reshape.365.asked_ref, bf16[48,64,512]{2,1,0:T(8,128)(2,1)} %refs_0_.1), custom_call_target="tpu_custom_call" | custom-call | bytes 6291456 | tf_op jit(solution)/shard_map/serve/pallas_call | solution.py:187
  177.2 3.4 collective-permute-start.3
  180.7 0.3 convert_reduce_fusion.1
  181.0 0.1 select_reduce_fusion.3
  181.1 0.1 copy.27
  181.3 0.1 fusion.12
  181.4 6.2 %gather_fusion.1 = bf16[16,2048,64]{1,2,0:T(8,128)(2,1)} fusion(bf16[32,2048,64]{1,2,0:T(8,128)(2,1)} %param.14, s32[1024]{0:T(1024)S(1)} %pad_clamp_fusion.1), kind=kCustom, calls=%fused_computation.1 | custom fusion | bytes 8388672 | tf_op jit(solution)/shard_map/gather | solution.py:281
  187.6 15.9 %fusion.23.base_hbm = f32[512,1024]{1,0:T(8,128)} fusion(bf16[512,8192]{1,0:T(8,128)(2,1)} %all-gather.2.cloned.1.call-done, bf16[8192,1024]{1,0:T(8,128)(2,1)} %param.12), kind=kOutput, calls=%fused_computation.88 | convolution fusion | flops 8589934592 | bytes 27262976 | tf_op jit(solution)/shard_map/dot_general | solution.py:285
  203.5 7.7 %convolution_convert_fusion.cache_hbm = bf16[512,512]{1,0:T(8,128)(2,1)} fusion(bf16[512,8192]{1,0:T(8,128)(2,1)S(1)} %copy-done.8, bf16[8192,512]{1,0:T(8,128)(2,1)} %param.13), kind=kOutput, calls=%fused_computation.7 | convolution fusion | flops 4295229440 | bytes 17301504 | tf_op jit(solution)/shard_map/dot_general | solution.py:286
  211.2 9.4 %collective-permute-done.3.refs_3_ = bf16[16,64,512]{2,1,0:T(8,128)(2,1)} collective-permute-done((bf16[16,64,512]{2,1,0:T(8,128)(2,1)}, bf16[16,64,512]{2,1,0:T(8,128)(2,1)}, u32[]{:S(2)}, u32[]{:S(2)}) %collective-permute-start.3) | collective-permute-done | bytes 1048608 | tf_op jit(solution)/shard_map/ppermute | solution.py:256
  220.7 1.7 copy-done
  222.3 4.5 %all-to-all-start = ((bf16[16,2048,64]{1,2,0:T(8,128)(2,1)}), bf16[16,2048,64]{1,2,0:T(8,128)(2,1)}, u32[]{:S(2)}, u32[]{:S(2)}) async-start(bf16[16,2048,64]{1,2,0:T(8,128)(2,1)} %gather_fusion.1), calls=%async_computation | async-start | bytes 8388608 | tf_op jit(solution)/shard_map/all_to_all | solution.py:291
  226.9 0.7 reshape.366.asked_ref
  227.6 6.9 %serve.3 = (bf16[16,64,512]{2,1,0:T(8,128)(2,1)}, bf16[16,64,512]{2,1,0:T(8,128)(2,1)}, bf16[16,64,512]{2,1,0:T(8,128)(2,1)}) custom-call(s32[48]{0:T(128)} %reshape.366.asked_ref, bf16[48,64,512]{2,1,0:T(8,128)(2,1)} %copy-done), custom_call_target="tpu_custom_call" | custom-call | bytes 6291456 | tf_op jit(solution)/shard_map/serve/pallas_call | solution.py:187
  234.5 1.7 collective-permute-start.4
  236.2 1.3 collective-permute-start.5
  237.6 4.2 %gather_fusion = bf16[16,64,1024]{2,1,0:T(8,128)(2,1)} fusion(bf16[32,64,1024]{2,1,0:T(8,128)(2,1)} %param.15, s32[1024]{0:T(1024)S(1)} %pad_clamp_fusion.1), kind=kCustom, calls=%fused_computation | custom fusion | bytes 4194368 | tf_op jit(solution)/shard_map/gather | solution.py:282
  241.8 49.4 %collective-permute-done.4.refs_5_ = bf16[16,64,512]{2,1,0:T(8,128)(2,1)S(1)} collective-permute-done((bf16[16,64,512]{2,1,0:T(8,128)(2,1)}, bf16[16,64,512]{2,1,0:T(8,128)(2,1)S(1)}, u32[]{:S(2)}, u32[]{:S(2)}) %collective-permute-start.4) | collective-permute-done | bytes 1048608 | tf_op jit(solution)/shard_map/ppermute | solution.py:256
  291.2 20.1 %collective-permute-done.5.refs_6_ = bf16[16,64,512]{2,1,0:T(8,128)(2,1)S(1)} collective-permute-done((bf16[16,64,512]{2,1,0:T(8,128)(2,1)}, bf16[16,64,512]{2,1,0:T(8,128)(2,1)S(1)}, u32[]{:S(2)}, u32[]{:S(2)}) %collective-permute-start.5) | collective-permute-done | bytes 1048608 | tf_op jit(solution)/shard_map/ppermute | solution.py:256
  311.3 2.7 all-to-all-done
  314.0 4.4 %all-to-all-start.1 = ((bf16[16,64,1024]{2,1,0:T(8,128)(2,1)}), bf16[16,64,1024]{2,1,0:T(8,128)(2,1)S(1)}, u32[]{:S(2)}, u32[]{:S(2)}) async-start(bf16[16,64,1024]{2,1,0:T(8,128)(2,1)} %gather_fusion), calls=%async_computation.1 | async-start | bytes 4194304 | tf_op jit(solution)/shard_map/all_to_all | solution.py:295
  318.4 0.1 copy.25
  318.5 0.1 fusion.22
  318.7 0.5 slice.35
  319.2 0.1 reduce
  319.9 0.2 convert_reduce_fusion.3
  320.1 0.2 convert_reduce_fusion.2
  320.3 0.1 convert_reduce_fusion.4
  320.4 0.1 select_reduce_fusion.2
  320.5 0.1 select_reduce_fusion.7
  320.6 0.6 compare_select_fusion.4
  321.2 3.0 collective-permute-start.6
  324.2 0.6 pad_add_fusion.steps_ref
  324.8 5.2 %fusion = f32[512,64]{0,1:T(8,128)S(1)} fusion(bf16[16,2048,64]{1,2,0:T(8,128)(2,1)} %all-to-all-done, bf16[512,2048]{1,0:T(8,128)(2,1)} %param.11, pred[512,16]{0,1:T(8,128)(4,1)S(1)} %iota_compare_fusion.2), kind=kOutput, calls=%fused_computation.4 | convolution fusion | flops 2148499456 | bytes 6430720 | tf_op jit(solution)/shard_map/tn,snk->tsk/dot_general | solution.py:306
  330.0 12.2 %all-reduce.2 = bf16[512,64]{0,1:T(8,128)(2,1)S(1)} all-reduce(f32[512,64]{0,1:T(8,128)S(1)} %fusion), channel_id=1, replica_groups=mesh['dp'=8,'tensor'=4] {'tensor'}, use_global_device_ids=true, to_apply=%region_15.16 | all-reduce | flops 32768 | bytes 196608 | tf_op jit(solution)/shard_map/psum | solution.py:308
  342.3 1.4 copy.31.spread_hbm
  343.7 33.4 %collective-permute-done.6.refs_7_ = bf16[16,64,512]{2,1,0:T(8,128)(2,1)} collective-permute-done((bf16[16,64,512]{2,1,0:T(8,128)(2,1)}, bf16[16,64,512]{2,1,0:T(8,128)(2,1)}, u32[]{:S(2)}, u32[]{:S(2)}) %collective-permute-start.6) | collective-permute-done | bytes 1048608 | tf_op jit(solution)/shard_map/ppermute | solution.py:256
  377.1 4.9 %assemble.1.pages_hbm = bf16[64,64,512]{2,1,0:T(8,128)(2,1)} custom-call(s32[64]{0:T(128)} %get-tuple-element.45.source_ref, s32[64]{0:T(128)} %get-tuple-element.44.place_ref, bf16[48,64,512]{2,1,0:T(8,128)(2,1)} %refs_0_.1, bf16[16,64,512]{2,1,0:T(8,128)(2,1)} %collective-permute-done.1.refs_1_, bf16[16,64,512]{2,1,0:T(8,128)(2,1)} %collective-permute-done.2.refs_2_, ...), custom_call_target="tpu_custom_call" | custom-call | bytes 8388608 | tf_op jit(solution)/shard_map/assemble/pallas_call | solution.py:222
  382.1 1.3 copy-done.1
  383.4 14.3 %attend.1 = bf16[512,1024]{1,0:T(8,128)(2,1)} custom-call(s32[4,32]{1,0:T(4,128)} %pad_add_fusion.steps_ref, bf16[512,1024]{1,0:T(8,128)(2,1)} %copy.31.spread_hbm, bf16[1024,1024]{1,0:T(8,128)(2,1)} %bitcast.55, f32[512,1024]{1,0:T(8,128)} %fusion.23.base_hbm, bf16[512,512]{1,0:T(8,128)(2,1)} %convolution_convert_fusion.cache_hbm, ...), custom_call_target="tpu_custom_call" | custom-call | flops 2818572288 | bytes 11010048 | tf_op jit(solution)/shard_map/attend/pallas_call | solution.py:153
  (46 shorter events, 0.7 us)
Async XLA Ops:
  7.2 180.5 %all-gather.2.cloned.1.call-start = ((), (), s32[]{:S(2)}) async-start(), calls=%async_computation.2 | async-start | bytes 10485760 | tf_op jit(solution)/shard_map/all_gather | solution.py:284
  7.9 212.8 %collective-permute-start = (bf16[48,64,512]{2,1,0:T(8,128)(2,1)}, bf16[48,64,512]{2,1,0:T(8,128)(2,1)S(1)}, u32[]{:S(2)}, u32[]{:S(2)}) collective-permute-start(bf16[48,64,512]{2,1,0:T(8,128)(2,1)} %refs_0_.1), channel_id=1, source_target_pairs={{0,16},{4,20},{8,24},{12,28},{16,0},{20,4},{24,8},{28,12},{1,17},{... | collective-permute-start | bytes 9437192 | tf_op jit(solution)/shard_map/ppermute | solution.py:256
  177.1 34.2 %collective-permute-start.1 = (bf16[16,64,512]{2,1,0:T(8,128)(2,1)}, bf16[16,64,512]{2,1,0:T(8,128)(2,1)}, u32[]{:S(2)}, u32[]{:S(2)}) collective-permute-start(bf16[16,64,512]{2,1,0:T(8,128)(2,1)} %get-tuple-element.20), channel_id=1, source_target_pairs={{0,4},{4,0},{8,12},{12,8},{16,20},{20,16},{24,28},{28,24},{1,5},{5... | collective-permute-start | bytes 3145736 | tf_op jit(solution)/shard_map/ppermute | solution.py:256
  177.2 34.1 %collective-permute-start.2 = (bf16[16,64,512]{2,1,0:T(8,128)(2,1)}, bf16[16,64,512]{2,1,0:T(8,128)(2,1)}, u32[]{:S(2)}, u32[]{:S(2)}) collective-permute-start(bf16[16,64,512]{2,1,0:T(8,128)(2,1)} %get-tuple-element.21), channel_id=1, source_target_pairs={{0,8},{4,12},{8,0},{12,4},{16,24},{20,28},{24,16},{28,20},{1,9},{5... | collective-permute-start | bytes 3145736 | tf_op jit(solution)/shard_map/ppermute | solution.py:256
  177.2 43.4 %collective-permute-start.3 = (bf16[16,64,512]{2,1,0:T(8,128)(2,1)}, bf16[16,64,512]{2,1,0:T(8,128)(2,1)}, u32[]{:S(2)}, u32[]{:S(2)}) collective-permute-start(bf16[16,64,512]{2,1,0:T(8,128)(2,1)} %get-tuple-element.22), channel_id=1, source_target_pairs={{0,12},{4,8},{8,4},{12,0},{16,28},{20,24},{24,20},{28,16},{1,13},{... | collective-permute-start | bytes 3145736 | tf_op jit(solution)/shard_map/ppermute | solution.py:256
  187.6 15.9 %copy-start.8 = (bf16[512,8192]{1,0:T(8,128)(2,1)S(1)}, bf16[512,8192]{1,0:T(8,128)(2,1)}, u32[]{:S(2)}) copy-start(bf16[512,8192]{1,0:T(8,128)(2,1)} %all-gather.2.cloned.1.call-done) | copy-start | bytes 25165828
  220.7 1.7 copy-start
  222.3 91.6 %all-to-all-start = ((bf16[16,2048,64]{1,2,0:T(8,128)(2,1)}), bf16[16,2048,64]{1,2,0:T(8,128)(2,1)}, u32[]{:S(2)}, u32[]{:S(2)}) async-start(bf16[16,2048,64]{1,2,0:T(8,128)(2,1)} %gather_fusion.1), calls=%async_computation | async-start | bytes 8388608 | tf_op jit(solution)/shard_map/all_to_all | solution.py:291
  234.5 56.7 %collective-permute-start.4 = (bf16[16,64,512]{2,1,0:T(8,128)(2,1)}, bf16[16,64,512]{2,1,0:T(8,128)(2,1)S(1)}, u32[]{:S(2)}, u32[]{:S(2)}) collective-permute-start(bf16[16,64,512]{2,1,0:T(8,128)(2,1)} %get-tuple-element.25), channel_id=1, source_target_pairs={{0,4},{4,0},{8,12},{12,8},{16,20},{20,16},{24,28},{28,24},{1,5},{5... | collective-permute-start | bytes 3145736 | tf_op jit(solution)/shard_map/ppermute | solution.py:256
  236.2 82.2 %copy-start.4 = (s32[1,16]{1,0:T(1,128)S(1)}, s32[1,16]{1,0:T(1,128)}, u32[]{:S(2)}) copy-start(s32[1,16]{1,0:T(1,128)} %param.17) | copy-start | bytes 196
  236.2 83.7 %copy-start.7 = (s32[16,1]{0,1:T(1,128)S(1)}, s32[16,1]{0,1:T(1,128)}, u32[]{:S(2)}) copy-start(s32[16,1]{0,1:T(1,128)} %param.18) | copy-start | bytes 196
  236.2 83.9 %copy-start.6 = (s32[64,1]{0,1:T(1,128)S(1)}, s32[64,1]{0,1:T(1,128)}, u32[]{:S(2)}) copy-start(s32[64,1]{0,1:T(1,128)} %param.20) | copy-start | bytes 772
  236.2 84.4 %copy-start.5 = (s32[64]{0:T(128)S(1)}, s32[64]{0:T(128)}, u32[]{:S(2)}) copy-start(s32[64]{0:T(128)} %param.21) | copy-start | bytes 772
  236.2 75.0 %collective-permute-start.5 = (bf16[16,64,512]{2,1,0:T(8,128)(2,1)}, bf16[16,64,512]{2,1,0:T(8,128)(2,1)S(1)}, u32[]{:S(2)}, u32[]{:S(2)}) collective-permute-start(bf16[16,64,512]{2,1,0:T(8,128)(2,1)} %get-tuple-element.26), channel_id=1, source_target_pairs={{0,8},{4,12},{8,0},{12,4},{16,24},{20,28},{24,16},{28,20},{1,9},{5... | collective-permute-start | bytes 3145736 | tf_op jit(solution)/shard_map/ppermute | solution.py:256
  291.2 22.8 %copy-start.2 = (bf16[16,64,512]{2,1,0:T(8,128)(2,1)}, bf16[16,64,512]{2,1,0:T(8,128)(2,1)S(1)}, u32[]{:S(2)}) copy-start(bf16[16,64,512]{2,1,0:T(8,128)(2,1)S(1)} %collective-permute-done.4.refs_5_) | copy-start | bytes 3145732
  311.3 2.7 copy-start.3
  314.0 68.1 %all-to-all-start.1 = ((bf16[16,64,1024]{2,1,0:T(8,128)(2,1)}), bf16[16,64,1024]{2,1,0:T(8,128)(2,1)S(1)}, u32[]{:S(2)}, u32[]{:S(2)}) async-start(bf16[16,64,1024]{2,1,0:T(8,128)(2,1)} %gather_fusion), calls=%async_computation.1 | async-start | bytes 4194304 | tf_op jit(solution)/shard_map/all_to_all | solution.py:295
  321.2 55.9 %collective-permute-start.6 = (bf16[16,64,512]{2,1,0:T(8,128)(2,1)}, bf16[16,64,512]{2,1,0:T(8,128)(2,1)}, u32[]{:S(2)}, u32[]{:S(2)}) collective-permute-start(bf16[16,64,512]{2,1,0:T(8,128)(2,1)} %get-tuple-element.37), channel_id=1, source_target_pairs={{0,12},{4,8},{8,4},{12,0},{16,28},{20,24},{24,20},{28,16},{1,13},{... | collective-permute-start | bytes 3145736 | tf_op jit(solution)/shard_map/ppermute | solution.py:256
  382.1 1.3 copy-start.1
Sparse Core Ops, SparseCore 0:
  9.6 60.9 all-gather.1

commit v11 on v9

--- a/solution.py
+++ b/solution.py
@@ -1,3 +1,4 @@
+import functools
 import math
 
 import jax
@@ -171,44 +172,47 @@
     )(steps, spread, up, query_base, cache, pages)
 
 
-def serve_kernel(asked_ref, store_ref, *refs):
+def serve_kernel(pieces, asked_ref, store_ref, *refs):
     outs, sems = refs[:-1], refs[-1]
-    for index, out in enumerate(outs):
+    for number, ((block, first, end), out) in enumerate(zip(pieces, outs)):
         for place in range(out.shape[0]):
-            page = asked_ref[index * out.shape[0] + place]
-            pltpu.make_async_copy(store_ref.at[page], out.at[place], sems.at[index]).start()
-    for index, out in enumerate(outs):
-        pltpu.make_async_copy(out, out, sems.at[index]).wait()
-
-
-def serve(asked, store):
-    blocks, capacity = asked.shape
-    shape = (capacity,) + store.shape[1:]
+            page = asked_ref[block * out.shape[0] + place]
+            rows = store_ref.at[page, first:end]
+            pltpu.make_async_copy(rows, out.at[place], sems.at[number]).start()
+    for number, out in enumerate(outs):
+        pltpu.make_async_copy(out, out, sems.at[number]).wait()
+
+
+def serve(asked, store, pieces):
+    capacity = asked.shape[1]
+    shapes = [(capacity, end - first, store.shape[2]) for _, first, end in pieces]
     return pl.pallas_call(
-        serve_kernel,
-        out_shape=[jax.ShapeDtypeStruct(shape, store.dtype)] * blocks,
+        functools.partial(serve_kernel, pieces),
+        out_shape=[jax.ShapeDtypeStruct(shape, store.dtype) for shape in shapes],
         in_specs=[pl.BlockSpec(memory_space=pltpu.SMEM), pl.BlockSpec(memory_space=pltpu.HBM)],
-        out_specs=[pl.BlockSpec(memory_space=pltpu.VMEM)] * blocks,
-        scratch_shapes=[pltpu.SemaphoreType.DMA((blocks,))],
+        out_specs=[pl.BlockSpec(memory_space=pltpu.VMEM)] * len(pieces),
+        scratch_shapes=[pltpu.SemaphoreType.DMA((len(pieces),))],
         compiler_params=pltpu.CompilerParams(vmem_limit_bytes=VMEM_GRANT),
         cost_estimate=pl.CostEstimate(
-            flops=0, bytes_accessed=4 * blocks * math.prod(shape), transcendentals=0
+            flops=0, bytes_accessed=4 * sum(math.prod(shape) for shape in shapes), transcendentals=0
         ),
         name="serve",
     )(asked.reshape(-1), store)
 
 
-def assemble_kernel(source_ref, place_ref, *refs):
-    sources, out, sem = refs[:-2], refs[-2], refs[-1]
+def assemble_kernel(pieces, source_ref, place_ref, *refs):
+    out, sem = refs[-2:]
 
     def one(index, carry):
         source = source_ref[index]
         place = place_ref[index]
-        for number, ref in enumerate(sources):
+        for number in range(max(block for block, _, _ in pieces) + 1):
 
             @pl.when(source == number)
             def _():
-                pltpu.make_async_copy(ref.at[place], out.at[index], sem).start()
+                for (block, first, end), ref in zip(pieces, refs):
+                    if block == number:
+                        pltpu.make_async_copy(ref.at[place], out.at[index, first:end], sem).start()
 
         return carry
 
@@ -216,19 +220,19 @@
     pltpu.make_async_copy(out, out, sem).wait()
 
 
-def assemble(source, place, sources):
+def assemble(source, place, arrays, pieces):
     scalars = pl.BlockSpec(memory_space=pltpu.SMEM)
-    shape = (source.shape[0],) + sources[0].shape[1:]
+    shape = (source.shape[0],) + arrays[0].shape[1:]
     return pl.pallas_call(
-        assemble_kernel,
-        out_shape=jax.ShapeDtypeStruct(shape, sources[0].dtype),
-        in_specs=[scalars, scalars] + [pl.BlockSpec(memory_space=pltpu.HBM)] * len(sources),
+        functools.partial(assemble_kernel, pieces),
+        out_shape=jax.ShapeDtypeStruct(shape, arrays[0].dtype),
+        in_specs=[scalars, scalars] + [pl.BlockSpec(memory_space=pltpu.HBM)] * len(arrays),
         out_specs=pl.BlockSpec(memory_space=pltpu.VMEM),
         scratch_shapes=[pltpu.SemaphoreType.DMA],
         compiler_params=pltpu.CompilerParams(vmem_limit_bytes=VMEM_GRANT),
         cost_estimate=pl.CostEstimate(flops=0, bytes_accessed=4 * math.prod(shape), transcendentals=0),
         name="assemble",
-    )(source, place, *sources)
+    )(source, place, *arrays)
 
 
 def on_device(
@@ -278,8 +282,10 @@
     page_source = page_owner[:, 0] ^ me
     page_place = jnp.where(page_source % half == 0, page_local_index, earlier_alike(page_owner[:, 0]))
 
-    near = list(serve(near_asked[1:], store))
-    near = [swap(pages, i + 1) for i, pages in enumerate(near)]
+    page = keyvalue_page_store.shape[1]
+    near_pieces = [(block, 0, page) for block in range(half - 1)]
+    near = serve(near_asked[1:], store, near_pieces)
+    near = [swap(pages, block + 1) for pages, (block, _, _) in zip(near, near_pieces)]
     down_rows = down_store[adapter_asked]
     up_rows = adapter_up_weight[adapter_asked]
 
@@ -291,8 +297,9 @@
         (down_rows, mirrored_store, query_base, new_cache, near)
     )
     down_sent = lax.all_to_all(down_rows, "dp", split_axis=0, concat_axis=0, tiled=True)
-    far = list(serve(far_asked[1:], mirrored_store))
-    far = [swap(pages, i + 1) for i, pages in enumerate(far[:-1])] + far[-1:]
+    far_pieces = near_pieces[:-1] + [(half - 2, 0, page // 2), (half - 2, page // 2, page)]
+    far = list(serve(far_asked[1:], mirrored_store, far_pieces))
+    far[:-1] = [swap(pages, block + 1) for pages, (block, _, _) in zip(far[:-1], far_pieces)]
     up_rows, down_sent, far = lax.optimization_barrier((up_rows, down_sent, far))
     up_sent = lax.all_to_all(up_rows, "dp", split_axis=0, concat_axis=0, tiled=True)
     far[-1] = swap(far[-1], half - 1)
@@ -309,7 +316,11 @@
     shrink_part = jnp.sum(jnp.where(in_slot[:, :, None], down_part, 0.0), axis=1)
     shrink = lax.psum(shrink_part, "tensor").astype(jnp.bfloat16)
     spread = jnp.where(in_slot[:, :, None], shrink[:, None, :], 0).reshape(tok_rows, adapter_slots * rank)
-    prefix_pages = assemble(page_source, page_place, [store, *near, mirrored_store, *far])
+    pieces = [(0, 0, page)]
+    pieces += [(block + 1, first, end) for block, first, end in near_pieces]
+    pieces += [(half, 0, page)]
+    pieces += [(half + block + 1, first, end) for block, first, end in far_pieces]
+    prefix_pages = assemble(page_source, page_place, [store, *near, mirrored_store, *far], pieces)
     up = up_sent.reshape(adapter_slots * rank, q_cols)
     out = attend(query_base, spread, up, new_cache, prefix_pages, starts, ends)
     return (out, new_cache)

time: 355 us -> 356 us (level)
    ppermute x7 -> x8, waiting for transfers between devices: 176 us -> 176 us  [swap(): lax.ppermute(array, 'dp', [(peer, peer ^ distance) for peer in range(peer...]
    ppermute x7 -> x8, starting transfers between devices: 10.2 us -> 10.7 us  [swap(): lax.ppermute(array, 'dp', [(peer, peer ^ distance) for peer in range(peer...]
  transfers between devices with their start and end apart: 11 -> 12, of which waited for: 9 -> 7; matrix products, arithmetic and copies ran while one was open for 14% -> 14% of each run, Pallas kernels for 5% -> 5%
where the time goes in v11:
time: 356 us; the launch traced here: 352 us
  waiting for transfers between devices  212 us (60%)
  Pallas kernels  32.1 us (9%)
  matrix products  31.2 us (9%)
  starting transfers between devices  26.3 us (7%)
  local copies, waits for them, and re-layouts  19.5 us (5%)
  between operations  14.9 us (4%)
  blocking collectives  12.2 us (3%)
  other arithmetic  4 us (1%)
    ppermute x8, waiting for transfers between devices, swap(): lax.ppermute(array, 'dp', [(peer, peer ^ distance) for peer in range(peer...  176 us
    all_gather x1, waiting for transfers between devices, on_device(): piece = lax.all_gather(tokens, 'tensor', axis=1, tiled=True)  28.6 us
    dot_general x1, matrix products, on_device(): jnp.dot(piece, query_weight, preferred_element_type=jnp.float32)  18.2 us
    pallas_call x1, Pallas kernels, attend(): pl.pallas_call(attention_kernel, out_shape=jax.ShapeDtypeStruct((rows, q_...  14.3 us
    pallas_call x2, Pallas kernels, serve(): pl.pallas_call(functools.partial(serve_kernel, pieces), out_shape=[jax.Sh...  12.9 us
    psum x1, blocking collectives, on_device(): shrink = lax.psum(shrink_part, 'tensor').astype(jnp.bfloat16)  12.2 us
    ppermute x8, starting transfers between devices, swap(): lax.ppermute(array, 'dp', [(peer, peer ^ distance) for peer in range(peer...  10.7 us
    dot_general x1, matrix products, on_device(): jnp.dot(piece, keyvalue_weight, preferred_element_type=jnp.float32)  7.7 us
  transfers between devices with their start and end apart: 12, of which 7 were waited for; matrix products, arithmetic and copies ran while one was open for 14% of the time, Pallas kernels for 5%

profile of v11, /device:TPU:0, one launch (start us, length us, event | category | flops | bytes accessed | tf_op | source)
XLA Modules:
  0.0 351.8 jit_solution(1967684683035014830)
XLA Ops:
  7.2 0.7 all-gather.2.cloned.1.call-update
  7.9 0.8 pad_add_fusion.1
  8.7 0.6 broadcast_in_dim.172
  9.3 7.3 %all-to-all-start = ((s32[8,1,160]{2,1,0:T(1,128)}), s32[8,1,160]{2,1,0:T(1,128)S(1)}, u32[]{:S(2)}, u32[]{:S(2)}) async-start(s32[8,1,160]{2,1,0:T(1,128)} %broadcast_in_dim.172), calls=%async_computation | async-start | bytes 16384 | tf_op jit(solution)/shard_map/all_to_all | solution.py:265
  16.6 6.5 %all-to-all-done = s32[8,1,160]{2,1,0:T(1,128)S(1)} async-done(((s32[8,1,160]{2,1,0:T(1,128)}), s32[8,1,160]{2,1,0:T(1,128)S(1)}, u32[]{:S(2)}, u32[]{:S(2)}) %all-to-all-start) | async-done | bytes 5152 | tf_op jit(solution)/shard_map/all_to_all | solution.py:265
  23.1 0.6 gather_fusion.2
  23.7 0.2 convert_reduce_fusion
  23.9 0.2 select_reduce_fusion
  24.2 0.6 reshape.363.asked_ref
  24.8 0.3 convert_reduce_fusion.1
  25.1 0.1 select_reduce_fusion.3
  25.4 0.6 collective-permute-start
  26.0 6.0 %serve.2 = (bf16[16,64,512]{2,1,0:T(8,128)(2,1)}, bf16[16,64,512]{2,1,0:T(8,128)(2,1)}, bf16[16,64,512]{2,1,0:T(8,128)(2,1)}) custom-call(s32[48]{0:T(128)} %reshape.363.asked_ref, bf16[48,64,512]{2,1,0:T(8,128)(2,1)} %refs_0_), custom_call_target="tpu_custom_call" | custom-call | bytes 6291456 | tf_op jit(solution)/shard_map/serve/pallas_call | solution.py:189
  32.1 0.1 collective-permute-start.2
  32.2 3.3 collective-permute-start.3
  35.7 6.3 %gather_fusion.1 = bf16[16,2048,64]{1,2,0:T(8,128)(2,1)} fusion(bf16[32,2048,64]{1,2,0:T(8,128)(2,1)} %param.14, s32[1024]{0:T(1024)S(1)} %pad_clamp_fusion.1), kind=kCustom, calls=%fused_computation.1 | custom fusion | bytes 8388672 | tf_op jit(solution)/shard_map/gather | solution.py:289
  41.9 28.6 %all-gather.2.cloned.1.call-done = bf16[512,8192]{1,0:T(8,128)(2,1)} async-done(((bf16[512,2048]{1,0:T(8,128)(2,1)}), bf16[512,8192]{1,0:T(8,128)(2,1)}) %all-gather.2.cloned.1.call-update) | async-done | bytes 8388624 | tf_op jit(solution)/shard_map/all_gather | solution.py:292
  70.6 18.2 %fusion.23.base_hbm = f32[512,1024]{1,0:T(8,128)} fusion(bf16[512,8192]{1,0:T(8,128)(2,1)} %all-gather.2.cloned.1.call-done, bf16[8192,1024]{1,0:T(8,128)(2,1)} %param.12), kind=kOutput, calls=%fused_computation.88 | convolution fusion | flops 8589934592 | bytes 27262976 | tf_op jit(solution)/shard_map/dot_general | solution.py:293
  88.8 7.7 %convolution_convert_fusion.cache_hbm = bf16[512,512]{1,0:T(8,128)(2,1)} fusion(bf16[512,8192]{1,0:T(8,128)(2,1)S(1)} %copy-done.9, bf16[8192,512]{1,0:T(8,128)(2,1)} %param.13), kind=kOutput, calls=%fused_computation.7 | convolution fusion | flops 4295229440 | bytes 17301504 | tf_op jit(solution)/shard_map/dot_general | solution.py:294
  96.5 20.8 %collective-permute-done.2.refs_2_ = bf16[16,64,512]{2,1,0:T(8,128)(2,1)} collective-permute-done((bf16[16,64,512]{2,1,0:T(8,128)(2,1)}, bf16[16,64,512]{2,1,0:T(8,128)(2,1)}, u32[]{:S(2)}, u32[]{:S(2)}) %collective-permute-start.2) | collective-permute-done | bytes 1048608 | tf_op jit(solution)/shard_map/ppermute | solution.py:260
  117.3 19.9 %collective-permute-done.3.refs_3_ = bf16[16,64,512]{2,1,0:T(8,128)(2,1)} collective-permute-done((bf16[16,64,512]{2,1,0:T(8,128)(2,1)}, bf16[16,64,512]{2,1,0:T(8,128)(2,1)}, u32[]{:S(2)}, u32[]{:S(2)}) %collective-permute-start.3) | collective-permute-done | bytes 1048608 | tf_op jit(solution)/shard_map/ppermute | solution.py:260
  137.2 25.1 %collective-permute-done.store_ref.refs_4_ = bf16[48,64,512]{2,1,0:T(8,128)(2,1)S(1)} collective-permute-done((bf16[48,64,512]{2,1,0:T(8,128)(2,1)}, bf16[48,64,512]{2,1,0:T(8,128)(2,1)S(1)}, u32[]{:S(2)}, u32[]{:S(2)}) %collective-permute-start) | collective-permute-done | bytes 3145760 | tf_op jit(solution)/shard_map/ppermute | solution.py:260
  162.3 1.7 copy-done
  164.0 4.5 %all-to-all-start.1 = ((bf16[16,2048,64]{1,2,0:T(8,128)(2,1)}), bf16[16,2048,64]{1,2,0:T(8,128)(2,1)}, u32[]{:S(2)}, u32[]{:S(2)}) async-start(bf16[16,2048,64]{1,2,0:T(8,128)(2,1)} %gather_fusion.1), calls=%async_computation.1 | async-start | bytes 8388608 | tf_op jit(solution)/shard_map/all_to_all | solution.py:299
  168.6 0.7 reshape.364.asked_ref
  169.2 6.9 %serve.3 = (bf16[16,64,512]{2,1,0:T(8,128)(2,1)}, bf16[16,64,512]{2,1,0:T(8,128)(2,1)}, bf16[16,32,512]{2,1,0:T(8,128)(2,1)}, bf16[16,32,512]{2,1,0:T(8,128)(2,1)}) custom-call(s32[48]{0:T(128)} %reshape.364.asked_ref, bf16[48,64,512]{2,1,0:T(8,128)(2,1)} %copy-done), custom_call_target="tpu_custom_call" | custom-call | bytes 6291456 | tf_op jit(solution)/shard_map/serve/pallas_call | solution.py:189
  176.2 2.6 collective-permute-start.5
  178.8 1.0 collective-permute-start.6
  179.8 4.2 %gather_fusion = bf16[16,64,1024]{2,1,0:T(8,128)(2,1)} fusion(bf16[32,64,1024]{2,1,0:T(8,128)(2,1)} %param.15, s32[1024]{0:T(1024)S(1)} %pad_clamp_fusion.1), kind=kCustom, calls=%fused_computation | custom fusion | bytes 4194368 | tf_op jit(solution)/shard_map/gather | solution.py:290
  184.0 89.3 %collective-permute-done.6.refs_7_ = bf16[16,32,512]{2,1,0:T(8,128)(2,1)S(1)} collective-permute-done((bf16[16,32,512]{2,1,0:T(8,128)(2,1)}, bf16[16,32,512]{2,1,0:T(8,128)(2,1)S(1)}, u32[]{:S(2)}, u32[]{:S(2)}) %collective-permute-start.6) | collective-permute-done | bytes 524320 | tf_op jit(solution)/shard_map/ppermute | solution.py:260
  273.4 1.0 copy-done.2
  274.3 0.3 copy-done.3
  274.7 3.8 %all-to-all-start.2 = ((bf16[16,64,1024]{2,1,0:T(8,128)(2,1)}), bf16[16,64,1024]{2,1,0:T(8,128)(2,1)S(1)}, u32[]{:S(2)}, u32[]{:S(2)}) async-start(bf16[16,64,1024]{2,1,0:T(8,128)(2,1)} %gather_fusion), calls=%async_computation.2 | async-start | bytes 4194304 | tf_op jit(solution)/shard_map/all_to_all | solution.py:304
  278.6 0.1 fusion.21
  278.8 0.5 slice.35
  279.2 0.1 reduce
  280.2 0.5 pad_add_fusion.steps_ref
  280.7 0.2 convert_reduce_fusion.3
  280.9 0.2 convert_reduce_fusion.2
  281.2 0.6 compare_select_fusion.4
  281.8 3.0 collective-permute-start.7
  284.8 5.2 %fusion = f32[512,64]{0,1:T(8,128)S(1)} fusion(bf16[16,2048,64]{1,2,0:T(8,128)(2,1)} %all-to-all-done.1, bf16[512,2048]{1,0:T(8,128)(2,1)} %param.11, pred[512,16]{0,1:T(8,128)(4,1)S(1)} %iota_compare_fusion.2), kind=kOutput, calls=%fused_computation.4 | convolution fusion | flops 2148499456 | bytes 6430720 | tf_op jit(solution)/shard_map/tn,snk->tsk/dot_general | solution.py:315
  290.0 12.2 %all-reduce.1 = bf16[512,64]{0,1:T(8,128)(2,1)S(1)} all-reduce(f32[512,64]{0,1:T(8,128)S(1)} %fusion), channel_id=1, replica_groups=mesh['dp'=8,'tensor'=4] {'tensor'}, use_global_device_ids=true, to_apply=%region_15.16 | all-reduce | flops 32768 | bytes 196608 | tf_op jit(solution)/shard_map/psum | solution.py:317
  302.3 1.4 copy.37.spread_hbm
  303.7 20.7 %collective-permute-done.7.refs_8_ = bf16[16,32,512]{2,1,0:T(8,128)(2,1)} collective-permute-done((bf16[16,32,512]{2,1,0:T(8,128)(2,1)}, bf16[16,32,512]{2,1,0:T(8,128)(2,1)}, u32[]{:S(2)}, u32[]{:S(2)}) %collective-permute-start.7) | collective-permute-done | bytes 524320 | tf_op jit(solution)/shard_map/ppermute | solution.py:260
  324.4 4.9 %assemble.1.pages_hbm = bf16[64,64,512]{2,1,0:T(8,128)(2,1)} custom-call(s32[64]{0:T(128)} %get-tuple-element.55.source_ref, s32[64]{0:T(128)} %get-tuple-element.54.place_ref, bf16[48,64,512]{2,1,0:T(8,128)(2,1)} %refs_0_, bf16[16,64,512]{2,1,0:T(8,128)(2,1)} %collective-permute-done.1.refs_1_, bf16[16,64,512]{2,1,0:T(8,128)(2,1)} %collective-permute-done.2.refs_2_, ...), custom_call_target="tpu_custom_call" | custom-call | bytes 8388608 | tf_op jit(solution)/shard_map/assemble/pallas_call | solution.py:226
  329.3 1.3 copy-done.1
  330.7 14.3 %attend.1 = bf16[512,1024]{1,0:T(8,128)(2,1)} custom-call(s32[4,32]{1,0:T(4,128)} %pad_add_fusion.steps_ref, bf16[512,1024]{1,0:T(8,128)(2,1)} %copy.37.spread_hbm, bf16[1024,1024]{1,0:T(8,128)(2,1)} %bitcast.56, f32[512,1024]{1,0:T(8,128)} %fusion.23.base_hbm, bf16[512,512]{1,0:T(8,128)(2,1)} %convolution_convert_fusion.cache_hbm, ...), custom_call_target="tpu_custom_call" | custom-call | flops 2818572288 | bytes 11010048 | tf_op jit(solution)/shard_map/attend/pallas_call | solution.py:154
  (51 shorter events, 1.3 us)
Async XLA Ops:
  7.2 63.4 %all-gather.2.cloned.1.call-start = ((), (), s32[]{:S(2)}) async-start(), calls=%async_computation.3 | async-start | bytes 10485760 | tf_op jit(solution)/shard_map/all_gather | solution.py:292
  9.3 13.8 %all-to-all-start = ((s32[8,1,160]{2,1,0:T(1,128)}), s32[8,1,160]{2,1,0:T(1,128)S(1)}, u32[]{:S(2)}, u32[]{:S(2)}) async-start(s32[8,1,160]{2,1,0:T(1,128)} %broadcast_in_dim.172), calls=%async_computation | async-start | bytes 16384 | tf_op jit(solution)/shard_map/all_to_all | solution.py:265
  25.4 136.9 %collective-permute-start = (bf16[48,64,512]{2,1,0:T(8,128)(2,1)}, bf16[48,64,512]{2,1,0:T(8,128)(2,1)S(1)}, u32[]{:S(2)}, u32[]{:S(2)}) collective-permute-start(bf16[48,64,512]{2,1,0:T(8,128)(2,1)} %refs_0_), channel_id=1, source_target_pairs={{0,16},{4,20},{8,24},{12,28},{16,0},{20,4},{24,8},{28,12},{1,17},{... | collective-permute-start | bytes 9437192 | tf_op jit(solution)/shard_map/ppermute | solution.py:260
  32.0 64.5 %collective-permute-start.1 = (bf16[16,64,512]{2,1,0:T(8,128)(2,1)}, bf16[16,64,512]{2,1,0:T(8,128)(2,1)}, u32[]{:S(2)}, u32[]{:S(2)}) collective-permute-start(bf16[16,64,512]{2,1,0:T(8,128)(2,1)} %get-tuple-element.28), channel_id=1, source_target_pairs={{0,4},{4,0},{8,12},{12,8},{16,20},{20,16},{24,28},{28,24},{1,5},{5... | collective-permute-start | bytes 3145736 | tf_op jit(solution)/shard_map/ppermute | solution.py:260
  32.1 85.3 %collective-permute-start.2 = (bf16[16,64,512]{2,1,0:T(8,128)(2,1)}, bf16[16,64,512]{2,1,0:T(8,128)(2,1)}, u32[]{:S(2)}, u32[]{:S(2)}) collective-permute-start(bf16[16,64,512]{2,1,0:T(8,128)(2,1)} %get-tuple-element.29), channel_id=1, source_target_pairs={{0,8},{4,12},{8,0},{12,4},{16,24},{20,28},{24,16},{28,20},{1,9},{5... | collective-permute-start | bytes 3145736 | tf_op jit(solution)/shard_map/ppermute | solution.py:260
  32.2 105.0 %collective-permute-start.3 = (bf16[16,64,512]{2,1,0:T(8,128)(2,1)}, bf16[16,64,512]{2,1,0:T(8,128)(2,1)}, u32[]{:S(2)}, u32[]{:S(2)}) collective-permute-start(bf16[16,64,512]{2,1,0:T(8,128)(2,1)} %get-tuple-element.30), channel_id=1, source_target_pairs={{0,12},{4,8},{8,4},{12,0},{16,28},{20,24},{24,20},{28,16},{1,13},{... | collective-permute-start | bytes 3145736 | tf_op jit(solution)/shard_map/ppermute | solution.py:260
  70.6 18.2 %copy-start.9 = (bf16[512,8192]{1,0:T(8,128)(2,1)S(1)}, bf16[512,8192]{1,0:T(8,128)(2,1)}, u32[]{:S(2)}) copy-start(bf16[512,8192]{1,0:T(8,128)(2,1)} %all-gather.2.cloned.1.call-done) | copy-start | bytes 25165828
  162.3 1.7 copy-start
  164.0 109.3 %all-to-all-start.1 = ((bf16[16,2048,64]{1,2,0:T(8,128)(2,1)}), bf16[16,2048,64]{1,2,0:T(8,128)(2,1)}, u32[]{:S(2)}, u32[]{:S(2)}) async-start(bf16[16,2048,64]{1,2,0:T(8,128)(2,1)} %gather_fusion.1), calls=%async_computation.1 | async-start | bytes 8388608 | tf_op jit(solution)/shard_map/all_to_all | solution.py:299
  176.2 97.2 %collective-permute-start.4 = (bf16[16,64,512]{2,1,0:T(8,128)(2,1)}, bf16[16,64,512]{2,1,0:T(8,128)(2,1)S(1)}, u32[]{:S(2)}, u32[]{:S(2)}) collective-permute-start(bf16[16,64,512]{2,1,0:T(8,128)(2,1)} %get-tuple-element.33), channel_id=1, source_target_pairs={{0,4},{4,0},{8,12},{12,8},{16,20},{20,16},{24,28},{28,24},{1,5},{5... | collective-permute-start | bytes 3145736 | tf_op jit(solution)/shard_map/ppermute | solution.py:260
  176.2 97.1 %collective-permute-start.5 = (bf16[16,64,512]{2,1,0:T(8,128)(2,1)}, bf16[16,64,512]{2,1,0:T(8,128)(2,1)S(1)}, u32[]{:S(2)}, u32[]{:S(2)}) collective-permute-start(bf16[16,64,512]{2,1,0:T(8,128)(2,1)} %get-tuple-element.34), channel_id=1, source_target_pairs={{0,8},{4,12},{8,0},{12,4},{16,24},{20,28},{24,16},{28,20},{1,9},{5... | collective-permute-start | bytes 3145736 | tf_op jit(solution)/shard_map/ppermute | solution.py:260
  178.8 99.7 %copy-start.5 = (s32[1,16]{1,0:T(1,128)S(1)}, s32[1,16]{1,0:T(1,128)}, u32[]{:S(2)}) copy-start(s32[1,16]{1,0:T(1,128)} %param.17) | copy-start | bytes 196
  178.8 101.9 %copy-start.8 = (s32[16,1]{0,1:T(1,128)S(1)}, s32[16,1]{0,1:T(1,128)}, u32[]{:S(2)}) copy-start(s32[16,1]{0,1:T(1,128)} %param.18) | copy-start | bytes 196
  178.8 102.1 %copy-start.7 = (s32[64,1]{0,1:T(1,128)S(1)}, s32[64,1]{0,1:T(1,128)}, u32[]{:S(2)}) copy-start(s32[64,1]{0,1:T(1,128)} %param.20) | copy-start | bytes 772
  178.8 102.4 %copy-start.6 = (s32[64]{0:T(128)S(1)}, s32[64]{0:T(128)}, u32[]{:S(2)}) copy-start(s32[64]{0:T(128)} %param.21) | copy-start | bytes 772
  178.8 94.5 %collective-permute-start.6 = (bf16[16,32,512]{2,1,0:T(8,128)(2,1)}, bf16[16,32,512]{2,1,0:T(8,128)(2,1)S(1)}, u32[]{:S(2)}, u32[]{:S(2)}) collective-permute-start(bf16[16,32,512]{2,1,0:T(8,128)(2,1)} %get-tuple-element.35), channel_id=1, source_target_pairs={{0,12},{4,8},{8,4},{12,0},{16,28},{20,24},{24,20},{28,16},{1,13},{... | collective-permute-start | bytes 1572872 | tf_op jit(solution)/shard_map/ppermute | solution.py:260
  273.3 16.7 %copy-start.4 = (bf16[16,32,512]{2,1,0:T(8,128)(2,1)}, bf16[16,32,512]{2,1,0:T(8,128)(2,1)S(1)}, u32[]{:S(2)}) copy-start(bf16[16,32,512]{2,1,0:T(8,128)(2,1)S(1)} %collective-permute-done.6.refs_7_) | copy-start | bytes 1572868
  273.3 1.0 copy-start.2
  273.3 1.3 copy-start.3
  274.7 54.7 %all-to-all-start.2 = ((bf16[16,64,1024]{2,1,0:T(8,128)(2,1)}), bf16[16,64,1024]{2,1,0:T(8,128)(2,1)S(1)}, u32[]{:S(2)}, u32[]{:S(2)}) async-start(bf16[16,64,1024]{2,1,0:T(8,128)(2,1)} %gather_fusion), calls=%async_computation.2 | async-start | bytes 4194304 | tf_op jit(solution)/shard_map/all_to_all | solution.py:304
  281.8 42.6 %collective-permute-start.7 = (bf16[16,32,512]{2,1,0:T(8,128)(2,1)}, bf16[16,32,512]{2,1,0:T(8,128)(2,1)}, u32[]{:S(2)}, u32[]{:S(2)}) collective-permute-start(bf16[16,32,512]{2,1,0:T(8,128)(2,1)} %get-tuple-element.47), channel_id=1, source_target_pairs={{0,12},{4,8},{8,4},{12,0},{16,28},{20,24},{24,20},{28,16},{1,13},{... | collective-permute-start | bytes 1572872 | tf_op jit(solution)/shard_map/ppermute | solution.py:260
  329.3 1.3 copy-start.1
Sparse Core Ops, SparseCore 0:
  9.6 60.9 all-gather.1

commit v12 on v11

--- a/solution.py
+++ b/solution.py
@@ -10,7 +10,6 @@
 
 HEAD_WIDTH = 128
 ADP_CAP = 2
-PAGE = 64
 HITS = 4
 MOST = 128
 BLOCK = 32
@@ -50,29 +49,32 @@
     return jnp.stack([request, block, at(starts), at(ends)])
 
 
-def attention_kernel(steps_ref, spread_hbm, up_hbm, base_hbm, cache_hbm, pages_hbm, out_ref, query_ref, *rest):
-    spread_ref, up_ref, base_ref, cache_ref, pages_ref, sems, tile_sems = rest
+def attention_kernel(steps_ref, spread_hbm, up_any, base_hbm, fresh_hbm, pages_hbm, out_ref, query_ref, *rest):
+    spread_ref, up_ref, base_ref, cache_ref, sems, tile_sems = rest
+    q_cols = base_ref.shape[1]
+    kv_heads = cache_ref.shape[2] // (2 * HEAD_WIDTH)
+    group = q_cols // HEAD_WIDTH // kv_heads
+    held = pages_hbm.shape[1]
+    sharp = HEAD_WIDTH ** -0.5 * math.log2(math.e)
 
     def tile_copies(index):
         cols = pl.ds(pl.multiple_of(index * TILE, TILE), TILE)
         return (
-            pltpu.make_async_copy(up_hbm.at[:, cols], up_ref.at[:, cols], tile_sems.at[0, index]),
+            pltpu.make_async_copy(up_any.at[:, cols], up_ref.at[:, cols], tile_sems.at[0, index]),
             pltpu.make_async_copy(base_hbm.at[:, cols], base_ref.at[:, cols], tile_sems.at[1, index]),
         )
 
-    pairs = [(spread_hbm, spread_ref), (cache_hbm, cache_ref), (pages_hbm, pages_ref)]
-    copies = [pltpu.make_async_copy(*pair, sems.at[index]) for index, pair in enumerate(pairs)]
+    copies = [
+        pltpu.make_async_copy(spread_hbm, spread_ref, sems.at[0]),
+        pltpu.make_async_copy(pages_hbm, cache_ref.at[:, :held], sems.at[1]),
+        pltpu.make_async_copy(fresh_hbm, cache_ref.at[:, held:], sems.at[2]),
+    ]
     copies[0].start()
-    for index in range(base_ref.shape[1] // TILE):
+    for index in range(q_cols // TILE):
         for copy in tile_copies(index):
             copy.start()
     for copy in copies[1:]:
         copy.start()
-    rows_total, q_cols = base_ref.shape
-    kv_heads = cache_ref.shape[1] // (2 * HEAD_WIDTH)
-    group = q_cols // HEAD_WIDTH // kv_heads
-    window = min(rows_total, MOST + BLOCK)
-    sharp = HEAD_WIDTH ** -0.5 * math.log2(math.e)
     copies[0].wait()
 
     def project(index, carry):
@@ -87,24 +89,21 @@
     for copy in copies[1:]:
         copy.wait()
     dims = (((1,), (1,)), ((), ()))
+    q_at = lax.broadcasted_iota(jnp.int32, (group * BLOCK, MOST), 0) % BLOCK
+    ahead = lax.broadcasted_iota(jnp.int32, (group * BLOCK, MOST), 1) - q_at
+    own_at = lax.broadcasted_iota(jnp.int32, (BLOCK, HEAD_WIDTH), 0)
 
     def several(turn, carry):
         places = []
         for lane in range(TOGETHER):
             index = turn * TOGETHER + lane
             row = pl.multiple_of(steps_ref[1, index] * BLOCK, BLOCK)
-            start = steps_ref[2, index]
-            base = pl.multiple_of(jnp.minimum(start // BLOCK * BLOCK, rows_total - window), BLOCK)
-            old = pl.ds(steps_ref[0, index] * HITS, HITS)
-            places.append((row, pl.ds(base, window), old, base, start, steps_ref[3, index]))
+            places.append((steps_ref[0, index], row, steps_ref[2, index], steps_ref[3, index]))
         chains = [(place, head) for place in places for head in range(kv_heads)]
         scores = []
-        for (row, new, old, base, start, _), head in chains:
+        for (request, row, start, _), head in chains:
             at = head * 2 * HEAD_WIDTH
             wide = head * group * HEAD_WIDTH
-            q_at = row + lax.broadcasted_iota(jnp.int32, (group * BLOCK, window), 0) % BLOCK
-            k_at = base + lax.broadcasted_iota(jnp.int32, (group * BLOCK, window), 1)
-            visible = (k_at >= start) & (k_at <= q_at)
             rows_q = jnp.concatenate(
                 [
                     query_ref[pl.ds(row, BLOCK), wide + g * HEAD_WIDTH : wide + (g + 1) * HEAD_WIDTH]
@@ -112,11 +111,9 @@
                 ],
                 axis=0,
             )
-            old_k = pages_ref[old, :, at : at + HEAD_WIDTH].reshape(HITS * PAGE, HEAD_WIDTH)
-            new_k = cache_ref[new, at : at + HEAD_WIDTH]
-            old_s = lax.dot_general(rows_q, old_k, dims, preferred_element_type=jnp.float32)
-            new_s = lax.dot_general(rows_q, new_k, dims, preferred_element_type=jnp.float32)
-            scores.append((old_s, jnp.where(visible, new_s, NEGATIVE)))
+            keys = cache_ref[request, :, at : at + HEAD_WIDTH]
+            score = lax.dot_general(rows_q, keys, dims, preferred_element_type=jnp.float32)
+            scores.append((score[:, :held], jnp.where(ahead <= row - start, score[:, held:], NEGATIVE)))
         weights = []
         for old_s, new_s in scores:
             top = jnp.maximum(
@@ -125,18 +122,15 @@
             old_e = jnp.exp2((old_s - top) * sharp)
             new_e = jnp.exp2((new_s - top) * sharp)
             total = jnp.sum(old_e, axis=1, keepdims=True) + jnp.sum(new_e, axis=1, keepdims=True)
-            weights.append((old_e.astype(jnp.bfloat16), new_e.astype(jnp.bfloat16), total))
+            weights.append((jnp.concatenate([old_e, new_e], axis=1).astype(jnp.bfloat16), total))
         results = []
-        for ((_, new, old, _, _, _), head), (old_e, new_e, total) in zip(chains, weights):
+        for ((request, _, _, _), head), (weight, total) in zip(chains, weights):
             at = head * 2 * HEAD_WIDTH + HEAD_WIDTH
-            old_v = pages_ref[old, :, at : at + HEAD_WIDTH].reshape(HITS * PAGE, HEAD_WIDTH)
-            new_v = cache_ref[new, at : at + HEAD_WIDTH]
-            summed = jnp.dot(old_e, old_v, preferred_element_type=jnp.float32)
-            summed += jnp.dot(new_e, new_v, preferred_element_type=jnp.float32)
+            values = cache_ref[request, :, at : at + HEAD_WIDTH]
+            summed = jnp.dot(weight, values, preferred_element_type=jnp.float32)
             results.append((summed / total).astype(jnp.bfloat16))
-        for ((row, _, _, _, start, end), head), result in zip(chains, results):
-            own_at = row + lax.broadcasted_iota(jnp.int32, (BLOCK, HEAD_WIDTH), 0)
-            own = (own_at >= start) & (own_at < end)
+        for ((_, row, start, end), head), result in zip(chains, results):
+            own = (own_at >= start - row) & (own_at < end - row)
             for g in range(group):
                 col = (head * group + g) * HEAD_WIDTH
                 cols = slice(col, col + HEAD_WIDTH)
@@ -147,29 +141,32 @@
     lax.fori_loop(0, steps_ref.shape[1] // TOGETHER, several, 0)
 
 
-def attend(query_base, spread, up, cache, pages, starts, ends):
+def attend(query_base, spread, up, fresh, pages, starts, ends):
     rows, q_cols = query_base.shape
-    steps_total = -(-(rows // BLOCK + starts.shape[0] - 1) // TOGETHER) * TOGETHER
+    requests, held, kv_cols = pages.shape
+    steps_total = -(-(rows // BLOCK + requests - 1) // TOGETHER) * TOGETHER
     steps = attention_steps(starts, ends, steps_total)
+    hbm = pl.BlockSpec(memory_space=pltpu.HBM)
     return pl.pallas_call(
         attention_kernel,
         out_shape=jax.ShapeDtypeStruct((rows, q_cols), jnp.bfloat16),
-        in_specs=[pl.BlockSpec(memory_space=pltpu.SMEM)] + [pl.BlockSpec(memory_space=pltpu.HBM)] * 5,
+        in_specs=[pl.BlockSpec(memory_space=pltpu.SMEM), hbm, pl.BlockSpec(memory_space=pl.ANY), hbm, hbm, hbm],
         out_specs=pl.BlockSpec(memory_space=pltpu.VMEM),
         scratch_shapes=[
             pltpu.VMEM((rows, q_cols), jnp.bfloat16),
-            *[pltpu.VMEM(each.shape, each.dtype) for each in (spread, up, query_base, cache, pages)],
+            *[pltpu.VMEM(each.shape, each.dtype) for each in (spread, up, query_base)],
+            pltpu.VMEM((requests, held + MOST, kv_cols), pages.dtype),
             pltpu.SemaphoreType.DMA((3,)),
             pltpu.SemaphoreType.DMA((2, q_cols // TILE)),
         ],
         compiler_params=pltpu.CompilerParams(vmem_limit_bytes=VMEM_GRANT),
         cost_estimate=pl.CostEstimate(
-            flops=4 * steps_total * BLOCK * q_cols * (HITS * PAGE + MOST + BLOCK) + 2 * spread.size * q_cols,
-            bytes_accessed=4 * query_base.size + 2 * (2 * spread.size + up.size + cache.size + pages.size),
+            flops=4 * steps_total * BLOCK * q_cols * (held + MOST) + 2 * spread.size * q_cols,
+            bytes_accessed=4 * query_base.size + 2 * (2 * spread.size + up.size + fresh.size + pages.size),
             transcendentals=0,
         ),
         name="attend",
-    )(steps, spread, up, query_base, cache, pages)
+    )(steps, spread, up, query_base, fresh, pages)
 
 
 def serve_kernel(pieces, asked_ref, store_ref, *refs):
@@ -265,8 +262,12 @@
     everyone = lax.all_to_all(
         jnp.broadcast_to(raw[None], (peers, raw.shape[0])), "dp", split_axis=0, concat_axis=0, tiled=True
     )
-    store, down_store, everyone = lax.optimization_barrier((keyvalue_page_store, adapter_down_weight, everyone))
-    mirrored_store = swap(store, half)
+    page = keyvalue_page_store.shape[1]
+    parts = [(0, page // 4), (page // 4, page)]
+    pools = [keyvalue_page_store[:, first:end] for first, end in parts]
+    store, down_store, everyone, pools = lax.optimization_barrier(
+        (keyvalue_page_store, adapter_down_weight, everyone, pools)
+    )
 
     page_cap = max(2, 2 * page_count // peers)
     group = everyone[jnp.arange(half, dtype=jnp.int32) ^ me]
@@ -282,7 +283,8 @@
     page_source = page_owner[:, 0] ^ me
     page_place = jnp.where(page_source % half == 0, page_local_index, earlier_alike(page_owner[:, 0]))
 
-    page = keyvalue_page_store.shape[1]
+    pools[1], near_asked, far_asked = lax.optimization_barrier((pools[1], near_asked, far_asked))
+    mirrored = [swap(pool, half) for pool in pools]
     near_pieces = [(block, 0, page) for block in range(half - 1)]
     near = serve(near_asked[1:], store, near_pieces)
     near = [swap(pages, block + 1) for pages, (block, _, _) in zip(near, near_pieces)]
@@ -293,16 +295,19 @@
     query_base = jnp.dot(piece, query_weight, preferred_element_type=jnp.float32)
     new_cache = jnp.dot(piece, keyvalue_weight, preferred_element_type=jnp.float32).astype(jnp.bfloat16)
 
-    down_rows, mirrored_store, query_base, new_cache, near = lax.optimization_barrier(
-        (down_rows, mirrored_store, query_base, new_cache, near)
+    def far_blocks(part):
+        first, end = parts[part]
+        pages = serve(far_asked[1:], mirrored[part], [(block, 0, end - first) for block in range(half - 1)])
+        return [swap(block, number + 1) for number, block in enumerate(pages)]
+
+    far = [far_blocks(0)]
+    down_rows, mirrored, query_base, new_cache, near, far = lax.optimization_barrier(
+        (down_rows, mirrored, query_base, new_cache, near, far)
     )
     down_sent = lax.all_to_all(down_rows, "dp", split_axis=0, concat_axis=0, tiled=True)
-    far_pieces = near_pieces[:-1] + [(half - 2, 0, page // 2), (half - 2, page // 2, page)]
-    far = list(serve(far_asked[1:], mirrored_store, far_pieces))
-    far[:-1] = [swap(pages, block + 1) for pages, (block, _, _) in zip(far[:-1], far_pieces)]
+    far.append(far_blocks(1))
     up_rows, down_sent, far = lax.optimization_barrier((up_rows, down_sent, far))
     up_sent = lax.all_to_all(up_rows, "dp", split_axis=0, concat_axis=0, tiled=True)
-    far[-1] = swap(far[-1], half - 1)
 
     lengths = span_token_length[0]
     ends = jnp.cumsum(lengths)
@@ -316,13 +321,19 @@
     shrink_part = jnp.sum(jnp.where(in_slot[:, :, None], down_part, 0.0), axis=1)
     shrink = lax.psum(shrink_part, "tensor").astype(jnp.bfloat16)
     spread = jnp.where(in_slot[:, :, None], shrink[:, None, :], 0).reshape(tok_rows, adapter_slots * rank)
-    pieces = [(0, 0, page)]
-    pieces += [(block + 1, first, end) for block, first, end in near_pieces]
-    pieces += [(half, 0, page)]
-    pieces += [(half + block + 1, first, end) for block, first, end in far_pieces]
-    prefix_pages = assemble(page_source, page_place, [store, *near, mirrored_store, *far], pieces)
+    pieces = [(0, 0, page)] + [(block + 1, first, end) for block, first, end in near_pieces]
+    arrays = [store, *near]
+    for part, (first, end) in enumerate(parts):
+        pieces += [(half + block, first, end) for block in range(half)]
+        arrays += [mirrored[part], *far[part]]
+    prefix_pages = assemble(page_source, page_place, arrays, pieces).reshape(request_count, HITS * page, -1)
+
+    place = starts[:, None] + jnp.arange(MOST, dtype=jnp.int32)[None, :]
+    pick = (place.reshape(-1, 1) == jnp.arange(tok_rows, dtype=jnp.int32)[None, :]).astype(jnp.bfloat16)
+    fresh = jnp.dot(pick, new_cache, preferred_element_type=jnp.float32).astype(jnp.bfloat16)
+    fresh = fresh.reshape(request_count, MOST, -1)
     up = up_sent.reshape(adapter_slots * rank, q_cols)
-    out = attend(query_base, spread, up, new_cache, prefix_pages, starts, ends)
+    out = attend(query_base, spread, up, fresh, prefix_pages, starts, ends)
     return (out, new_cache)
 
 

time: 356 us -> 358 us (level)
  waiting for transfers between devices: 212 us -> 204 us
  local copies, waits for them, and re-layouts: 19.5 us -> 24.9 us
    all_gather x1, waiting for transfers between devices: 28.6 us -> 0.01 us  [on_device(): piece = lax.all_gather(tokens, 'tensor', axis=1, tiled=True)]
    all_to_all x1, waiting for transfers between devices: 0.01 us -> 19.9 us  [on_device(): lax.all_to_all(up_rows, 'dp', split_axis=0, concat_axis=0, tiled=True)]
    ppermute x8 -> x11, waiting for transfers between devices: 176 us -> 180 us  [swap(): lax.ppermute(array, 'dp', [(peer, peer ^ distance) for peer in range(peer...]
    all_to_all x1, waiting for transfers between devices: 6.46 us -> 2.71 us  [on_device(): lax.all_to_all(jnp.broadcast_to(raw[None], (peers, raw.shape[0])), 'dp',...]
    slice x1 -> x3, local copies, waits for them, and re-layouts: 0.01 us -> 3.75 us  [the longest x2 3.75 us: on_device(): pools = [keyvalue_page_store[:, first:end] for first, end in parts]]
    ppermute x8 -> x11, starting transfers between devices: 10.7 us -> 14.1 us  [swap(): lax.ppermute(array, 'dp', [(peer, peer ^ distance) for peer in range(peer...]
    pallas_call x2 -> x3, Pallas kernels: 12.9 us -> 15.4 us  [serve(): pl.pallas_call(functools.partial(serve_kernel, pieces), out_shape=[jax.Sh...]
  transfers between devices with their start and end apart: 12 -> 15, of which waited for: 7 -> 8; matrix products, arithmetic and copies ran while one was open for 14% -> 16% of each run, Pallas kernels for 5% -> 6%
where the time goes in v12:
time: 358 us; the launch traced here: 357 us
  waiting for transfers between devices  204 us (57%)
  Pallas kernels  33.6 us (9%)
  matrix products  33 us (9%)
  starting transfers between devices  29.8 us (8%)
  local copies, waits for them, and re-layouts  24.9 us (7%)
  between operations  15 us (4%)
  blocking collectives  12.5 us (3%)
  other arithmetic  4.36 us (1%)
    ppermute x11, waiting for transfers between devices, swap(): lax.ppermute(array, 'dp', [(peer, peer ^ distance) for peer in range(peer...  180 us
    all_to_all x1, waiting for transfers between devices, on_device(): lax.all_to_all(up_rows, 'dp', split_axis=0, concat_axis=0, tiled=True)  19.9 us
    dot_general x1, matrix products, on_device(): jnp.dot(piece, query_weight, preferred_element_type=jnp.float32)  18.2 us
    pallas_call x3, Pallas kernels, serve(): pl.pallas_call(functools.partial(serve_kernel, pieces), out_shape=[jax.Sh...  15.4 us
    ppermute x11, starting transfers between devices, swap(): lax.ppermute(array, 'dp', [(peer, peer ^ distance) for peer in range(peer...  14.1 us
    pallas_call x1, Pallas kernels, attend(): pl.pallas_call(attention_kernel, out_shape=jax.ShapeDtypeStruct((rows, q_...  13.3 us
    psum x1, blocking collectives, on_device(): shrink = lax.psum(shrink_part, 'tensor').astype(jnp.bfloat16)  12.5 us
    dot_general x1, matrix products, on_device(): jnp.dot(piece, keyvalue_weight, preferred_element_type=jnp.float32)  7.7 us
  transfers between devices with their start and end apart: 15, of which 8 were waited for; matrix products, arithmetic and copies ran while one was open for 16% of the time, Pallas kernels for 6%

profile of v12, /device:TPU:0, one launch (start us, length us, event | category | flops | bytes accessed | tf_op | source)
XLA Modules:
  0.0 357.1 jit_solution(9634924802369386442)
XLA Ops:
  7.2 0.7 all-gather.2.cloned.1.call-update
  7.9 1.0 pad_add_fusion.1
  8.9 0.6 broadcast_in_dim.175
  9.5 7.3 %all-to-all-start = ((s32[8,1,160]{2,1,0:T(1,128)}), s32[8,1,160]{2,1,0:T(1,128)S(1)}, u32[]{:S(2)}, u32[]{:S(2)}) async-start(s32[8,1,160]{2,1,0:T(1,128)} %broadcast_in_dim.175), calls=%async_computation | async-start | bytes 16384 | tf_op jit(solution)/shard_map/all_to_all | solution.py:262
  16.8 2.1 slice.30
  18.9 1.7 slice.31
  20.6 2.7 all-to-all-done
  25.6 2.4 collective-permute-start.1
  28.0 0.6 reshape.391.asked_ref
  28.6 5.7 %serve.3 = (bf16[16,64,512]{2,1,0:T(8,128)(2,1)}, bf16[16,64,512]{2,1,0:T(8,128)(2,1)}, bf16[16,64,512]{2,1,0:T(8,128)(2,1)}) custom-call(s32[48]{0:T(128)} %reshape.391.asked_ref, bf16[48,64,512]{2,1,0:T(8,128)(2,1)} %refs_0_), custom_call_target="tpu_custom_call" | custom-call | bytes 6291456 | tf_op jit(solution)/shard_map/serve/pallas_call | solution.py:186
  34.4 1.2 collective-permute-start.3
  35.6 2.3 collective-permute-start.4
  37.9 0.6 reshape.392.asked_ref
  38.6 6.2 %gather_fusion.1 = bf16[16,2048,64]{1,2,0:T(8,128)(2,1)} fusion(bf16[32,2048,64]{1,2,0:T(8,128)(2,1)} %param.14, s32[1024]{0:T(1024)S(1)} %pad_clamp_fusion.1), kind=kCustom, calls=%fused_computation.1 | custom fusion | bytes 8388672 | tf_op jit(solution)/shard_map/gather | solution.py:291
  44.8 64.9 %collective-permute-done.store_ref.refs_4_ = bf16[48,16,512]{2,1,0:T(8,128)(2,1)S(1)} collective-permute-done((bf16[48,16,512]{2,1,0:T(8,128)(2,1)}, bf16[48,16,512]{2,1,0:T(8,128)(2,1)S(1)}, u32[]{:S(2)}, u32[]{:S(2)}) %collective-permute-start) | collective-permute-done | bytes 786464 | tf_op jit(solution)/shard_map/ppermute | solution.py:257
  109.7 0.9 copy-done.3
  110.6 3.5 serve.4
  114.1 0.9 collective-permute-start.5
  115.1 18.2 %fusion.26.base_hbm = f32[512,1024]{1,0:T(8,128)} fusion(bf16[512,8192]{1,0:T(8,128)(2,1)} %all-gather.2.cloned.1.call-done, bf16[8192,1024]{1,0:T(8,128)(2,1)} %param.12), kind=kOutput, calls=%fused_computation.94 | convolution fusion | flops 8589934592 | bytes 27262976 | tf_op jit(solution)/shard_map/dot_general | solution.py:295
  133.4 2.6 collective-permute-start.7
  136.0 7.7 %convolution_convert_fusion = bf16[512,512]{1,0:T(8,128)(2,1)} fusion(bf16[512,8192]{1,0:T(8,128)(2,1)S(1)} %copy-done.15, bf16[8192,512]{1,0:T(8,128)(2,1)} %param.13), kind=kOutput, calls=%fused_computation.11 | convolution fusion | flops 4295229440 | bytes 17301504 | tf_op jit(solution)/shard_map/dot_general | solution.py:296
  143.7 22.2 %collective-permute-done.6.refs_6_ = bf16[16,16,512]{2,1,0:T(8,128)(2,1)S(1)} collective-permute-done((bf16[16,16,512]{2,1,0:T(8,128)(2,1)S(1)}, bf16[16,16,512]{2,1,0:T(8,128)(2,1)S(1)}, u32[]{:S(2)}, u32[]{:S(2)}) %collective-permute-start.6) | collective-permute-done | bytes 262176 | tf_op jit(solution)/shard_map/ppermute | solution.py:257
  165.9 0.7 copy-done.9
  166.6 4.8 %collective-permute-done.7.refs_7_ = bf16[16,16,512]{2,1,0:T(8,128)(2,1)S(1)} collective-permute-done((bf16[16,16,512]{2,1,0:T(8,128)(2,1)S(1)}, bf16[16,16,512]{2,1,0:T(8,128)(2,1)S(1)}, u32[]{:S(2)}, u32[]{:S(2)}) %collective-permute-start.7) | collective-permute-done | bytes 262176 | tf_op jit(solution)/shard_map/ppermute | solution.py:257
  171.4 0.7 copy-done.10
  172.1 1.4 copy-done.1
  173.5 4.5 %all-to-all-start.1 = ((bf16[16,2048,64]{1,2,0:T(8,128)(2,1)}), bf16[16,2048,64]{1,2,0:T(8,128)(2,1)}, u32[]{:S(2)}, u32[]{:S(2)}) async-start(bf16[16,2048,64]{1,2,0:T(8,128)(2,1)} %gather_fusion.1), calls=%async_computation.1 | async-start | bytes 8388608 | tf_op jit(solution)/shard_map/all_to_all | solution.py:307
  178.1 6.2 %serve.5 = (bf16[16,48,512]{2,1,0:T(8,128)(2,1)}, bf16[16,48,512]{2,1,0:T(8,128)(2,1)}, bf16[16,48,512]{2,1,0:T(8,128)(2,1)}) custom-call(s32[48]{0:T(128)} %reshape.392.asked_ref, bf16[48,48,512]{2,1,0:T(8,128)(2,1)} %copy-done.1), custom_call_target="tpu_custom_call" | custom-call | bytes 4718592 | tf_op jit(solution)/shard_map/serve/pallas_call | solution.py:186
  184.3 1.1 collective-permute-start.8
  185.4 1.8 collective-permute-start.9
  187.3 1.1 collective-permute-start.10
  188.7 0.6 slice.44
  190.0 4.3 %gather_fusion = bf16[16,64,1024]{2,1,0:T(8,128)(2,1)} fusion(bf16[32,64,1024]{2,1,0:T(8,128)(2,1)} %param.15, s32[1024]{0:T(1024)S(1)} %pad_clamp_fusion.1), kind=kCustom, calls=%fused_computation | custom fusion | bytes 4194368 | tf_op jit(solution)/shard_map/gather | solution.py:292
  194.3 48.3 %collective-permute-done.8.refs_9_ = bf16[16,48,512]{2,1,0:T(8,128)(2,1)S(1)} collective-permute-done((bf16[16,48,512]{2,1,0:T(8,128)(2,1)}, bf16[16,48,512]{2,1,0:T(8,128)(2,1)S(1)}, u32[]{:S(2)}, u32[]{:S(2)}) %collective-permute-start.8) | collective-permute-done | bytes 786464 | tf_op jit(solution)/shard_map/ppermute | solution.py:257
  242.6 22.3 %collective-permute-done.9.refs_10_ = bf16[16,48,512]{2,1,0:T(8,128)(2,1)S(1)} collective-permute-done((bf16[16,48,512]{2,1,0:T(8,128)(2,1)}, bf16[16,48,512]{2,1,0:T(8,128)(2,1)S(1)}, u32[]{:S(2)}, u32[]{:S(2)}) %collective-permute-start.9) | collective-permute-done | bytes 786464 | tf_op jit(solution)/shard_map/ppermute | solution.py:257
  264.9 17.9 %collective-permute-done.10.refs_11_ = bf16[16,48,512]{2,1,0:T(8,128)(2,1)S(1)} collective-permute-done((bf16[16,48,512]{2,1,0:T(8,128)(2,1)}, bf16[16,48,512]{2,1,0:T(8,128)(2,1)S(1)}, u32[]{:S(2)}, u32[]{:S(2)}) %collective-permute-start.10) | collective-permute-done | bytes 786464 | tf_op jit(solution)/shard_map/ppermute | solution.py:257
  282.9 0.9 copy-done.7
  283.7 3.8 %all-to-all-start.2 = ((bf16[16,64,1024]{2,1,0:T(8,128)(2,1)}), bf16[16,64,1024]{2,1,0:T(8,128)(2,1)S(1)}, u32[]{:S(2)}, u32[]{:S(2)}) async-start(bf16[16,64,1024]{2,1,0:T(8,128)(2,1)} %gather_fusion), calls=%async_computation.2 | async-start | bytes 4194304 | tf_op jit(solution)/shard_map/all_to_all | solution.py:310
  287.8 0.6 pad_add_fusion.steps_ref
  288.9 0.6 compare_select_fusion.4
  289.6 2.6 fusion.1
  292.1 4.6 %fusion.2 = f32[512,64]{0,1:T(8,128)S(1)} fusion(bf16[16,2048,64]{1,2,0:T(8,128)(2,1)} %all-to-all-done.1, bf16[512,2048]{1,0:T(8,128)(2,1)S(1)} %copy-done.4, pred[512,16]{0,1:T(8,128)(4,1)S(1)} %iota_compare_fusion.6), kind=kOutput, calls=%fused_computation.7 | convolution fusion | flops 2148499456 | bytes 6430720 | tf_op jit(solution)/shard_map/tn,snk->tsk/dot_general | solution.py:320
  296.7 12.5 %all-reduce.1 = bf16[512,64]{0,1:T(8,128)(2,1)S(1)} all-reduce(f32[512,64]{0,1:T(8,128)S(1)} %fusion.2), channel_id=1, replica_groups=mesh['dp'=8,'tensor'=4] {'tensor'}, use_global_device_ids=true, to_apply=%region_15.16 | all-reduce | flops 32768 | bytes 196608 | tf_op jit(solution)/shard_map/psum | solution.py:322
  309.3 1.4 copy.37.spread_hbm
  310.7 5.0 %assemble.1 = bf16[64,64,512]{2,1,0:T(8,128)(2,1)} custom-call(s32[64]{0:T(128)} %get-tuple-element.81.source_ref, s32[64]{0:T(128)} %get-tuple-element.80.place_ref, bf16[48,64,512]{2,1,0:T(8,128)(2,1)} %refs_0_, bf16[16,64,512]{2,1,0:T(8,128)(2,1)} %collective-permute-done.2.refs_1_, bf16[16,64,512]{2,1,0:T(8,128)(2,1)} %collective-permute-done.3.refs_2_, ...), custom_call_target="tpu_custom_call" | custom-call | bytes 8388608 | tf_op jit(solution)/shard_map/assemble/pallas_call | solution.py:223
  315.6 19.9 %all-to-all-done.2 = bf16[16,64,1024]{2,1,0:T(8,128)(2,1)S(1)} async-done(((bf16[16,64,1024]{2,1,0:T(8,128)(2,1)}), bf16[16,64,1024]{2,1,0:T(8,128)(2,1)S(1)}, u32[]{:S(2)}, u32[]{:S(2)}) %all-to-all-start.2) | async-done | bytes 2097184 | tf_op jit(solution)/shard_map/all_to_all | solution.py:310
  335.6 1.3 copy-done.2
  336.9 13.3 %attend.1 = bf16[512,1024]{1,0:T(8,128)(2,1)} custom-call(s32[4,32]{1,0:T(4,128)} %pad_add_fusion.steps_ref, bf16[512,1024]{1,0:T(8,128)(2,1)} %copy.37.spread_hbm, bf16[1024,1024]{1,0:T(8,128)(2,1)} %bitcast.64, f32[512,1024]{1,0:T(8,128)} %fusion.26.base_hbm, bf16[16,128,512]{2,1,0:T(8,128)(2,1)} %bitcast.66, bf16[16,256,512]{2,1,0:T(8,128)(2,1)} %bitcast.63), custom_call_target="tpu_custom_call" | custom-call | flops 2684354560 | bytes 12582912 | tf_op jit(solution)/shard_map/attend/pallas_call | solution.py:150
  (81 shorter events, 4.0 us)
Async XLA Ops:
  7.2 11.7 %copy-start = (bf16[48,64,512]{2,1,0:T(8,128)(2,1)S(1)}, bf16[48,64,512]{2,1,0:T(8,128)(2,1)}, u32[]{:S(2)}) copy-start(bf16[48,64,512]{2,1,0:T(8,128)(2,1)} %refs_0_) | copy-start | bytes 9437188
  7.2 107.9 %all-gather.2.cloned.1.call-start = ((), (), s32[]{:S(2)}) async-start(), calls=%async_computation.3 | async-start | bytes 10485760 | tf_op jit(solution)/shard_map/all_gather | solution.py:294
  9.5 13.8 %all-to-all-start = ((s32[8,1,160]{2,1,0:T(1,128)}), s32[8,1,160]{2,1,0:T(1,128)S(1)}, u32[]{:S(2)}, u32[]{:S(2)}) async-start(s32[8,1,160]{2,1,0:T(1,128)} %broadcast_in_dim.175), calls=%async_computation | async-start | bytes 16384 | tf_op jit(solution)/shard_map/all_to_all | solution.py:262
  23.3 86.4 %collective-permute-start = (bf16[48,16,512]{2,1,0:T(8,128)(2,1)}, bf16[48,16,512]{2,1,0:T(8,128)(2,1)S(1)}, u32[]{:S(2)}, u32[]{:S(2)}) collective-permute-start(bf16[48,16,512]{2,1,0:T(8,128)(2,1)} %slice.30), channel_id=1, source_target_pairs={{0,16},{4,20},{8,24},{12,28},{16,0},{20,4},{24,8},{28,12},{1,17},{... | collective-permute-start | bytes 2359304 | tf_op jit(solution)/shard_map/ppermute | solution.py:257
  25.6 146.5 %collective-permute-start.1 = (bf16[48,48,512]{2,1,0:T(8,128)(2,1)}, bf16[48,48,512]{2,1,0:T(8,128)(2,1)S(1)}, u32[]{:S(2)}, u32[]{:S(2)}) collective-permute-start(bf16[48,48,512]{2,1,0:T(8,128)(2,1)} %slice.31), channel_id=1, source_target_pairs={{0,16},{4,20},{8,24},{12,28},{16,0},{20,4},{24,8},{28,12},{1,17},{... | collective-permute-start | bytes 7077896 | tf_op jit(solution)/shard_map/ppermute | solution.py:257
  34.3 99.0 %collective-permute-start.2 = (bf16[16,64,512]{2,1,0:T(8,128)(2,1)}, bf16[16,64,512]{2,1,0:T(8,128)(2,1)}, u32[]{:S(2)}, u32[]{:S(2)}) collective-permute-start(bf16[16,64,512]{2,1,0:T(8,128)(2,1)} %get-tuple-element.45), channel_id=1, source_target_pairs={{0,4},{4,0},{8,12},{12,8},{16,20},{20,16},{24,28},{28,24},{1,5},{5... | collective-permute-start | bytes 3145736 | tf_op jit(solution)/shard_map/ppermute | solution.py:257
  34.4 99.0 %collective-permute-start.3 = (bf16[16,64,512]{2,1,0:T(8,128)(2,1)}, bf16[16,64,512]{2,1,0:T(8,128)(2,1)}, u32[]{:S(2)}, u32[]{:S(2)}) collective-permute-start(bf16[16,64,512]{2,1,0:T(8,128)(2,1)} %get-tuple-element.46), channel_id=1, source_target_pairs={{0,8},{4,12},{8,0},{12,4},{16,24},{20,28},{24,16},{28,20},{1,9},{5... | collective-permute-start | bytes 3145736 | tf_op jit(solution)/shard_map/ppermute | solution.py:257
  35.6 108.1 %collective-permute-start.4 = (bf16[16,64,512]{2,1,0:T(8,128)(2,1)}, bf16[16,64,512]{2,1,0:T(8,128)(2,1)}, u32[]{:S(2)}, u32[]{:S(2)}) collective-permute-start(bf16[16,64,512]{2,1,0:T(8,128)(2,1)} %get-tuple-element.47), channel_id=1, source_target_pairs={{0,12},{4,8},{8,4},{12,0},{16,28},{20,24},{24,20},{28,16},{1,13},{... | collective-permute-start | bytes 3145736 | tf_op jit(solution)/shard_map/ppermute | solution.py:257
  109.7 0.9 copy-start.3
  114.1 19.2 %copy-start.17 = (bf16[16,16,512]{2,1,0:T(8,128)(2,1)S(1)}, bf16[16,16,512]{2,1,0:T(8,128)(2,1)}, u32[]{:S(2)}) copy-start(bf16[16,16,512]{2,1,0:T(8,128)(2,1)} %get-tuple-element.50) | copy-start | bytes 786436
  114.1 19.3 %copy-start.16 = (bf16[16,16,512]{2,1,0:T(8,128)(2,1)S(1)}, bf16[16,16,512]{2,1,0:T(8,128)(2,1)}, u32[]{:S(2)}) copy-start(bf16[16,16,512]{2,1,0:T(8,128)(2,1)} %get-tuple-element.51) | copy-start | bytes 786436
  114.1 29.6 %collective-permute-start.5 = (bf16[16,16,512]{2,1,0:T(8,128)(2,1)}, bf16[16,16,512]{2,1,0:T(8,128)(2,1)S(1)}, u32[]{:S(2)}, u32[]{:S(2)}) collective-permute-start(bf16[16,16,512]{2,1,0:T(8,128)(2,1)} %get-tuple-element.49), channel_id=1, source_target_pairs={{0,4},{4,0},{8,12},{12,8},{16,20},{20,16},{24,28},{28,24},{1,5},{5... | collective-permute-start | bytes 786440 | tf_op jit(solution)/shard_map/ppermute | solution.py:257
  115.1 20.9 %copy-start.15 = (bf16[512,8192]{1,0:T(8,128)(2,1)S(1)}, bf16[512,8192]{1,0:T(8,128)(2,1)}, u32[]{:S(2)}) copy-start(bf16[512,8192]{1,0:T(8,128)(2,1)} %all-gather.2.cloned.1.call-done) | copy-start | bytes 25165828
  133.3 32.6 %collective-permute-start.6 = (bf16[16,16,512]{2,1,0:T(8,128)(2,1)S(1)}, bf16[16,16,512]{2,1,0:T(8,128)(2,1)S(1)}, u32[]{:S(2)}, u32[]{:S(2)}) collective-permute-start(bf16[16,16,512]{2,1,0:T(8,128)(2,1)S(1)} %copy-done.17), channel_id=1, source_target_pairs={{0,8},{4,12},{8,0},{12,4},{16,24},{20,28},{24,16},{28,20},{1,9},{5... | collective-permute-start | bytes 786440 | tf_op jit(solution)/shard_map/ppermute | solution.py:257
  133.4 38.0 %collective-permute-start.7 = (bf16[16,16,512]{2,1,0:T(8,128)(2,1)S(1)}, bf16[16,16,512]{2,1,0:T(8,128)(2,1)S(1)}, u32[]{:S(2)}, u32[]{:S(2)}) collective-permute-start(bf16[16,16,512]{2,1,0:T(8,128)(2,1)S(1)} %copy-done.16), channel_id=1, source_target_pairs={{0,12},{4,8},{8,4},{12,0},{16,28},{20,24},{24,20},{28,16},{1,13},{... | collective-permute-start | bytes 786440 | tf_op jit(solution)/shard_map/ppermute | solution.py:257
  143.7 44.7 %copy-start.11 = (s32[1,16]{1,0:T(1,128)S(1)}, s32[1,16]{1,0:T(1,128)}, u32[]{:S(2)}) copy-start(s32[1,16]{1,0:T(1,128)} %param.17) | copy-start | bytes 196
  143.7 28.4 %copy-start.8 = (bf16[16,16,512]{2,1,0:T(8,128)(2,1)}, bf16[16,16,512]{2,1,0:T(8,128)(2,1)S(1)}, u32[]{:S(2)}) copy-start(bf16[16,16,512]{2,1,0:T(8,128)(2,1)S(1)} %collective-permute-done.5.refs_5_) | copy-start | bytes 786436
  165.9 0.7 copy-start.9
  171.4 0.7 copy-start.10
  172.1 1.4 copy-start.1
  173.5 109.3 %all-to-all-start.1 = ((bf16[16,2048,64]{1,2,0:T(8,128)(2,1)}), bf16[16,2048,64]{1,2,0:T(8,128)(2,1)}, u32[]{:S(2)}, u32[]{:S(2)}) async-start(bf16[16,2048,64]{1,2,0:T(8,128)(2,1)} %gather_fusion.1), calls=%async_computation.1 | async-start | bytes 8388608 | tf_op jit(solution)/shard_map/all_to_all | solution.py:307
  184.3 58.3 %collective-permute-start.8 = (bf16[16,48,512]{2,1,0:T(8,128)(2,1)}, bf16[16,48,512]{2,1,0:T(8,128)(2,1)S(1)}, u32[]{:S(2)}, u32[]{:S(2)}) collective-permute-start(bf16[16,48,512]{2,1,0:T(8,128)(2,1)} %get-tuple-element.57), channel_id=1, source_target_pairs={{0,4},{4,0},{8,12},{12,8},{16,20},{20,16},{24,28},{28,24},{1,5},{5... | collective-permute-start | bytes 2359304 | tf_op jit(solution)/shard_map/ppermute | solution.py:257
  185.4 79.5 %collective-permute-start.9 = (bf16[16,48,512]{2,1,0:T(8,128)(2,1)}, bf16[16,48,512]{2,1,0:T(8,128)(2,1)S(1)}, u32[]{:S(2)}, u32[]{:S(2)}) collective-permute-start(bf16[16,48,512]{2,1,0:T(8,128)(2,1)} %get-tuple-element.58), channel_id=1, source_target_pairs={{0,8},{4,12},{8,0},{12,4},{16,24},{20,28},{24,16},{28,20},{1,9},{5... | collective-permute-start | bytes 2359304 | tf_op jit(solution)/shard_map/ppermute | solution.py:257
  187.3 95.6 %collective-permute-start.10 = (bf16[16,48,512]{2,1,0:T(8,128)(2,1)}, bf16[16,48,512]{2,1,0:T(8,128)(2,1)S(1)}, u32[]{:S(2)}, u32[]{:S(2)}) collective-permute-start(bf16[16,48,512]{2,1,0:T(8,128)(2,1)} %get-tuple-element.59), channel_id=1, source_target_pairs={{0,12},{4,8},{8,4},{12,0},{16,28},{20,24},{24,20},{28,16},{1,13},{... | collective-permute-start | bytes 2359304 | tf_op jit(solution)/shard_map/ppermute | solution.py:257
  190.0 98.4 %copy-start.14 = (s32[16,1]{0,1:T(1,128)S(1)}, s32[16,1]{0,1:T(1,128)}, u32[]{:S(2)}) copy-start(s32[16,1]{0,1:T(1,128)} %param.18) | copy-start | bytes 196
  190.0 98.6 %copy-start.13 = (s32[64,1]{0,1:T(1,128)S(1)}, s32[64,1]{0,1:T(1,128)}, u32[]{:S(2)}) copy-start(s32[64,1]{0,1:T(1,128)} %param.20) | copy-start | bytes 772
  190.0 98.9 %copy-start.12 = (s32[64]{0:T(128)S(1)}, s32[64]{0:T(128)}, u32[]{:S(2)}) copy-start(s32[64]{0:T(128)} %param.21) | copy-start | bytes 772
  190.0 99.6 %copy-start.18 = (bf16[512,512]{1,0:T(8,128)(2,1)S(1)}, bf16[512,512]{1,0:T(8,128)(2,1)}, u32[]{:S(2)}) copy-start(bf16[512,512]{1,0:T(8,128)(2,1)} %convolution_convert_fusion) | copy-start | bytes 1572868
  242.6 40.3 %copy-start.5 = (bf16[16,48,512]{2,1,0:T(8,128)(2,1)}, bf16[16,48,512]{2,1,0:T(8,128)(2,1)S(1)}, u32[]{:S(2)}) copy-start(bf16[16,48,512]{2,1,0:T(8,128)(2,1)S(1)} %collective-permute-done.8.refs_9_) | copy-start | bytes 2359300
  264.9 18.0 %copy-start.6 = (bf16[16,48,512]{2,1,0:T(8,128)(2,1)}, bf16[16,48,512]{2,1,0:T(8,128)(2,1)S(1)}, u32[]{:S(2)}) copy-start(bf16[16,48,512]{2,1,0:T(8,128)(2,1)S(1)} %collective-permute-done.9.refs_10_) | copy-start | bytes 2359300
  282.9 0.9 copy-start.7
  283.7 51.8 %all-to-all-start.2 = ((bf16[16,64,1024]{2,1,0:T(8,128)(2,1)}), bf16[16,64,1024]{2,1,0:T(8,128)(2,1)S(1)}, u32[]{:S(2)}, u32[]{:S(2)}) async-start(bf16[16,64,1024]{2,1,0:T(8,128)(2,1)} %gather_fusion), calls=%async_computation.2 | async-start | bytes 4194304 | tf_op jit(solution)/shard_map/all_to_all | solution.py:310
  287.5 4.6 %copy-start.4 = (bf16[512,2048]{1,0:T(8,128)(2,1)S(1)}, bf16[512,2048]{1,0:T(8,128)(2,1)}, u32[]{:S(2)}) copy-start(bf16[512,2048]{1,0:T(8,128)(2,1)} %param.11) | copy-start | bytes 6291460
  335.6 1.3 copy-start.2
Sparse Core Ops, SparseCore 0:
  9.6 60.9 all-gather.1

commit v13 on v9

--- a/solution.py
+++ b/solution.py
@@ -1,3 +1,4 @@
+import functools
 import math
 
 import jax
@@ -9,7 +10,6 @@
 
 HEAD_WIDTH = 128
 ADP_CAP = 2
-PAGE = 64
 HITS = 4
 MOST = 128
 BLOCK = 32
@@ -49,30 +49,48 @@
     return jnp.stack([request, block, at(starts), at(ends)])
 
 
-def attention_kernel(steps_ref, spread_hbm, up_hbm, base_hbm, cache_hbm, pages_hbm, out_ref, query_ref, *rest):
-    spread_ref, up_ref, base_ref, cache_ref, pages_ref, sems, tile_sems = rest
+def attention_kernel(
+    last, steps_ref, source_ref, place_ref, spread_hbm, up_any, base_hbm, fresh_hbm, pages_hbm, last_hbm, *rest
+):
+    out_ref, query_ref, spread_ref, up_ref, base_ref, cache_ref, sems, tile_sems = rest
+    q_cols = base_ref.shape[1]
+    kv_heads = cache_ref.shape[2] // (2 * HEAD_WIDTH)
+    group = q_cols // HEAD_WIDTH // kv_heads
+    page = pages_hbm.shape[1]
+    held = HITS * page
+    sharp = HEAD_WIDTH ** -0.5 * math.log2(math.e)
 
     def tile_copies(index):
         cols = pl.ds(pl.multiple_of(index * TILE, TILE), TILE)
         return (
-            pltpu.make_async_copy(up_hbm.at[:, cols], up_ref.at[:, cols], tile_sems.at[0, index]),
+            pltpu.make_async_copy(up_any.at[:, cols], up_ref.at[:, cols], tile_sems.at[0, index]),
             pltpu.make_async_copy(base_hbm.at[:, cols], base_ref.at[:, cols], tile_sems.at[1, index]),
         )
 
-    pairs = [(spread_hbm, spread_ref), (cache_hbm, cache_ref), (pages_hbm, pages_ref)]
-    copies = [pltpu.make_async_copy(*pair, sems.at[index]) for index, pair in enumerate(pairs)]
-    copies[0].start()
-    for index in range(base_ref.shape[1] // TILE):
+    def fetch(index, carry):
+        rows = pl.ds(pl.multiple_of(index % HITS * page, page), page)
+        to = cache_ref.at[index // HITS, rows]
+        late = source_ref[index] == last
+
+        @pl.when(late)
+        def _():
+            pltpu.make_async_copy(last_hbm.at[place_ref[index]], to, sems.at[1]).start()
+
+        @pl.when(jnp.logical_not(late))
+        def _():
+            pltpu.make_async_copy(pages_hbm.at[index], to, sems.at[1]).start()
+
+        return carry
+
+    spread_copy = pltpu.make_async_copy(spread_hbm, spread_ref, sems.at[0])
+    fresh_copy = pltpu.make_async_copy(fresh_hbm, cache_ref.at[:, held:], sems.at[2])
+    spread_copy.start()
+    for index in range(q_cols // TILE):
         for copy in tile_copies(index):
             copy.start()
-    for copy in copies[1:]:
-        copy.start()
-    rows_total, q_cols = base_ref.shape
-    kv_heads = cache_ref.shape[1] // (2 * HEAD_WIDTH)
-    group = q_cols // HEAD_WIDTH // kv_heads
-    window = min(rows_total, MOST + BLOCK)
-    sharp = HEAD_WIDTH ** -0.5 * math.log2(math.e)
-    copies[0].wait()
+    fresh_copy.start()
+    lax.fori_loop(0, pages_hbm.shape[0], fetch, 0)
+    spread_copy.wait()
 
     def project(index, carry):
         for copy in tile_copies(index):
@@ -83,27 +101,25 @@
         return carry
 
     lax.fori_loop(0, q_cols // TILE, project, 0)
-    for copy in copies[1:]:
-        copy.wait()
+    fresh_copy.wait()
+    prefix = cache_ref.at[:, :held]
+    pltpu.make_async_copy(prefix, prefix, sems.at[1]).wait()
     dims = (((1,), (1,)), ((), ()))
+    q_at = lax.broadcasted_iota(jnp.int32, (group * BLOCK, MOST), 0) % BLOCK
+    ahead = lax.broadcasted_iota(jnp.int32, (group * BLOCK, MOST), 1) - q_at
+    own_at = lax.broadcasted_iota(jnp.int32, (BLOCK, HEAD_WIDTH), 0)
 
     def several(turn, carry):
         places = []
         for lane in range(TOGETHER):
             index = turn * TOGETHER + lane
             row = pl.multiple_of(steps_ref[1, index] * BLOCK, BLOCK)
-            start = steps_ref[2, index]
-            base = pl.multiple_of(jnp.minimum(start // BLOCK * BLOCK, rows_total - window), BLOCK)
-            old = pl.ds(steps_ref[0, index] * HITS, HITS)
-            places.append((row, pl.ds(base, window), old, base, start, steps_ref[3, index]))
+            places.append((steps_ref[0, index], row, steps_ref[2, index], steps_ref[3, index]))
         chains = [(place, head) for place in places for head in range(kv_heads)]
         scores = []
-        for (row, new, old, base, start, _), head in chains:
+        for (request, row, start, _), head in chains:
             at = head * 2 * HEAD_WIDTH
             wide = head * group * HEAD_WIDTH
-            q_at = row + lax.broadcasted_iota(jnp.int32, (group * BLOCK, window), 0) % BLOCK
-            k_at = base + lax.broadcasted_iota(jnp.int32, (group * BLOCK, window), 1)
-            visible = (k_at >= start) & (k_at <= q_at)
             rows_q = jnp.concatenate(
                 [
                     query_ref[pl.ds(row, BLOCK), wide + g * HEAD_WIDTH : wide + (g + 1) * HEAD_WIDTH]
@@ -111,11 +127,9 @@
                 ],
                 axis=0,
             )
-            old_k = pages_ref[old, :, at : at + HEAD_WIDTH].reshape(HITS * PAGE, HEAD_WIDTH)
-            new_k = cache_ref[new, at : at + HEAD_WIDTH]
-            old_s = lax.dot_general(rows_q, old_k, dims, preferred_element_type=jnp.float32)
-            new_s = lax.dot_general(rows_q, new_k, dims, preferred_element_type=jnp.float32)
-            scores.append((old_s, jnp.where(visible, new_s, NEGATIVE)))
+            keys = cache_ref[request, :, at : at + HEAD_WIDTH]
+            score = lax.dot_general(rows_q, keys, dims, preferred_element_type=jnp.float32)
+            scores.append((score[:, :held], jnp.where(ahead <= row - start, score[:, held:], NEGATIVE)))
         weights = []
         for old_s, new_s in scores:
             top = jnp.maximum(
@@ -124,18 +138,15 @@
             old_e = jnp.exp2((old_s - top) * sharp)
             new_e = jnp.exp2((new_s - top) * sharp)
             total = jnp.sum(old_e, axis=1, keepdims=True) + jnp.sum(new_e, axis=1, keepdims=True)
-            weights.append((old_e.astype(jnp.bfloat16), new_e.astype(jnp.bfloat16), total))
+            weights.append((jnp.concatenate([old_e, new_e], axis=1).astype(jnp.bfloat16), total))
         results = []
-        for ((_, new, old, _, _, _), head), (old_e, new_e, total) in zip(chains, weights):
+        for ((request, _, _, _), head), (weight, total) in zip(chains, weights):
             at = head * 2 * HEAD_WIDTH + HEAD_WIDTH
-            old_v = pages_ref[old, :, at : at + HEAD_WIDTH].reshape(HITS * PAGE, HEAD_WIDTH)
-            new_v = cache_ref[new, at : at + HEAD_WIDTH]
-            summed = jnp.dot(old_e, old_v, preferred_element_type=jnp.float32)
-            summed += jnp.dot(new_e, new_v, preferred_element_type=jnp.float32)
+            values = cache_ref[request, :, at : at + HEAD_WIDTH]
+            summed = jnp.dot(weight, values, preferred_element_type=jnp.float32)
             results.append((summed / total).astype(jnp.bfloat16))
-        for ((row, _, _, _, start, end), head), result in zip(chains, results):
-            own_at = row + lax.broadcasted_iota(jnp.int32, (BLOCK, HEAD_WIDTH), 0)
-            own = (own_at >= start) & (own_at < end)
+        for ((_, row, start, end), head), result in zip(chains, results):
+            own = (own_at >= start - row) & (own_at < end - row)
             for g in range(group):
                 col = (head * group + g) * HEAD_WIDTH
                 cols = slice(col, col + HEAD_WIDTH)
@@ -146,29 +157,34 @@
     lax.fori_loop(0, steps_ref.shape[1] // TOGETHER, several, 0)
 
 
-def attend(query_base, spread, up, cache, pages, starts, ends):
+def attend(query_base, spread, up, fresh, pages, last_pages, source, place, last, starts, ends):
     rows, q_cols = query_base.shape
-    steps_total = -(-(rows // BLOCK + starts.shape[0] - 1) // TOGETHER) * TOGETHER
+    requests = fresh.shape[0]
+    keys = HITS * pages.shape[1] + MOST
+    steps_total = -(-(rows // BLOCK + requests - 1) // TOGETHER) * TOGETHER
     steps = attention_steps(starts, ends, steps_total)
+    hbm = pl.BlockSpec(memory_space=pltpu.HBM)
+    scalars = pl.BlockSpec(memory_space=pltpu.SMEM)
     return pl.pallas_call(
-        attention_kernel,
+        functools.partial(attention_kernel, last),
         out_shape=jax.ShapeDtypeStruct((rows, q_cols), jnp.bfloat16),
-        in_specs=[pl.BlockSpec(memory_space=pltpu.SMEM)] + [pl.BlockSpec(memory_space=pltpu.HBM)] * 5,
+        in_specs=[scalars] * 3 + [hbm] * 6,
         out_specs=pl.BlockSpec(memory_space=pltpu.VMEM),
         scratch_shapes=[
             pltpu.VMEM((rows, q_cols), jnp.bfloat16),
-            *[pltpu.VMEM(each.shape, each.dtype) for each in (spread, up, query_base, cache, pages)],
+            *[pltpu.VMEM(each.shape, each.dtype) for each in (spread, up, query_base)],
+            pltpu.VMEM((requests, keys, pages.shape[2]), pages.dtype),
             pltpu.SemaphoreType.DMA((3,)),
             pltpu.SemaphoreType.DMA((2, q_cols // TILE)),
         ],
         compiler_params=pltpu.CompilerParams(vmem_limit_bytes=VMEM_GRANT),
         cost_estimate=pl.CostEstimate(
-            flops=4 * steps_total * BLOCK * q_cols * (HITS * PAGE + MOST + BLOCK) + 2 * spread.size * q_cols,
-            bytes_accessed=4 * query_base.size + 2 * (2 * spread.size + up.size + cache.size + pages.size),
+            flops=4 * steps_total * BLOCK * q_cols * keys + 2 * spread.size * q_cols,
+            bytes_accessed=4 * query_base.size + 2 * (2 * spread.size + up.size + fresh.size + pages.size),
             transcendentals=0,
         ),
         name="attend",
-    )(steps, spread, up, query_base, cache, pages)
+    )(steps, source, place, spread, up, query_base, fresh, pages, last_pages)
 
 
 def serve_kernel(asked_ref, store_ref, *refs):
@@ -187,7 +203,7 @@
     return pl.pallas_call(
         serve_kernel,
         out_shape=[jax.ShapeDtypeStruct(shape, store.dtype)] * blocks,
-        in_specs=[pl.BlockSpec(memory_space=pltpu.SMEM), pl.BlockSpec(memory_space=pltpu.HBM)],
+        in_specs=[pl.BlockSpec(memory_space=pltpu.SMEM), pl.BlockSpec(memory_space=pl.ANY)],
         out_specs=[pl.BlockSpec(memory_space=pltpu.VMEM)] * blocks,
         scratch_shapes=[pltpu.SemaphoreType.DMA((blocks,))],
         compiler_params=pltpu.CompilerParams(vmem_limit_bytes=VMEM_GRANT),
@@ -209,6 +225,10 @@
             @pl.when(source == number)
             def _():
                 pltpu.make_async_copy(ref.at[place], out.at[index], sem).start()
+
+        @pl.when(source == len(sources))
+        def _():
+            pltpu.make_async_copy(sources[0].at[0], out.at[index], sem).start()
 
         return carry
 
@@ -278,8 +298,7 @@
     page_source = page_owner[:, 0] ^ me
     page_place = jnp.where(page_source % half == 0, page_local_index, earlier_alike(page_owner[:, 0]))
 
-    near = list(serve(near_asked[1:], store))
-    near = [swap(pages, i + 1) for i, pages in enumerate(near)]
+    near = [swap(pages, i + 1) for i, pages in enumerate(serve(near_asked[1:], store))]
     down_rows = down_store[adapter_asked]
     up_rows = adapter_up_weight[adapter_asked]
 
@@ -309,9 +328,16 @@
     shrink_part = jnp.sum(jnp.where(in_slot[:, :, None], down_part, 0.0), axis=1)
     shrink = lax.psum(shrink_part, "tensor").astype(jnp.bfloat16)
     spread = jnp.where(in_slot[:, :, None], shrink[:, None, :], 0).reshape(tok_rows, adapter_slots * rank)
-    prefix_pages = assemble(page_source, page_place, [store, *near, mirrored_store, *far])
+    prefix_pages = assemble(page_source, page_place, [store, *near, mirrored_store, *far[:-1]])
+
+    taken = starts[:, None] + jnp.arange(MOST, dtype=jnp.int32)[None, :]
+    pick = (taken.reshape(-1, 1) == jnp.arange(tok_rows, dtype=jnp.int32)[None, :]).astype(jnp.bfloat16)
+    fresh = jnp.dot(pick, new_cache, preferred_element_type=jnp.float32).astype(jnp.bfloat16)
+    fresh = fresh.reshape(request_count, MOST, -1)
     up = up_sent.reshape(adapter_slots * rank, q_cols)
-    out = attend(query_base, spread, up, new_cache, prefix_pages, starts, ends)
+    out = attend(
+        query_base, spread, up, fresh, prefix_pages, far[-1], page_source, page_place, peers - 1, starts, ends
+    )
     return (out, new_cache)
 
 

time: 355 us -> 348 us (0.980)
  waiting for transfers between devices: 214 us -> 206 us
    ppermute x7, waiting for transfers between devices: 176 us -> 169 us  [swap(): lax.ppermute(array, 'dp', [(peer, peer ^ distance) for peer in range(peer...]
  transfers between devices with their start and end apart: 11 -> 11, of which waited for: 9 -> 9; matrix products, arithmetic and copies ran while one was open for 14% -> 15% of each run, Pallas kernels for 5% -> 5%
where the time goes in v13:
time: 348 us; the launch traced here: 346 us
  waiting for transfers between devices  206 us (59%)
  matrix products  33.1 us (10%)
  Pallas kernels  30.2 us (9%)
  starting transfers between devices  26.3 us (8%)
  local copies, waits for them, and re-layouts  18.2 us (5%)
  between operations  14.9 us (4%)
  blocking collectives  12.2 us (4%)
  other arithmetic  4.07 us (1%)
    ppermute x7, waiting for transfers between devices, swap(): lax.ppermute(array, 'dp', [(peer, peer ^ distance) for peer in range(peer...  169 us
    all_gather x1, waiting for transfers between devices, on_device(): piece = lax.all_gather(tokens, 'tensor', axis=1, tiled=True)  28.6 us
    dot_general x1, matrix products, on_device(): jnp.dot(piece, query_weight, preferred_element_type=jnp.float32)  18.3 us
    pallas_call x1, Pallas kernels, attend(): pl.pallas_call(functools.partial(attention_kernel, last), out_shape=jax.S...  13.3 us
    psum x1, blocking collectives, on_device(): shrink = lax.psum(shrink_part, 'tensor').astype(jnp.bfloat16)  12.2 us
    pallas_call x2, Pallas kernels, serve(): pl.pallas_call(serve_kernel, out_shape=[jax.ShapeDtypeStruct(shape, store...  11.7 us
    ppermute x7, starting transfers between devices, swap(): lax.ppermute(array, 'dp', [(peer, peer ^ distance) for peer in range(peer...  9.83 us
    dot_general x1, matrix products, on_device(): jnp.dot(piece, keyvalue_weight, preferred_element_type=jnp.float32)  7.7 us
  transfers between devices with their start and end apart: 11, of which 9 were waited for; matrix products, arithmetic and copies ran while one was open for 15% of the time, Pallas kernels for 5%

profile of v13, /device:TPU:0, one launch (start us, length us, event | category | flops | bytes accessed | tf_op | source)
XLA Modules:
  0.0 345.5 jit_solution(7019865265932307015)
XLA Ops:
  7.2 0.7 all-gather.2.cloned.1.call-update
  7.9 0.8 pad_add_fusion.1
  8.7 0.6 broadcast_in_dim.175
  9.3 7.3 %all-to-all-start = ((s32[8,1,160]{2,1,0:T(1,128)}), s32[8,1,160]{2,1,0:T(1,128)S(1)}, u32[]{:S(2)}, u32[]{:S(2)}) async-start(s32[8,1,160]{2,1,0:T(1,128)} %broadcast_in_dim.175), calls=%async_computation | async-start | bytes 16384 | tf_op jit(solution)/shard_map/all_to_all | solution.py:281
  16.6 6.5 %all-to-all-done = s32[8,1,160]{2,1,0:T(1,128)S(1)} async-done(((s32[8,1,160]{2,1,0:T(1,128)}), s32[8,1,160]{2,1,0:T(1,128)S(1)}, u32[]{:S(2)}, u32[]{:S(2)}) %all-to-all-start) | async-done | bytes 5152 | tf_op jit(solution)/shard_map/all_to_all | solution.py:281
  23.1 0.3 convert_reduce_fusion.1
  23.4 0.1 select_reduce_fusion.3
  23.7 0.6 collective-permute-start
  24.3 0.6 gather_fusion.2
  24.9 0.2 convert_reduce_fusion
  25.2 0.2 select_reduce_fusion
  25.4 0.6 reshape.387.asked_ref
  26.0 6.1 %serve.2 = (bf16[16,64,512]{2,1,0:T(8,128)(2,1)}, bf16[16,64,512]{2,1,0:T(8,128)(2,1)}, bf16[16,64,512]{2,1,0:T(8,128)(2,1)}) custom-call(s32[48]{0:T(128)} %reshape.387.asked_ref, bf16[48,64,512]{2,1,0:T(8,128)(2,1)} %refs_0_), custom_call_target="tpu_custom_call" | custom-call | bytes 6291456 | tf_op jit(solution)/shard_map/serve/pallas_call | solution.py:203
  32.1 0.3 collective-permute-start.1
  32.4 3.2 collective-permute-start.3
  35.8 6.2 %gather_fusion.1 = bf16[16,2048,64]{1,2,0:T(8,128)(2,1)} fusion(bf16[32,2048,64]{1,2,0:T(8,128)(2,1)} %param.14, s32[1024]{0:T(1024)S(1)} %pad_clamp_fusion.1), kind=kCustom, calls=%fused_computation.1 | custom fusion | bytes 8388672 | tf_op jit(solution)/shard_map/gather | solution.py:302
  42.0 28.6 %all-gather.2.cloned.1.call-done = bf16[512,8192]{1,0:T(8,128)(2,1)} async-done(((bf16[512,2048]{1,0:T(8,128)(2,1)}), bf16[512,8192]{1,0:T(8,128)(2,1)}) %all-gather.2.cloned.1.call-update) | async-done | bytes 8388624 | tf_op jit(solution)/shard_map/all_gather | solution.py:305
  70.6 18.3 %fusion.26.base_hbm = f32[512,1024]{1,0:T(8,128)} fusion(bf16[512,8192]{1,0:T(8,128)(2,1)} %all-gather.2.cloned.1.call-done, bf16[8192,1024]{1,0:T(8,128)(2,1)} %param.12), kind=kOutput, calls=%fused_computation.94 | convolution fusion | flops 8589934592 | bytes 27262976 | tf_op jit(solution)/shard_map/dot_general | solution.py:306
  89.0 7.7 %convolution_convert_fusion = bf16[512,512]{1,0:T(8,128)(2,1)} fusion(bf16[512,8192]{1,0:T(8,128)(2,1)S(1)} %copy-done.9, bf16[8192,512]{1,0:T(8,128)(2,1)} %param.13), kind=kOutput, calls=%fused_computation.11 | convolution fusion | flops 4295229440 | bytes 17301504 | tf_op jit(solution)/shard_map/dot_general | solution.py:307
  96.7 19.0 %collective-permute-done.2.refs_2_ = bf16[16,64,512]{2,1,0:T(8,128)(2,1)} collective-permute-done((bf16[16,64,512]{2,1,0:T(8,128)(2,1)}, bf16[16,64,512]{2,1,0:T(8,128)(2,1)}, u32[]{:S(2)}, u32[]{:S(2)}) %collective-permute-start.2) | collective-permute-done | bytes 1048608 | tf_op jit(solution)/shard_map/ppermute | solution.py:276
  115.6 19.9 %collective-permute-done.3.refs_3_ = bf16[16,64,512]{2,1,0:T(8,128)(2,1)} collective-permute-done((bf16[16,64,512]{2,1,0:T(8,128)(2,1)}, bf16[16,64,512]{2,1,0:T(8,128)(2,1)}, u32[]{:S(2)}, u32[]{:S(2)}) %collective-permute-start.3) | collective-permute-done | bytes 1048608 | tf_op jit(solution)/shard_map/ppermute | solution.py:276
  135.5 25.1 %collective-permute-done.store_ref.refs_4_ = bf16[48,64,512]{2,1,0:T(8,128)(2,1)S(1)} collective-permute-done((bf16[48,64,512]{2,1,0:T(8,128)(2,1)}, bf16[48,64,512]{2,1,0:T(8,128)(2,1)S(1)}, u32[]{:S(2)}, u32[]{:S(2)}) %collective-permute-start) | collective-permute-done | bytes 3145760 | tf_op jit(solution)/shard_map/ppermute | solution.py:276
  160.6 1.7 copy-done
  162.3 4.5 %all-to-all-start.1 = ((bf16[16,2048,64]{1,2,0:T(8,128)(2,1)}), bf16[16,2048,64]{1,2,0:T(8,128)(2,1)}, u32[]{:S(2)}, u32[]{:S(2)}) async-start(bf16[16,2048,64]{1,2,0:T(8,128)(2,1)} %gather_fusion.1), calls=%async_computation.1 | async-start | bytes 8388608 | tf_op jit(solution)/shard_map/all_to_all | solution.py:312
  166.8 0.6 reshape.388.asked_ref
  167.5 5.6 %serve.3 = (bf16[16,64,512]{2,1,0:T(8,128)(2,1)}, bf16[16,64,512]{2,1,0:T(8,128)(2,1)}, bf16[16,64,512]{2,1,0:T(8,128)(2,1)}) custom-call(s32[48]{0:T(128)} %reshape.388.asked_ref, bf16[48,64,512]{2,1,0:T(8,128)(2,1)} %copy-done), custom_call_target="tpu_custom_call" | custom-call | bytes 6291456 | tf_op jit(solution)/shard_map/serve/pallas_call | solution.py:203
  173.1 2.1 collective-permute-start.4
  175.2 0.7 collective-permute-start.5
  176.0 0.1 fusion.24
  176.3 0.6 slice.35
  177.6 4.2 %gather_fusion = bf16[16,64,1024]{2,1,0:T(8,128)(2,1)} fusion(bf16[32,64,1024]{2,1,0:T(8,128)(2,1)} %param.15, s32[1024]{0:T(1024)S(1)} %pad_clamp_fusion.1), kind=kCustom, calls=%fused_computation | custom fusion | bytes 4194368 | tf_op jit(solution)/shard_map/gather | solution.py:303
  181.8 55.1 %collective-permute-done.4.refs_5_ = bf16[16,64,512]{2,1,0:T(8,128)(2,1)S(1)} collective-permute-done((bf16[16,64,512]{2,1,0:T(8,128)(2,1)}, bf16[16,64,512]{2,1,0:T(8,128)(2,1)S(1)}, u32[]{:S(2)}, u32[]{:S(2)}) %collective-permute-start.4) | collective-permute-done | bytes 1048608 | tf_op jit(solution)/shard_map/ppermute | solution.py:276
  236.9 21.7 %collective-permute-done.5.refs_6_ = bf16[16,64,512]{2,1,0:T(8,128)(2,1)S(1)} collective-permute-done((bf16[16,64,512]{2,1,0:T(8,128)(2,1)}, bf16[16,64,512]{2,1,0:T(8,128)(2,1)S(1)}, u32[]{:S(2)}, u32[]{:S(2)}) %collective-permute-start.5) | collective-permute-done | bytes 1048608 | tf_op jit(solution)/shard_map/ppermute | solution.py:276
  258.6 1.8 all-to-all-done.1
  260.5 4.7 %all-to-all-start.2 = ((bf16[16,64,1024]{2,1,0:T(8,128)(2,1)}), bf16[16,64,1024]{2,1,0:T(8,128)(2,1)S(1)}, u32[]{:S(2)}, u32[]{:S(2)}) async-start(bf16[16,64,1024]{2,1,0:T(8,128)(2,1)} %gather_fusion), calls=%async_computation.2 | async-start | bytes 4194304 | tf_op jit(solution)/shard_map/all_to_all | solution.py:316
  265.4 0.6 pad_add_fusion.steps_ref
  266.0 0.2 convert_reduce_fusion.2
  266.2 0.2 convert_reduce_fusion.3
  266.5 0.5 compare_select_fusion.4
  267.1 3.0 collective-permute-start.6
  270.1 2.5 fusion.1
  272.6 4.6 %fusion.2 = f32[512,64]{0,1:T(8,128)S(1)} fusion(bf16[16,2048,64]{1,2,0:T(8,128)(2,1)} %all-to-all-done.1, bf16[512,2048]{1,0:T(8,128)(2,1)S(1)} %copy-done.2, pred[512,16]{0,1:T(8,128)(4,1)S(1)} %iota_compare_fusion.5), kind=kOutput, calls=%fused_computation.7 | convolution fusion | flops 2148499456 | bytes 6430720 | tf_op jit(solution)/shard_map/tn,snk->tsk/dot_general | solution.py:327
  277.1 12.2 %all-reduce.1 = bf16[512,64]{0,1:T(8,128)(2,1)S(1)} all-reduce(f32[512,64]{0,1:T(8,128)S(1)} %fusion.2), channel_id=1, replica_groups=mesh['dp'=8,'tensor'=4] {'tensor'}, use_global_device_ids=true, to_apply=%region_16.17 | all-reduce | flops 32768 | bytes 196608 | tf_op jit(solution)/shard_map/psum | solution.py:329
  289.5 1.3 copy.37.spread_hbm
  290.8 5.2 %assemble.1.pages_hbm = bf16[64,64,512]{2,1,0:T(8,128)(2,1)} custom-call(s32[64]{0:T(128)} %get-tuple-element.51.source_ref, s32[64]{0:T(128)} %get-tuple-element.50.place_ref, bf16[48,64,512]{2,1,0:T(8,128)(2,1)} %refs_0_, bf16[16,64,512]{2,1,0:T(8,128)(2,1)} %collective-permute-done.1.refs_1_, bf16[16,64,512]{2,1,0:T(8,128)(2,1)} %collective-permute-done.2.refs_2_, ...), custom_call_target="tpu_custom_call" | custom-call | bytes 8388608 | tf_op jit(solution)/shard_map/assemble/pallas_call | solution.py:242
  296.0 28.1 %collective-permute-done.6.last_hbm = bf16[16,64,512]{2,1,0:T(8,128)(2,1)} collective-permute-done((bf16[16,64,512]{2,1,0:T(8,128)(2,1)}, bf16[16,64,512]{2,1,0:T(8,128)(2,1)}, u32[]{:S(2)}, u32[]{:S(2)}) %collective-permute-start.6) | collective-permute-done | bytes 1048608 | tf_op jit(solution)/shard_map/ppermute | solution.py:276
  324.0 1.3 copy-done.1
  325.3 13.3 %attend.1 = bf16[512,1024]{1,0:T(8,128)(2,1)} custom-call(s32[4,32]{1,0:T(4,128)} %pad_add_fusion.steps_ref, s32[64]{0:T(128)} %get-tuple-element.51.source_ref, s32[64]{0:T(128)} %get-tuple-element.50.place_ref, bf16[512,1024]{1,0:T(8,128)(2,1)} %copy.37.spread_hbm, bf16[1024,1024]{1,0:T(8,128)(2,1)} %bitcast.62, f32[512,1024]{1,0:T(8,128)} %fusion.26.base_hbm, ...), custom_call_target="tpu_custom_call" | custom-call | flops 2684354560 | bytes 12582912 | tf_op jit(solution)/shard_map/attend/pallas_call | solution.py:168
  (54 shorter events, 1.3 us)
Async XLA Ops:
  7.2 63.5 %all-gather.2.cloned.1.call-start = ((), (), s32[]{:S(2)}) async-start(), calls=%async_computation.3 | async-start | bytes 10485760 | tf_op jit(solution)/shard_map/all_gather | solution.py:305
  9.3 13.8 %all-to-all-start = ((s32[8,1,160]{2,1,0:T(1,128)}), s32[8,1,160]{2,1,0:T(1,128)S(1)}, u32[]{:S(2)}, u32[]{:S(2)}) async-start(s32[8,1,160]{2,1,0:T(1,128)} %broadcast_in_dim.175), calls=%async_computation | async-start | bytes 16384 | tf_op jit(solution)/shard_map/all_to_all | solution.py:281
  23.7 136.9 %collective-permute-start = (bf16[48,64,512]{2,1,0:T(8,128)(2,1)}, bf16[48,64,512]{2,1,0:T(8,128)(2,1)S(1)}, u32[]{:S(2)}, u32[]{:S(2)}) collective-permute-start(bf16[48,64,512]{2,1,0:T(8,128)(2,1)} %refs_0_), channel_id=1, source_target_pairs={{0,16},{4,20},{8,24},{12,28},{16,0},{20,4},{24,8},{28,12},{1,17},{... | collective-permute-start | bytes 9437192 | tf_op jit(solution)/shard_map/ppermute | solution.py:276
  32.1 64.6 %collective-permute-start.1 = (bf16[16,64,512]{2,1,0:T(8,128)(2,1)}, bf16[16,64,512]{2,1,0:T(8,128)(2,1)}, u32[]{:S(2)}, u32[]{:S(2)}) collective-permute-start(bf16[16,64,512]{2,1,0:T(8,128)(2,1)} %get-tuple-element.26), channel_id=1, source_target_pairs={{0,4},{4,0},{8,12},{12,8},{16,20},{20,16},{24,28},{28,24},{1,5},{5... | collective-permute-start | bytes 3145736 | tf_op jit(solution)/shard_map/ppermute | solution.py:276
  32.4 83.2 %collective-permute-start.2 = (bf16[16,64,512]{2,1,0:T(8,128)(2,1)}, bf16[16,64,512]{2,1,0:T(8,128)(2,1)}, u32[]{:S(2)}, u32[]{:S(2)}) collective-permute-start(bf16[16,64,512]{2,1,0:T(8,128)(2,1)} %get-tuple-element.27), channel_id=1, source_target_pairs={{0,8},{4,12},{8,0},{12,4},{16,24},{20,28},{24,16},{28,20},{1,9},{5... | collective-permute-start | bytes 3145736 | tf_op jit(solution)/shard_map/ppermute | solution.py:276
  32.4 103.1 %collective-permute-start.3 = (bf16[16,64,512]{2,1,0:T(8,128)(2,1)}, bf16[16,64,512]{2,1,0:T(8,128)(2,1)}, u32[]{:S(2)}, u32[]{:S(2)}) collective-permute-start(bf16[16,64,512]{2,1,0:T(8,128)(2,1)} %get-tuple-element.28), channel_id=1, source_target_pairs={{0,12},{4,8},{8,4},{12,0},{16,28},{20,24},{24,20},{28,16},{1,13},{... | collective-permute-start | bytes 3145736 | tf_op jit(solution)/shard_map/ppermute | solution.py:276
  70.6 18.3 %copy-start.9 = (bf16[512,8192]{1,0:T(8,128)(2,1)S(1)}, bf16[512,8192]{1,0:T(8,128)(2,1)}, u32[]{:S(2)}) copy-start(bf16[512,8192]{1,0:T(8,128)(2,1)} %all-gather.2.cloned.1.call-done) | copy-start | bytes 25165828
  96.7 79.2 %copy-start.5 = (s32[1,16]{1,0:T(1,128)S(1)}, s32[1,16]{1,0:T(1,128)}, u32[]{:S(2)}) copy-start(s32[1,16]{1,0:T(1,128)} %param.17) | copy-start | bytes 196
  160.6 1.7 copy-start
  162.3 98.2 %all-to-all-start.1 = ((bf16[16,2048,64]{1,2,0:T(8,128)(2,1)}), bf16[16,2048,64]{1,2,0:T(8,128)(2,1)}, u32[]{:S(2)}, u32[]{:S(2)}) async-start(bf16[16,2048,64]{1,2,0:T(8,128)(2,1)} %gather_fusion.1), calls=%async_computation.1 | async-start | bytes 8388608 | tf_op jit(solution)/shard_map/all_to_all | solution.py:312
  173.1 63.8 %collective-permute-start.4 = (bf16[16,64,512]{2,1,0:T(8,128)(2,1)}, bf16[16,64,512]{2,1,0:T(8,128)(2,1)S(1)}, u32[]{:S(2)}, u32[]{:S(2)}) collective-permute-start(bf16[16,64,512]{2,1,0:T(8,128)(2,1)} %get-tuple-element.31), channel_id=1, source_target_pairs={{0,4},{4,0},{8,12},{12,8},{16,20},{20,16},{24,28},{28,24},{1,5},{5... | collective-permute-start | bytes 3145736 | tf_op jit(solution)/shard_map/ppermute | solution.py:276
  175.2 83.4 %collective-permute-start.5 = (bf16[16,64,512]{2,1,0:T(8,128)(2,1)}, bf16[16,64,512]{2,1,0:T(8,128)(2,1)S(1)}, u32[]{:S(2)}, u32[]{:S(2)}) collective-permute-start(bf16[16,64,512]{2,1,0:T(8,128)(2,1)} %get-tuple-element.32), channel_id=1, source_target_pairs={{0,8},{4,12},{8,0},{12,4},{16,24},{20,28},{24,16},{28,20},{1,9},{5... | collective-permute-start | bytes 3145736 | tf_op jit(solution)/shard_map/ppermute | solution.py:276
  177.6 88.4 %copy-start.7 = (s32[64,1]{0,1:T(1,128)S(1)}, s32[64,1]{0,1:T(1,128)}, u32[]{:S(2)}) copy-start(s32[64,1]{0,1:T(1,128)} %param.20) | copy-start | bytes 772
  177.6 88.6 %copy-start.8 = (s32[16,1]{0,1:T(1,128)S(1)}, s32[16,1]{0,1:T(1,128)}, u32[]{:S(2)}) copy-start(s32[16,1]{0,1:T(1,128)} %param.18) | copy-start | bytes 196
  177.6 88.9 %copy-start.6 = (s32[64]{0:T(128)S(1)}, s32[64]{0:T(128)}, u32[]{:S(2)}) copy-start(s32[64]{0:T(128)} %param.21) | copy-start | bytes 772
  177.6 92.5 %copy-start.10 = (bf16[512,512]{1,0:T(8,128)(2,1)S(1)}, bf16[512,512]{1,0:T(8,128)(2,1)}, u32[]{:S(2)}) copy-start(bf16[512,512]{1,0:T(8,128)(2,1)} %convolution_convert_fusion) | copy-start | bytes 1572868
  236.9 23.5 %copy-start.3 = (bf16[16,64,512]{2,1,0:T(8,128)(2,1)}, bf16[16,64,512]{2,1,0:T(8,128)(2,1)S(1)}, u32[]{:S(2)}) copy-start(bf16[16,64,512]{2,1,0:T(8,128)(2,1)S(1)} %collective-permute-done.4.refs_5_) | copy-start | bytes 3145732
  258.6 1.8 copy-start.4
  260.5 63.5 %all-to-all-start.2 = ((bf16[16,64,1024]{2,1,0:T(8,128)(2,1)}), bf16[16,64,1024]{2,1,0:T(8,128)(2,1)S(1)}, u32[]{:S(2)}, u32[]{:S(2)}) async-start(bf16[16,64,1024]{2,1,0:T(8,128)(2,1)} %gather_fusion), calls=%async_computation.2 | async-start | bytes 4194304 | tf_op jit(solution)/shard_map/all_to_all | solution.py:316
  265.1 7.4 %copy-start.2 = (bf16[512,2048]{1,0:T(8,128)(2,1)S(1)}, bf16[512,2048]{1,0:T(8,128)(2,1)}, u32[]{:S(2)}) copy-start(bf16[512,2048]{1,0:T(8,128)(2,1)} %param.11) | copy-start | bytes 6291460
  267.1 56.9 %collective-permute-start.6 = (bf16[16,64,512]{2,1,0:T(8,128)(2,1)}, bf16[16,64,512]{2,1,0:T(8,128)(2,1)}, u32[]{:S(2)}, u32[]{:S(2)}) collective-permute-start(bf16[16,64,512]{2,1,0:T(8,128)(2,1)} %get-tuple-element.43), channel_id=1, source_target_pairs={{0,12},{4,8},{8,4},{12,0},{16,28},{20,24},{24,20},{28,16},{1,13},{... | collective-permute-start | bytes 3145736 | tf_op jit(solution)/shard_map/ppermute | solution.py:276
  324.0 1.3 copy-start.1
Sparse Core Ops, SparseCore 0:
  9.6 61.0 all-gather.1

commit v14 on v13

--- a/solution.py
+++ b/solution.py
@@ -16,6 +16,7 @@
 TOGETHER = 4
 TILE = 256
 VMEM_GRANT = 60 * 1024 * 1024
+SMALL_GRANT = 16 * 1024 * 1024
 
 ADAPTER_SCALE = 0.5
 NEGATIVE = -1e30
@@ -105,9 +106,23 @@
     prefix = cache_ref.at[:, :held]
     pltpu.make_async_copy(prefix, prefix, sems.at[1]).wait()
     dims = (((1,), (1,)), ((), ()))
-    q_at = lax.broadcasted_iota(jnp.int32, (group * BLOCK, MOST), 0) % BLOCK
-    ahead = lax.broadcasted_iota(jnp.int32, (group * BLOCK, MOST), 1) - q_at
+    tall = group * BLOCK
+    q_at = lax.broadcasted_iota(jnp.int32, (kv_heads * tall, MOST), 0) % BLOCK
+    ahead = lax.broadcasted_iota(jnp.int32, (kv_heads * tall, MOST), 1) - q_at
     own_at = lax.broadcasted_iota(jnp.int32, (BLOCK, HEAD_WIDTH), 0)
+    blank = jnp.zeros((tall, HEAD_WIDTH), jnp.bfloat16)
+
+    def side_by_side(request, offset):
+        columns = [(2 * head + offset) * HEAD_WIDTH for head in range(kv_heads)]
+        return jnp.concatenate([cache_ref[request, :, col : col + HEAD_WIDTH] for col in columns], axis=1)
+
+    def queries(row):
+        heads = []
+        for head in range(kv_heads):
+            columns = [(head * group + g) * HEAD_WIDTH for g in range(group)]
+            own = jnp.concatenate([query_ref[pl.ds(row, BLOCK), col : col + HEAD_WIDTH] for col in columns], axis=0)
+            heads.append(jnp.concatenate([own if other == head else blank for other in range(kv_heads)], axis=1))
+        return jnp.concatenate(heads, axis=0)
 
     def several(turn, carry):
         places = []
@@ -115,20 +130,9 @@
             index = turn * TOGETHER + lane
             row = pl.multiple_of(steps_ref[1, index] * BLOCK, BLOCK)
             places.append((steps_ref[0, index], row, steps_ref[2, index], steps_ref[3, index]))
-        chains = [(place, head) for place in places for head in range(kv_heads)]
         scores = []
-        for (request, row, start, _), head in chains:
-            at = head * 2 * HEAD_WIDTH
-            wide = head * group * HEAD_WIDTH
-            rows_q = jnp.concatenate(
-                [
-                    query_ref[pl.ds(row, BLOCK), wide + g * HEAD_WIDTH : wide + (g + 1) * HEAD_WIDTH]
-                    for g in range(group)
-                ],
-                axis=0,
-            )
-            keys = cache_ref[request, :, at : at + HEAD_WIDTH]
-            score = lax.dot_general(rows_q, keys, dims, preferred_element_type=jnp.float32)
+        for request, row, start, _ in places:
+            score = lax.dot_general(queries(row), side_by_side(request, 0), dims, preferred_element_type=jnp.float32)
             scores.append((score[:, :held], jnp.where(ahead <= row - start, score[:, held:], NEGATIVE)))
         weights = []
         for old_s, new_s in scores:
@@ -140,18 +144,20 @@
             total = jnp.sum(old_e, axis=1, keepdims=True) + jnp.sum(new_e, axis=1, keepdims=True)
             weights.append((jnp.concatenate([old_e, new_e], axis=1).astype(jnp.bfloat16), total))
         results = []
-        for ((request, _, _, _), head), (weight, total) in zip(chains, weights):
-            at = head * 2 * HEAD_WIDTH + HEAD_WIDTH
-            values = cache_ref[request, :, at : at + HEAD_WIDTH]
-            summed = jnp.dot(weight, values, preferred_element_type=jnp.float32)
-            results.append((summed / total).astype(jnp.bfloat16))
-        for ((_, row, start, end), head), result in zip(chains, results):
+        for (request, _, _, _), (weight, total) in zip(places, weights):
+            summed = jnp.dot(weight, side_by_side(request, 1), preferred_element_type=jnp.float32)
+            results.append((summed, total))
+        for (_, row, start, end), (summed, total) in zip(places, results):
             own = (own_at >= start - row) & (own_at < end - row)
-            for g in range(group):
-                col = (head * group + g) * HEAD_WIDTH
-                cols = slice(col, col + HEAD_WIDTH)
-                before = out_ref[pl.ds(row, BLOCK), cols]
-                out_ref[pl.ds(row, BLOCK), cols] = jnp.where(own, result[g * BLOCK : (g + 1) * BLOCK], before)
+            for head in range(kv_heads):
+                rows = slice(head * tall, (head + 1) * tall)
+                result = summed[rows, head * HEAD_WIDTH : (head + 1) * HEAD_WIDTH] / total[rows]
+                result = result.astype(jnp.bfloat16)
+                for g in range(group):
+                    col = (head * group + g) * HEAD_WIDTH
+                    cols = slice(col, col + HEAD_WIDTH)
+                    before = out_ref[pl.ds(row, BLOCK), cols]
+                    out_ref[pl.ds(row, BLOCK), cols] = jnp.where(own, result[g * BLOCK : (g + 1) * BLOCK], before)
         return carry
 
     lax.fori_loop(0, steps_ref.shape[1] // TOGETHER, several, 0)
@@ -197,7 +203,7 @@
         pltpu.make_async_copy(out, out, sems.at[index]).wait()
 
 
-def serve(asked, store):
+def serve(asked, store, grant):
     blocks, capacity = asked.shape
     shape = (capacity,) + store.shape[1:]
     return pl.pallas_call(
@@ -206,7 +212,7 @@
         in_specs=[pl.BlockSpec(memory_space=pltpu.SMEM), pl.BlockSpec(memory_space=pl.ANY)],
         out_specs=[pl.BlockSpec(memory_space=pltpu.VMEM)] * blocks,
         scratch_shapes=[pltpu.SemaphoreType.DMA((blocks,))],
-        compiler_params=pltpu.CompilerParams(vmem_limit_bytes=VMEM_GRANT),
+        compiler_params=pltpu.CompilerParams(vmem_limit_bytes=grant),
         cost_estimate=pl.CostEstimate(
             flops=0, bytes_accessed=4 * blocks * math.prod(shape), transcendentals=0
         ),
@@ -298,7 +304,7 @@
     page_source = page_owner[:, 0] ^ me
     page_place = jnp.where(page_source % half == 0, page_local_index, earlier_alike(page_owner[:, 0]))
 
-    near = [swap(pages, i + 1) for i, pages in enumerate(serve(near_asked[1:], store))]
+    near = [swap(pages, i + 1) for i, pages in enumerate(serve(near_asked[1:], store, VMEM_GRANT))]
     down_rows = down_store[adapter_asked]
     up_rows = adapter_up_weight[adapter_asked]
 
@@ -310,7 +316,7 @@
         (down_rows, mirrored_store, query_base, new_cache, near)
     )
     down_sent = lax.all_to_all(down_rows, "dp", split_axis=0, concat_axis=0, tiled=True)
-    far = list(serve(far_asked[1:], mirrored_store))
+    far = list(serve(far_asked[1:], mirrored_store, SMALL_GRANT))
     far = [swap(pages, i + 1) for i, pages in enumerate(far[:-1])] + far[-1:]
     up_rows, down_sent, far = lax.optimization_barrier((up_rows, down_sent, far))
     up_sent = lax.all_to_all(up_rows, "dp", split_axis=0, concat_axis=0, tiled=True)

time: 348 us -> 346 us (level)
  waiting for transfers between devices: 206 us -> 202 us
    ppermute x7, waiting for transfers between devices: 169 us -> 164 us  [swap(): lax.ppermute(array, 'dp', [(peer, peer ^ distance) for peer in range(peer...]
  transfers between devices with their start and end apart: 11 -> 11, of which waited for: 9 -> 9; matrix products, arithmetic and copies ran while one was open for 15% -> 16% of each run, Pallas kernels for 5% -> 5%
where the time goes in v14:
time: 346 us; the launch traced here: 344 us
  waiting for transfers between devices  202 us (58%)
  matrix products  34.1 us (10%)
  Pallas kernels  30.2 us (9%)
  starting transfers between devices  26.9 us (8%)
  local copies, waits for them, and re-layouts  18 us (5%)
  between operations  14.9 us (4%)
  blocking collectives  12.2 us (4%)
  other arithmetic  5.1 us (1%)
    ppermute x7, waiting for transfers between devices, swap(): lax.ppermute(array, 'dp', [(peer, peer ^ distance) for peer in range(peer...  164 us
    all_gather x1, waiting for transfers between devices, on_device(): piece = lax.all_gather(tokens, 'tensor', axis=1, tiled=True)  28.9 us
    dot_general x1, matrix products, on_device(): jnp.dot(piece, query_weight, preferred_element_type=jnp.float32)  18.2 us
    pallas_call x1, Pallas kernels, attend(): pl.pallas_call(functools.partial(attention_kernel, last), out_shape=jax.S...  13 us
    psum x1, blocking collectives, on_device(): shrink = lax.psum(shrink_part, 'tensor').astype(jnp.bfloat16)  12.2 us
    pallas_call x2, Pallas kernels, serve(): pl.pallas_call(serve_kernel, out_shape=[jax.ShapeDtypeStruct(shape, store...  11.9 us
    ppermute x7, starting transfers between devices, swap(): lax.ppermute(array, 'dp', [(peer, peer ^ distance) for peer in range(peer...  10.4 us
    dot_general x1, matrix products, on_device(): jnp.dot(piece, keyvalue_weight, preferred_element_type=jnp.float32)  7.7 us
  transfers between devices with their start and end apart: 11, of which 9 were waited for; matrix products, arithmetic and copies ran while one was open for 16% of the time, Pallas kernels for 5%

profile of v14, /device:TPU:0, one launch (start us, length us, event | category | flops | bytes accessed | tf_op | source)
XLA Modules:
  0.0 343.6 jit_solution(6790080761635335332)
XLA Ops:
  7.2 0.7 all-gather.2.cloned.1.call-update
  7.9 0.8 pad_add_fusion.1
  8.7 0.6 broadcast_in_dim.175
  9.3 7.3 %all-to-all-start = ((s32[8,1,160]{2,1,0:T(1,128)}), s32[8,1,160]{2,1,0:T(1,128)S(1)}, u32[]{:S(2)}, u32[]{:S(2)}) async-start(s32[8,1,160]{2,1,0:T(1,128)} %broadcast_in_dim.175), calls=%async_computation | async-start | bytes 16384 | tf_op jit(solution)/shard_map/all_to_all | solution.py:287
  16.6 6.5 %all-to-all-done = s32[8,1,160]{2,1,0:T(1,128)S(1)} async-done(((s32[8,1,160]{2,1,0:T(1,128)}), s32[8,1,160]{2,1,0:T(1,128)S(1)}, u32[]{:S(2)}, u32[]{:S(2)}) %all-to-all-start) | async-done | bytes 5152 | tf_op jit(solution)/shard_map/all_to_all | solution.py:287
  23.1 0.3 convert_reduce_fusion.1
  23.4 0.1 select_reduce_fusion.3
  23.7 0.6 collective-permute-start
  24.3 0.6 gather_fusion.2
  24.9 0.2 convert_reduce_fusion
  25.2 0.2 select_reduce_fusion
  25.4 0.6 reshape.387.asked_ref
  26.0 5.8 %serve.2 = (bf16[16,64,512]{2,1,0:T(8,128)(2,1)}, bf16[16,64,512]{2,1,0:T(8,128)(2,1)}, bf16[16,64,512]{2,1,0:T(8,128)(2,1)}) custom-call(s32[48]{0:T(128)} %reshape.387.asked_ref, bf16[48,64,512]{2,1,0:T(8,128)(2,1)} %refs_0_), custom_call_target="tpu_custom_call" | custom-call | bytes 6291456 | tf_op jit(solution)/shard_map/serve/pallas_call | solution.py:209
  31.9 1.2 collective-permute-start.2
  33.1 2.3 collective-permute-start.3
  35.5 6.3 %gather_fusion.1 = bf16[16,2048,64]{1,2,0:T(8,128)(2,1)} fusion(bf16[32,2048,64]{1,2,0:T(8,128)(2,1)} %param.14, s32[1024]{0:T(1024)S(1)} %pad_clamp_fusion.1), kind=kCustom, calls=%fused_computation.1 | custom fusion | bytes 8388672 | tf_op jit(solution)/shard_map/gather | solution.py:308
  41.8 28.9 %all-gather.2.cloned.1.call-done = bf16[512,8192]{1,0:T(8,128)(2,1)} async-done(((bf16[512,2048]{1,0:T(8,128)(2,1)}), bf16[512,8192]{1,0:T(8,128)(2,1)}) %all-gather.2.cloned.1.call-update) | async-done | bytes 8388624 | tf_op jit(solution)/shard_map/all_gather | solution.py:311
  70.6 18.2 %fusion.26.base_hbm = f32[512,1024]{1,0:T(8,128)} fusion(bf16[512,8192]{1,0:T(8,128)(2,1)} %all-gather.2.cloned.1.call-done, bf16[8192,1024]{1,0:T(8,128)(2,1)} %param.12), kind=kOutput, calls=%fused_computation.94 | convolution fusion | flops 8589934592 | bytes 27262976 | tf_op jit(solution)/shard_map/dot_general | solution.py:312
  88.9 7.7 %convolution_convert_fusion = bf16[512,512]{1,0:T(8,128)(2,1)} fusion(bf16[512,8192]{1,0:T(8,128)(2,1)S(1)} %copy-done.11, bf16[8192,512]{1,0:T(8,128)(2,1)} %param.13), kind=kOutput, calls=%fused_computation.11 | convolution fusion | flops 4295229440 | bytes 17301504 | tf_op jit(solution)/shard_map/dot_general | solution.py:313
  96.6 19.0 %collective-permute-done.2.refs_2_ = bf16[16,64,512]{2,1,0:T(8,128)(2,1)} collective-permute-done((bf16[16,64,512]{2,1,0:T(8,128)(2,1)}, bf16[16,64,512]{2,1,0:T(8,128)(2,1)}, u32[]{:S(2)}, u32[]{:S(2)}) %collective-permute-start.2) | collective-permute-done | bytes 1048608 | tf_op jit(solution)/shard_map/ppermute | solution.py:282
  115.6 19.9 %collective-permute-done.3.refs_3_ = bf16[16,64,512]{2,1,0:T(8,128)(2,1)} collective-permute-done((bf16[16,64,512]{2,1,0:T(8,128)(2,1)}, bf16[16,64,512]{2,1,0:T(8,128)(2,1)}, u32[]{:S(2)}, u32[]{:S(2)}) %collective-permute-start.3) | collective-permute-done | bytes 1048608 | tf_op jit(solution)/shard_map/ppermute | solution.py:282
  135.5 25.1 %collective-permute-done.store_ref.refs_4_ = bf16[48,64,512]{2,1,0:T(8,128)(2,1)S(1)} collective-permute-done((bf16[48,64,512]{2,1,0:T(8,128)(2,1)}, bf16[48,64,512]{2,1,0:T(8,128)(2,1)S(1)}, u32[]{:S(2)}, u32[]{:S(2)}) %collective-permute-start) | collective-permute-done | bytes 3145760 | tf_op jit(solution)/shard_map/ppermute | solution.py:282
  160.6 4.5 %all-to-all-start.1 = ((bf16[16,2048,64]{1,2,0:T(8,128)(2,1)}), bf16[16,2048,64]{1,2,0:T(8,128)(2,1)}, u32[]{:S(2)}, u32[]{:S(2)}) async-start(bf16[16,2048,64]{1,2,0:T(8,128)(2,1)} %gather_fusion.1), calls=%async_computation.1 | async-start | bytes 8388608 | tf_op jit(solution)/shard_map/all_to_all | solution.py:318
  165.3 6.1 %serve.3 = (bf16[16,64,512]{2,1,0:T(8,128)(2,1)}, bf16[16,64,512]{2,1,0:T(8,128)(2,1)}, bf16[16,64,512]{2,1,0:T(8,128)(2,1)S(1)}) custom-call(s32[48]{0:T(128)S(1)} %reshape.388.asked_ref, bf16[48,64,512]{2,1,0:T(8,128)(2,1)S(1)} %collective-permute-done.store_ref.refs_4_), custom_call_target="tpu_custom_call" | custom-call | bytes 6291456 | tf_op jit(solution)/shard_map/serve/pallas_call | solution.py:209
  171.4 1.0 copy-done.1
  172.4 1.9 collective-permute-start.4
  174.3 1.5 collective-permute-start.5
  175.9 0.1 fusion.24
  176.1 0.6 slice.35
  177.4 4.3 %gather_fusion = bf16[16,64,1024]{2,1,0:T(8,128)(2,1)} fusion(bf16[32,64,1024]{2,1,0:T(8,128)(2,1)} %param.15, s32[1024]{0:T(1024)S(1)} %pad_clamp_fusion.1), kind=kCustom, calls=%fused_computation | custom fusion | bytes 4194368 | tf_op jit(solution)/shard_map/gather | solution.py:309
  181.7 53.6 %collective-permute-done.4.refs_5_ = bf16[16,64,512]{2,1,0:T(8,128)(2,1)S(1)} collective-permute-done((bf16[16,64,512]{2,1,0:T(8,128)(2,1)}, bf16[16,64,512]{2,1,0:T(8,128)(2,1)S(1)}, u32[]{:S(2)}, u32[]{:S(2)}) %collective-permute-start.4) | collective-permute-done | bytes 1048608 | tf_op jit(solution)/shard_map/ppermute | solution.py:282
  235.3 21.7 %collective-permute-done.5.refs_6_ = bf16[16,64,512]{2,1,0:T(8,128)(2,1)S(1)} collective-permute-done((bf16[16,64,512]{2,1,0:T(8,128)(2,1)}, bf16[16,64,512]{2,1,0:T(8,128)(2,1)S(1)}, u32[]{:S(2)}, u32[]{:S(2)}) %collective-permute-start.5) | collective-permute-done | bytes 1048608 | tf_op jit(solution)/shard_map/ppermute | solution.py:282
  257.0 1.8 all-to-all-done.1
  258.8 4.7 %all-to-all-start.2 = ((bf16[16,64,1024]{2,1,0:T(8,128)(2,1)}), bf16[16,64,1024]{2,1,0:T(8,128)(2,1)S(1)}, u32[]{:S(2)}, u32[]{:S(2)}) async-start(bf16[16,64,1024]{2,1,0:T(8,128)(2,1)} %gather_fusion), calls=%async_computation.2 | async-start | bytes 4194304 | tf_op jit(solution)/shard_map/all_to_all | solution.py:322
  263.7 0.6 pad_add_fusion.steps_ref
  264.3 0.2 convert_reduce_fusion.2
  264.5 0.2 convert_reduce_fusion.3
  264.8 0.6 compare_select_fusion.4
  265.5 3.0 collective-permute-start.6
  268.5 3.6 %fusion.1 = bf16[2048,512]{1,0:T(8,128)(2,1)} fusion(bf16[512,512]{1,0:T(8,128)(2,1)} %convolution_convert_fusion, s32[2048]{0:T(1024)S(1)} %add_bitcast_fusion), kind=kOutput, calls=%fused_computation.5 | convolution fusion | flops 1075838976 | bytes 2629632 | tf_op jit(solution)/shard_map/dot_general | solution.py:341
  272.1 4.6 %fusion.2 = f32[512,64]{0,1:T(8,128)S(1)} fusion(bf16[16,2048,64]{1,2,0:T(8,128)(2,1)} %all-to-all-done.1, bf16[512,2048]{1,0:T(8,128)(2,1)S(1)} %copy-done.4, pred[512,16]{0,1:T(8,128)(4,1)S(1)} %iota_compare_fusion.5), kind=kOutput, calls=%fused_computation.7 | convolution fusion | flops 2148499456 | bytes 6430720 | tf_op jit(solution)/shard_map/tn,snk->tsk/dot_general | solution.py:333
  276.7 12.2 %all-reduce.1 = bf16[512,64]{0,1:T(8,128)(2,1)S(1)} all-reduce(f32[512,64]{0,1:T(8,128)S(1)} %fusion.2), channel_id=1, replica_groups=mesh['dp'=8,'tensor'=4] {'tensor'}, use_global_device_ids=true, to_apply=%region_16.17 | all-reduce | flops 32768 | bytes 196608 | tf_op jit(solution)/shard_map/psum | solution.py:335
  288.9 1.0 broadcast_select_fusion
  289.9 2.3 copy.37.spread_hbm
  292.2 5.3 %assemble.1.pages_hbm = bf16[64,64,512]{2,1,0:T(8,128)(2,1)} custom-call(s32[64]{0:T(128)} %get-tuple-element.51.source_ref, s32[64]{0:T(128)} %get-tuple-element.50.place_ref, bf16[48,64,512]{2,1,0:T(8,128)(2,1)} %refs_0_, bf16[16,64,512]{2,1,0:T(8,128)(2,1)} %collective-permute-done.1.refs_1_, bf16[16,64,512]{2,1,0:T(8,128)(2,1)} %collective-permute-done.2.refs_2_, ...), custom_call_target="tpu_custom_call" | custom-call | bytes 8388608 | tf_op jit(solution)/shard_map/assemble/pallas_call | solution.py:248
  297.5 24.9 %collective-permute-done.6.last_hbm = bf16[16,64,512]{2,1,0:T(8,128)(2,1)} collective-permute-done((bf16[16,64,512]{2,1,0:T(8,128)(2,1)S(1)}, bf16[16,64,512]{2,1,0:T(8,128)(2,1)}, u32[]{:S(2)}, u32[]{:S(2)}) %collective-permute-start.6) | collective-permute-done | bytes 1048608 | tf_op jit(solution)/shard_map/ppermute | solution.py:282
  322.4 1.3 copy-done.3
  323.7 13.0 %attend.1 = bf16[512,1024]{1,0:T(8,128)(2,1)} custom-call(s32[4,32]{1,0:T(4,128)} %pad_add_fusion.steps_ref, s32[64]{0:T(128)} %get-tuple-element.51.source_ref, s32[64]{0:T(128)} %get-tuple-element.50.place_ref, bf16[512,1024]{1,0:T(8,128)(2,1)} %copy.37.spread_hbm, bf16[1024,1024]{1,0:T(8,128)(2,1)} %bitcast.62, f32[512,1024]{1,0:T(8,128)} %fusion.26.base_hbm, ...), custom_call_target="tpu_custom_call" | custom-call | flops 2684354560 | bytes 12582912 | tf_op jit(solution)/shard_map/attend/pallas_call | solution.py:174
  (56 shorter events, 1.4 us)
Async XLA Ops:
  7.2 63.5 %all-gather.2.cloned.1.call-start = ((), (), s32[]{:S(2)}) async-start(), calls=%async_computation.3 | async-start | bytes 10485760 | tf_op jit(solution)/shard_map/all_gather | solution.py:311
  9.3 13.8 %all-to-all-start = ((s32[8,1,160]{2,1,0:T(1,128)}), s32[8,1,160]{2,1,0:T(1,128)S(1)}, u32[]{:S(2)}, u32[]{:S(2)}) async-start(s32[8,1,160]{2,1,0:T(1,128)} %broadcast_in_dim.175), calls=%async_computation | async-start | bytes 16384 | tf_op jit(solution)/shard_map/all_to_all | solution.py:287
  23.7 136.9 %collective-permute-start = (bf16[48,64,512]{2,1,0:T(8,128)(2,1)}, bf16[48,64,512]{2,1,0:T(8,128)(2,1)S(1)}, u32[]{:S(2)}, u32[]{:S(2)}) collective-permute-start(bf16[48,64,512]{2,1,0:T(8,128)(2,1)} %refs_0_), channel_id=1, source_target_pairs={{0,16},{4,20},{8,24},{12,28},{16,0},{20,4},{24,8},{28,12},{1,17},{... | collective-permute-start | bytes 9437192 | tf_op jit(solution)/shard_map/ppermute | solution.py:282
  31.8 64.8 %collective-permute-start.1 = (bf16[16,64,512]{2,1,0:T(8,128)(2,1)}, bf16[16,64,512]{2,1,0:T(8,128)(2,1)}, u32[]{:S(2)}, u32[]{:S(2)}) collective-permute-start(bf16[16,64,512]{2,1,0:T(8,128)(2,1)} %get-tuple-element.26), channel_id=1, source_target_pairs={{0,4},{4,0},{8,12},{12,8},{16,20},{20,16},{24,28},{28,24},{1,5},{5... | collective-permute-start | bytes 3145736 | tf_op jit(solution)/shard_map/ppermute | solution.py:282
  31.9 83.7 %collective-permute-start.2 = (bf16[16,64,512]{2,1,0:T(8,128)(2,1)}, bf16[16,64,512]{2,1,0:T(8,128)(2,1)}, u32[]{:S(2)}, u32[]{:S(2)}) collective-permute-start(bf16[16,64,512]{2,1,0:T(8,128)(2,1)} %get-tuple-element.27), channel_id=1, source_target_pairs={{0,8},{4,12},{8,0},{12,4},{16,24},{20,28},{24,16},{28,20},{1,9},{5... | collective-permute-start | bytes 3145736 | tf_op jit(solution)/shard_map/ppermute | solution.py:282
  33.1 102.4 %collective-permute-start.3 = (bf16[16,64,512]{2,1,0:T(8,128)(2,1)}, bf16[16,64,512]{2,1,0:T(8,128)(2,1)}, u32[]{:S(2)}, u32[]{:S(2)}) collective-permute-start(bf16[16,64,512]{2,1,0:T(8,128)(2,1)} %get-tuple-element.28), channel_id=1, source_target_pairs={{0,12},{4,8},{8,4},{12,0},{16,28},{20,24},{24,20},{28,16},{1,13},{... | collective-permute-start | bytes 3145736 | tf_op jit(solution)/shard_map/ppermute | solution.py:282
  70.6 18.2 %copy-start.11 = (bf16[512,8192]{1,0:T(8,128)(2,1)S(1)}, bf16[512,8192]{1,0:T(8,128)(2,1)}, u32[]{:S(2)}) copy-start(bf16[512,8192]{1,0:T(8,128)(2,1)} %all-gather.2.cloned.1.call-done) | copy-start | bytes 25165828
  96.6 79.2 %copy-start.7 = (s32[1,16]{1,0:T(1,128)S(1)}, s32[1,16]{1,0:T(1,128)}, u32[]{:S(2)}) copy-start(s32[1,16]{1,0:T(1,128)} %param.17) | copy-start | bytes 196
  160.6 4.7 %copy-start = (bf16[48,64,512]{2,1,0:T(8,128)(2,1)}, bf16[48,64,512]{2,1,0:T(8,128)(2,1)S(1)}, u32[]{:S(2)}) copy-start(bf16[48,64,512]{2,1,0:T(8,128)(2,1)S(1)} %collective-permute-done.store_ref.refs_4_) | copy-start | bytes 9437188
  160.6 98.2 %all-to-all-start.1 = ((bf16[16,2048,64]{1,2,0:T(8,128)(2,1)}), bf16[16,2048,64]{1,2,0:T(8,128)(2,1)}, u32[]{:S(2)}, u32[]{:S(2)}) async-start(bf16[16,2048,64]{1,2,0:T(8,128)(2,1)} %gather_fusion.1), calls=%async_computation.1 | async-start | bytes 8388608 | tf_op jit(solution)/shard_map/all_to_all | solution.py:318
  171.4 1.0 copy-start.1
  172.4 62.9 %collective-permute-start.4 = (bf16[16,64,512]{2,1,0:T(8,128)(2,1)}, bf16[16,64,512]{2,1,0:T(8,128)(2,1)S(1)}, u32[]{:S(2)}, u32[]{:S(2)}) collective-permute-start(bf16[16,64,512]{2,1,0:T(8,128)(2,1)} %get-tuple-element.31), channel_id=1, source_target_pairs={{0,4},{4,0},{8,12},{12,8},{16,20},{20,16},{24,28},{28,24},{1,5},{5... | collective-permute-start | bytes 3145736 | tf_op jit(solution)/shard_map/ppermute | solution.py:282
  174.3 82.7 %collective-permute-start.5 = (bf16[16,64,512]{2,1,0:T(8,128)(2,1)}, bf16[16,64,512]{2,1,0:T(8,128)(2,1)S(1)}, u32[]{:S(2)}, u32[]{:S(2)}) collective-permute-start(bf16[16,64,512]{2,1,0:T(8,128)(2,1)} %get-tuple-element.32), channel_id=1, source_target_pairs={{0,8},{4,12},{8,0},{12,4},{16,24},{20,28},{24,16},{28,20},{1,9},{5... | collective-permute-start | bytes 3145736 | tf_op jit(solution)/shard_map/ppermute | solution.py:282
  177.4 87.0 %copy-start.9 = (s32[64,1]{0,1:T(1,128)S(1)}, s32[64,1]{0,1:T(1,128)}, u32[]{:S(2)}) copy-start(s32[64,1]{0,1:T(1,128)} %param.20) | copy-start | bytes 772
  177.4 87.1 %copy-start.10 = (s32[16,1]{0,1:T(1,128)S(1)}, s32[16,1]{0,1:T(1,128)}, u32[]{:S(2)}) copy-start(s32[16,1]{0,1:T(1,128)} %param.18) | copy-start | bytes 196
  177.4 87.4 %copy-start.8 = (s32[64]{0:T(128)S(1)}, s32[64]{0:T(128)}, u32[]{:S(2)}) copy-start(s32[64]{0:T(128)} %param.21) | copy-start | bytes 772
  177.4 88.1 %copy-start.2 = (bf16[16,64,512]{2,1,0:T(8,128)(2,1)S(1)}, bf16[16,64,512]{2,1,0:T(8,128)(2,1)}, u32[]{:S(2)}) copy-start(bf16[16,64,512]{2,1,0:T(8,128)(2,1)} %copy-done.1) | copy-start | bytes 3145732
  235.3 23.5 %copy-start.5 = (bf16[16,64,512]{2,1,0:T(8,128)(2,1)}, bf16[16,64,512]{2,1,0:T(8,128)(2,1)S(1)}, u32[]{:S(2)}) copy-start(bf16[16,64,512]{2,1,0:T(8,128)(2,1)S(1)} %collective-permute-done.4.refs_5_) | copy-start | bytes 3145732
  257.0 1.8 copy-start.6
  258.8 63.5 %all-to-all-start.2 = ((bf16[16,64,1024]{2,1,0:T(8,128)(2,1)}), bf16[16,64,1024]{2,1,0:T(8,128)(2,1)S(1)}, u32[]{:S(2)}, u32[]{:S(2)}) async-start(bf16[16,64,1024]{2,1,0:T(8,128)(2,1)} %gather_fusion), calls=%async_computation.2 | async-start | bytes 4194304 | tf_op jit(solution)/shard_map/all_to_all | solution.py:322
  263.5 8.6 %copy-start.4 = (bf16[512,2048]{1,0:T(8,128)(2,1)S(1)}, bf16[512,2048]{1,0:T(8,128)(2,1)}, u32[]{:S(2)}) copy-start(bf16[512,2048]{1,0:T(8,128)(2,1)} %param.11) | copy-start | bytes 6291460
  265.5 56.9 %collective-permute-start.6 = (bf16[16,64,512]{2,1,0:T(8,128)(2,1)S(1)}, bf16[16,64,512]{2,1,0:T(8,128)(2,1)}, u32[]{:S(2)}, u32[]{:S(2)}) collective-permute-start(bf16[16,64,512]{2,1,0:T(8,128)(2,1)S(1)} %copy-done.2), channel_id=1, source_target_pairs={{0,12},{4,8},{8,4},{12,0},{16,28},{20,24},{24,20},{28,16},{1,13},{... | collective-permute-start | bytes 3145736 | tf_op jit(solution)/shard_map/ppermute | solution.py:282
  322.4 1.3 copy-start.3
Sparse Core Ops, SparseCore 0:
  9.6 61.0 all-gather.1

commit v15 on v14

--- a/solution.py
+++ b/solution.py
@@ -220,6 +220,42 @@
     )(asked.reshape(-1), store)
 
 
+def serve_both_kernel(asked_ref, adapters_ref, store_ref, down_ref, *refs):
+    outs, sems = refs[:-1], refs[-1]
+    columns = store_ref.shape[2]
+    cuts = down_ref.shape[2] // columns
+    pages = outs[0].shape[0] - ADP_CAP * cuts
+    for index, out in enumerate(outs):
+        for place in range(pages):
+            page = asked_ref[index * pages + place]
+            pltpu.make_async_copy(store_ref.at[page], out.at[place], sems.at[index]).start()
+        for number in range(ADP_CAP):
+            factor = down_ref.at[adapters_ref[index * ADP_CAP + number]]
+            for cut in range(cuts):
+                cols = factor.at[:, cut * columns : (cut + 1) * columns]
+                pltpu.make_async_copy(cols, out.at[pages + number * cuts + cut], sems.at[index]).start()
+    for index, out in enumerate(outs):
+        pltpu.make_async_copy(out, out, sems.at[index]).wait()
+
+
+def serve_both(asked, adapters, store, down):
+    blocks, capacity = asked.shape
+    shape = (capacity + ADP_CAP * (down.shape[2] // store.shape[2]),) + store.shape[1:]
+    scalars = pl.BlockSpec(memory_space=pltpu.SMEM)
+    return pl.pallas_call(
+        serve_both_kernel,
+        out_shape=[jax.ShapeDtypeStruct(shape, store.dtype)] * blocks,
+        in_specs=[scalars, scalars, pl.BlockSpec(memory_space=pltpu.HBM), pl.BlockSpec(memory_space=pltpu.HBM)],
+        out_specs=[pl.BlockSpec(memory_space=pltpu.VMEM)] * blocks,
+        scratch_shapes=[pltpu.SemaphoreType.DMA((blocks,))],
+        compiler_params=pltpu.CompilerParams(vmem_limit_bytes=VMEM_GRANT),
+        cost_estimate=pl.CostEstimate(
+            flops=0, bytes_accessed=4 * blocks * math.prod(shape), transcendentals=0
+        ),
+        name="serve_both",
+    )(asked.reshape(-1), adapters.reshape(-1), store, down)
+
+
 def assemble_kernel(source_ref, place_ref, *refs):
     sources, out, sem = refs[:-2], refs[-2], refs[-1]
 
@@ -287,7 +323,8 @@
     everyone = lax.all_to_all(
         jnp.broadcast_to(raw[None], (peers, raw.shape[0])), "dp", split_axis=0, concat_axis=0, tiled=True
     )
-    store, down_store, everyone = lax.optimization_barrier((keyvalue_page_store, adapter_down_weight, everyone))
+    down_store = jnp.swapaxes(adapter_down_weight, 1, 2)
+    store, down_store, everyone = lax.optimization_barrier((keyvalue_page_store, down_store, everyone))
     mirrored_store = swap(store, half)
 
     page_cap = max(2, 2 * page_count // peers)
@@ -299,41 +336,52 @@
     far_asked = asked_of(me ^ half, group_owner, group_order, group_local, page_cap)
     all_owner = everyone[:, 2 * page_count : 2 * page_count + request_count]
     all_local = everyone[:, 2 * page_count + request_count :]
-    adapter_asked = asked_of(me, all_owner, earlier_alike(all_owner), all_local, ADP_CAP).reshape(-1)
-    adapter_pos = adapter_owner[:, 0] * ADP_CAP + earlier_alike(adapter_owner[:, 0])
+    adapter_asked = asked_of(me, all_owner, earlier_alike(all_owner), all_local, ADP_CAP)
+    adapter_near = adapter_asked[jnp.arange(peers, dtype=jnp.int32) ^ me]
+    adapter_order = earlier_alike(adapter_owner[:, 0])
+    down_pos = (adapter_owner[:, 0] ^ me) * ADP_CAP + adapter_order
+    up_pos = adapter_owner[:, 0] * ADP_CAP + adapter_order
     page_source = page_owner[:, 0] ^ me
     page_place = jnp.where(page_source % half == 0, page_local_index, earlier_alike(page_owner[:, 0]))
 
-    near = [swap(pages, i + 1) for i, pages in enumerate(serve(near_asked[1:], store, VMEM_GRANT))]
-    down_rows = down_store[adapter_asked]
-    up_rows = adapter_up_weight[adapter_asked]
+    near = serve_both(near_asked[1:], adapter_near[1:half], store, down_store)
+    near = [swap(pages, i + 1) for i, pages in enumerate(near)]
+    own_down, *cross = serve(jnp.concatenate([adapter_near[:1], adapter_near[half:]]), down_store, VMEM_GRANT)
+    up_rows = adapter_up_weight[adapter_asked.reshape(-1)]
 
     piece = lax.all_gather(tokens, "tensor", axis=1, tiled=True)
     query_base = jnp.dot(piece, query_weight, preferred_element_type=jnp.float32)
     new_cache = jnp.dot(piece, keyvalue_weight, preferred_element_type=jnp.float32).astype(jnp.bfloat16)
 
-    down_rows, mirrored_store, query_base, new_cache, near = lax.optimization_barrier(
-        (down_rows, mirrored_store, query_base, new_cache, near)
+    cross, mirrored_store, query_base, new_cache, near = lax.optimization_barrier(
+        (cross, mirrored_store, query_base, new_cache, near)
     )
-    down_sent = lax.all_to_all(down_rows, "dp", split_axis=0, concat_axis=0, tiled=True)
-    far = list(serve(far_asked[1:], mirrored_store, SMALL_GRANT))
-    far = [swap(pages, i + 1) for i, pages in enumerate(far[:-1])] + far[-1:]
-    up_rows, down_sent, far = lax.optimization_barrier((up_rows, down_sent, far))
+    cross = [swap(rows, half + i) for i, rows in enumerate(cross)]
+    far = serve(far_asked[1:], mirrored_store, SMALL_GRANT)
+    far = [swap(pages, i + 1) for i, pages in enumerate(far)]
+    up_rows, cross, far = lax.optimization_barrier((up_rows, cross, far))
     up_sent = lax.all_to_all(up_rows, "dp", split_axis=0, concat_axis=0, tiled=True)
-    far[-1] = swap(far[-1], half - 1)
 
     lengths = span_token_length[0]
     ends = jnp.cumsum(lengths)
     starts = ends - lengths
     steps = jnp.arange(tok_rows, dtype=jnp.int32)[:, None]
     member = (steps >= starts[None, :]) & (steps < ends[None, :])
-    slot = jnp.sum(jnp.where(member, adapter_pos[None, :], 0), axis=1)
-    in_slot = slot[:, None] == jnp.arange(adapter_slots, dtype=jnp.int32)[None, :]
-
-    down_part = jnp.einsum("tn,snk->tsk", tokens, down_sent, preferred_element_type=jnp.float32)
-    shrink_part = jnp.sum(jnp.where(in_slot[:, :, None], down_part, 0.0), axis=1)
+
+    def in_slot(position):
+        slot = jnp.sum(jnp.where(member, position[None, :], 0), axis=1)
+        return slot[:, None] == jnp.arange(adapter_slots, dtype=jnp.int32)[None, :]
+
+    def joined(pieces):
+        cut = pieces.reshape(ADP_CAP, -1, rank, pieces.shape[2])
+        return jnp.swapaxes(cut, 1, 2).reshape(ADP_CAP, rank, tokens.shape[1])
+
+    near_down = [joined(block[page_cap:]) for block in near]
+    down_sent = jnp.concatenate([own_down, *near_down, *cross], axis=0)
+    down_part = jnp.einsum("tn,skn->tsk", tokens, down_sent, preferred_element_type=jnp.float32)
+    shrink_part = jnp.sum(jnp.where(in_slot(down_pos)[:, :, None], down_part, 0.0), axis=1)
     shrink = lax.psum(shrink_part, "tensor").astype(jnp.bfloat16)
-    spread = jnp.where(in_slot[:, :, None], shrink[:, None, :], 0).reshape(tok_rows, adapter_slots * rank)
+    spread = jnp.where(in_slot(up_pos)[:, :, None], shrink[:, None, :], 0).reshape(tok_rows, adapter_slots * rank)
     prefix_pages = assemble(page_source, page_place, [store, *near, mirrored_store, *far[:-1]])
 
     taken = starts[:, None] + jnp.arange(MOST, dtype=jnp.int32)[None, :]

time: 346 us -> 365 us (1.055)
  starting transfers between devices: 26.9 us -> 50 us
  waiting for transfers between devices: 202 us -> 194 us
  Pallas kernels: 30.2 us -> 34.9 us
    all_to_all x1, starting transfers between devices: 4.67 us -> 24.3 us  [on_device(): lax.all_to_all(up_rows, 'dp', split_axis=0, concat_axis=0, tiled=True)]
    all_to_all x1, waiting for transfers between devices: 0.01 us -> 15.1 us  [on_device(): lax.all_to_all(up_rows, 'dp', split_axis=0, concat_axis=0, tiled=True)]
    ppermute x7 -> x11, waiting for transfers between devices: 164 us -> 150 us  [swap(): lax.ppermute(array, 'dp', [(peer, peer ^ distance) for peer in range(peer...]
    ppermute x7 -> x11, starting transfers between devices: 10.4 us -> 18.4 us  [swap(): lax.ppermute(array, 'dp', [(peer, peer ^ distance) for peer in range(peer...]
    pallas_call x0 -> x1, Pallas kernels: none -> 6.53 us  [serve_both(): pl.pallas_call(serve_both_kernel, out_shape=[jax.ShapeDtypeStruct(shape,...]
    gather x2, local copies, waits for them, and re-layouts: 10.6 us -> 4.73 us  [the longest x1 4.17 us: on_device(): up_rows = adapter_up_weight[adapter_asked.reshape(-1)]]
    all_to_all x1, waiting for transfers between devices: 6.46 us -> 1 us  [on_device(): lax.all_to_all(jnp.broadcast_to(raw[None], (peers, raw.shape[0])), 'dp',...]
    all_to_all x1 -> x0, starting transfers between devices: 4.54 us -> none  [on_device(): lax.all_to_all(down_rows, 'dp', split_axis=0, concat_axis=0, tiled=True)]
  transfers between devices with their start and end apart: 11 -> 14, of which waited for: 9 -> 9; matrix products, arithmetic and copies ran while one was open for 16% -> 16% of each run, Pallas kernels for 5% -> 4%
where the time goes in v15:
time: 365 us
  waiting for transfers between devices  194 us (53%)
  starting transfers between devices  50 us (14%)
  Pallas kernels  34.9 us (10%)
  matrix products  31 us (8%)
  local copies, waits for them, and re-layouts  19.6 us (5%)
  between operations  15 us (4%)
  blocking collectives  13.4 us (4%)
  other arithmetic  6.89 us (2%)
    ppermute x11, waiting for transfers between devices, swap(): lax.ppermute(array, 'dp', [(peer, peer ^ distance) for peer in range(peer...  150 us
    all_gather x1, waiting for transfers between devices, on_device(): piece = lax.all_gather(tokens, 'tensor', axis=1, tiled=True)  27.4 us
    all_to_all x1, starting transfers between devices, on_device(): lax.all_to_all(up_rows, 'dp', split_axis=0, concat_axis=0, tiled=True)  24.3 us
    ppermute x11, starting transfers between devices, swap(): lax.ppermute(array, 'dp', [(peer, peer ^ distance) for peer in range(peer...  18.4 us
    dot_general x1, matrix products, on_device(): jnp.dot(piece, query_weight, preferred_element_type=jnp.float32)  18.3 us
    all_to_all x1, waiting for transfers between devices, on_device(): lax.all_to_all(up_rows, 'dp', split_axis=0, concat_axis=0, tiled=True)  15.1 us
    psum x1, blocking collectives, on_device(): shrink = lax.psum(shrink_part, 'tensor').astype(jnp.bfloat16)  13.4 us
    pallas_call x1, Pallas kernels, attend(): pl.pallas_call(functools.partial(attention_kernel, last), out_shape=jax.S...  13 us
  transfers between devices with their start and end apart: 14, of which 9 were waited for; matrix products, arithmetic and copies ran while one was open for 16% of the time, Pallas kernels for 4%

profile of v15, /device:TPU:0, one launch (start us, length us, event | category | flops | bytes accessed | tf_op | source)
XLA Modules:
  0.0 364.7 jit_solution(14239552185699218227)
XLA Ops:
  7.2 0.7 all-gather.2.cloned.1.call-update
  7.9 0.8 pad_add_fusion.2
  8.7 0.6 broadcast_in_dim.188
  9.3 7.3 %all-to-all-start = ((s32[8,1,160]{2,1,0:T(1,128)}), s32[8,1,160]{2,1,0:T(1,128)S(1)}, u32[]{:S(2)}, u32[]{:S(2)}) async-start(s32[8,1,160]{2,1,0:T(1,128)} %broadcast_in_dim.188), calls=%async_computation | async-start | bytes 16384 | tf_op jit(solution)/shard_map/all_to_all | solution.py:323
  16.5 0.7 copy.42
  18.8 0.9 convert_reduce_fusion.3
  19.8 0.7 multiply_add_fusion.1
  20.5 0.7 fusion.22
  21.4 0.7 bitcast_subtract_fusion.2
  22.1 1.0 all-to-all-done
  25.4 0.6 reshape.457.asked_ref
  26.6 1.9 collective-permute-start
  28.5 6.5 %serve_both.1 = (bf16[24,64,512]{2,1,0:T(8,128)(2,1)}, bf16[24,64,512]{2,1,0:T(8,128)(2,1)}, bf16[24,64,512]{2,1,0:T(8,128)(2,1)}) custom-call(s32[48]{0:T(128)} %reshape.457.asked_ref, s32[6]{0:T(128)} %reshape.458.adapters_ref, bf16[48,64,512]{2,1,0:T(8,128)(2,1)} %refs_0_, bf16[32,64,2048]{2,1,0:T(8,128)(2,1)} %bitcast.81), custom_call_target="tpu_custom_call" | custom-call | bytes 9437184 | tf_op jit(solution)/shard_map/serve_both/pallas_call | solution.py:245
  35.4 3.3 collective-permute-start.2
  39.2 3.9 %serve.2 = (bf16[2,64,2048]{2,1,0:T(8,128)(2,1)}, bf16[2,64,2048]{2,1,0:T(8,128)(2,1)}, bf16[2,64,2048]{2,1,0:T(8,128)(2,1)}, bf16[2,64,2048]{2,1,0:T(8,128)(2,1)}, bf16[2,64,2048]{2,1,0:T(8,128)(2,1)}) custom-call(s32[10]{0:T(128)} %reshape.456.asked_ref, bf16[32,64,2048]{2,1,0:T(8,128)(2,1)} %bitcast.82), custom_call_target="tpu_custom_call" | custom-call | bytes 5242880 | tf_op jit(solution)/shard_map/serve/pallas_call | solution.py:209
  43.2 27.4 %all-gather.2.cloned.1.call-done = bf16[512,8192]{1,0:T(8,128)(2,1)} async-done(((bf16[512,2048]{1,0:T(8,128)(2,1)}), bf16[512,8192]{1,0:T(8,128)(2,1)}) %all-gather.2.cloned.1.call-update) | async-done | bytes 8388624 | tf_op jit(solution)/shard_map/all_gather | solution.py:352
  70.6 18.3 %fusion.27.base_hbm = f32[512,1024]{1,0:T(8,128)} fusion(bf16[512,8192]{1,0:T(8,128)(2,1)} %all-gather.2.cloned.1.call-done, bf16[8192,1024]{1,0:T(8,128)(2,1)} %param.12), kind=kOutput, calls=%fused_computation.109 | convolution fusion | flops 8589934592 | bytes 27262976 | tf_op jit(solution)/shard_map/dot_general | solution.py:353
  88.9 7.8 %convolution_convert_fusion = bf16[512,512]{1,0:T(8,128)(2,1)} fusion(bf16[512,8192]{1,0:T(8,128)(2,1)S(1)} %copy-done.4, bf16[8192,512]{1,0:T(8,128)(2,1)} %param.13), kind=kOutput, calls=%fused_computation.11 | convolution fusion | flops 4295229440 | bytes 17301504 | tf_op jit(solution)/shard_map/dot_general | solution.py:354
  96.7 34.4 %collective-permute-done.2.refs_2_ = bf16[24,64,512]{2,1,0:T(8,128)(2,1)} collective-permute-done((bf16[24,64,512]{2,1,0:T(8,128)(2,1)}, bf16[24,64,512]{2,1,0:T(8,128)(2,1)}, u32[]{:S(2)}, u32[]{:S(2)}) %collective-permute-start.2) | collective-permute-done | bytes 1572896 | tf_op jit(solution)/shard_map/ppermute | solution.py:318
  131.1 41.0 %collective-permute-done.3.refs_3_ = bf16[24,64,512]{2,1,0:T(8,128)(2,1)} collective-permute-done((bf16[24,64,512]{2,1,0:T(8,128)(2,1)}, bf16[24,64,512]{2,1,0:T(8,128)(2,1)}, u32[]{:S(2)}, u32[]{:S(2)}) %collective-permute-start.3) | collective-permute-done | bytes 1572896 | tf_op jit(solution)/shard_map/ppermute | solution.py:318
  172.1 6.5 %serve.3 = (bf16[16,64,512]{2,1,0:T(8,128)(2,1)}, bf16[16,64,512]{2,1,0:T(8,128)(2,1)}, bf16[16,64,512]{2,1,0:T(8,128)(2,1)}) custom-call(s32[48]{0:T(128)S(1)} %reshape.466.asked_ref, bf16[48,64,512]{2,1,0:T(8,128)(2,1)S(1)} %collective-permute-done.store_ref.refs_4_), custom_call_target="tpu_custom_call" | custom-call | bytes 6291456 | tf_op jit(solution)/shard_map/serve/pallas_call | solution.py:209
  178.7 1.5 collective-permute-start.8
  180.2 2.0 collective-permute-start.9
  182.2 1.1 collective-permute-start.4
  183.3 2.7 collective-permute-start.5
  186.2 50.1 %collective-permute-done.4 = bf16[2,64,2048]{2,1,0:T(8,128)(2,1)} collective-permute-done((bf16[2,64,2048]{2,1,0:T(8,128)(2,1)S(1)}, bf16[2,64,2048]{2,1,0:T(8,128)(2,1)}, u32[]{:S(2)}, u32[]{:S(2)}) %collective-permute-start.4) | collective-permute-done | bytes 524320 | tf_op jit(solution)/shard_map/ppermute | solution.py:318
  236.3 2.2 collective-permute-start.6
  238.6 9.0 %collective-permute-done.5 = bf16[2,64,2048]{2,1,0:T(8,128)(2,1)} collective-permute-done((bf16[2,64,2048]{2,1,0:T(8,128)(2,1)S(1)}, bf16[2,64,2048]{2,1,0:T(8,128)(2,1)}, u32[]{:S(2)}, u32[]{:S(2)}) %collective-permute-start.5) | collective-permute-done | bytes 524320 | tf_op jit(solution)/shard_map/ppermute | solution.py:318
  247.6 3.3 collective-permute-start.7
  251.7 4.2 %gather_fusion.2 = bf16[16,64,1024]{2,1,0:T(8,128)(2,1)} fusion(bf16[32,64,1024]{2,1,0:T(8,128)(2,1)} %param.15, s32[1024]{0:T(1024)S(1)} %pad_clamp_fusion), kind=kCustom, calls=%fused_computation.2 | custom fusion | bytes 4194368 | tf_op jit(solution)/shard_map/gather | solution.py:350
  255.9 5.9 %collective-permute-done.6 = bf16[2,64,2048]{2,1,0:T(8,128)(2,1)} collective-permute-done((bf16[2,64,2048]{2,1,0:T(8,128)(2,1)}, bf16[2,64,2048]{2,1,0:T(8,128)(2,1)}, u32[]{:S(2)}, u32[]{:S(2)}) %collective-permute-start.6) | collective-permute-done | bytes 524320 | tf_op jit(solution)/shard_map/ppermute | solution.py:318
  261.8 9.3 %collective-permute-done.7 = bf16[2,64,2048]{2,1,0:T(8,128)(2,1)} collective-permute-done((bf16[2,64,2048]{2,1,0:T(8,128)(2,1)}, bf16[2,64,2048]{2,1,0:T(8,128)(2,1)}, u32[]{:S(2)}, u32[]{:S(2)}) %collective-permute-start.7) | collective-permute-done | bytes 524320 | tf_op jit(solution)/shard_map/ppermute | solution.py:318
  271.1 24.3 %all-to-all-start.1 = ((bf16[16,64,1024]{2,1,0:T(8,128)(2,1)}), bf16[16,64,1024]{2,1,0:T(8,128)(2,1)}, u32[]{:S(2)}, u32[]{:S(2)}) async-start(bf16[16,64,1024]{2,1,0:T(8,128)(2,1)} %gather_fusion.2), calls=%async_computation.1 | async-start | bytes 4194304 | tf_op jit(solution)/shard_map/all_to_all | solution.py:363
  296.0 1.1 constant_dynamic-update-slice_fusion.7
  297.1 1.1 slice.49
  298.3 1.1 slice.50
  299.4 1.1 slice.51
  300.8 2.5 fusion.1
  303.3 1.1 constant_dynamic-update-slice_fusion.3
  304.4 1.1 constant_dynamic-update-slice_fusion.2
  305.5 1.1 constant_dynamic-update-slice_fusion.1
  306.5 1.1 constant_dynamic-update-slice_fusion
  307.6 2.4 fusion.2
  310.0 13.4 %all-reduce.1 = bf16[512,64]{0,1:T(8,128)(2,1)S(1)} all-reduce(f32[512,64]{0,1:T(8,128)S(1)} %fusion.2), channel_id=1, replica_groups=mesh['dp'=8,'tensor'=4] {'tensor'}, use_global_device_ids=true, to_apply=%region_17.18 | all-reduce | flops 32768 | bytes 196608 | tf_op jit(solution)/shard_map/psum | solution.py:383
  323.5 1.3 copy.52.spread_hbm
  324.8 5.0 %assemble.1.pages_hbm = bf16[64,64,512]{2,1,0:T(8,128)(2,1)} custom-call(s32[64]{0:T(128)} %get-tuple-element.75.source_ref, s32[64]{0:T(128)} %get-tuple-element.74.place_ref, bf16[48,64,512]{2,1,0:T(8,128)(2,1)} %refs_0_, bf16[24,64,512]{2,1,0:T(8,128)(2,1)} %collective-permute-done.1.refs_1_, bf16[24,64,512]{2,1,0:T(8,128)(2,1)} %collective-permute-done.2.refs_2_, ...), custom_call_target="tpu_custom_call" | custom-call | bytes 8388608 | tf_op jit(solution)/shard_map/assemble/pallas_call | solution.py:284
  329.7 15.1 %all-to-all-done.1 = bf16[16,64,1024]{2,1,0:T(8,128)(2,1)} async-done(((bf16[16,64,1024]{2,1,0:T(8,128)(2,1)}), bf16[16,64,1024]{2,1,0:T(8,128)(2,1)}, u32[]{:S(2)}, u32[]{:S(2)}) %all-to-all-start.1) | async-done | bytes 2097184 | tf_op jit(solution)/shard_map/all_to_all | solution.py:363
  344.8 13.0 %attend.1 = bf16[512,1024]{1,0:T(8,128)(2,1)} custom-call(s32[4,32]{1,0:T(4,128)} %pad_add_fusion.1.steps_ref, s32[64]{0:T(128)} %get-tuple-element.75.source_ref, s32[64]{0:T(128)} %get-tuple-element.74.place_ref, bf16[512,1024]{1,0:T(8,128)(2,1)} %copy.52.spread_hbm, bf16[1024,1024]{1,0:T(8,128)(2,1)} %bitcast.24.up_any, f32[512,1024]{1,0:T(8,128)} %fusion.27.base_hbm, ...), custom_call_target="tpu_custom_call" | custom-call | flops 2684354560 | bytes 12582912 | tf_op jit(solution)/shard_map/attend/pallas_call | solution.py:174
  (77 shorter events, 7.2 us)
Async XLA Ops:
  7.2 63.4 %all-gather.2.cloned.1.call-start = ((), (), s32[]{:S(2)}) async-start(), calls=%async_computation.2 | async-start | bytes 10485760 | tf_op jit(solution)/shard_map/all_gather | solution.py:352
  9.3 13.8 %all-to-all-start = ((s32[8,1,160]{2,1,0:T(1,128)}), s32[8,1,160]{2,1,0:T(1,128)S(1)}, u32[]{:S(2)}, u32[]{:S(2)}) async-start(s32[8,1,160]{2,1,0:T(1,128)} %broadcast_in_dim.188), calls=%async_computation | async-start | bytes 16384 | tf_op jit(solution)/shard_map/all_to_all | solution.py:323
  26.6 145.6 %collective-permute-start = (bf16[48,64,512]{2,1,0:T(8,128)(2,1)}, bf16[48,64,512]{2,1,0:T(8,128)(2,1)S(1)}, u32[]{:S(2)}, u32[]{:S(2)}) collective-permute-start(bf16[48,64,512]{2,1,0:T(8,128)(2,1)} %refs_0_), channel_id=1, source_target_pairs={{0,16},{4,20},{8,24},{12,28},{16,0},{20,4},{24,8},{28,12},{1,17},{... | collective-permute-start | bytes 9437192 | tf_op jit(solution)/shard_map/ppermute | solution.py:318
  35.0 61.7 %collective-permute-start.1 = (bf16[24,64,512]{2,1,0:T(8,128)(2,1)}, bf16[24,64,512]{2,1,0:T(8,128)(2,1)}, u32[]{:S(2)}, u32[]{:S(2)}) collective-permute-start(bf16[24,64,512]{2,1,0:T(8,128)(2,1)} %get-tuple-element.42), channel_id=1, source_target_pairs={{0,4},{4,0},{8,12},{12,8},{16,20},{20,16},{24,28},{28,24},{1,5},{5... | collective-permute-start | bytes 4718600 | tf_op jit(solution)/shard_map/ppermute | solution.py:318
  35.4 95.7 %collective-permute-start.2 = (bf16[24,64,512]{2,1,0:T(8,128)(2,1)}, bf16[24,64,512]{2,1,0:T(8,128)(2,1)}, u32[]{:S(2)}, u32[]{:S(2)}) collective-permute-start(bf16[24,64,512]{2,1,0:T(8,128)(2,1)} %get-tuple-element.43), channel_id=1, source_target_pairs={{0,8},{4,12},{8,0},{12,4},{16,24},{20,28},{24,16},{28,20},{1,9},{5... | collective-permute-start | bytes 4718600 | tf_op jit(solution)/shard_map/ppermute | solution.py:318
  38.6 133.5 %collective-permute-start.3 = (bf16[24,64,512]{2,1,0:T(8,128)(2,1)}, bf16[24,64,512]{2,1,0:T(8,128)(2,1)}, u32[]{:S(2)}, u32[]{:S(2)}) collective-permute-start(bf16[24,64,512]{2,1,0:T(8,128)(2,1)} %get-tuple-element.44), channel_id=1, source_target_pairs={{0,12},{4,8},{8,4},{12,0},{16,28},{20,24},{24,20},{28,16},{1,13},{... | collective-permute-start | bytes 4718600 | tf_op jit(solution)/shard_map/ppermute | solution.py:318
  70.6 18.3 %copy-start.4 = (bf16[512,8192]{1,0:T(8,128)(2,1)S(1)}, bf16[512,8192]{1,0:T(8,128)(2,1)}, u32[]{:S(2)}) copy-start(bf16[512,8192]{1,0:T(8,128)(2,1)} %all-gather.2.cloned.1.call-done) | copy-start | bytes 25165828
  88.9 93.3 %copy-start.6 = (bf16[2,64,2048]{2,1,0:T(8,128)(2,1)S(1)}, bf16[2,64,2048]{2,1,0:T(8,128)(2,1)}, u32[]{:S(2)}) copy-start(bf16[2,64,2048]{2,1,0:T(8,128)(2,1)} %get-tuple-element.48) | copy-start | bytes 1572868
  88.9 94.4 %copy-start.5 = (bf16[2,64,2048]{2,1,0:T(8,128)(2,1)S(1)}, bf16[2,64,2048]{2,1,0:T(8,128)(2,1)}, u32[]{:S(2)}) copy-start(bf16[2,64,2048]{2,1,0:T(8,128)(2,1)} %get-tuple-element.49) | copy-start | bytes 1572868
  88.9 97.1 %copy-start.3 = (s32[64,1]{0,1:T(1,128)S(1)}, s32[64,1]{0,1:T(1,128)}, u32[]{:S(2)}) copy-start(s32[64,1]{0,1:T(1,128)} %param.20) | copy-start | bytes 772
  172.1 98.9 %copy-start = (bf16[48,64,512]{2,1,0:T(8,128)(2,1)}, bf16[48,64,512]{2,1,0:T(8,128)(2,1)S(1)}, u32[]{:S(2)}) copy-start(bf16[48,64,512]{2,1,0:T(8,128)(2,1)S(1)} %collective-permute-done.store_ref.refs_4_) | copy-start | bytes 9437188
  178.6 92.4 %collective-permute-start.10 = (bf16[16,64,512]{2,1,0:T(8,128)(2,1)}, bf16[16,64,512]{2,1,0:T(8,128)(2,1)}, u32[]{:S(2)}, u32[]{:S(2)}) collective-permute-start(bf16[16,64,512]{2,1,0:T(8,128)(2,1)} %get-tuple-element.55), channel_id=1, source_target_pairs={{0,12},{4,8},{8,4},{12,0},{16,28},{20,24},{24,20},{28,16},{1,13},{... | collective-permute-start | bytes 3145736 | tf_op jit(solution)/shard_map/ppermute | solution.py:318
  178.7 92.3 %collective-permute-start.8 = (bf16[16,64,512]{2,1,0:T(8,128)(2,1)}, bf16[16,64,512]{2,1,0:T(8,128)(2,1)}, u32[]{:S(2)}, u32[]{:S(2)}) collective-permute-start(bf16[16,64,512]{2,1,0:T(8,128)(2,1)} %get-tuple-element.53), channel_id=1, source_target_pairs={{0,4},{4,0},{8,12},{12,8},{16,20},{20,16},{24,28},{28,24},{1,5},{5... | collective-permute-start | bytes 3145736 | tf_op jit(solution)/shard_map/ppermute | solution.py:318
  180.2 90.9 %collective-permute-start.9 = (bf16[16,64,512]{2,1,0:T(8,128)(2,1)}, bf16[16,64,512]{2,1,0:T(8,128)(2,1)}, u32[]{:S(2)}, u32[]{:S(2)}) collective-permute-start(bf16[16,64,512]{2,1,0:T(8,128)(2,1)} %get-tuple-element.54), channel_id=1, source_target_pairs={{0,8},{4,12},{8,0},{12,4},{16,24},{20,28},{24,16},{28,20},{1,9},{5... | collective-permute-start | bytes 3145736 | tf_op jit(solution)/shard_map/ppermute | solution.py:318
  182.2 54.1 %collective-permute-start.4 = (bf16[2,64,2048]{2,1,0:T(8,128)(2,1)S(1)}, bf16[2,64,2048]{2,1,0:T(8,128)(2,1)}, u32[]{:S(2)}, u32[]{:S(2)}) collective-permute-start(bf16[2,64,2048]{2,1,0:T(8,128)(2,1)S(1)} %copy-done.6), channel_id=1, source_target_pairs={{0,16},{4,20},{8,24},{12,28},{16,0},{20,4},{24,8},{28,12},{1,17},{... | collective-permute-start | bytes 1572872 | tf_op jit(solution)/shard_map/ppermute | solution.py:318
  183.3 64.3 %collective-permute-start.5 = (bf16[2,64,2048]{2,1,0:T(8,128)(2,1)S(1)}, bf16[2,64,2048]{2,1,0:T(8,128)(2,1)}, u32[]{:S(2)}, u32[]{:S(2)}) collective-permute-start(bf16[2,64,2048]{2,1,0:T(8,128)(2,1)S(1)} %copy-done.5), channel_id=1, source_target_pairs={{0,20},{4,16},{8,28},{12,24},{16,4},{20,0},{24,12},{28,8},{1,21},{... | collective-permute-start | bytes 1572872 | tf_op jit(solution)/shard_map/ppermute | solution.py:318
  236.3 25.4 %collective-permute-start.6 = (bf16[2,64,2048]{2,1,0:T(8,128)(2,1)}, bf16[2,64,2048]{2,1,0:T(8,128)(2,1)}, u32[]{:S(2)}, u32[]{:S(2)}) collective-permute-start(bf16[2,64,2048]{2,1,0:T(8,128)(2,1)} %get-tuple-element.50), channel_id=1, source_target_pairs={{0,24},{4,28},{8,16},{12,20},{16,8},{20,12},{24,0},{28,4},{1,25},{... | collective-permute-start | bytes 1572872 | tf_op jit(solution)/shard_map/ppermute | solution.py:318
  247.6 23.5 %collective-permute-start.7 = (bf16[2,64,2048]{2,1,0:T(8,128)(2,1)}, bf16[2,64,2048]{2,1,0:T(8,128)(2,1)}, u32[]{:S(2)}, u32[]{:S(2)}) collective-permute-start(bf16[2,64,2048]{2,1,0:T(8,128)(2,1)} %get-tuple-element.51), channel_id=1, source_target_pairs={{0,28},{4,24},{8,20},{12,16},{16,12},{20,8},{24,4},{28,0},{1,29},{... | collective-permute-start | bytes 1572872 | tf_op jit(solution)/shard_map/ppermute | solution.py:318
  251.7 43.7 %copy-start.2 = (s32[64]{0:T(128)S(1)}, s32[64]{0:T(128)}, u32[]{:S(2)}) copy-start(s32[64]{0:T(128)} %param.21) | copy-start | bytes 772
  271.1 73.8 %all-to-all-start.1 = ((bf16[16,64,1024]{2,1,0:T(8,128)(2,1)}), bf16[16,64,1024]{2,1,0:T(8,128)(2,1)}, u32[]{:S(2)}, u32[]{:S(2)}) async-start(bf16[16,64,1024]{2,1,0:T(8,128)(2,1)} %gather_fusion.2), calls=%async_computation.1 | async-start | bytes 4194304 | tf_op jit(solution)/shard_map/all_to_all | solution.py:363
  298.2 2.5 copy-start.7
  300.7 6.9 %copy-start.1 = (bf16[512,2048]{1,0:T(8,128)(2,1)S(1)}, bf16[512,2048]{1,0:T(8,128)(2,1)}, u32[]{:S(2)}) copy-start(bf16[512,2048]{1,0:T(8,128)(2,1)} %param.11) | copy-start | bytes 6291460
Sparse Core Ops, SparseCore 0:
  9.6 60.9 all-gather.1

commit v16 on v14

--- a/solution.py
+++ b/solution.py
@@ -53,12 +53,13 @@
 def attention_kernel(
     last, steps_ref, source_ref, place_ref, spread_hbm, up_any, base_hbm, fresh_hbm, pages_hbm, last_hbm, *rest
 ):
-    out_ref, query_ref, spread_ref, up_ref, base_ref, cache_ref, sems, tile_sems = rest
+    out_ref, query_ref, spread_ref, up_ref, base_ref, cache_ref, spread_sem, group_sems, tile_sems = rest
     q_cols = base_ref.shape[1]
     kv_heads = cache_ref.shape[2] // (2 * HEAD_WIDTH)
     group = q_cols // HEAD_WIDTH // kv_heads
     page = pages_hbm.shape[1]
     held = HITS * page
+    groups = cache_ref.shape[0] // TOGETHER
     sharp = HEAD_WIDTH ** -0.5 * math.log2(math.e)
 
     def tile_copies(index):
@@ -71,25 +72,27 @@
     def fetch(index, carry):
         rows = pl.ds(pl.multiple_of(index % HITS * page, page), page)
         to = cache_ref.at[index // HITS, rows]
+        sem = group_sems.at[index // (HITS * TOGETHER)]
         late = source_ref[index] == last
 
         @pl.when(late)
         def _():
-            pltpu.make_async_copy(last_hbm.at[place_ref[index]], to, sems.at[1]).start()
+            pltpu.make_async_copy(last_hbm.at[place_ref[index]], to, sem).start()
 
         @pl.when(jnp.logical_not(late))
         def _():
-            pltpu.make_async_copy(pages_hbm.at[index], to, sems.at[1]).start()
+            pltpu.make_async_copy(pages_hbm.at[index], to, sem).start()
 
         return carry
 
-    spread_copy = pltpu.make_async_copy(spread_hbm, spread_ref, sems.at[0])
-    fresh_copy = pltpu.make_async_copy(fresh_hbm, cache_ref.at[:, held:], sems.at[2])
+    spread_copy = pltpu.make_async_copy(spread_hbm, spread_ref, spread_sem)
     spread_copy.start()
     for index in range(q_cols // TILE):
         for copy in tile_copies(index):
             copy.start()
-    fresh_copy.start()
+    for index in range(groups):
+        rows = pl.ds(index * TOGETHER, TOGETHER)
+        pltpu.make_async_copy(fresh_hbm.at[rows], cache_ref.at[rows, held:], group_sems.at[index]).start()
     lax.fori_loop(0, pages_hbm.shape[0], fetch, 0)
     spread_copy.wait()
 
@@ -102,9 +105,6 @@
         return carry
 
     lax.fori_loop(0, q_cols // TILE, project, 0)
-    fresh_copy.wait()
-    prefix = cache_ref.at[:, :held]
-    pltpu.make_async_copy(prefix, prefix, sems.at[1]).wait()
     dims = (((1,), (1,)), ((), ()))
     tall = group * BLOCK
     q_at = lax.broadcasted_iota(jnp.int32, (kv_heads * tall, MOST), 0) % BLOCK
@@ -125,6 +125,11 @@
         return jnp.concatenate(heads, axis=0)
 
     def several(turn, carry):
+        @pl.when(turn < groups)
+        def _():
+            mine = cache_ref.at[pl.ds(turn * TOGETHER, TOGETHER)]
+            pltpu.make_async_copy(mine, mine, group_sems.at[turn]).wait()
+
         places = []
         for lane in range(TOGETHER):
             index = turn * TOGETHER + lane
@@ -174,16 +179,17 @@
     return pl.pallas_call(
         functools.partial(attention_kernel, last),
         out_shape=jax.ShapeDtypeStruct((rows, q_cols), jnp.bfloat16),
-        in_specs=[scalars] * 3 + [hbm] * 6,
+        in_specs=[scalars] * 3 + [hbm, pl.BlockSpec(memory_space=pl.ANY)] + [hbm] * 4,
         out_specs=pl.BlockSpec(memory_space=pltpu.VMEM),
         scratch_shapes=[
             pltpu.VMEM((rows, q_cols), jnp.bfloat16),
             *[pltpu.VMEM(each.shape, each.dtype) for each in (spread, up, query_base)],
             pltpu.VMEM((requests, keys, pages.shape[2]), pages.dtype),
-            pltpu.SemaphoreType.DMA((3,)),
+            pltpu.SemaphoreType.DMA,
+            pltpu.SemaphoreType.DMA((requests // TOGETHER,)),
             pltpu.SemaphoreType.DMA((2, q_cols // TILE)),
         ],
-        compiler_params=pltpu.CompilerParams(vmem_limit_bytes=VMEM_GRANT),
+        compiler_params=pltpu.CompilerParams(vmem_limit_bytes=VMEM_GRANT - 2 * up.size),
         cost_estimate=pl.CostEstimate(
             flops=4 * steps_total * BLOCK * q_cols * keys + 2 * spread.size * q_cols,
             bytes_accessed=4 * query_base.size + 2 * (2 * spread.size + up.size + fresh.size + pages.size),

time: 346 us -> 346 us (level)
  no operation moved by 1% of the time
where the time goes in v16:
time: 346 us; the launch traced here: 344 us
  waiting for transfers between devices  203 us (59%)
  matrix products  34.1 us (10%)
  Pallas kernels  30 us (9%)
  starting transfers between devices  26.9 us (8%)
  local copies, waits for them, and re-layouts  18 us (5%)
  between operations  14.9 us (4%)
  blocking collectives  12.2 us (4%)
  other arithmetic  5.1 us (1%)
    ppermute x7, waiting for transfers between devices, swap(): lax.ppermute(array, 'dp', [(peer, peer ^ distance) for peer in range(peer...  164 us
    all_gather x1, waiting for transfers between devices, on_device(): piece = lax.all_gather(tokens, 'tensor', axis=1, tiled=True)  29.3 us
    dot_general x1, matrix products, on_device(): jnp.dot(piece, query_weight, preferred_element_type=jnp.float32)  18.2 us
    pallas_call x1, Pallas kernels, attend(): pl.pallas_call(functools.partial(attention_kernel, last), out_shape=jax.S...  13.4 us
    psum x1, blocking collectives, on_device(): shrink = lax.psum(shrink_part, 'tensor').astype(jnp.bfloat16)  12.2 us
    pallas_call x2, Pallas kernels, serve(): pl.pallas_call(serve_kernel, out_shape=[jax.ShapeDtypeStruct(shape, store...  11.5 us
    ppermute x7, starting transfers between devices, swap(): lax.ppermute(array, 'dp', [(peer, peer ^ distance) for peer in range(peer...  10.4 us
    dot_general x1, matrix products, on_device(): jnp.dot(piece, keyvalue_weight, preferred_element_type=jnp.float32)  7.7 us
  transfers between devices with their start and end apart: 11, of which 9 were waited for; matrix products, arithmetic and copies ran while one was open for 16% of the time, Pallas kernels for 5%

profile of v16, /device:TPU:0, one launch (start us, length us, event | category | flops | bytes accessed | tf_op | source)
XLA Modules:
  0.0 343.9 jit_solution(1701347060114062585)
XLA Ops:
  7.2 0.7 all-gather.2.cloned.1.call-update
  7.9 0.8 pad_add_fusion.1
  8.7 0.6 broadcast_in_dim.175
  9.3 7.3 %all-to-all-start = ((s32[8,1,160]{2,1,0:T(1,128)}), s32[8,1,160]{2,1,0:T(1,128)S(1)}, u32[]{:S(2)}, u32[]{:S(2)}) async-start(s32[8,1,160]{2,1,0:T(1,128)} %broadcast_in_dim.175), calls=%async_computation | async-start | bytes 16384 | tf_op jit(solution)/shard_map/all_to_all | solution.py:293
  16.6 6.5 %all-to-all-done = s32[8,1,160]{2,1,0:T(1,128)S(1)} async-done(((s32[8,1,160]{2,1,0:T(1,128)}), s32[8,1,160]{2,1,0:T(1,128)S(1)}, u32[]{:S(2)}, u32[]{:S(2)}) %all-to-all-start) | async-done | bytes 5152 | tf_op jit(solution)/shard_map/all_to_all | solution.py:293
  23.1 0.3 convert_reduce_fusion.1
  23.4 0.1 select_reduce_fusion.3
  23.7 0.6 collective-permute-start
  24.3 0.6 gather_fusion.2
  24.9 0.2 convert_reduce_fusion
  25.2 0.2 select_reduce_fusion
  25.4 0.6 reshape.387.asked_ref
  26.0 5.4 %serve.2 = (bf16[16,64,512]{2,1,0:T(8,128)(2,1)}, bf16[16,64,512]{2,1,0:T(8,128)(2,1)}, bf16[16,64,512]{2,1,0:T(8,128)(2,1)}) custom-call(s32[48]{0:T(128)} %reshape.387.asked_ref, bf16[48,64,512]{2,1,0:T(8,128)(2,1)} %refs_0_), custom_call_target="tpu_custom_call" | custom-call | bytes 6291456 | tf_op jit(solution)/shard_map/serve/pallas_call | solution.py:215
  31.5 1.7 collective-permute-start.2
  33.2 1.8 collective-permute-start.3
  35.1 6.3 %gather_fusion.1 = bf16[16,2048,64]{1,2,0:T(8,128)(2,1)} fusion(bf16[32,2048,64]{1,2,0:T(8,128)(2,1)} %param.14, s32[1024]{0:T(1024)S(1)} %pad_clamp_fusion.1), kind=kCustom, calls=%fused_computation.1 | custom fusion | bytes 8388672 | tf_op jit(solution)/shard_map/gather | solution.py:314
  41.4 29.3 %all-gather.2.cloned.1.call-done = bf16[512,8192]{1,0:T(8,128)(2,1)} async-done(((bf16[512,2048]{1,0:T(8,128)(2,1)}), bf16[512,8192]{1,0:T(8,128)(2,1)}) %all-gather.2.cloned.1.call-update) | async-done | bytes 8388624 | tf_op jit(solution)/shard_map/all_gather | solution.py:317
  70.6 18.2 %fusion.26.base_hbm = f32[512,1024]{1,0:T(8,128)} fusion(bf16[512,8192]{1,0:T(8,128)(2,1)} %all-gather.2.cloned.1.call-done, bf16[8192,1024]{1,0:T(8,128)(2,1)} %param.12), kind=kOutput, calls=%fused_computation.94 | convolution fusion | flops 8589934592 | bytes 27262976 | tf_op jit(solution)/shard_map/dot_general | solution.py:318
  88.9 7.7 %convolution_convert_fusion = bf16[512,512]{1,0:T(8,128)(2,1)} fusion(bf16[512,8192]{1,0:T(8,128)(2,1)S(1)} %copy-done.11, bf16[8192,512]{1,0:T(8,128)(2,1)} %param.13), kind=kOutput, calls=%fused_computation.11 | convolution fusion | flops 4295229440 | bytes 17301504 | tf_op jit(solution)/shard_map/dot_general | solution.py:319
  96.6 19.0 %collective-permute-done.2.refs_2_ = bf16[16,64,512]{2,1,0:T(8,128)(2,1)} collective-permute-done((bf16[16,64,512]{2,1,0:T(8,128)(2,1)}, bf16[16,64,512]{2,1,0:T(8,128)(2,1)}, u32[]{:S(2)}, u32[]{:S(2)}) %collective-permute-start.2) | collective-permute-done | bytes 1048608 | tf_op jit(solution)/shard_map/ppermute | solution.py:288
  115.6 19.9 %collective-permute-done.3.refs_3_ = bf16[16,64,512]{2,1,0:T(8,128)(2,1)} collective-permute-done((bf16[16,64,512]{2,1,0:T(8,128)(2,1)}, bf16[16,64,512]{2,1,0:T(8,128)(2,1)}, u32[]{:S(2)}, u32[]{:S(2)}) %collective-permute-start.3) | collective-permute-done | bytes 1048608 | tf_op jit(solution)/shard_map/ppermute | solution.py:288
  135.5 25.1 %collective-permute-done.store_ref.refs_4_ = bf16[48,64,512]{2,1,0:T(8,128)(2,1)S(1)} collective-permute-done((bf16[48,64,512]{2,1,0:T(8,128)(2,1)}, bf16[48,64,512]{2,1,0:T(8,128)(2,1)S(1)}, u32[]{:S(2)}, u32[]{:S(2)}) %collective-permute-start) | collective-permute-done | bytes 3145760 | tf_op jit(solution)/shard_map/ppermute | solution.py:288
  160.6 4.5 %all-to-all-start.1 = ((bf16[16,2048,64]{1,2,0:T(8,128)(2,1)}), bf16[16,2048,64]{1,2,0:T(8,128)(2,1)}, u32[]{:S(2)}, u32[]{:S(2)}) async-start(bf16[16,2048,64]{1,2,0:T(8,128)(2,1)} %gather_fusion.1), calls=%async_computation.1 | async-start | bytes 8388608 | tf_op jit(solution)/shard_map/all_to_all | solution.py:324
  165.3 6.1 %serve.3 = (bf16[16,64,512]{2,1,0:T(8,128)(2,1)}, bf16[16,64,512]{2,1,0:T(8,128)(2,1)}, bf16[16,64,512]{2,1,0:T(8,128)(2,1)S(1)}) custom-call(s32[48]{0:T(128)S(1)} %reshape.388.asked_ref, bf16[48,64,512]{2,1,0:T(8,128)(2,1)S(1)} %collective-permute-done.store_ref.refs_4_), custom_call_target="tpu_custom_call" | custom-call | bytes 6291456 | tf_op jit(solution)/shard_map/serve/pallas_call | solution.py:215
  171.4 1.0 copy-done.1
  172.4 1.9 collective-permute-start.4
  174.3 1.5 collective-permute-start.5
  175.9 0.1 fusion.24
  176.1 0.6 slice.35
  177.4 4.3 %gather_fusion = bf16[16,64,1024]{2,1,0:T(8,128)(2,1)} fusion(bf16[32,64,1024]{2,1,0:T(8,128)(2,1)} %param.15, s32[1024]{0:T(1024)S(1)} %pad_clamp_fusion.1), kind=kCustom, calls=%fused_computation | custom fusion | bytes 4194368 | tf_op jit(solution)/shard_map/gather | solution.py:315
  181.7 53.6 %collective-permute-done.4.refs_5_ = bf16[16,64,512]{2,1,0:T(8,128)(2,1)S(1)} collective-permute-done((bf16[16,64,512]{2,1,0:T(8,128)(2,1)}, bf16[16,64,512]{2,1,0:T(8,128)(2,1)S(1)}, u32[]{:S(2)}, u32[]{:S(2)}) %collective-permute-start.4) | collective-permute-done | bytes 1048608 | tf_op jit(solution)/shard_map/ppermute | solution.py:288
  235.3 21.7 %collective-permute-done.5.refs_6_ = bf16[16,64,512]{2,1,0:T(8,128)(2,1)S(1)} collective-permute-done((bf16[16,64,512]{2,1,0:T(8,128)(2,1)}, bf16[16,64,512]{2,1,0:T(8,128)(2,1)S(1)}, u32[]{:S(2)}, u32[]{:S(2)}) %collective-permute-start.5) | collective-permute-done | bytes 1048608 | tf_op jit(solution)/shard_map/ppermute | solution.py:288
  257.0 1.8 all-to-all-done.1
  258.8 4.7 %all-to-all-start.2 = ((bf16[16,64,1024]{2,1,0:T(8,128)(2,1)}), bf16[16,64,1024]{2,1,0:T(8,128)(2,1)S(1)}, u32[]{:S(2)}, u32[]{:S(2)}) async-start(bf16[16,64,1024]{2,1,0:T(8,128)(2,1)} %gather_fusion), calls=%async_computation.2 | async-start | bytes 4194304 | tf_op jit(solution)/shard_map/all_to_all | solution.py:328
  263.7 0.6 pad_add_fusion.steps_ref
  264.3 0.2 convert_reduce_fusion.2
  264.5 0.2 convert_reduce_fusion.3
  264.8 0.6 compare_select_fusion.4
  265.5 3.0 collective-permute-start.6
  268.5 3.6 %fusion.1 = bf16[2048,512]{1,0:T(8,128)(2,1)} fusion(bf16[512,512]{1,0:T(8,128)(2,1)} %convolution_convert_fusion, s32[2048]{0:T(1024)S(1)} %add_bitcast_fusion), kind=kOutput, calls=%fused_computation.5 | convolution fusion | flops 1075838976 | bytes 2629632 | tf_op jit(solution)/shard_map/dot_general | solution.py:347
  272.1 4.6 %fusion.2 = f32[512,64]{0,1:T(8,128)S(1)} fusion(bf16[16,2048,64]{1,2,0:T(8,128)(2,1)} %all-to-all-done.1, bf16[512,2048]{1,0:T(8,128)(2,1)S(1)} %copy-done.4, pred[512,16]{0,1:T(8,128)(4,1)S(1)} %iota_compare_fusion.5), kind=kOutput, calls=%fused_computation.7 | convolution fusion | flops 2148499456 | bytes 6430720 | tf_op jit(solution)/shard_map/tn,snk->tsk/dot_general | solution.py:339
  276.7 12.2 %all-reduce.1 = bf16[512,64]{0,1:T(8,128)(2,1)S(1)} all-reduce(f32[512,64]{0,1:T(8,128)S(1)} %fusion.2), channel_id=1, replica_groups=mesh['dp'=8,'tensor'=4] {'tensor'}, use_global_device_ids=true, to_apply=%region_16.17 | all-reduce | flops 32768 | bytes 196608 | tf_op jit(solution)/shard_map/psum | solution.py:341
  288.9 1.0 broadcast_select_fusion
  289.9 2.3 copy.37.spread_hbm
  292.2 5.1 %assemble.1.pages_hbm = bf16[64,64,512]{2,1,0:T(8,128)(2,1)} custom-call(s32[64]{0:T(128)} %get-tuple-element.51.source_ref, s32[64]{0:T(128)} %get-tuple-element.50.place_ref, bf16[48,64,512]{2,1,0:T(8,128)(2,1)} %refs_0_, bf16[16,64,512]{2,1,0:T(8,128)(2,1)} %collective-permute-done.1.refs_1_, bf16[16,64,512]{2,1,0:T(8,128)(2,1)} %collective-permute-done.2.refs_2_, ...), custom_call_target="tpu_custom_call" | custom-call | bytes 8388608 | tf_op jit(solution)/shard_map/assemble/pallas_call | solution.py:254
  297.3 25.1 %collective-permute-done.6.last_hbm = bf16[16,64,512]{2,1,0:T(8,128)(2,1)} collective-permute-done((bf16[16,64,512]{2,1,0:T(8,128)(2,1)S(1)}, bf16[16,64,512]{2,1,0:T(8,128)(2,1)}, u32[]{:S(2)}, u32[]{:S(2)}) %collective-permute-start.6) | collective-permute-done | bytes 1048608 | tf_op jit(solution)/shard_map/ppermute | solution.py:288
  322.4 1.3 copy-done.3
  323.7 13.4 %attend.1 = bf16[512,1024]{1,0:T(8,128)(2,1)} custom-call(s32[4,32]{1,0:T(4,128)} %pad_add_fusion.steps_ref, s32[64]{0:T(128)} %get-tuple-element.51.source_ref, s32[64]{0:T(128)} %get-tuple-element.50.place_ref, bf16[512,1024]{1,0:T(8,128)(2,1)} %copy.37.spread_hbm, bf16[1024,1024]{1,0:T(8,128)(2,1)} %bitcast.62, f32[512,1024]{1,0:T(8,128)} %fusion.26.base_hbm, ...), custom_call_target="tpu_custom_call" | custom-call | flops 2684354560 | bytes 12582912 | tf_op jit(solution)/shard_map/attend/pallas_call | solution.py:179
  (56 shorter events, 1.4 us)
Async XLA Ops:
  7.2 63.5 %all-gather.2.cloned.1.call-start = ((), (), s32[]{:S(2)}) async-start(), calls=%async_computation.3 | async-start | bytes 10485760 | tf_op jit(solution)/shard_map/all_gather | solution.py:317
  9.3 13.8 %all-to-all-start = ((s32[8,1,160]{2,1,0:T(1,128)}), s32[8,1,160]{2,1,0:T(1,128)S(1)}, u32[]{:S(2)}, u32[]{:S(2)}) async-start(s32[8,1,160]{2,1,0:T(1,128)} %broadcast_in_dim.175), calls=%async_computation | async-start | bytes 16384 | tf_op jit(solution)/shard_map/all_to_all | solution.py:293
  23.7 136.9 %collective-permute-start = (bf16[48,64,512]{2,1,0:T(8,128)(2,1)}, bf16[48,64,512]{2,1,0:T(8,128)(2,1)S(1)}, u32[]{:S(2)}, u32[]{:S(2)}) collective-permute-start(bf16[48,64,512]{2,1,0:T(8,128)(2,1)} %refs_0_), channel_id=1, source_target_pairs={{0,16},{4,20},{8,24},{12,28},{16,0},{20,4},{24,8},{28,12},{1,17},{... | collective-permute-start | bytes 9437192 | tf_op jit(solution)/shard_map/ppermute | solution.py:288
  31.4 65.2 %collective-permute-start.1 = (bf16[16,64,512]{2,1,0:T(8,128)(2,1)}, bf16[16,64,512]{2,1,0:T(8,128)(2,1)}, u32[]{:S(2)}, u32[]{:S(2)}) collective-permute-start(bf16[16,64,512]{2,1,0:T(8,128)(2,1)} %get-tuple-element.26), channel_id=1, source_target_pairs={{0,4},{4,0},{8,12},{12,8},{16,20},{20,16},{24,28},{28,24},{1,5},{5... | collective-permute-start | bytes 3145736 | tf_op jit(solution)/shard_map/ppermute | solution.py:288
  31.5 84.1 %collective-permute-start.2 = (bf16[16,64,512]{2,1,0:T(8,128)(2,1)}, bf16[16,64,512]{2,1,0:T(8,128)(2,1)}, u32[]{:S(2)}, u32[]{:S(2)}) collective-permute-start(bf16[16,64,512]{2,1,0:T(8,128)(2,1)} %get-tuple-element.27), channel_id=1, source_target_pairs={{0,8},{4,12},{8,0},{12,4},{16,24},{20,28},{24,16},{28,20},{1,9},{5... | collective-permute-start | bytes 3145736 | tf_op jit(solution)/shard_map/ppermute | solution.py:288
  33.2 102.3 %collective-permute-start.3 = (bf16[16,64,512]{2,1,0:T(8,128)(2,1)}, bf16[16,64,512]{2,1,0:T(8,128)(2,1)}, u32[]{:S(2)}, u32[]{:S(2)}) collective-permute-start(bf16[16,64,512]{2,1,0:T(8,128)(2,1)} %get-tuple-element.28), channel_id=1, source_target_pairs={{0,12},{4,8},{8,4},{12,0},{16,28},{20,24},{24,20},{28,16},{1,13},{... | collective-permute-start | bytes 3145736 | tf_op jit(solution)/shard_map/ppermute | solution.py:288
  70.6 18.2 %copy-start.11 = (bf16[512,8192]{1,0:T(8,128)(2,1)S(1)}, bf16[512,8192]{1,0:T(8,128)(2,1)}, u32[]{:S(2)}) copy-start(bf16[512,8192]{1,0:T(8,128)(2,1)} %all-gather.2.cloned.1.call-done) | copy-start | bytes 25165828
  96.6 79.2 %copy-start.7 = (s32[1,16]{1,0:T(1,128)S(1)}, s32[1,16]{1,0:T(1,128)}, u32[]{:S(2)}) copy-start(s32[1,16]{1,0:T(1,128)} %param.17) | copy-start | bytes 196
  160.6 4.7 %copy-start = (bf16[48,64,512]{2,1,0:T(8,128)(2,1)}, bf16[48,64,512]{2,1,0:T(8,128)(2,1)S(1)}, u32[]{:S(2)}) copy-start(bf16[48,64,512]{2,1,0:T(8,128)(2,1)S(1)} %collective-permute-done.store_ref.refs_4_) | copy-start | bytes 9437188
  160.6 98.2 %all-to-all-start.1 = ((bf16[16,2048,64]{1,2,0:T(8,128)(2,1)}), bf16[16,2048,64]{1,2,0:T(8,128)(2,1)}, u32[]{:S(2)}, u32[]{:S(2)}) async-start(bf16[16,2048,64]{1,2,0:T(8,128)(2,1)} %gather_fusion.1), calls=%async_computation.1 | async-start | bytes 8388608 | tf_op jit(solution)/shard_map/all_to_all | solution.py:324
  171.4 1.0 copy-start.1
  172.4 62.9 %collective-permute-start.4 = (bf16[16,64,512]{2,1,0:T(8,128)(2,1)}, bf16[16,64,512]{2,1,0:T(8,128)(2,1)S(1)}, u32[]{:S(2)}, u32[]{:S(2)}) collective-permute-start(bf16[16,64,512]{2,1,0:T(8,128)(2,1)} %get-tuple-element.31), channel_id=1, source_target_pairs={{0,4},{4,0},{8,12},{12,8},{16,20},{20,16},{24,28},{28,24},{1,5},{5... | collective-permute-start | bytes 3145736 | tf_op jit(solution)/shard_map/ppermute | solution.py:288
  174.3 82.7 %collective-permute-start.5 = (bf16[16,64,512]{2,1,0:T(8,128)(2,1)}, bf16[16,64,512]{2,1,0:T(8,128)(2,1)S(1)}, u32[]{:S(2)}, u32[]{:S(2)}) collective-permute-start(bf16[16,64,512]{2,1,0:T(8,128)(2,1)} %get-tuple-element.32), channel_id=1, source_target_pairs={{0,8},{4,12},{8,0},{12,4},{16,24},{20,28},{24,16},{28,20},{1,9},{5... | collective-permute-start | bytes 3145736 | tf_op jit(solution)/shard_map/ppermute | solution.py:288
  177.4 87.0 %copy-start.9 = (s32[64,1]{0,1:T(1,128)S(1)}, s32[64,1]{0,1:T(1,128)}, u32[]{:S(2)}) copy-start(s32[64,1]{0,1:T(1,128)} %param.20) | copy-start | bytes 772
  177.4 87.1 %copy-start.10 = (s32[16,1]{0,1:T(1,128)S(1)}, s32[16,1]{0,1:T(1,128)}, u32[]{:S(2)}) copy-start(s32[16,1]{0,1:T(1,128)} %param.18) | copy-start | bytes 196
  177.4 87.4 %copy-start.8 = (s32[64]{0:T(128)S(1)}, s32[64]{0:T(128)}, u32[]{:S(2)}) copy-start(s32[64]{0:T(128)} %param.21) | copy-start | bytes 772
  177.4 88.1 %copy-start.2 = (bf16[16,64,512]{2,1,0:T(8,128)(2,1)S(1)}, bf16[16,64,512]{2,1,0:T(8,128)(2,1)}, u32[]{:S(2)}) copy-start(bf16[16,64,512]{2,1,0:T(8,128)(2,1)} %copy-done.1) | copy-start | bytes 3145732
  235.3 23.5 %copy-start.5 = (bf16[16,64,512]{2,1,0:T(8,128)(2,1)}, bf16[16,64,512]{2,1,0:T(8,128)(2,1)S(1)}, u32[]{:S(2)}) copy-start(bf16[16,64,512]{2,1,0:T(8,128)(2,1)S(1)} %collective-permute-done.4.refs_5_) | copy-start | bytes 3145732
  257.0 1.8 copy-start.6
  258.8 63.5 %all-to-all-start.2 = ((bf16[16,64,1024]{2,1,0:T(8,128)(2,1)}), bf16[16,64,1024]{2,1,0:T(8,128)(2,1)S(1)}, u32[]{:S(2)}, u32[]{:S(2)}) async-start(bf16[16,64,1024]{2,1,0:T(8,128)(2,1)} %gather_fusion), calls=%async_computation.2 | async-start | bytes 4194304 | tf_op jit(solution)/shard_map/all_to_all | solution.py:328
  263.5 8.6 %copy-start.4 = (bf16[512,2048]{1,0:T(8,128)(2,1)S(1)}, bf16[512,2048]{1,0:T(8,128)(2,1)}, u32[]{:S(2)}) copy-start(bf16[512,2048]{1,0:T(8,128)(2,1)} %param.11) | copy-start | bytes 6291460
  265.5 56.9 %collective-permute-start.6 = (bf16[16,64,512]{2,1,0:T(8,128)(2,1)S(1)}, bf16[16,64,512]{2,1,0:T(8,128)(2,1)}, u32[]{:S(2)}, u32[]{:S(2)}) collective-permute-start(bf16[16,64,512]{2,1,0:T(8,128)(2,1)S(1)} %copy-done.2), channel_id=1, source_target_pairs={{0,12},{4,8},{8,4},{12,0},{16,28},{20,24},{24,20},{28,16},{1,13},{... | collective-permute-start | bytes 3145736 | tf_op jit(solution)/shard_map/ppermute | solution.py:288
  322.4 1.3 copy-start.3
Sparse Core Ops, SparseCore 0:
  9.6 61.0 all-gather.1

commit v17 on v14

--- a/solution.py
+++ b/solution.py
@@ -12,8 +12,8 @@
 ADP_CAP = 2
 HITS = 4
 MOST = 128
-BLOCK = 32
-TOGETHER = 4
+BLOCK = 16
+TOGETHER = 8
 TILE = 256
 VMEM_GRANT = 60 * 1024 * 1024
 SMALL_GRANT = 16 * 1024 * 1024
@@ -163,12 +163,10 @@
     lax.fori_loop(0, steps_ref.shape[1] // TOGETHER, several, 0)
 
 
-def attend(query_base, spread, up, fresh, pages, last_pages, source, place, last, starts, ends):
+def attend(query_base, spread, up, fresh, pages, last_pages, source, place, last, steps):
     rows, q_cols = query_base.shape
     requests = fresh.shape[0]
     keys = HITS * pages.shape[1] + MOST
-    steps_total = -(-(rows // BLOCK + requests - 1) // TOGETHER) * TOGETHER
-    steps = attention_steps(starts, ends, steps_total)
     hbm = pl.BlockSpec(memory_space=pltpu.HBM)
     scalars = pl.BlockSpec(memory_space=pltpu.SMEM)
     return pl.pallas_call(
@@ -185,7 +183,7 @@
         ],
         compiler_params=pltpu.CompilerParams(vmem_limit_bytes=VMEM_GRANT),
         cost_estimate=pl.CostEstimate(
-            flops=4 * steps_total * BLOCK * q_cols * keys + 2 * spread.size * q_cols,
+            flops=4 * steps.shape[1] * BLOCK * q_cols * keys + 2 * spread.size * q_cols,
             bytes_accessed=4 * query_base.size + 2 * (2 * spread.size + up.size + fresh.size + pages.size),
             transcendentals=0,
         ),
@@ -315,20 +313,24 @@
     down_rows, mirrored_store, query_base, new_cache, near = lax.optimization_barrier(
         (down_rows, mirrored_store, query_base, new_cache, near)
     )
+    lengths = span_token_length[0]
+    ends = jnp.cumsum(lengths)
+    starts = ends - lengths
+    row = jnp.arange(tok_rows, dtype=jnp.int32)[:, None]
+    member = (row >= starts[None, :]) & (row < ends[None, :])
+    slot = jnp.sum(jnp.where(member, adapter_pos[None, :], 0), axis=1)
+    in_slot = slot[:, None] == jnp.arange(adapter_slots, dtype=jnp.int32)[None, :]
+    steps_total = -(-(tok_rows // BLOCK + request_count - 1) // TOGETHER) * TOGETHER
+    steps = attention_steps(starts, ends, steps_total)
+
     down_sent = lax.all_to_all(down_rows, "dp", split_axis=0, concat_axis=0, tiled=True)
     far = list(serve(far_asked[1:], mirrored_store, SMALL_GRANT))
     far = [swap(pages, i + 1) for i, pages in enumerate(far[:-1])] + far[-1:]
-    up_rows, down_sent, far = lax.optimization_barrier((up_rows, down_sent, far))
+    up_rows, down_sent, far, in_slot, steps, page_source, page_place = lax.optimization_barrier(
+        (up_rows, down_sent, far, in_slot, steps, page_source, page_place)
+    )
     up_sent = lax.all_to_all(up_rows, "dp", split_axis=0, concat_axis=0, tiled=True)
     far[-1] = swap(far[-1], half - 1)
-
-    lengths = span_token_length[0]
-    ends = jnp.cumsum(lengths)
-    starts = ends - lengths
-    steps = jnp.arange(tok_rows, dtype=jnp.int32)[:, None]
-    member = (steps >= starts[None, :]) & (steps < ends[None, :])
-    slot = jnp.sum(jnp.where(member, adapter_pos[None, :], 0), axis=1)
-    in_slot = slot[:, None] == jnp.arange(adapter_slots, dtype=jnp.int32)[None, :]
 
     down_part = jnp.einsum("tn,snk->tsk", tokens, down_sent, preferred_element_type=jnp.float32)
     shrink_part = jnp.sum(jnp.where(in_slot[:, :, None], down_part, 0.0), axis=1)
@@ -342,7 +344,7 @@
     fresh = fresh.reshape(request_count, MOST, -1)
     up = up_sent.reshape(adapter_slots * rank, q_cols)
     out = attend(
-        query_base, spread, up, fresh, prefix_pages, far[-1], page_source, page_place, peers - 1, starts, ends
+        query_base, spread, up, fresh, prefix_pages, far[-1], page_source, page_place, peers - 1, steps
     )
     return (out, new_cache)
 

time: 346 us -> 344 us (level)
  no operation moved by 1% of the time
where the time goes in v17:
time: 344 us; the launch traced here: 342 us
  waiting for transfers between devices  203 us (59%)
  matrix products  34.1 us (10%)
  Pallas kernels  28.1 us (8%)
  starting transfers between devices  26.9 us (8%)
  local copies, waits for them, and re-layouts  17.9 us (5%)
  between operations  14.9 us (4%)
  blocking collectives  12.2 us (4%)
  other arithmetic  5.05 us (1%)
    ppermute x7, waiting for transfers between devices, swap(): lax.ppermute(array, 'dp', [(peer, peer ^ distance) for peer in range(peer...  165 us
    all_gather x1, waiting for transfers between devices, on_device(): piece = lax.all_gather(tokens, 'tensor', axis=1, tiled=True)  29.4 us
    dot_general x1, matrix products, on_device(): jnp.dot(piece, query_weight, preferred_element_type=jnp.float32)  18.2 us
    psum x1, blocking collectives, on_device(): shrink = lax.psum(shrink_part, 'tensor').astype(jnp.bfloat16)  12.2 us
    pallas_call x1, Pallas kernels, attend(): pl.pallas_call(functools.partial(attention_kernel, last), out_shape=jax.S...  11.8 us
    pallas_call x2, Pallas kernels, serve(): pl.pallas_call(serve_kernel, out_shape=[jax.ShapeDtypeStruct(shape, store...  11.4 us
    ppermute x7, starting transfers between devices, swap(): lax.ppermute(array, 'dp', [(peer, peer ^ distance) for peer in range(peer...  10.4 us
    dot_general x1, matrix products, on_device(): jnp.dot(piece, keyvalue_weight, preferred_element_type=jnp.float32)  7.7 us
  transfers between devices with their start and end apart: 11, of which 9 were waited for; matrix products, arithmetic and copies ran while one was open for 16% of the time, Pallas kernels for 5%

profile of v17, /device:TPU:0, one launch (start us, length us, event | category | flops | bytes accessed | tf_op | source)
XLA Modules:
  0.0 342.3 jit_solution(7030816016252897056)
XLA Ops:
  7.2 0.7 all-gather.2.cloned.1.call-update
  7.9 0.8 pad_add_fusion.1
  8.7 0.6 broadcast_in_dim.106
  9.3 7.3 %all-to-all-start = ((s32[8,1,160]{2,1,0:T(1,128)}), s32[8,1,160]{2,1,0:T(1,128)S(1)}, u32[]{:S(2)}, u32[]{:S(2)}) async-start(s32[8,1,160]{2,1,0:T(1,128)} %broadcast_in_dim.106), calls=%async_computation | async-start | bytes 16384 | tf_op jit(solution)/shard_map/all_to_all | solution.py:285
  16.6 6.5 %all-to-all-done = s32[8,1,160]{2,1,0:T(1,128)S(1)} async-done(((s32[8,1,160]{2,1,0:T(1,128)}), s32[8,1,160]{2,1,0:T(1,128)S(1)}, u32[]{:S(2)}, u32[]{:S(2)}) %all-to-all-start) | async-done | bytes 5152 | tf_op jit(solution)/shard_map/all_to_all | solution.py:285
  23.1 0.3 convert_reduce_fusion.1
  23.4 0.1 select_reduce_fusion.7
  23.7 0.6 collective-permute-start
  24.3 0.6 gather_fusion.2
  24.9 0.2 convert_reduce_fusion
  25.2 0.2 select_reduce_fusion.1
  25.4 0.6 reshape.365.asked_ref
  26.0 5.3 %serve.2 = (bf16[16,64,512]{2,1,0:T(8,128)(2,1)}, bf16[16,64,512]{2,1,0:T(8,128)(2,1)}, bf16[16,64,512]{2,1,0:T(8,128)(2,1)}) custom-call(s32[48]{0:T(128)} %reshape.365.asked_ref, bf16[48,64,512]{2,1,0:T(8,128)(2,1)} %refs_0_), custom_call_target="tpu_custom_call" | custom-call | bytes 6291456 | tf_op jit(solution)/shard_map/serve/pallas_call | solution.py:207
  31.3 1.3 collective-permute-start.1
  32.6 2.3 collective-permute-start.3
  35.0 6.3 %gather_fusion.1 = bf16[16,2048,64]{1,2,0:T(8,128)(2,1)} fusion(bf16[32,2048,64]{1,2,0:T(8,128)(2,1)} %param.14, s32[1024]{0:T(1024)S(1)} %pad_clamp_fusion.1), kind=kCustom, calls=%fused_computation.1 | custom fusion | bytes 8388672 | tf_op jit(solution)/shard_map/gather | solution.py:306
  41.2 29.4 %all-gather.2.cloned.1.call-done = bf16[512,8192]{1,0:T(8,128)(2,1)} async-done(((bf16[512,2048]{1,0:T(8,128)(2,1)}), bf16[512,8192]{1,0:T(8,128)(2,1)}) %all-gather.2.cloned.1.call-update) | async-done | bytes 8388624 | tf_op jit(solution)/shard_map/all_gather | solution.py:309
  70.6 18.2 %fusion.25.base_hbm = f32[512,1024]{1,0:T(8,128)} fusion(bf16[512,8192]{1,0:T(8,128)(2,1)} %all-gather.2.cloned.1.call-done, bf16[8192,1024]{1,0:T(8,128)(2,1)} %param.12), kind=kOutput, calls=%fused_computation.93 | convolution fusion | flops 8589934592 | bytes 27262976 | tf_op jit(solution)/shard_map/dot_general | solution.py:310
  88.9 7.7 %convolution_convert_fusion = bf16[512,512]{1,0:T(8,128)(2,1)} fusion(bf16[512,8192]{1,0:T(8,128)(2,1)S(1)} %copy-done.11, bf16[8192,512]{1,0:T(8,128)(2,1)} %param.13), kind=kOutput, calls=%fused_computation.11 | convolution fusion | flops 4295229440 | bytes 17301504 | tf_op jit(solution)/shard_map/dot_general | solution.py:311
  96.6 19.0 %collective-permute-done.2.refs_2_ = bf16[16,64,512]{2,1,0:T(8,128)(2,1)} collective-permute-done((bf16[16,64,512]{2,1,0:T(8,128)(2,1)}, bf16[16,64,512]{2,1,0:T(8,128)(2,1)}, u32[]{:S(2)}, u32[]{:S(2)}) %collective-permute-start.2) | collective-permute-done | bytes 1048608 | tf_op jit(solution)/shard_map/ppermute | solution.py:280
  115.6 19.9 %collective-permute-done.3.refs_3_ = bf16[16,64,512]{2,1,0:T(8,128)(2,1)} collective-permute-done((bf16[16,64,512]{2,1,0:T(8,128)(2,1)}, bf16[16,64,512]{2,1,0:T(8,128)(2,1)}, u32[]{:S(2)}, u32[]{:S(2)}) %collective-permute-start.3) | collective-permute-done | bytes 1048608 | tf_op jit(solution)/shard_map/ppermute | solution.py:280
  135.5 25.1 %collective-permute-done.store_ref.refs_4_ = bf16[48,64,512]{2,1,0:T(8,128)(2,1)S(1)} collective-permute-done((bf16[48,64,512]{2,1,0:T(8,128)(2,1)}, bf16[48,64,512]{2,1,0:T(8,128)(2,1)S(1)}, u32[]{:S(2)}, u32[]{:S(2)}) %collective-permute-start) | collective-permute-done | bytes 3145760 | tf_op jit(solution)/shard_map/ppermute | solution.py:280
  160.6 4.5 %all-to-all-start.1 = ((bf16[16,2048,64]{1,2,0:T(8,128)(2,1)}), bf16[16,2048,64]{1,2,0:T(8,128)(2,1)}, u32[]{:S(2)}, u32[]{:S(2)}) async-start(bf16[16,2048,64]{1,2,0:T(8,128)(2,1)} %gather_fusion.1), calls=%async_computation.1 | async-start | bytes 8388608 | tf_op jit(solution)/shard_map/all_to_all | solution.py:326
  165.3 0.1 fusion.13
  165.6 0.5 slice.37
  167.1 6.1 %serve.3 = (bf16[16,64,512]{2,1,0:T(8,128)(2,1)}, bf16[16,64,512]{2,1,0:T(8,128)(2,1)}, bf16[16,64,512]{2,1,0:T(8,128)(2,1)S(1)}) custom-call(s32[48]{0:T(128)S(1)} %reshape.366.asked_ref, bf16[48,64,512]{2,1,0:T(8,128)(2,1)S(1)} %collective-permute-done.store_ref.refs_4_), custom_call_target="tpu_custom_call" | custom-call | bytes 6291456 | tf_op jit(solution)/shard_map/serve/pallas_call | solution.py:207
  173.2 1.0 copy-done.1
  174.2 1.9 collective-permute-start.4
  176.1 1.5 collective-permute-start.5
  177.5 0.6 pad_add_fusion.steps_ref
  178.1 0.2 convert_reduce_fusion.4
  178.3 0.2 convert_reduce_fusion.2
  178.6 0.5 compare_select_fusion.4
  179.2 4.3 %gather_fusion = bf16[16,64,1024]{2,1,0:T(8,128)(2,1)} fusion(bf16[32,64,1024]{2,1,0:T(8,128)(2,1)} %param.15, s32[1024]{0:T(1024)S(1)} %pad_clamp_fusion.1), kind=kCustom, calls=%fused_computation | custom fusion | bytes 4194368 | tf_op jit(solution)/shard_map/gather | solution.py:307
  183.5 51.8 %collective-permute-done.4.refs_5_ = bf16[16,64,512]{2,1,0:T(8,128)(2,1)S(1)} collective-permute-done((bf16[16,64,512]{2,1,0:T(8,128)(2,1)}, bf16[16,64,512]{2,1,0:T(8,128)(2,1)S(1)}, u32[]{:S(2)}, u32[]{:S(2)}) %collective-permute-start.4) | collective-permute-done | bytes 1048608 | tf_op jit(solution)/shard_map/ppermute | solution.py:280
  235.3 21.7 %collective-permute-done.5.refs_6_ = bf16[16,64,512]{2,1,0:T(8,128)(2,1)S(1)} collective-permute-done((bf16[16,64,512]{2,1,0:T(8,128)(2,1)}, bf16[16,64,512]{2,1,0:T(8,128)(2,1)S(1)}, u32[]{:S(2)}, u32[]{:S(2)}) %collective-permute-start.5) | collective-permute-done | bytes 1048608 | tf_op jit(solution)/shard_map/ppermute | solution.py:280
  257.0 1.8 all-to-all-done.1
  258.8 4.7 %all-to-all-start.2 = ((bf16[16,64,1024]{2,1,0:T(8,128)(2,1)}), bf16[16,64,1024]{2,1,0:T(8,128)(2,1)S(1)}, u32[]{:S(2)}, u32[]{:S(2)}) async-start(bf16[16,64,1024]{2,1,0:T(8,128)(2,1)} %gather_fusion), calls=%async_computation.2 | async-start | bytes 4194304 | tf_op jit(solution)/shard_map/all_to_all | solution.py:332
  263.6 2.9 collective-permute-start.6
  266.5 3.6 %fusion.1 = bf16[2048,512]{1,0:T(8,128)(2,1)} fusion(bf16[512,512]{1,0:T(8,128)(2,1)} %convolution_convert_fusion, s32[2048]{0:T(1024)S(1)} %add_bitcast_fusion), kind=kOutput, calls=%fused_computation.5 | convolution fusion | flops 1075838976 | bytes 2629632 | tf_op jit(solution)/shard_map/dot_general | solution.py:343
  270.1 4.6 %fusion.2 = f32[512,64]{0,1:T(8,128)S(1)} fusion(bf16[16,2048,64]{1,2,0:T(8,128)(2,1)} %all-to-all-done.1, bf16[512,2048]{1,0:T(8,128)(2,1)S(1)} %copy-done.4, pred[512,16]{0,1:T(8,128)(4,1)S(1)} %iota_compare_fusion.4), kind=kOutput, calls=%fused_computation.7 | convolution fusion | flops 2148499456 | bytes 6430720 | tf_op jit(solution)/shard_map/tn,snk->tsk/dot_general | solution.py:335
  274.7 12.2 %all-reduce.1 = bf16[512,64]{0,1:T(8,128)(2,1)S(1)} all-reduce(f32[512,64]{0,1:T(8,128)S(1)} %fusion.2), channel_id=1, replica_groups=mesh['dp'=8,'tensor'=4] {'tensor'}, use_global_device_ids=true, to_apply=%region_16.17 | all-reduce | flops 32768 | bytes 196608 | tf_op jit(solution)/shard_map/psum | solution.py:337
  286.9 1.0 broadcast_select_fusion
  288.0 2.3 copy.37.spread_hbm
  290.3 4.9 %assemble.1.pages_hbm = bf16[64,64,512]{2,1,0:T(8,128)(2,1)} custom-call(s32[64]{0:T(128)} %get-tuple-element.39.source_ref, s32[64]{0:T(128)} %get-tuple-element.40.place_ref, bf16[48,64,512]{2,1,0:T(8,128)(2,1)} %refs_0_, bf16[16,64,512]{2,1,0:T(8,128)(2,1)} %collective-permute-done.1.refs_1_, bf16[16,64,512]{2,1,0:T(8,128)(2,1)} %collective-permute-done.2.refs_2_, ...), custom_call_target="tpu_custom_call" | custom-call | bytes 8388608 | tf_op jit(solution)/shard_map/assemble/pallas_call | solution.py:246
  295.2 27.1 %collective-permute-done.6.last_hbm = bf16[16,64,512]{2,1,0:T(8,128)(2,1)} collective-permute-done((bf16[16,64,512]{2,1,0:T(8,128)(2,1)S(1)}, bf16[16,64,512]{2,1,0:T(8,128)(2,1)}, u32[]{:S(2)}, u32[]{:S(2)}) %collective-permute-start.6) | collective-permute-done | bytes 1048608 | tf_op jit(solution)/shard_map/ppermute | solution.py:280
  322.4 1.3 copy-done.3
  323.7 11.8 %attend.1 = bf16[512,1024]{1,0:T(8,128)(2,1)} custom-call(s32[4,48]{1,0:T(4,128)} %pad_add_fusion.steps_ref, s32[64]{0:T(128)} %get-tuple-element.39.source_ref, s32[64]{0:T(128)} %get-tuple-element.40.place_ref, bf16[512,1024]{1,0:T(8,128)(2,1)} %copy.37.spread_hbm, bf16[1024,1024]{1,0:T(8,128)(2,1)} %bitcast.62, f32[512,1024]{1,0:T(8,128)} %fusion.25.base_hbm, ...), custom_call_target="tpu_custom_call" | custom-call | flops 2281701376 | bytes 12582912 | tf_op jit(solution)/shard_map/attend/pallas_call | solution.py:172
  (56 shorter events, 1.3 us)
Async XLA Ops:
  7.2 63.5 %all-gather.2.cloned.1.call-start = ((), (), s32[]{:S(2)}) async-start(), calls=%async_computation.3 | async-start | bytes 10485760 | tf_op jit(solution)/shard_map/all_gather | solution.py:309
  9.3 13.8 %all-to-all-start = ((s32[8,1,160]{2,1,0:T(1,128)}), s32[8,1,160]{2,1,0:T(1,128)S(1)}, u32[]{:S(2)}, u32[]{:S(2)}) async-start(s32[8,1,160]{2,1,0:T(1,128)} %broadcast_in_dim.106), calls=%async_computation | async-start | bytes 16384 | tf_op jit(solution)/shard_map/all_to_all | solution.py:285
  23.7 136.9 %collective-permute-start = (bf16[48,64,512]{2,1,0:T(8,128)(2,1)}, bf16[48,64,512]{2,1,0:T(8,128)(2,1)S(1)}, u32[]{:S(2)}, u32[]{:S(2)}) collective-permute-start(bf16[48,64,512]{2,1,0:T(8,128)(2,1)} %refs_0_), channel_id=1, source_target_pairs={{0,16},{4,20},{8,24},{12,28},{16,0},{20,4},{24,8},{28,12},{1,17},{... | collective-permute-start | bytes 9437192 | tf_op jit(solution)/shard_map/ppermute | solution.py:280
  31.3 65.3 %collective-permute-start.1 = (bf16[16,64,512]{2,1,0:T(8,128)(2,1)}, bf16[16,64,512]{2,1,0:T(8,128)(2,1)}, u32[]{:S(2)}, u32[]{:S(2)}) collective-permute-start(bf16[16,64,512]{2,1,0:T(8,128)(2,1)} %get-tuple-element.30), channel_id=1, source_target_pairs={{0,4},{4,0},{8,12},{12,8},{16,20},{20,16},{24,28},{28,24},{1,5},{5... | collective-permute-start | bytes 3145736 | tf_op jit(solution)/shard_map/ppermute | solution.py:280
  32.6 83.1 %collective-permute-start.2 = (bf16[16,64,512]{2,1,0:T(8,128)(2,1)}, bf16[16,64,512]{2,1,0:T(8,128)(2,1)}, u32[]{:S(2)}, u32[]{:S(2)}) collective-permute-start(bf16[16,64,512]{2,1,0:T(8,128)(2,1)} %get-tuple-element.31), channel_id=1, source_target_pairs={{0,8},{4,12},{8,0},{12,4},{16,24},{20,28},{24,16},{28,20},{1,9},{5... | collective-permute-start | bytes 3145736 | tf_op jit(solution)/shard_map/ppermute | solution.py:280
  32.6 102.9 %collective-permute-start.3 = (bf16[16,64,512]{2,1,0:T(8,128)(2,1)}, bf16[16,64,512]{2,1,0:T(8,128)(2,1)}, u32[]{:S(2)}, u32[]{:S(2)}) collective-permute-start(bf16[16,64,512]{2,1,0:T(8,128)(2,1)} %get-tuple-element.32), channel_id=1, source_target_pairs={{0,12},{4,8},{8,4},{12,0},{16,28},{20,24},{24,20},{28,16},{1,13},{... | collective-permute-start | bytes 3145736 | tf_op jit(solution)/shard_map/ppermute | solution.py:280
  70.6 18.2 %copy-start.11 = (bf16[512,8192]{1,0:T(8,128)(2,1)S(1)}, bf16[512,8192]{1,0:T(8,128)(2,1)}, u32[]{:S(2)}) copy-start(bf16[512,8192]{1,0:T(8,128)(2,1)} %all-gather.2.cloned.1.call-done) | copy-start | bytes 25165828
  96.6 68.6 %copy-start.7 = (s32[1,16]{1,0:T(1,128)S(1)}, s32[1,16]{1,0:T(1,128)}, u32[]{:S(2)}) copy-start(s32[1,16]{1,0:T(1,128)} %param.17) | copy-start | bytes 196
  96.6 81.5 %copy-start.10 = (s32[16,1]{0,1:T(1,128)S(1)}, s32[16,1]{0,1:T(1,128)}, u32[]{:S(2)}) copy-start(s32[16,1]{0,1:T(1,128)} %param.18) | copy-start | bytes 196
  96.6 81.7 %copy-start.9 = (s32[64,1]{0,1:T(1,128)S(1)}, s32[64,1]{0,1:T(1,128)}, u32[]{:S(2)}) copy-start(s32[64,1]{0,1:T(1,128)} %param.20) | copy-start | bytes 772
  96.6 82.0 %copy-start.8 = (s32[64]{0:T(128)S(1)}, s32[64]{0:T(128)}, u32[]{:S(2)}) copy-start(s32[64]{0:T(128)} %param.21) | copy-start | bytes 772
  160.6 6.5 %copy-start = (bf16[48,64,512]{2,1,0:T(8,128)(2,1)}, bf16[48,64,512]{2,1,0:T(8,128)(2,1)S(1)}, u32[]{:S(2)}) copy-start(bf16[48,64,512]{2,1,0:T(8,128)(2,1)S(1)} %collective-permute-done.store_ref.refs_4_) | copy-start | bytes 9437188
  160.6 98.2 %all-to-all-start.1 = ((bf16[16,2048,64]{1,2,0:T(8,128)(2,1)}), bf16[16,2048,64]{1,2,0:T(8,128)(2,1)}, u32[]{:S(2)}, u32[]{:S(2)}) async-start(bf16[16,2048,64]{1,2,0:T(8,128)(2,1)} %gather_fusion.1), calls=%async_computation.1 | async-start | bytes 8388608 | tf_op jit(solution)/shard_map/all_to_all | solution.py:326
  173.2 1.0 copy-start.1
  174.2 61.1 %collective-permute-start.4 = (bf16[16,64,512]{2,1,0:T(8,128)(2,1)}, bf16[16,64,512]{2,1,0:T(8,128)(2,1)S(1)}, u32[]{:S(2)}, u32[]{:S(2)}) collective-permute-start(bf16[16,64,512]{2,1,0:T(8,128)(2,1)} %get-tuple-element.35), channel_id=1, source_target_pairs={{0,4},{4,0},{8,12},{12,8},{16,20},{20,16},{24,28},{28,24},{1,5},{5... | collective-permute-start | bytes 3145736 | tf_op jit(solution)/shard_map/ppermute | solution.py:280
  176.1 80.9 %collective-permute-start.5 = (bf16[16,64,512]{2,1,0:T(8,128)(2,1)}, bf16[16,64,512]{2,1,0:T(8,128)(2,1)S(1)}, u32[]{:S(2)}, u32[]{:S(2)}) collective-permute-start(bf16[16,64,512]{2,1,0:T(8,128)(2,1)} %get-tuple-element.36), channel_id=1, source_target_pairs={{0,8},{4,12},{8,0},{12,4},{16,24},{20,28},{24,16},{28,20},{1,9},{5... | collective-permute-start | bytes 3145736 | tf_op jit(solution)/shard_map/ppermute | solution.py:280
  179.2 84.4 %copy-start.2 = (bf16[16,64,512]{2,1,0:T(8,128)(2,1)S(1)}, bf16[16,64,512]{2,1,0:T(8,128)(2,1)}, u32[]{:S(2)}) copy-start(bf16[16,64,512]{2,1,0:T(8,128)(2,1)} %copy-done.1) | copy-start | bytes 3145732
  235.3 23.5 %copy-start.5 = (bf16[16,64,512]{2,1,0:T(8,128)(2,1)}, bf16[16,64,512]{2,1,0:T(8,128)(2,1)S(1)}, u32[]{:S(2)}) copy-start(bf16[16,64,512]{2,1,0:T(8,128)(2,1)S(1)} %collective-permute-done.4.refs_5_) | copy-start | bytes 3145732
  257.0 1.8 copy-start.6
  258.8 63.5 %all-to-all-start.2 = ((bf16[16,64,1024]{2,1,0:T(8,128)(2,1)}), bf16[16,64,1024]{2,1,0:T(8,128)(2,1)S(1)}, u32[]{:S(2)}, u32[]{:S(2)}) async-start(bf16[16,64,1024]{2,1,0:T(8,128)(2,1)} %gather_fusion), calls=%async_computation.2 | async-start | bytes 4194304 | tf_op jit(solution)/shard_map/all_to_all | solution.py:332
  263.5 6.7 %copy-start.4 = (bf16[512,2048]{1,0:T(8,128)(2,1)S(1)}, bf16[512,2048]{1,0:T(8,128)(2,1)}, u32[]{:S(2)}) copy-start(bf16[512,2048]{1,0:T(8,128)(2,1)} %param.11) | copy-start | bytes 6291460
  263.6 58.8 %collective-permute-start.6 = (bf16[16,64,512]{2,1,0:T(8,128)(2,1)S(1)}, bf16[16,64,512]{2,1,0:T(8,128)(2,1)}, u32[]{:S(2)}, u32[]{:S(2)}) collective-permute-start(bf16[16,64,512]{2,1,0:T(8,128)(2,1)S(1)} %copy-done.2), channel_id=1, source_target_pairs={{0,12},{4,8},{8,4},{12,0},{16,28},{20,24},{24,20},{28,16},{1,13},{... | collective-permute-start | bytes 3145736 | tf_op jit(solution)/shard_map/ppermute | solution.py:280
  322.4 1.3 copy-start.3
Sparse Core Ops, SparseCore 0:
  9.6 61.0 all-gather.1

commit v18 on v17

--- a/solution.py
+++ b/solution.py
@@ -13,7 +13,7 @@
 HITS = 4
 MOST = 128
 BLOCK = 16
-TOGETHER = 8
+TOGETHER = 16
 TILE = 256
 VMEM_GRANT = 60 * 1024 * 1024
 SMALL_GRANT = 16 * 1024 * 1024

time: 344 us -> 344 us (level)
  no operation moved by 1% of the time
where the time goes in v18:
time: 344 us; the launch traced here: 342 us
  waiting for transfers between devices  203 us (59%)
  matrix products  34.1 us (10%)
  Pallas kernels  27.7 us (8%)
  starting transfers between devices  26.9 us (8%)
  local copies, waits for them, and re-layouts  17.9 us (5%)
  between operations  14.9 us (4%)
  blocking collectives  12.4 us (4%)
  other arithmetic  5.05 us (1%)
    ppermute x7, waiting for transfers between devices, swap(): lax.ppermute(array, 'dp', [(peer, peer ^ distance) for peer in range(peer...  165 us
    all_gather x1, waiting for transfers between devices, on_device(): piece = lax.all_gather(tokens, 'tensor', axis=1, tiled=True)  29.4 us
    dot_general x1, matrix products, on_device(): jnp.dot(piece, query_weight, preferred_element_type=jnp.float32)  18.2 us
    psum x1, blocking collectives, on_device(): shrink = lax.psum(shrink_part, 'tensor').astype(jnp.bfloat16)  12.4 us
    pallas_call x1, Pallas kernels, attend(): pl.pallas_call(functools.partial(attention_kernel, last), out_shape=jax.S...  11.4 us
    pallas_call x2, Pallas kernels, serve(): pl.pallas_call(serve_kernel, out_shape=[jax.ShapeDtypeStruct(shape, store...  11.4 us
    ppermute x7, starting transfers between devices, swap(): lax.ppermute(array, 'dp', [(peer, peer ^ distance) for peer in range(peer...  10.4 us
    dot_general x1, matrix products, on_device(): jnp.dot(piece, keyvalue_weight, preferred_element_type=jnp.float32)  7.7 us
  transfers between devices with their start and end apart: 11, of which 9 were waited for; matrix products, arithmetic and copies ran while one was open for 16% of the time, Pallas kernels for 5%

profile of v18, /device:TPU:0, one launch (start us, length us, event | category | flops | bytes accessed | tf_op | source)
XLA Modules:
  0.0 341.9 jit_solution(9329702240957936378)
XLA Ops:
  7.2 0.7 all-gather.2.cloned.1.call-update
  7.9 0.8 pad_add_fusion.1
  8.7 0.6 broadcast_in_dim.106
  9.3 7.3 %all-to-all-start = ((s32[8,1,160]{2,1,0:T(1,128)}), s32[8,1,160]{2,1,0:T(1,128)S(1)}, u32[]{:S(2)}, u32[]{:S(2)}) async-start(s32[8,1,160]{2,1,0:T(1,128)} %broadcast_in_dim.106), calls=%async_computation | async-start | bytes 16384 | tf_op jit(solution)/shard_map/all_to_all | solution.py:285
  16.6 6.5 %all-to-all-done = s32[8,1,160]{2,1,0:T(1,128)S(1)} async-done(((s32[8,1,160]{2,1,0:T(1,128)}), s32[8,1,160]{2,1,0:T(1,128)S(1)}, u32[]{:S(2)}, u32[]{:S(2)}) %all-to-all-start) | async-done | bytes 5152 | tf_op jit(solution)/shard_map/all_to_all | solution.py:285
  23.1 0.3 convert_reduce_fusion.1
  23.4 0.1 select_reduce_fusion.7
  23.7 0.6 collective-permute-start
  24.3 0.6 gather_fusion.2
  24.9 0.2 convert_reduce_fusion
  25.2 0.2 select_reduce_fusion.1
  25.4 0.6 reshape.365.asked_ref
  26.0 5.2 %serve.2 = (bf16[16,64,512]{2,1,0:T(8,128)(2,1)}, bf16[16,64,512]{2,1,0:T(8,128)(2,1)}, bf16[16,64,512]{2,1,0:T(8,128)(2,1)}) custom-call(s32[48]{0:T(128)} %reshape.365.asked_ref, bf16[48,64,512]{2,1,0:T(8,128)(2,1)} %refs_0_), custom_call_target="tpu_custom_call" | custom-call | bytes 6291456 | tf_op jit(solution)/shard_map/serve/pallas_call | solution.py:207
  31.3 1.6 collective-permute-start.2
  33.0 1.8 collective-permute-start.3
  34.9 6.3 %gather_fusion.1 = bf16[16,2048,64]{1,2,0:T(8,128)(2,1)} fusion(bf16[32,2048,64]{1,2,0:T(8,128)(2,1)} %param.14, s32[1024]{0:T(1024)S(1)} %pad_clamp_fusion.1), kind=kCustom, calls=%fused_computation.1 | custom fusion | bytes 8388672 | tf_op jit(solution)/shard_map/gather | solution.py:306
  41.2 29.4 %all-gather.2.cloned.1.call-done = bf16[512,8192]{1,0:T(8,128)(2,1)} async-done(((bf16[512,2048]{1,0:T(8,128)(2,1)}), bf16[512,8192]{1,0:T(8,128)(2,1)}) %all-gather.2.cloned.1.call-update) | async-done | bytes 8388624 | tf_op jit(solution)/shard_map/all_gather | solution.py:309
  70.6 18.2 %fusion.25.base_hbm = f32[512,1024]{1,0:T(8,128)} fusion(bf16[512,8192]{1,0:T(8,128)(2,1)} %all-gather.2.cloned.1.call-done, bf16[8192,1024]{1,0:T(8,128)(2,1)} %param.12), kind=kOutput, calls=%fused_computation.93 | convolution fusion | flops 8589934592 | bytes 27262976 | tf_op jit(solution)/shard_map/dot_general | solution.py:310
  88.9 7.7 %convolution_convert_fusion = bf16[512,512]{1,0:T(8,128)(2,1)} fusion(bf16[512,8192]{1,0:T(8,128)(2,1)S(1)} %copy-done.11, bf16[8192,512]{1,0:T(8,128)(2,1)} %param.13), kind=kOutput, calls=%fused_computation.11 | convolution fusion | flops 4295229440 | bytes 17301504 | tf_op jit(solution)/shard_map/dot_general | solution.py:311
  96.6 19.0 %collective-permute-done.2.refs_2_ = bf16[16,64,512]{2,1,0:T(8,128)(2,1)} collective-permute-done((bf16[16,64,512]{2,1,0:T(8,128)(2,1)}, bf16[16,64,512]{2,1,0:T(8,128)(2,1)}, u32[]{:S(2)}, u32[]{:S(2)}) %collective-permute-start.2) | collective-permute-done | bytes 1048608 | tf_op jit(solution)/shard_map/ppermute | solution.py:280
  115.6 19.9 %collective-permute-done.3.refs_3_ = bf16[16,64,512]{2,1,0:T(8,128)(2,1)} collective-permute-done((bf16[16,64,512]{2,1,0:T(8,128)(2,1)}, bf16[16,64,512]{2,1,0:T(8,128)(2,1)}, u32[]{:S(2)}, u32[]{:S(2)}) %collective-permute-start.3) | collective-permute-done | bytes 1048608 | tf_op jit(solution)/shard_map/ppermute | solution.py:280
  135.5 25.1 %collective-permute-done.store_ref.refs_4_ = bf16[48,64,512]{2,1,0:T(8,128)(2,1)S(1)} collective-permute-done((bf16[48,64,512]{2,1,0:T(8,128)(2,1)}, bf16[48,64,512]{2,1,0:T(8,128)(2,1)S(1)}, u32[]{:S(2)}, u32[]{:S(2)}) %collective-permute-start) | collective-permute-done | bytes 3145760 | tf_op jit(solution)/shard_map/ppermute | solution.py:280
  160.6 4.5 %all-to-all-start.1 = ((bf16[16,2048,64]{1,2,0:T(8,128)(2,1)}), bf16[16,2048,64]{1,2,0:T(8,128)(2,1)}, u32[]{:S(2)}, u32[]{:S(2)}) async-start(bf16[16,2048,64]{1,2,0:T(8,128)(2,1)} %gather_fusion.1), calls=%async_computation.1 | async-start | bytes 8388608 | tf_op jit(solution)/shard_map/all_to_all | solution.py:326
  165.3 0.1 fusion.13
  165.6 0.5 slice.37
  167.1 6.1 %serve.3 = (bf16[16,64,512]{2,1,0:T(8,128)(2,1)}, bf16[16,64,512]{2,1,0:T(8,128)(2,1)}, bf16[16,64,512]{2,1,0:T(8,128)(2,1)S(1)}) custom-call(s32[48]{0:T(128)S(1)} %reshape.366.asked_ref, bf16[48,64,512]{2,1,0:T(8,128)(2,1)S(1)} %collective-permute-done.store_ref.refs_4_), custom_call_target="tpu_custom_call" | custom-call | bytes 6291456 | tf_op jit(solution)/shard_map/serve/pallas_call | solution.py:207
  173.2 1.0 copy-done.1
  174.2 1.9 collective-permute-start.4
  176.1 1.5 collective-permute-start.5
  177.5 0.6 pad_add_fusion.steps_ref
  178.1 0.2 convert_reduce_fusion.4
  178.3 0.2 convert_reduce_fusion.2
  178.6 0.5 compare_select_fusion.4
  179.2 4.3 %gather_fusion = bf16[16,64,1024]{2,1,0:T(8,128)(2,1)} fusion(bf16[32,64,1024]{2,1,0:T(8,128)(2,1)} %param.15, s32[1024]{0:T(1024)S(1)} %pad_clamp_fusion.1), kind=kCustom, calls=%fused_computation | custom fusion | bytes 4194368 | tf_op jit(solution)/shard_map/gather | solution.py:307
  183.5 51.8 %collective-permute-done.4.refs_5_ = bf16[16,64,512]{2,1,0:T(8,128)(2,1)S(1)} collective-permute-done((bf16[16,64,512]{2,1,0:T(8,128)(2,1)}, bf16[16,64,512]{2,1,0:T(8,128)(2,1)S(1)}, u32[]{:S(2)}, u32[]{:S(2)}) %collective-permute-start.4) | collective-permute-done | bytes 1048608 | tf_op jit(solution)/shard_map/ppermute | solution.py:280
  235.3 21.7 %collective-permute-done.5.refs_6_ = bf16[16,64,512]{2,1,0:T(8,128)(2,1)S(1)} collective-permute-done((bf16[16,64,512]{2,1,0:T(8,128)(2,1)}, bf16[16,64,512]{2,1,0:T(8,128)(2,1)S(1)}, u32[]{:S(2)}, u32[]{:S(2)}) %collective-permute-start.5) | collective-permute-done | bytes 1048608 | tf_op jit(solution)/shard_map/ppermute | solution.py:280
  257.0 1.8 all-to-all-done.1
  258.8 4.7 %all-to-all-start.2 = ((bf16[16,64,1024]{2,1,0:T(8,128)(2,1)}), bf16[16,64,1024]{2,1,0:T(8,128)(2,1)S(1)}, u32[]{:S(2)}, u32[]{:S(2)}) async-start(bf16[16,64,1024]{2,1,0:T(8,128)(2,1)} %gather_fusion), calls=%async_computation.2 | async-start | bytes 4194304 | tf_op jit(solution)/shard_map/all_to_all | solution.py:332
  263.6 2.9 collective-permute-start.6
  266.5 3.6 %fusion.1 = bf16[2048,512]{1,0:T(8,128)(2,1)} fusion(bf16[512,512]{1,0:T(8,128)(2,1)} %convolution_convert_fusion, s32[2048]{0:T(1024)S(1)} %add_bitcast_fusion), kind=kOutput, calls=%fused_computation.5 | convolution fusion | flops 1075838976 | bytes 2629632 | tf_op jit(solution)/shard_map/dot_general | solution.py:343
  270.1 4.6 %fusion.2 = f32[512,64]{0,1:T(8,128)S(1)} fusion(bf16[16,2048,64]{1,2,0:T(8,128)(2,1)} %all-to-all-done.1, bf16[512,2048]{1,0:T(8,128)(2,1)S(1)} %copy-done.4, pred[512,16]{0,1:T(8,128)(4,1)S(1)} %iota_compare_fusion.4), kind=kOutput, calls=%fused_computation.7 | convolution fusion | flops 2148499456 | bytes 6430720 | tf_op jit(solution)/shard_map/tn,snk->tsk/dot_general | solution.py:335
  274.7 12.4 %all-reduce.1 = bf16[512,64]{0,1:T(8,128)(2,1)S(1)} all-reduce(f32[512,64]{0,1:T(8,128)S(1)} %fusion.2), channel_id=1, replica_groups=mesh['dp'=8,'tensor'=4] {'tensor'}, use_global_device_ids=true, to_apply=%region_16.17 | all-reduce | flops 32768 | bytes 196608 | tf_op jit(solution)/shard_map/psum | solution.py:337
  287.1 1.0 broadcast_select_fusion
  288.2 2.3 copy.37.spread_hbm
  290.4 4.9 %assemble.1.pages_hbm = bf16[64,64,512]{2,1,0:T(8,128)(2,1)} custom-call(s32[64]{0:T(128)} %get-tuple-element.39.source_ref, s32[64]{0:T(128)} %get-tuple-element.40.place_ref, bf16[48,64,512]{2,1,0:T(8,128)(2,1)} %refs_0_, bf16[16,64,512]{2,1,0:T(8,128)(2,1)} %collective-permute-done.1.refs_1_, bf16[16,64,512]{2,1,0:T(8,128)(2,1)} %collective-permute-done.2.refs_2_, ...), custom_call_target="tpu_custom_call" | custom-call | bytes 8388608 | tf_op jit(solution)/shard_map/assemble/pallas_call | solution.py:246
  295.4 27.0 %collective-permute-done.6.last_hbm = bf16[16,64,512]{2,1,0:T(8,128)(2,1)} collective-permute-done((bf16[16,64,512]{2,1,0:T(8,128)(2,1)S(1)}, bf16[16,64,512]{2,1,0:T(8,128)(2,1)}, u32[]{:S(2)}, u32[]{:S(2)}) %collective-permute-start.6) | collective-permute-done | bytes 1048608 | tf_op jit(solution)/shard_map/ppermute | solution.py:280
  322.4 1.3 copy-done.3
  323.7 11.4 %attend.1 = bf16[512,1024]{1,0:T(8,128)(2,1)} custom-call(s32[4,48]{1,0:T(4,128)} %pad_add_fusion.steps_ref, s32[64]{0:T(128)} %get-tuple-element.39.source_ref, s32[64]{0:T(128)} %get-tuple-element.40.place_ref, bf16[512,1024]{1,0:T(8,128)(2,1)} %copy.37.spread_hbm, bf16[1024,1024]{1,0:T(8,128)(2,1)} %bitcast.62, f32[512,1024]{1,0:T(8,128)} %fusion.25.base_hbm, ...), custom_call_target="tpu_custom_call" | custom-call | flops 2281701376 | bytes 12582912 | tf_op jit(solution)/shard_map/attend/pallas_call | solution.py:172
  (56 shorter events, 1.4 us)
Async XLA Ops:
  7.2 63.5 %all-gather.2.cloned.1.call-start = ((), (), s32[]{:S(2)}) async-start(), calls=%async_computation.3 | async-start | bytes 10485760 | tf_op jit(solution)/shard_map/all_gather | solution.py:309
  9.3 13.8 %all-to-all-start = ((s32[8,1,160]{2,1,0:T(1,128)}), s32[8,1,160]{2,1,0:T(1,128)S(1)}, u32[]{:S(2)}, u32[]{:S(2)}) async-start(s32[8,1,160]{2,1,0:T(1,128)} %broadcast_in_dim.106), calls=%async_computation | async-start | bytes 16384 | tf_op jit(solution)/shard_map/all_to_all | solution.py:285
  23.7 136.9 %collective-permute-start = (bf16[48,64,512]{2,1,0:T(8,128)(2,1)}, bf16[48,64,512]{2,1,0:T(8,128)(2,1)S(1)}, u32[]{:S(2)}, u32[]{:S(2)}) collective-permute-start(bf16[48,64,512]{2,1,0:T(8,128)(2,1)} %refs_0_), channel_id=1, source_target_pairs={{0,16},{4,20},{8,24},{12,28},{16,0},{20,4},{24,8},{28,12},{1,17},{... | collective-permute-start | bytes 9437192 | tf_op jit(solution)/shard_map/ppermute | solution.py:280
  31.2 65.4 %collective-permute-start.1 = (bf16[16,64,512]{2,1,0:T(8,128)(2,1)}, bf16[16,64,512]{2,1,0:T(8,128)(2,1)}, u32[]{:S(2)}, u32[]{:S(2)}) collective-permute-start(bf16[16,64,512]{2,1,0:T(8,128)(2,1)} %get-tuple-element.30), channel_id=1, source_target_pairs={{0,4},{4,0},{8,12},{12,8},{16,20},{20,16},{24,28},{28,24},{1,5},{5... | collective-permute-start | bytes 3145736 | tf_op jit(solution)/shard_map/ppermute | solution.py:280
  31.3 84.3 %collective-permute-start.2 = (bf16[16,64,512]{2,1,0:T(8,128)(2,1)}, bf16[16,64,512]{2,1,0:T(8,128)(2,1)}, u32[]{:S(2)}, u32[]{:S(2)}) collective-permute-start(bf16[16,64,512]{2,1,0:T(8,128)(2,1)} %get-tuple-element.31), channel_id=1, source_target_pairs={{0,8},{4,12},{8,0},{12,4},{16,24},{20,28},{24,16},{28,20},{1,9},{5... | collective-permute-start | bytes 3145736 | tf_op jit(solution)/shard_map/ppermute | solution.py:280
  33.0 102.6 %collective-permute-start.3 = (bf16[16,64,512]{2,1,0:T(8,128)(2,1)}, bf16[16,64,512]{2,1,0:T(8,128)(2,1)}, u32[]{:S(2)}, u32[]{:S(2)}) collective-permute-start(bf16[16,64,512]{2,1,0:T(8,128)(2,1)} %get-tuple-element.32), channel_id=1, source_target_pairs={{0,12},{4,8},{8,4},{12,0},{16,28},{20,24},{24,20},{28,16},{1,13},{... | collective-permute-start | bytes 3145736 | tf_op jit(solution)/shard_map/ppermute | solution.py:280
  70.6 18.2 %copy-start.11 = (bf16[512,8192]{1,0:T(8,128)(2,1)S(1)}, bf16[512,8192]{1,0:T(8,128)(2,1)}, u32[]{:S(2)}) copy-start(bf16[512,8192]{1,0:T(8,128)(2,1)} %all-gather.2.cloned.1.call-done) | copy-start | bytes 25165828
  96.6 68.6 %copy-start.7 = (s32[1,16]{1,0:T(1,128)S(1)}, s32[1,16]{1,0:T(1,128)}, u32[]{:S(2)}) copy-start(s32[1,16]{1,0:T(1,128)} %param.17) | copy-start | bytes 196
  96.6 81.5 %copy-start.10 = (s32[16,1]{0,1:T(1,128)S(1)}, s32[16,1]{0,1:T(1,128)}, u32[]{:S(2)}) copy-start(s32[16,1]{0,1:T(1,128)} %param.18) | copy-start | bytes 196
  96.6 81.7 %copy-start.9 = (s32[64,1]{0,1:T(1,128)S(1)}, s32[64,1]{0,1:T(1,128)}, u32[]{:S(2)}) copy-start(s32[64,1]{0,1:T(1,128)} %param.20) | copy-start | bytes 772
  96.6 82.0 %copy-start.8 = (s32[64]{0:T(128)S(1)}, s32[64]{0:T(128)}, u32[]{:S(2)}) copy-start(s32[64]{0:T(128)} %param.21) | copy-start | bytes 772
  160.6 6.5 %copy-start = (bf16[48,64,512]{2,1,0:T(8,128)(2,1)}, bf16[48,64,512]{2,1,0:T(8,128)(2,1)S(1)}, u32[]{:S(2)}) copy-start(bf16[48,64,512]{2,1,0:T(8,128)(2,1)S(1)} %collective-permute-done.store_ref.refs_4_) | copy-start | bytes 9437188
  160.6 98.2 %all-to-all-start.1 = ((bf16[16,2048,64]{1,2,0:T(8,128)(2,1)}), bf16[16,2048,64]{1,2,0:T(8,128)(2,1)}, u32[]{:S(2)}, u32[]{:S(2)}) async-start(bf16[16,2048,64]{1,2,0:T(8,128)(2,1)} %gather_fusion.1), calls=%async_computation.1 | async-start | bytes 8388608 | tf_op jit(solution)/shard_map/all_to_all | solution.py:326
  173.2 1.0 copy-start.1
  174.2 61.1 %collective-permute-start.4 = (bf16[16,64,512]{2,1,0:T(8,128)(2,1)}, bf16[16,64,512]{2,1,0:T(8,128)(2,1)S(1)}, u32[]{:S(2)}, u32[]{:S(2)}) collective-permute-start(bf16[16,64,512]{2,1,0:T(8,128)(2,1)} %get-tuple-element.35), channel_id=1, source_target_pairs={{0,4},{4,0},{8,12},{12,8},{16,20},{20,16},{24,28},{28,24},{1,5},{5... | collective-permute-start | bytes 3145736 | tf_op jit(solution)/shard_map/ppermute | solution.py:280
  176.1 80.9 %collective-permute-start.5 = (bf16[16,64,512]{2,1,0:T(8,128)(2,1)}, bf16[16,64,512]{2,1,0:T(8,128)(2,1)S(1)}, u32[]{:S(2)}, u32[]{:S(2)}) collective-permute-start(bf16[16,64,512]{2,1,0:T(8,128)(2,1)} %get-tuple-element.36), channel_id=1, source_target_pairs={{0,8},{4,12},{8,0},{12,4},{16,24},{20,28},{24,16},{28,20},{1,9},{5... | collective-permute-start | bytes 3145736 | tf_op jit(solution)/shard_map/ppermute | solution.py:280
  179.2 84.4 %copy-start.2 = (bf16[16,64,512]{2,1,0:T(8,128)(2,1)S(1)}, bf16[16,64,512]{2,1,0:T(8,128)(2,1)}, u32[]{:S(2)}) copy-start(bf16[16,64,512]{2,1,0:T(8,128)(2,1)} %copy-done.1) | copy-start | bytes 3145732
  235.3 23.5 %copy-start.5 = (bf16[16,64,512]{2,1,0:T(8,128)(2,1)}, bf16[16,64,512]{2,1,0:T(8,128)(2,1)S(1)}, u32[]{:S(2)}) copy-start(bf16[16,64,512]{2,1,0:T(8,128)(2,1)S(1)} %collective-permute-done.4.refs_5_) | copy-start | bytes 3145732
  257.0 1.8 copy-start.6
  258.8 63.5 %all-to-all-start.2 = ((bf16[16,64,1024]{2,1,0:T(8,128)(2,1)}), bf16[16,64,1024]{2,1,0:T(8,128)(2,1)S(1)}, u32[]{:S(2)}, u32[]{:S(2)}) async-start(bf16[16,64,1024]{2,1,0:T(8,128)(2,1)} %gather_fusion), calls=%async_computation.2 | async-start | bytes 4194304 | tf_op jit(solution)/shard_map/all_to_all | solution.py:332
  263.5 6.7 %copy-start.4 = (bf16[512,2048]{1,0:T(8,128)(2,1)S(1)}, bf16[512,2048]{1,0:T(8,128)(2,1)}, u32[]{:S(2)}) copy-start(bf16[512,2048]{1,0:T(8,128)(2,1)} %param.11) | copy-start | bytes 6291460
  263.6 58.8 %collective-permute-start.6 = (bf16[16,64,512]{2,1,0:T(8,128)(2,1)S(1)}, bf16[16,64,512]{2,1,0:T(8,128)(2,1)}, u32[]{:S(2)}, u32[]{:S(2)}) collective-permute-start(bf16[16,64,512]{2,1,0:T(8,128)(2,1)S(1)} %copy-done.2), channel_id=1, source_target_pairs={{0,12},{4,8},{8,4},{12,0},{16,28},{20,24},{24,20},{28,16},{1,13},{... | collective-permute-start | bytes 3145736 | tf_op jit(solution)/shard_map/ppermute | solution.py:280
  322.4 1.3 copy-start.3
Sparse Core Ops, SparseCore 0:
  9.6 61.0 all-gather.1

commit v19 on v17

--- a/solution.py
+++ b/solution.py
@@ -51,13 +51,14 @@
 
 
 def attention_kernel(
-    last, steps_ref, source_ref, place_ref, spread_hbm, up_any, base_hbm, fresh_hbm, pages_hbm, last_hbm, *rest
+    last, steps_ref, source_ref, place_ref, spread_hbm, up_any, base_hbm, fresh_hbm, pages_hbm, last_hbm, lower_hbm, *rest
 ):
     out_ref, query_ref, spread_ref, up_ref, base_ref, cache_ref, sems, tile_sems = rest
     q_cols = base_ref.shape[1]
     kv_heads = cache_ref.shape[2] // (2 * HEAD_WIDTH)
     group = q_cols // HEAD_WIDTH // kv_heads
     page = pages_hbm.shape[1]
+    cut = last_hbm.shape[1]
     held = HITS * page
     sharp = HEAD_WIDTH ** -0.5 * math.log2(math.e)
 
@@ -75,7 +76,10 @@
 
         @pl.when(late)
         def _():
-            pltpu.make_async_copy(last_hbm.at[place_ref[index]], to, sems.at[1]).start()
+            upper = cache_ref.at[index // HITS, pl.ds(pl.multiple_of(index % HITS * page, page), cut)]
+            lower = cache_ref.at[index // HITS, pl.ds(pl.multiple_of(index % HITS * page + cut, cut), page - cut)]
+            pltpu.make_async_copy(last_hbm.at[place_ref[index]], upper, sems.at[1]).start()
+            pltpu.make_async_copy(lower_hbm.at[place_ref[index]], lower, sems.at[1]).start()
 
         @pl.when(jnp.logical_not(late))
         def _():
@@ -163,7 +167,7 @@
     lax.fori_loop(0, steps_ref.shape[1] // TOGETHER, several, 0)
 
 
-def attend(query_base, spread, up, fresh, pages, last_pages, source, place, last, steps):
+def attend(query_base, spread, up, fresh, pages, last_pages, lower_pages, source, place, last, steps):
     rows, q_cols = query_base.shape
     requests = fresh.shape[0]
     keys = HITS * pages.shape[1] + MOST
@@ -172,7 +176,7 @@
     return pl.pallas_call(
         functools.partial(attention_kernel, last),
         out_shape=jax.ShapeDtypeStruct((rows, q_cols), jnp.bfloat16),
-        in_specs=[scalars] * 3 + [hbm] * 6,
+        in_specs=[scalars] * 3 + [hbm] * 7,
         out_specs=pl.BlockSpec(memory_space=pltpu.VMEM),
         scratch_shapes=[
             pltpu.VMEM((rows, q_cols), jnp.bfloat16),
@@ -188,26 +192,30 @@
             transcendentals=0,
         ),
         name="attend",
-    )(steps, source, place, spread, up, query_base, fresh, pages, last_pages)
-
-
-def serve_kernel(asked_ref, store_ref, *refs):
-    outs, sems = refs[:-1], refs[-1]
+    )(steps, source, place, spread, up, query_base, fresh, pages, last_pages, lower_pages)
+
+
+def serve_kernel(parts, asked_ref, *refs):
+    stores, outs, sems = refs[:parts], refs[parts:-1], refs[-1]
     for index, out in enumerate(outs):
         for place in range(out.shape[0]):
             page = asked_ref[index * out.shape[0] + place]
-            pltpu.make_async_copy(store_ref.at[page], out.at[place], sems.at[index]).start()
+            first = 0
+            for store_ref in stores:
+                rows = out.at[place, first : first + store_ref.shape[1]]
+                pltpu.make_async_copy(store_ref.at[page], rows, sems.at[index]).start()
+                first += store_ref.shape[1]
     for index, out in enumerate(outs):
         pltpu.make_async_copy(out, out, sems.at[index]).wait()
 
 
-def serve(asked, store, grant):
+def serve(asked, stores, grant):
     blocks, capacity = asked.shape
-    shape = (capacity,) + store.shape[1:]
+    shape = (capacity, sum(store.shape[1] for store in stores), stores[0].shape[2])
     return pl.pallas_call(
-        serve_kernel,
-        out_shape=[jax.ShapeDtypeStruct(shape, store.dtype)] * blocks,
-        in_specs=[pl.BlockSpec(memory_space=pltpu.SMEM), pl.BlockSpec(memory_space=pl.ANY)],
+        functools.partial(serve_kernel, len(stores)),
+        out_shape=[jax.ShapeDtypeStruct(shape, stores[0].dtype)] * blocks,
+        in_specs=[pl.BlockSpec(memory_space=pltpu.SMEM)] + [pl.BlockSpec(memory_space=pl.ANY)] * len(stores),
         out_specs=[pl.BlockSpec(memory_space=pltpu.VMEM)] * blocks,
         scratch_shapes=[pltpu.SemaphoreType.DMA((blocks,))],
         compiler_params=pltpu.CompilerParams(vmem_limit_bytes=grant),
@@ -215,11 +223,12 @@
             flops=0, bytes_accessed=4 * blocks * math.prod(shape), transcendentals=0
         ),
         name="serve",
-    )(asked.reshape(-1), store)
-
-
-def assemble_kernel(source_ref, place_ref, *refs):
-    sources, out, sem = refs[:-2], refs[-2], refs[-1]
+    )(asked.reshape(-1), *stores)
+
+
+def assemble_kernel(mirror, source_ref, place_ref, *refs):
+    sources, lower, out, sem = refs[:-3], refs[-3], refs[-2], refs[-1]
+    cut = sources[mirror].shape[1]
 
     def one(index, carry):
         source = source_ref[index]
@@ -228,7 +237,11 @@
 
             @pl.when(source == number)
             def _():
-                pltpu.make_async_copy(ref.at[place], out.at[index], sem).start()
+                if number == mirror:
+                    pltpu.make_async_copy(ref.at[place], out.at[index, :cut], sem).start()
+                    pltpu.make_async_copy(lower.at[place], out.at[index, cut:], sem).start()
+                else:
+                    pltpu.make_async_copy(ref.at[place], out.at[index], sem).start()
 
         @pl.when(source == len(sources))
         def _():
@@ -240,19 +253,19 @@
     pltpu.make_async_copy(out, out, sem).wait()
 
 
-def assemble(source, place, sources):
+def assemble(source, place, sources, mirror, lower):
     scalars = pl.BlockSpec(memory_space=pltpu.SMEM)
     shape = (source.shape[0],) + sources[0].shape[1:]
     return pl.pallas_call(
-        assemble_kernel,
+        functools.partial(assemble_kernel, mirror),
         out_shape=jax.ShapeDtypeStruct(shape, sources[0].dtype),
-        in_specs=[scalars, scalars] + [pl.BlockSpec(memory_space=pltpu.HBM)] * len(sources),
+        in_specs=[scalars, scalars] + [pl.BlockSpec(memory_space=pltpu.HBM)] * (len(sources) + 1),
         out_specs=pl.BlockSpec(memory_space=pltpu.VMEM),
         scratch_shapes=[pltpu.SemaphoreType.DMA],
         compiler_params=pltpu.CompilerParams(vmem_limit_bytes=VMEM_GRANT),
         cost_estimate=pl.CostEstimate(flops=0, bytes_accessed=4 * math.prod(shape), transcendentals=0),
         name="assemble",
-    )(source, place, *sources)
+    )(source, place, *sources, lower)
 
 
 def on_device(
@@ -285,8 +298,14 @@
     everyone = lax.all_to_all(
         jnp.broadcast_to(raw[None], (peers, raw.shape[0])), "dp", split_axis=0, concat_axis=0, tiled=True
     )
-    store, down_store, everyone = lax.optimization_barrier((keyvalue_page_store, adapter_down_weight, everyone))
-    mirrored_store = swap(store, half)
+    cut = keyvalue_page_store.shape[1] // 2
+    pools = [keyvalue_page_store[:, :cut], keyvalue_page_store[:, cut:]]
+    store, down_store, everyone, pools = lax.optimization_barrier(
+        (keyvalue_page_store, adapter_down_weight, everyone, pools)
+    )
+    upper = swap(pools[0], half)
+    upper, pools[1] = lax.optimization_barrier((upper, pools[1]))
+    lower = swap(pools[1], half)
 
     page_cap = max(2, 2 * page_count // peers)
     group = everyone[jnp.arange(half, dtype=jnp.int32) ^ me]
@@ -302,7 +321,7 @@
     page_source = page_owner[:, 0] ^ me
     page_place = jnp.where(page_source % half == 0, page_local_index, earlier_alike(page_owner[:, 0]))
 
-    near = [swap(pages, i + 1) for i, pages in enumerate(serve(near_asked[1:], store, VMEM_GRANT))]
+    near = [swap(pages, i + 1) for i, pages in enumerate(serve(near_asked[1:], [store], VMEM_GRANT))]
     down_rows = down_store[adapter_asked]
     up_rows = adapter_up_weight[adapter_asked]
 
@@ -310,8 +329,10 @@
     query_base = jnp.dot(piece, query_weight, preferred_element_type=jnp.float32)
     new_cache = jnp.dot(piece, keyvalue_weight, preferred_element_type=jnp.float32).astype(jnp.bfloat16)
 
-    down_rows, mirrored_store, query_base, new_cache, near = lax.optimization_barrier(
-        (down_rows, mirrored_store, query_base, new_cache, near)
+    (last_upper,) = serve(far_asked[half - 1 :], [upper], SMALL_GRANT)
+    last_upper = swap(last_upper, half - 1)
+    down_rows, upper, lower, query_base, new_cache, near, last_upper = lax.optimization_barrier(
+        (down_rows, upper, lower, query_base, new_cache, near, last_upper)
     )
     lengths = span_token_length[0]
     ends = jnp.cumsum(lengths)
@@ -324,19 +345,20 @@
     steps = attention_steps(starts, ends, steps_total)
 
     down_sent = lax.all_to_all(down_rows, "dp", split_axis=0, concat_axis=0, tiled=True)
-    far = list(serve(far_asked[1:], mirrored_store, SMALL_GRANT))
-    far = [swap(pages, i + 1) for i, pages in enumerate(far[:-1])] + far[-1:]
-    up_rows, down_sent, far, in_slot, steps, page_source, page_place = lax.optimization_barrier(
-        (up_rows, down_sent, far, in_slot, steps, page_source, page_place)
+    far = serve(far_asked[1 : half - 1], [upper, lower], SMALL_GRANT)
+    far = [swap(pages, i + 1) for i, pages in enumerate(far)]
+    (last_lower,) = serve(far_asked[half - 1 :], [lower], SMALL_GRANT)
+    up_rows, down_sent, far, last_lower, in_slot, steps, page_source, page_place = lax.optimization_barrier(
+        (up_rows, down_sent, far, last_lower, in_slot, steps, page_source, page_place)
     )
     up_sent = lax.all_to_all(up_rows, "dp", split_axis=0, concat_axis=0, tiled=True)
-    far[-1] = swap(far[-1], half - 1)
+    last_lower = swap(last_lower, half - 1)
 
     down_part = jnp.einsum("tn,snk->tsk", tokens, down_sent, preferred_element_type=jnp.float32)
     shrink_part = jnp.sum(jnp.where(in_slot[:, :, None], down_part, 0.0), axis=1)
     shrink = lax.psum(shrink_part, "tensor").astype(jnp.bfloat16)
     spread = jnp.where(in_slot[:, :, None], shrink[:, None, :], 0).reshape(tok_rows, adapter_slots * rank)
-    prefix_pages = assemble(page_source, page_place, [store, *near, mirrored_store, *far[:-1]])
+    prefix_pages = assemble(page_source, page_place, [store, *near, upper, *far], half, lower)
 
     taken = starts[:, None] + jnp.arange(MOST, dtype=jnp.int32)[None, :]
     pick = (taken.reshape(-1, 1) == jnp.arange(tok_rows, dtype=jnp.int32)[None, :]).astype(jnp.bfloat16)
@@ -344,7 +366,7 @@
     fresh = fresh.reshape(request_count, MOST, -1)
     up = up_sent.reshape(adapter_slots * rank, q_cols)
     out = attend(
-        query_base, spread, up, fresh, prefix_pages, far[-1], page_source, page_place, peers - 1, steps
+        query_base, spread, up, fresh, prefix_pages, last_upper, last_lower, page_source, page_place, peers - 1, steps
     )
     return (out, new_cache)
 

time: 344 us -> 336 us (0.977)
  waiting for transfers between devices: 203 us -> 188 us
    all_gather x1, waiting for transfers between devices: 29.4 us -> 0.01 us  [on_device(): piece = lax.all_gather(tokens, 'tensor', axis=1, tiled=True)]
    ppermute x7 -> x9, waiting for transfers between devices: 165 us -> 180 us  [swap(): lax.ppermute(array, 'dp', [(peer, peer ^ distance) for peer in range(peer...]
    ppermute x7 -> x9, starting transfers between devices: 10.4 us -> 14.6 us  [swap(): lax.ppermute(array, 'dp', [(peer, peer ^ distance) for peer in range(peer...]
    slice x1 -> x2, local copies, waits for them, and re-layouts: 0.01 us -> 3.56 us  [the longest x1 3.56 us: on_device(): pools = [keyvalue_page_store[:, :cut], keyvalue_page_store[:, cut:]]]
    all_to_all x1, waiting for transfers between devices: 6.46 us -> 2.91 us  [on_device(): lax.all_to_all(jnp.broadcast_to(raw[None], (peers, raw.shape[0])), 'dp',...]
    pallas_call x3 -> x5, Pallas kernels: 16.3 us -> 17.3 us  [the longest x4 12.4 us: serve(): pl.pallas_call(functools.partial(serve_kernel, len(stores)), out_shape=[j...]
  transfers between devices with their start and end apart: 11 -> 13, of which waited for: 9 -> 9; matrix products, arithmetic and copies ran while one was open for 16% -> 17% of each run, Pallas kernels for 5% -> 5%
where the time goes in v19:
time: 336 us; the launch traced here: 333 us
  waiting for transfers between devices  188 us (56%)
  matrix products  33 us (10%)
  starting transfers between devices  30.3 us (9%)
  Pallas kernels  29.1 us (9%)
  local copies, waits for them, and re-layouts  20.5 us (6%)
  between operations  14.9 us (4%)
  blocking collectives  12.3 us (4%)
  other arithmetic  5.12 us (2%)
    ppermute x9, waiting for transfers between devices, swap(): lax.ppermute(array, 'dp', [(peer, peer ^ distance) for peer in range(peer...  180 us
    dot_general x1, matrix products, on_device(): jnp.dot(piece, query_weight, preferred_element_type=jnp.float32)  18.2 us
    ppermute x9, starting transfers between devices, swap(): lax.ppermute(array, 'dp', [(peer, peer ^ distance) for peer in range(peer...  14.6 us
    pallas_call x4, Pallas kernels, serve(): pl.pallas_call(functools.partial(serve_kernel, len(stores)), out_shape=[j...  12.4 us
    psum x1, blocking collectives, on_device(): shrink = lax.psum(shrink_part, 'tensor').astype(jnp.bfloat16)  12.3 us
    pallas_call x1, Pallas kernels, attend(): pl.pallas_call(functools.partial(attention_kernel, last), out_shape=jax.S...  11.8 us
    dot_general x1, matrix products, on_device(): jnp.dot(piece, keyvalue_weight, preferred_element_type=jnp.float32)  7.7 us
    all_to_all x1, starting transfers between devices, on_device(): lax.all_to_all(jnp.broadcast_to(raw[None], (peers, raw.shape[0])), 'dp',...  7.25 us
  transfers between devices with their start and end apart: 13, of which 9 were waited for; matrix products, arithmetic and copies ran while one was open for 17% of the time, Pallas kernels for 5%

profile of v19, /device:TPU:0, one launch (start us, length us, event | category | flops | bytes accessed | tf_op | source)
XLA Modules:
  0.0 333.1 jit_solution(10722907819173542249)
XLA Ops:
  7.2 0.7 all-gather.2.cloned.1.call-update
  7.9 0.8 pad_add_fusion.1
  8.7 0.6 broadcast_in_dim.106
  9.3 7.3 %all-to-all-start = ((s32[8,1,160]{2,1,0:T(1,128)}), s32[8,1,160]{2,1,0:T(1,128)S(1)}, u32[]{:S(2)}, u32[]{:S(2)}) async-start(s32[8,1,160]{2,1,0:T(1,128)} %broadcast_in_dim.106), calls=%async_computation | async-start | bytes 16384 | tf_op jit(solution)/shard_map/all_to_all | solution.py:298
  16.6 3.6 %fusion.23 = (bf16[48,32,512]{2,1,0:T(8,128)(2,1)}, bf16[48,32,512]{2,1,0:T(8,128)(2,1)S(1)}) fusion(bf16[48,64,512]{2,1,0:T(8,128)(2,1)} %refs_0_.1), kind=kLoop, calls=%fused_computation.92 | loop fusion | bytes 6291456 | tf_op jit(solution)/shard_map/slice | solution.py:302
  20.1 2.9 all-to-all-done
  23.1 0.6 collective-permute-start
  23.7 0.3 convert_reduce_fusion.1
  24.3 0.6 gather_fusion.2
  24.9 0.2 convert_reduce_fusion
  25.2 0.2 select_reduce_fusion.1
  25.4 0.6 reshape.369.asked_ref
  26.0 4.3 %serve.4 = (bf16[16,64,512]{2,1,0:T(8,128)(2,1)}, bf16[16,64,512]{2,1,0:T(8,128)(2,1)}, bf16[16,64,512]{2,1,0:T(8,128)(2,1)}) custom-call(s32[48]{0:T(128)} %reshape.369.asked_ref, bf16[48,64,512]{2,1,0:T(8,128)(2,1)} %refs_0_.1), custom_call_target="tpu_custom_call" | custom-call | bytes 6291456 | tf_op jit(solution)/shard_map/serve/pallas_call | solution.py:215
  30.3 2.2 collective-permute-start.2
  32.5 2.3 collective-permute-start.3
  34.9 6.3 %gather_fusion.1 = bf16[16,2048,64]{1,2,0:T(8,128)(2,1)} fusion(bf16[32,2048,64]{1,2,0:T(8,128)(2,1)} %param.14, s32[1024]{0:T(1024)S(1)} %pad_clamp_fusion.1), kind=kCustom, calls=%fused_computation.1 | custom fusion | bytes 8388672 | tf_op jit(solution)/shard_map/gather | solution.py:325
  41.2 51.2 %collective-permute-done.refs_0_.refs_4_ = bf16[48,32,512]{2,1,0:T(8,128)(2,1)S(1)} collective-permute-done((bf16[48,32,512]{2,1,0:T(8,128)(2,1)S(1)}, bf16[48,32,512]{2,1,0:T(8,128)(2,1)S(1)}, u32[]{:S(2)}, u32[]{:S(2)}) %collective-permute-start) | collective-permute-done | bytes 1572896 | tf_op jit(solution)/shard_map/ppermute | solution.py:293
  92.4 2.1 serve.5
  94.5 3.2 collective-permute-start.5
  97.8 18.2 %fusion.26.base_hbm = f32[512,1024]{1,0:T(8,128)} fusion(bf16[512,8192]{1,0:T(8,128)(2,1)} %all-gather.2.cloned.1.call-done, bf16[8192,1024]{1,0:T(8,128)(2,1)} %param.12), kind=kOutput, calls=%fused_computation.95 | convolution fusion | flops 8589934592 | bytes 27262976 | tf_op jit(solution)/shard_map/dot_general | solution.py:329
  116.0 7.7 %convolution_convert_fusion = bf16[512,512]{1,0:T(8,128)(2,1)} fusion(bf16[512,8192]{1,0:T(8,128)(2,1)S(1)} %copy-done.10, bf16[8192,512]{1,0:T(8,128)(2,1)} %param.13), kind=kOutput, calls=%fused_computation.11 | convolution fusion | flops 4295229440 | bytes 17301504 | tf_op jit(solution)/shard_map/dot_general | solution.py:330
  123.8 22.4 %collective-permute-done.5.last_hbm = bf16[16,32,512]{2,1,0:T(8,128)(2,1)} collective-permute-done((bf16[16,32,512]{2,1,0:T(8,128)(2,1)}, bf16[16,32,512]{2,1,0:T(8,128)(2,1)}, u32[]{:S(2)}, u32[]{:S(2)}) %collective-permute-start.5) | collective-permute-done | bytes 524320 | tf_op jit(solution)/shard_map/ppermute | solution.py:293
  146.1 17.5 %collective-permute-done.1.refs_1_.refs_0_.refs_7_ = bf16[48,32,512]{2,1,0:T(8,128)(2,1)S(1)} collective-permute-done((bf16[48,32,512]{2,1,0:T(8,128)(2,1)}, bf16[48,32,512]{2,1,0:T(8,128)(2,1)S(1)}, u32[]{:S(2)}, u32[]{:S(2)}) %collective-permute-start.1) | collective-permute-done | bytes 1572896 | tf_op jit(solution)/shard_map/ppermute | solution.py:293
  163.7 4.5 %all-to-all-start.1 = ((bf16[16,2048,64]{1,2,0:T(8,128)(2,1)}), bf16[16,2048,64]{1,2,0:T(8,128)(2,1)}, u32[]{:S(2)}, u32[]{:S(2)}) async-start(bf16[16,2048,64]{1,2,0:T(8,128)(2,1)} %gather_fusion.1), calls=%async_computation.1 | async-start | bytes 8388608 | tf_op jit(solution)/shard_map/all_to_all | solution.py:347
  168.6 0.5 slice.50
  170.1 4.7 %serve.6 = (bf16[16,64,512]{2,1,0:T(8,128)(2,1)}, bf16[16,64,512]{2,1,0:T(8,128)(2,1)}) custom-call(s32[32]{0:T(128)S(1)} %reshape.371.asked_ref, bf16[48,32,512]{2,1,0:T(8,128)(2,1)S(1)} %collective-permute-done.refs_0_.refs_4_, bf16[48,32,512]{2,1,0:T(8,128)(2,1)S(1)} %collective-permute-done.1.refs_1_.refs_0_.refs_7_), custom_call_target="tpu_custom_call" | custom-call | bytes 4194304 | tf_op jit(solution)/shard_map/serve/pallas_call | solution.py:215
  174.8 1.9 collective-permute-start.6
  176.8 1.5 collective-permute-start.7
  178.3 0.6 pad_add_fusion.steps_ref
  178.9 0.2 convert_reduce_fusion.4
  179.3 0.6 compare_select_fusion.4
  179.9 4.2 %gather_fusion = bf16[16,64,1024]{2,1,0:T(8,128)(2,1)} fusion(bf16[32,64,1024]{2,1,0:T(8,128)(2,1)} %param.15, s32[1024]{0:T(1024)S(1)} %pad_clamp_fusion.1), kind=kCustom, calls=%fused_computation | custom fusion | bytes 4194368 | tf_op jit(solution)/shard_map/gather | solution.py:326
  184.2 1.3 serve.7
  185.5 52.1 %collective-permute-done.6.refs_5_ = bf16[16,64,512]{2,1,0:T(8,128)(2,1)S(1)} collective-permute-done((bf16[16,64,512]{2,1,0:T(8,128)(2,1)}, bf16[16,64,512]{2,1,0:T(8,128)(2,1)S(1)}, u32[]{:S(2)}, u32[]{:S(2)}) %collective-permute-start.6) | collective-permute-done | bytes 1048608 | tf_op jit(solution)/shard_map/ppermute | solution.py:293
  237.5 21.3 %collective-permute-done.7.refs_6_ = bf16[16,64,512]{2,1,0:T(8,128)(2,1)} collective-permute-done((bf16[16,64,512]{2,1,0:T(8,128)(2,1)}, bf16[16,64,512]{2,1,0:T(8,128)(2,1)}, u32[]{:S(2)}, u32[]{:S(2)}) %collective-permute-start.7) | collective-permute-done | bytes 1048608 | tf_op jit(solution)/shard_map/ppermute | solution.py:293
  258.9 2.2 all-to-all-done.1
  261.1 3.8 %all-to-all-start.2 = ((bf16[16,64,1024]{2,1,0:T(8,128)(2,1)}), bf16[16,64,1024]{2,1,0:T(8,128)(2,1)S(1)}, u32[]{:S(2)}, u32[]{:S(2)}) async-start(bf16[16,64,1024]{2,1,0:T(8,128)(2,1)} %gather_fusion), calls=%async_computation.2 | async-start | bytes 4194304 | tf_op jit(solution)/shard_map/all_to_all | solution.py:354
  265.0 2.5 fusion.1
  267.5 2.9 collective-permute-start.8
  270.4 4.6 %fusion.2 = f32[512,64]{0,1:T(8,128)S(1)} fusion(bf16[16,2048,64]{1,2,0:T(8,128)(2,1)} %all-to-all-done.1, bf16[512,2048]{1,0:T(8,128)(2,1)S(1)} %copy-done.3, pred[512,16]{0,1:T(8,128)(4,1)S(1)} %iota_compare_fusion.4), kind=kOutput, calls=%fused_computation.7 | convolution fusion | flops 2148499456 | bytes 6430720 | tf_op jit(solution)/shard_map/tn,snk->tsk/dot_general | solution.py:357
  275.0 12.3 %all-reduce.1 = bf16[512,64]{0,1:T(8,128)(2,1)S(1)} all-reduce(f32[512,64]{0,1:T(8,128)S(1)} %fusion.2), channel_id=1, replica_groups=mesh['dp'=8,'tensor'=4] {'tensor'}, use_global_device_ids=true, to_apply=%region_16.17 | all-reduce | flops 32768 | bytes 196608 | tf_op jit(solution)/shard_map/psum | solution.py:359
  287.3 1.0 broadcast_select_fusion
  288.3 2.3 copy.37.spread_hbm
  290.7 4.9 %assemble.1.pages_hbm = bf16[64,64,512]{2,1,0:T(8,128)(2,1)} custom-call(s32[64]{0:T(128)} %get-tuple-element.48.source_ref, s32[64]{0:T(128)} %get-tuple-element.49.place_ref, bf16[48,64,512]{2,1,0:T(8,128)(2,1)} %refs_0_.1, bf16[16,64,512]{2,1,0:T(8,128)(2,1)} %collective-permute-done.2.refs_1_, bf16[16,64,512]{2,1,0:T(8,128)(2,1)} %collective-permute-done.3.refs_2_, ...), custom_call_target="tpu_custom_call" | custom-call | bytes 8388608 | tf_op jit(solution)/shard_map/assemble/pallas_call | solution.py:259
  295.6 15.5 %collective-permute-done.8.lower_hbm = bf16[16,32,512]{2,1,0:T(8,128)(2,1)S(1)} collective-permute-done((bf16[16,32,512]{2,1,0:T(8,128)(2,1)S(1)}, bf16[16,32,512]{2,1,0:T(8,128)(2,1)S(1)}, u32[]{:S(2)}, u32[]{:S(2)}) %collective-permute-start.8) | collective-permute-done | bytes 524320 | tf_op jit(solution)/shard_map/ppermute | solution.py:293
  311.1 2.0 all-to-all-done.2
  313.1 1.3 copy-done.2
  314.5 11.8 %attend.1 = bf16[512,1024]{1,0:T(8,128)(2,1)} custom-call(s32[4,48]{1,0:T(4,128)} %pad_add_fusion.steps_ref, s32[64]{0:T(128)} %get-tuple-element.48.source_ref, s32[64]{0:T(128)} %get-tuple-element.49.place_ref, bf16[512,1024]{1,0:T(8,128)(2,1)} %copy.37.spread_hbm, bf16[1024,1024]{1,0:T(8,128)(2,1)} %bitcast.64, f32[512,1024]{1,0:T(8,128)} %fusion.26.base_hbm, ...), custom_call_target="tpu_custom_call" | custom-call | flops 2281701376 | bytes 12582912 | tf_op jit(solution)/shard_map/attend/pallas_call | solution.py:176
  (64 shorter events, 1.8 us)
Async XLA Ops:
  7.2 90.6 %all-gather.2.cloned.1.call-start = ((), (), s32[]{:S(2)}) async-start(), calls=%async_computation.3 | async-start | bytes 10485760 | tf_op jit(solution)/shard_map/all_gather | solution.py:328
  9.3 13.8 %all-to-all-start = ((s32[8,1,160]{2,1,0:T(1,128)}), s32[8,1,160]{2,1,0:T(1,128)S(1)}, u32[]{:S(2)}, u32[]{:S(2)}) async-start(s32[8,1,160]{2,1,0:T(1,128)} %broadcast_in_dim.106), calls=%async_computation | async-start | bytes 16384 | tf_op jit(solution)/shard_map/all_to_all | solution.py:298
  23.1 69.4 %collective-permute-start = (bf16[48,32,512]{2,1,0:T(8,128)(2,1)S(1)}, bf16[48,32,512]{2,1,0:T(8,128)(2,1)S(1)}, u32[]{:S(2)}, u32[]{:S(2)}) collective-permute-start(bf16[48,32,512]{2,1,0:T(8,128)(2,1)S(1)} %get-tuple-element.34), channel_id=1, source_target_pairs={{0,16},{4,20},{8,24},{12,28},{16,0},{20,4},{24,8},{28,12},{1,17},{... | collective-permute-start | bytes 4718600 | tf_op jit(solution)/shard_map/ppermute | solution.py:293
  30.3 93.5 %collective-permute-start.2 = (bf16[16,64,512]{2,1,0:T(8,128)(2,1)}, bf16[16,64,512]{2,1,0:T(8,128)(2,1)}, u32[]{:S(2)}, u32[]{:S(2)}) collective-permute-start(bf16[16,64,512]{2,1,0:T(8,128)(2,1)} %get-tuple-element.39), channel_id=1, source_target_pairs={{0,4},{4,0},{8,12},{12,8},{16,20},{20,16},{24,28},{28,24},{1,5},{5... | collective-permute-start | bytes 3145736 | tf_op jit(solution)/shard_map/ppermute | solution.py:293
  32.5 91.2 %collective-permute-start.3 = (bf16[16,64,512]{2,1,0:T(8,128)(2,1)}, bf16[16,64,512]{2,1,0:T(8,128)(2,1)}, u32[]{:S(2)}, u32[]{:S(2)}) collective-permute-start(bf16[16,64,512]{2,1,0:T(8,128)(2,1)} %get-tuple-element.40), channel_id=1, source_target_pairs={{0,8},{4,12},{8,0},{12,4},{16,24},{20,28},{24,16},{28,20},{1,9},{5... | collective-permute-start | bytes 3145736 | tf_op jit(solution)/shard_map/ppermute | solution.py:293
  34.8 89.0 %collective-permute-start.4 = (bf16[16,64,512]{2,1,0:T(8,128)(2,1)}, bf16[16,64,512]{2,1,0:T(8,128)(2,1)}, u32[]{:S(2)}, u32[]{:S(2)}) collective-permute-start(bf16[16,64,512]{2,1,0:T(8,128)(2,1)} %get-tuple-element.41), channel_id=1, source_target_pairs={{0,12},{4,8},{8,4},{12,0},{16,28},{20,24},{24,20},{28,16},{1,13},{... | collective-permute-start | bytes 3145736 | tf_op jit(solution)/shard_map/ppermute | solution.py:293
  92.4 77.7 %copy-start = (bf16[48,32,512]{2,1,0:T(8,128)(2,1)}, bf16[48,32,512]{2,1,0:T(8,128)(2,1)S(1)}, u32[]{:S(2)}) copy-start(bf16[48,32,512]{2,1,0:T(8,128)(2,1)S(1)} %collective-permute-done.refs_0_.refs_4_) | copy-start | bytes 4718596
  92.4 71.2 %collective-permute-start.1 = (bf16[48,32,512]{2,1,0:T(8,128)(2,1)}, bf16[48,32,512]{2,1,0:T(8,128)(2,1)S(1)}, u32[]{:S(2)}, u32[]{:S(2)}) collective-permute-start(bf16[48,32,512]{2,1,0:T(8,128)(2,1)} %get-tuple-element.37), channel_id=1, source_target_pairs={{0,16},{4,20},{8,24},{12,28},{16,0},{20,4},{24,8},{28,12},{1,17},{... | collective-permute-start | bytes 4718600 | tf_op jit(solution)/shard_map/ppermute | solution.py:293
  94.5 51.6 %collective-permute-start.5 = (bf16[16,32,512]{2,1,0:T(8,128)(2,1)}, bf16[16,32,512]{2,1,0:T(8,128)(2,1)}, u32[]{:S(2)}, u32[]{:S(2)}) collective-permute-start(bf16[16,32,512]{2,1,0:T(8,128)(2,1)} %serve.5), channel_id=1, source_target_pairs={{0,12},{4,8},{8,4},{12,0},{16,28},{20,24},{24,20},{28,16},{1,13},{... | collective-permute-start | bytes 1572872 | tf_op jit(solution)/shard_map/ppermute | solution.py:293
  97.8 18.2 %copy-start.10 = (bf16[512,8192]{1,0:T(8,128)(2,1)S(1)}, bf16[512,8192]{1,0:T(8,128)(2,1)}, u32[]{:S(2)}) copy-start(bf16[512,8192]{1,0:T(8,128)(2,1)} %all-gather.2.cloned.1.call-done) | copy-start | bytes 25165828
  123.7 44.5 %copy-start.6 = (s32[1,16]{1,0:T(1,128)S(1)}, s32[1,16]{1,0:T(1,128)}, u32[]{:S(2)}) copy-start(s32[1,16]{1,0:T(1,128)} %param.17) | copy-start | bytes 196
  123.7 55.1 %copy-start.9 = (s32[16,1]{0,1:T(1,128)S(1)}, s32[16,1]{0,1:T(1,128)}, u32[]{:S(2)}) copy-start(s32[16,1]{0,1:T(1,128)} %param.18) | copy-start | bytes 196
  123.7 55.3 %copy-start.8 = (s32[64,1]{0,1:T(1,128)S(1)}, s32[64,1]{0,1:T(1,128)}, u32[]{:S(2)}) copy-start(s32[64,1]{0,1:T(1,128)} %param.20) | copy-start | bytes 772
  123.7 55.6 %copy-start.7 = (s32[64]{0:T(128)S(1)}, s32[64]{0:T(128)}, u32[]{:S(2)}) copy-start(s32[64]{0:T(128)} %param.21) | copy-start | bytes 772
  163.7 20.5 %copy-start.1 = (bf16[48,32,512]{2,1,0:T(8,128)(2,1)}, bf16[48,32,512]{2,1,0:T(8,128)(2,1)S(1)}, u32[]{:S(2)}) copy-start(bf16[48,32,512]{2,1,0:T(8,128)(2,1)S(1)} %collective-permute-done.1.refs_1_.refs_0_.refs_7_) | copy-start | bytes 4718596
  163.7 97.4 %all-to-all-start.1 = ((bf16[16,2048,64]{1,2,0:T(8,128)(2,1)}), bf16[16,2048,64]{1,2,0:T(8,128)(2,1)}, u32[]{:S(2)}, u32[]{:S(2)}) async-start(bf16[16,2048,64]{1,2,0:T(8,128)(2,1)} %gather_fusion.1), calls=%async_computation.1 | async-start | bytes 8388608 | tf_op jit(solution)/shard_map/all_to_all | solution.py:347
  174.8 62.7 %collective-permute-start.6 = (bf16[16,64,512]{2,1,0:T(8,128)(2,1)}, bf16[16,64,512]{2,1,0:T(8,128)(2,1)S(1)}, u32[]{:S(2)}, u32[]{:S(2)}) collective-permute-start(bf16[16,64,512]{2,1,0:T(8,128)(2,1)} %get-tuple-element.45), channel_id=1, source_target_pairs={{0,4},{4,0},{8,12},{12,8},{16,20},{20,16},{24,28},{28,24},{1,5},{5... | collective-permute-start | bytes 3145736 | tf_op jit(solution)/shard_map/ppermute | solution.py:293
  176.8 82.1 %collective-permute-start.7 = (bf16[16,64,512]{2,1,0:T(8,128)(2,1)}, bf16[16,64,512]{2,1,0:T(8,128)(2,1)}, u32[]{:S(2)}, u32[]{:S(2)}) collective-permute-start(bf16[16,64,512]{2,1,0:T(8,128)(2,1)} %get-tuple-element.46), channel_id=1, source_target_pairs={{0,8},{4,12},{8,0},{12,4},{16,24},{20,28},{24,16},{28,20},{1,9},{5... | collective-permute-start | bytes 3145736 | tf_op jit(solution)/shard_map/ppermute | solution.py:293
  185.4 79.5 %copy-start.11 = (bf16[512,512]{1,0:T(8,128)(2,1)S(1)}, bf16[512,512]{1,0:T(8,128)(2,1)}, u32[]{:S(2)}) copy-start(bf16[512,512]{1,0:T(8,128)(2,1)} %convolution_convert_fusion) | copy-start | bytes 1572868
  237.5 23.5 %copy-start.4 = (bf16[16,64,512]{2,1,0:T(8,128)(2,1)}, bf16[16,64,512]{2,1,0:T(8,128)(2,1)S(1)}, u32[]{:S(2)}) copy-start(bf16[16,64,512]{2,1,0:T(8,128)(2,1)S(1)} %collective-permute-done.6.refs_5_) | copy-start | bytes 3145732
  261.1 52.1 %all-to-all-start.2 = ((bf16[16,64,1024]{2,1,0:T(8,128)(2,1)}), bf16[16,64,1024]{2,1,0:T(8,128)(2,1)S(1)}, u32[]{:S(2)}, u32[]{:S(2)}) async-start(bf16[16,64,1024]{2,1,0:T(8,128)(2,1)} %gather_fusion), calls=%async_computation.2 | async-start | bytes 4194304 | tf_op jit(solution)/shard_map/all_to_all | solution.py:354
  264.9 5.6 %copy-start.3 = (bf16[512,2048]{1,0:T(8,128)(2,1)S(1)}, bf16[512,2048]{1,0:T(8,128)(2,1)}, u32[]{:S(2)}) copy-start(bf16[512,2048]{1,0:T(8,128)(2,1)} %param.11) | copy-start | bytes 6291460
  267.5 43.6 %collective-permute-start.8 = (bf16[16,32,512]{2,1,0:T(8,128)(2,1)S(1)}, bf16[16,32,512]{2,1,0:T(8,128)(2,1)S(1)}, u32[]{:S(2)}, u32[]{:S(2)}) collective-permute-start(bf16[16,32,512]{2,1,0:T(8,128)(2,1)S(1)} %serve.7), channel_id=1, source_target_pairs={{0,12},{4,8},{8,4},{12,0},{16,28},{20,24},{24,20},{28,16},{1,13},{... | collective-permute-start | bytes 1572872 | tf_op jit(solution)/shard_map/ppermute | solution.py:293
  311.1 2.0 copy-start.5
  313.1 1.3 copy-start.2
Sparse Core Ops, SparseCore 0:
  9.6 60.9 all-gather.1

commit v20 on v19

--- a/solution.py
+++ b/solution.py
@@ -13,8 +13,8 @@
 HITS = 4
 MOST = 128
 BLOCK = 16
-TOGETHER = 8
-TILE = 256
+TOGETHER = 16
+TILE = 512
 VMEM_GRANT = 60 * 1024 * 1024
 SMALL_GRANT = 16 * 1024 * 1024
 

time: 336 us -> 335 us (level)
  transfers between devices with their start and end apart: 13 -> 13, of which waited for: 9 -> 9; matrix products, arithmetic and copies ran while one was open for 17% -> 17% of each run, Pallas kernels for 5% -> 6%
where the time goes in v20:
time: 335 us; the launch traced here: 332 us
  waiting for transfers between devices  187 us (56%)
  matrix products  33 us (10%)
  Pallas kernels  30.2 us (9%)
  starting transfers between devices  29.3 us (9%)
  local copies, waits for them, and re-layouts  20.5 us (6%)
  between operations  14.9 us (4%)
  blocking collectives  12.5 us (4%)
  other arithmetic  5.12 us (2%)
    ppermute x9, waiting for transfers between devices, swap(): lax.ppermute(array, 'dp', [(peer, peer ^ distance) for peer in range(peer...  179 us
    dot_general x1, matrix products, on_device(): jnp.dot(piece, query_weight, preferred_element_type=jnp.float32)  18.2 us
    pallas_call x4, Pallas kernels, serve(): pl.pallas_call(functools.partial(serve_kernel, len(stores)), out_shape=[j...  14 us
    ppermute x9, starting transfers between devices, swap(): lax.ppermute(array, 'dp', [(peer, peer ^ distance) for peer in range(peer...  13.7 us
    psum x1, blocking collectives, on_device(): shrink = lax.psum(shrink_part, 'tensor').astype(jnp.bfloat16)  12.5 us
    pallas_call x1, Pallas kernels, attend(): pl.pallas_call(functools.partial(attention_kernel, last), out_shape=jax.S...  11.3 us
    dot_general x1, matrix products, on_device(): jnp.dot(piece, keyvalue_weight, preferred_element_type=jnp.float32)  7.7 us
    all_to_all x1, starting transfers between devices, on_device(): lax.all_to_all(jnp.broadcast_to(raw[None], (peers, raw.shape[0])), 'dp',...  7.25 us
  transfers between devices with their start and end apart: 13, of which 9 were waited for; matrix products, arithmetic and copies ran while one was open for 17% of the time, Pallas kernels for 6%

profile of v20, /device:TPU:0, one launch (start us, length us, event | category | flops | bytes accessed | tf_op | source)
XLA Modules:
  0.0 332.5 jit_solution(10710043541551284131)
XLA Ops:
  7.2 0.7 all-gather.2.cloned.1.call-update
  7.9 0.8 pad_add_fusion.1
  8.7 0.6 broadcast_in_dim.106
  9.3 7.3 %all-to-all-start = ((s32[8,1,160]{2,1,0:T(1,128)}), s32[8,1,160]{2,1,0:T(1,128)S(1)}, u32[]{:S(2)}, u32[]{:S(2)}) async-start(s32[8,1,160]{2,1,0:T(1,128)} %broadcast_in_dim.106), calls=%async_computation | async-start | bytes 16384 | tf_op jit(solution)/shard_map/all_to_all | solution.py:298
  16.6 3.6 %fusion.23 = (bf16[48,32,512]{2,1,0:T(8,128)(2,1)}, bf16[48,32,512]{2,1,0:T(8,128)(2,1)S(1)}) fusion(bf16[48,64,512]{2,1,0:T(8,128)(2,1)} %refs_0_.1), kind=kLoop, calls=%fused_computation.92 | loop fusion | bytes 6291456 | tf_op jit(solution)/shard_map/slice | solution.py:302
  20.1 2.9 all-to-all-done
  23.1 0.6 collective-permute-start
  23.7 0.3 convert_reduce_fusion.1
  24.3 0.6 gather_fusion.2
  24.9 0.2 convert_reduce_fusion
  25.2 0.2 select_reduce_fusion.1
  25.4 0.6 reshape.369.asked_ref
  26.0 5.9 %serve.4 = (bf16[16,64,512]{2,1,0:T(8,128)(2,1)}, bf16[16,64,512]{2,1,0:T(8,128)(2,1)}, bf16[16,64,512]{2,1,0:T(8,128)(2,1)}) custom-call(s32[48]{0:T(128)} %reshape.369.asked_ref, bf16[48,64,512]{2,1,0:T(8,128)(2,1)} %refs_0_.1), custom_call_target="tpu_custom_call" | custom-call | bytes 6291456 | tf_op jit(solution)/shard_map/serve/pallas_call | solution.py:215
  31.9 0.4 collective-permute-start.2
  32.2 1.7 collective-permute-start.3
  33.9 1.5 collective-permute-start.4
  35.6 6.3 %gather_fusion.1 = bf16[16,2048,64]{1,2,0:T(8,128)(2,1)} fusion(bf16[32,2048,64]{1,2,0:T(8,128)(2,1)} %param.14, s32[1024]{0:T(1024)S(1)} %pad_clamp_fusion.1), kind=kCustom, calls=%fused_computation.1 | custom fusion | bytes 8388672 | tf_op jit(solution)/shard_map/gather | solution.py:325
  41.8 50.6 %collective-permute-done.refs_0_.refs_4_ = bf16[48,32,512]{2,1,0:T(8,128)(2,1)S(1)} collective-permute-done((bf16[48,32,512]{2,1,0:T(8,128)(2,1)S(1)}, bf16[48,32,512]{2,1,0:T(8,128)(2,1)S(1)}, u32[]{:S(2)}, u32[]{:S(2)}) %collective-permute-start) | collective-permute-done | bytes 1572896 | tf_op jit(solution)/shard_map/ppermute | solution.py:293
  92.4 2.1 serve.5
  94.5 3.2 collective-permute-start.5
  97.8 18.2 %fusion.26.base_hbm = f32[512,1024]{1,0:T(8,128)} fusion(bf16[512,8192]{1,0:T(8,128)(2,1)} %all-gather.2.cloned.1.call-done, bf16[8192,1024]{1,0:T(8,128)(2,1)} %param.12), kind=kOutput, calls=%fused_computation.95 | convolution fusion | flops 8589934592 | bytes 27262976 | tf_op jit(solution)/shard_map/dot_general | solution.py:329
  116.0 7.7 %convolution_convert_fusion = bf16[512,512]{1,0:T(8,128)(2,1)} fusion(bf16[512,8192]{1,0:T(8,128)(2,1)S(1)} %copy-done.10, bf16[8192,512]{1,0:T(8,128)(2,1)} %param.13), kind=kOutput, calls=%fused_computation.11 | convolution fusion | flops 4295229440 | bytes 17301504 | tf_op jit(solution)/shard_map/dot_general | solution.py:330
  123.8 22.4 %collective-permute-done.5.last_hbm = bf16[16,32,512]{2,1,0:T(8,128)(2,1)} collective-permute-done((bf16[16,32,512]{2,1,0:T(8,128)(2,1)}, bf16[16,32,512]{2,1,0:T(8,128)(2,1)}, u32[]{:S(2)}, u32[]{:S(2)}) %collective-permute-start.5) | collective-permute-done | bytes 524320 | tf_op jit(solution)/shard_map/ppermute | solution.py:293
  146.1 17.4 %collective-permute-done.1.refs_1_.refs_0_.refs_7_ = bf16[48,32,512]{2,1,0:T(8,128)(2,1)S(1)} collective-permute-done((bf16[48,32,512]{2,1,0:T(8,128)(2,1)}, bf16[48,32,512]{2,1,0:T(8,128)(2,1)S(1)}, u32[]{:S(2)}, u32[]{:S(2)}) %collective-permute-start.1) | collective-permute-done | bytes 1572896 | tf_op jit(solution)/shard_map/ppermute | solution.py:293
  163.6 4.5 %all-to-all-start.1 = ((bf16[16,2048,64]{1,2,0:T(8,128)(2,1)}), bf16[16,2048,64]{1,2,0:T(8,128)(2,1)}, u32[]{:S(2)}, u32[]{:S(2)}) async-start(bf16[16,2048,64]{1,2,0:T(8,128)(2,1)} %gather_fusion.1), calls=%async_computation.1 | async-start | bytes 8388608 | tf_op jit(solution)/shard_map/all_to_all | solution.py:347
  168.5 0.5 slice.50
  170.0 4.7 %serve.6 = (bf16[16,64,512]{2,1,0:T(8,128)(2,1)}, bf16[16,64,512]{2,1,0:T(8,128)(2,1)}) custom-call(s32[32]{0:T(128)S(1)} %reshape.371.asked_ref, bf16[48,32,512]{2,1,0:T(8,128)(2,1)S(1)} %collective-permute-done.refs_0_.refs_4_, bf16[48,32,512]{2,1,0:T(8,128)(2,1)S(1)} %collective-permute-done.1.refs_1_.refs_0_.refs_7_), custom_call_target="tpu_custom_call" | custom-call | bytes 4194304 | tf_op jit(solution)/shard_map/serve/pallas_call | solution.py:215
  174.7 1.9 collective-permute-start.6
  176.7 1.5 collective-permute-start.7
  178.1 0.6 pad_add_fusion.steps_ref
  179.2 0.6 compare_select_fusion.4
  179.8 4.2 %gather_fusion = bf16[16,64,1024]{2,1,0:T(8,128)(2,1)} fusion(bf16[32,64,1024]{2,1,0:T(8,128)(2,1)} %param.15, s32[1024]{0:T(1024)S(1)} %pad_clamp_fusion.1), kind=kCustom, calls=%fused_computation | custom fusion | bytes 4194368 | tf_op jit(solution)/shard_map/gather | solution.py:326
  184.1 1.3 serve.7
  185.4 52.0 %collective-permute-done.6.refs_5_ = bf16[16,64,512]{2,1,0:T(8,128)(2,1)S(1)} collective-permute-done((bf16[16,64,512]{2,1,0:T(8,128)(2,1)}, bf16[16,64,512]{2,1,0:T(8,128)(2,1)S(1)}, u32[]{:S(2)}, u32[]{:S(2)}) %collective-permute-start.6) | collective-permute-done | bytes 1048608 | tf_op jit(solution)/shard_map/ppermute | solution.py:293
  237.3 21.3 %collective-permute-done.7.refs_6_ = bf16[16,64,512]{2,1,0:T(8,128)(2,1)} collective-permute-done((bf16[16,64,512]{2,1,0:T(8,128)(2,1)}, bf16[16,64,512]{2,1,0:T(8,128)(2,1)}, u32[]{:S(2)}, u32[]{:S(2)}) %collective-permute-start.7) | collective-permute-done | bytes 1048608 | tf_op jit(solution)/shard_map/ppermute | solution.py:293
  258.6 2.2 all-to-all-done.1
  260.9 3.8 %all-to-all-start.2 = ((bf16[16,64,1024]{2,1,0:T(8,128)(2,1)}), bf16[16,64,1024]{2,1,0:T(8,128)(2,1)S(1)}, u32[]{:S(2)}, u32[]{:S(2)}) async-start(bf16[16,64,1024]{2,1,0:T(8,128)(2,1)} %gather_fusion), calls=%async_computation.2 | async-start | bytes 4194304 | tf_op jit(solution)/shard_map/all_to_all | solution.py:354
  264.8 2.5 fusion.1
  267.3 2.9 collective-permute-start.8
  270.2 4.6 %fusion.2 = f32[512,64]{0,1:T(8,128)S(1)} fusion(bf16[16,2048,64]{1,2,0:T(8,128)(2,1)} %all-to-all-done.1, bf16[512,2048]{1,0:T(8,128)(2,1)S(1)} %copy-done.3, pred[512,16]{0,1:T(8,128)(4,1)S(1)} %iota_compare_fusion.4), kind=kOutput, calls=%fused_computation.7 | convolution fusion | flops 2148499456 | bytes 6430720 | tf_op jit(solution)/shard_map/tn,snk->tsk/dot_general | solution.py:357
  274.8 12.5 %all-reduce.1 = bf16[512,64]{0,1:T(8,128)(2,1)S(1)} all-reduce(f32[512,64]{0,1:T(8,128)S(1)} %fusion.2), channel_id=1, replica_groups=mesh['dp'=8,'tensor'=4] {'tensor'}, use_global_device_ids=true, to_apply=%region_16.17 | all-reduce | flops 32768 | bytes 196608 | tf_op jit(solution)/shard_map/psum | solution.py:359
  287.3 1.0 broadcast_select_fusion
  288.3 2.3 copy.37.spread_hbm
  290.7 4.9 %assemble.1.pages_hbm = bf16[64,64,512]{2,1,0:T(8,128)(2,1)} custom-call(s32[64]{0:T(128)} %get-tuple-element.48.source_ref, s32[64]{0:T(128)} %get-tuple-element.49.place_ref, bf16[48,64,512]{2,1,0:T(8,128)(2,1)} %refs_0_.1, bf16[16,64,512]{2,1,0:T(8,128)(2,1)} %collective-permute-done.2.refs_1_, bf16[16,64,512]{2,1,0:T(8,128)(2,1)} %collective-permute-done.3.refs_2_, ...), custom_call_target="tpu_custom_call" | custom-call | bytes 8388608 | tf_op jit(solution)/shard_map/assemble/pallas_call | solution.py:259
  295.6 15.3 %collective-permute-done.8.lower_hbm = bf16[16,32,512]{2,1,0:T(8,128)(2,1)S(1)} collective-permute-done((bf16[16,32,512]{2,1,0:T(8,128)(2,1)S(1)}, bf16[16,32,512]{2,1,0:T(8,128)(2,1)S(1)}, u32[]{:S(2)}, u32[]{:S(2)}) %collective-permute-start.8) | collective-permute-done | bytes 524320 | tf_op jit(solution)/shard_map/ppermute | solution.py:293
  310.9 2.0 all-to-all-done.2
  313.0 1.3 copy-done.2
  314.3 11.3 %attend.1 = bf16[512,1024]{1,0:T(8,128)(2,1)} custom-call(s32[4,48]{1,0:T(4,128)} %pad_add_fusion.steps_ref, s32[64]{0:T(128)} %get-tuple-element.48.source_ref, s32[64]{0:T(128)} %get-tuple-element.49.place_ref, bf16[512,1024]{1,0:T(8,128)(2,1)} %copy.37.spread_hbm, bf16[1024,1024]{1,0:T(8,128)(2,1)} %bitcast.64, f32[512,1024]{1,0:T(8,128)} %fusion.26.base_hbm, ...), custom_call_target="tpu_custom_call" | custom-call | flops 2281701376 | bytes 12582912 | tf_op jit(solution)/shard_map/attend/pallas_call | solution.py:176
  (64 shorter events, 1.9 us)
Async XLA Ops:
  7.2 90.6 %all-gather.2.cloned.1.call-start = ((), (), s32[]{:S(2)}) async-start(), calls=%async_computation.3 | async-start | bytes 10485760 | tf_op jit(solution)/shard_map/all_gather | solution.py:328
  9.3 13.8 %all-to-all-start = ((s32[8,1,160]{2,1,0:T(1,128)}), s32[8,1,160]{2,1,0:T(1,128)S(1)}, u32[]{:S(2)}, u32[]{:S(2)}) async-start(s32[8,1,160]{2,1,0:T(1,128)} %broadcast_in_dim.106), calls=%async_computation | async-start | bytes 16384 | tf_op jit(solution)/shard_map/all_to_all | solution.py:298
  23.1 69.4 %collective-permute-start = (bf16[48,32,512]{2,1,0:T(8,128)(2,1)S(1)}, bf16[48,32,512]{2,1,0:T(8,128)(2,1)S(1)}, u32[]{:S(2)}, u32[]{:S(2)}) collective-permute-start(bf16[48,32,512]{2,1,0:T(8,128)(2,1)S(1)} %get-tuple-element.34), channel_id=1, source_target_pairs={{0,16},{4,20},{8,24},{12,28},{16,0},{20,4},{24,8},{28,12},{1,17},{... | collective-permute-start | bytes 4718600 | tf_op jit(solution)/shard_map/ppermute | solution.py:293
  31.9 91.9 %collective-permute-start.2 = (bf16[16,64,512]{2,1,0:T(8,128)(2,1)}, bf16[16,64,512]{2,1,0:T(8,128)(2,1)}, u32[]{:S(2)}, u32[]{:S(2)}) collective-permute-start(bf16[16,64,512]{2,1,0:T(8,128)(2,1)} %get-tuple-element.39), channel_id=1, source_target_pairs={{0,4},{4,0},{8,12},{12,8},{16,20},{20,16},{24,28},{28,24},{1,5},{5... | collective-permute-start | bytes 3145736 | tf_op jit(solution)/shard_map/ppermute | solution.py:293
  32.2 91.5 %collective-permute-start.3 = (bf16[16,64,512]{2,1,0:T(8,128)(2,1)}, bf16[16,64,512]{2,1,0:T(8,128)(2,1)}, u32[]{:S(2)}, u32[]{:S(2)}) collective-permute-start(bf16[16,64,512]{2,1,0:T(8,128)(2,1)} %get-tuple-element.40), channel_id=1, source_target_pairs={{0,8},{4,12},{8,0},{12,4},{16,24},{20,28},{24,16},{28,20},{1,9},{5... | collective-permute-start | bytes 3145736 | tf_op jit(solution)/shard_map/ppermute | solution.py:293
  33.9 89.8 %collective-permute-start.4 = (bf16[16,64,512]{2,1,0:T(8,128)(2,1)}, bf16[16,64,512]{2,1,0:T(8,128)(2,1)}, u32[]{:S(2)}, u32[]{:S(2)}) collective-permute-start(bf16[16,64,512]{2,1,0:T(8,128)(2,1)} %get-tuple-element.41), channel_id=1, source_target_pairs={{0,12},{4,8},{8,4},{12,0},{16,28},{20,24},{24,20},{28,16},{1,13},{... | collective-permute-start | bytes 3145736 | tf_op jit(solution)/shard_map/ppermute | solution.py:293
  92.4 77.6 %copy-start = (bf16[48,32,512]{2,1,0:T(8,128)(2,1)}, bf16[48,32,512]{2,1,0:T(8,128)(2,1)S(1)}, u32[]{:S(2)}) copy-start(bf16[48,32,512]{2,1,0:T(8,128)(2,1)S(1)} %collective-permute-done.refs_0_.refs_4_) | copy-start | bytes 4718596
  92.4 71.1 %collective-permute-start.1 = (bf16[48,32,512]{2,1,0:T(8,128)(2,1)}, bf16[48,32,512]{2,1,0:T(8,128)(2,1)S(1)}, u32[]{:S(2)}, u32[]{:S(2)}) collective-permute-start(bf16[48,32,512]{2,1,0:T(8,128)(2,1)} %get-tuple-element.37), channel_id=1, source_target_pairs={{0,16},{4,20},{8,24},{12,28},{16,0},{20,4},{24,8},{28,12},{1,17},{... | collective-permute-start | bytes 4718600 | tf_op jit(solution)/shard_map/ppermute | solution.py:293
  94.5 51.6 %collective-permute-start.5 = (bf16[16,32,512]{2,1,0:T(8,128)(2,1)}, bf16[16,32,512]{2,1,0:T(8,128)(2,1)}, u32[]{:S(2)}, u32[]{:S(2)}) collective-permute-start(bf16[16,32,512]{2,1,0:T(8,128)(2,1)} %serve.5), channel_id=1, source_target_pairs={{0,12},{4,8},{8,4},{12,0},{16,28},{20,24},{24,20},{28,16},{1,13},{... | collective-permute-start | bytes 1572872 | tf_op jit(solution)/shard_map/ppermute | solution.py:293
  97.8 18.2 %copy-start.10 = (bf16[512,8192]{1,0:T(8,128)(2,1)S(1)}, bf16[512,8192]{1,0:T(8,128)(2,1)}, u32[]{:S(2)}) copy-start(bf16[512,8192]{1,0:T(8,128)(2,1)} %all-gather.2.cloned.1.call-done) | copy-start | bytes 25165828
  123.7 44.4 %copy-start.6 = (s32[1,16]{1,0:T(1,128)S(1)}, s32[1,16]{1,0:T(1,128)}, u32[]{:S(2)}) copy-start(s32[1,16]{1,0:T(1,128)} %param.17) | copy-start | bytes 196
  123.7 55.0 %copy-start.9 = (s32[16,1]{0,1:T(1,128)S(1)}, s32[16,1]{0,1:T(1,128)}, u32[]{:S(2)}) copy-start(s32[16,1]{0,1:T(1,128)} %param.18) | copy-start | bytes 196
  123.7 55.2 %copy-start.8 = (s32[64,1]{0,1:T(1,128)S(1)}, s32[64,1]{0,1:T(1,128)}, u32[]{:S(2)}) copy-start(s32[64,1]{0,1:T(1,128)} %param.20) | copy-start | bytes 772
  123.7 55.5 %copy-start.7 = (s32[64]{0:T(128)S(1)}, s32[64]{0:T(128)}, u32[]{:S(2)}) copy-start(s32[64]{0:T(128)} %param.21) | copy-start | bytes 772
  163.5 20.5 %copy-start.1 = (bf16[48,32,512]{2,1,0:T(8,128)(2,1)}, bf16[48,32,512]{2,1,0:T(8,128)(2,1)S(1)}, u32[]{:S(2)}) copy-start(bf16[48,32,512]{2,1,0:T(8,128)(2,1)S(1)} %collective-permute-done.1.refs_1_.refs_0_.refs_7_) | copy-start | bytes 4718596
  163.6 97.3 %all-to-all-start.1 = ((bf16[16,2048,64]{1,2,0:T(8,128)(2,1)}), bf16[16,2048,64]{1,2,0:T(8,128)(2,1)}, u32[]{:S(2)}, u32[]{:S(2)}) async-start(bf16[16,2048,64]{1,2,0:T(8,128)(2,1)} %gather_fusion.1), calls=%async_computation.1 | async-start | bytes 8388608 | tf_op jit(solution)/shard_map/all_to_all | solution.py:347
  174.7 62.6 %collective-permute-start.6 = (bf16[16,64,512]{2,1,0:T(8,128)(2,1)}, bf16[16,64,512]{2,1,0:T(8,128)(2,1)S(1)}, u32[]{:S(2)}, u32[]{:S(2)}) collective-permute-start(bf16[16,64,512]{2,1,0:T(8,128)(2,1)} %get-tuple-element.45), channel_id=1, source_target_pairs={{0,4},{4,0},{8,12},{12,8},{16,20},{20,16},{24,28},{28,24},{1,5},{5... | collective-permute-start | bytes 3145736 | tf_op jit(solution)/shard_map/ppermute | solution.py:293
  176.7 82.0 %collective-permute-start.7 = (bf16[16,64,512]{2,1,0:T(8,128)(2,1)}, bf16[16,64,512]{2,1,0:T(8,128)(2,1)}, u32[]{:S(2)}, u32[]{:S(2)}) collective-permute-start(bf16[16,64,512]{2,1,0:T(8,128)(2,1)} %get-tuple-element.46), channel_id=1, source_target_pairs={{0,8},{4,12},{8,0},{12,4},{16,24},{20,28},{24,16},{28,20},{1,9},{5... | collective-permute-start | bytes 3145736 | tf_op jit(solution)/shard_map/ppermute | solution.py:293
  185.3 79.4 %copy-start.11 = (bf16[512,512]{1,0:T(8,128)(2,1)S(1)}, bf16[512,512]{1,0:T(8,128)(2,1)}, u32[]{:S(2)}) copy-start(bf16[512,512]{1,0:T(8,128)(2,1)} %convolution_convert_fusion) | copy-start | bytes 1572868
  237.3 23.5 %copy-start.4 = (bf16[16,64,512]{2,1,0:T(8,128)(2,1)}, bf16[16,64,512]{2,1,0:T(8,128)(2,1)S(1)}, u32[]{:S(2)}) copy-start(bf16[16,64,512]{2,1,0:T(8,128)(2,1)S(1)} %collective-permute-done.6.refs_5_) | copy-start | bytes 3145732
  260.9 52.1 %all-to-all-start.2 = ((bf16[16,64,1024]{2,1,0:T(8,128)(2,1)}), bf16[16,64,1024]{2,1,0:T(8,128)(2,1)S(1)}, u32[]{:S(2)}, u32[]{:S(2)}) async-start(bf16[16,64,1024]{2,1,0:T(8,128)(2,1)} %gather_fusion), calls=%async_computation.2 | async-start | bytes 4194304 | tf_op jit(solution)/shard_map/all_to_all | solution.py:354
  264.7 5.6 %copy-start.3 = (bf16[512,2048]{1,0:T(8,128)(2,1)S(1)}, bf16[512,2048]{1,0:T(8,128)(2,1)}, u32[]{:S(2)}) copy-start(bf16[512,2048]{1,0:T(8,128)(2,1)} %param.11) | copy-start | bytes 6291460
  267.3 43.6 %collective-permute-start.8 = (bf16[16,32,512]{2,1,0:T(8,128)(2,1)S(1)}, bf16[16,32,512]{2,1,0:T(8,128)(2,1)S(1)}, u32[]{:S(2)}, u32[]{:S(2)}) collective-permute-start(bf16[16,32,512]{2,1,0:T(8,128)(2,1)S(1)} %serve.7), channel_id=1, source_target_pairs={{0,12},{4,8},{8,4},{12,0},{16,28},{20,24},{24,20},{28,16},{1,13},{... | collective-permute-start | bytes 1572872 | tf_op jit(solution)/shard_map/ppermute | solution.py:293
  310.9 2.0 copy-start.5
  313.0 1.3 copy-start.2
Sparse Core Ops, SparseCore 0:
  9.6 60.9 all-gather.1
